TPU v7x, 128 devices: a whole 4x4x4 slice. The times are simulated.
128 devices in a mesh: gx: 8 (over y, core), gy: 16 (over x, z).
Axes of the slice: x: 4, y: 4, z: 4, core: 2. Of those that a mesh axis runs over, the one named last changes fastest.
Arguments:
- level_input: bfloat16 [32, 128, 64, 64], P('gx', 'gy'), may hold values from -6 to 6
- weight_upper: bfloat16 [3, 3, 3, 64, 64], replicated, may hold values from -0.15625 to 0.15625
- weight_deep: bfloat16 [3, 3, 3, 64, 128], replicated, may hold values from -0.15625 to 0.15625
- deep_cotangent: bfloat16 [16, 64, 64, 128], P('gx', 'gy'), may hold values from -6 to 6
Outputs:
- input_grad: bfloat16 [32, 128, 64, 64], P('gx', 'gy')
- upper_weight_grad: float32 [3, 3, 3, 64, 64], replicated
- deep_weight_grad: float32 [3, 3, 3, 64, 128], replicated
All inputs are finite; a program needn't handle non-finite values.
Results may differ from a plain program's by a relative error of at most 0.015.
Values may be sent and summed in bfloat16 or wider, within the bound.
No kernel may reach another device: no remote copies, remote signals or barrier semaphores. Data moves between devices by JAX's collectives and lax.ppermute only.
A program may use at most 128 MiB of HBM per device.

v0:
```python
import math

import jax
import jax.numpy as jnp
from jax import lax
from jax.sharding import PartitionSpec as P


def extended(cells, sides, width):
    for axis, dim in sides:
        count = lax.axis_size(axis)
        ends = count - 1
        head = lax.slice_in_dim(cells, 0, width, axis=dim)
        tail = lax.slice_in_dim(cells, cells.shape[dim] - width, cells.shape[dim], axis=dim)
        cells = jnp.concatenate(
            [
                lax.ppermute(tail, axis, [(i, (i + 1) % count) for i in range(ends)]),
                cells,
                lax.ppermute(head, axis, [((i + 1) % count, i) for i in range(ends)]),
            ],
            axis=dim,
        )
    return cells


def pad_depth(field):
    return jnp.pad(field, ((0, 0), (0, 0), (1, 1), (0, 0)))


def conv_forward(padded, weight):
    size_x, size_y, size_z = (padded.shape[0] - 2, padded.shape[1] - 2, padded.shape[2] - 2)
    total = jnp.zeros((size_x * size_y * size_z, weight.shape[4]), jnp.float32)
    for shift_x in range(3):
        for shift_y in range(3):
            for shift_z in range(3):
                window = padded[
                    shift_x : shift_x + size_x,
                    shift_y : shift_y + size_y,
                    shift_z : shift_z + size_z,
                ]
                total = total + jnp.dot(
                    window.reshape(-1, weight.shape[3]),
                    weight[shift_x, shift_y, shift_z],
                    preferred_element_type=jnp.float32,
                )
    return total.reshape(size_x, size_y, size_z, weight.shape[4])


def conv_transpose(padded, weight):
    size_x, size_y, size_z = (padded.shape[0] - 2, padded.shape[1] - 2, padded.shape[2] - 2)
    total = jnp.zeros((size_x * size_y * size_z, weight.shape[3]), jnp.float32)
    for shift_x in range(3):
        for shift_y in range(3):
            for shift_z in range(3):
                window = padded[
                    2 - shift_x : 2 - shift_x + size_x,
                    2 - shift_y : 2 - shift_y + size_y,
                    2 - shift_z : 2 - shift_z + size_z,
                ]
                total = total + jnp.dot(
                    window.reshape(-1, weight.shape[4]),
                    weight[shift_x, shift_y, shift_z].T,
                    preferred_element_type=jnp.float32,
                )
    return total.reshape(size_x, size_y, size_z, weight.shape[3])


def kernel_grad(padded, grad):
    size_x, size_y, size_z = (grad.shape[0], grad.shape[1], grad.shape[2])
    flat_grad = grad.reshape(-1, grad.shape[3])
    pieces = []
    for shift_x in range(3):
        for shift_y in range(3):
            for shift_z in range(3):
                window = padded[
                    shift_x : shift_x + size_x,
                    shift_y : shift_y + size_y,
                    shift_z : shift_z + size_z,
                ]
                pieces.append(
                    lax.dot_general(
                        window.reshape(-1, padded.shape[3]),
                        flat_grad,
                        (((0,), (0,)), ((), ())),
                        preferred_element_type=jnp.float32,
                    )
                )
    return jnp.stack(pieces).reshape(3, 3, 3, padded.shape[3], grad.shape[3])


def pool_relu(pre):
    size_x, size_y, size_z, chans = pre.shape
    active = (pre * jax.nn.sigmoid(pre)).reshape(size_x // 2, 2, size_y // 2, 2, size_z, chans)
    return 0.25 * jnp.sum(active, axis=(1, 3))


def spread_back(grad, pre):
    size_x, size_y, size_z, chans = pre.shape
    wide = jnp.broadcast_to(
        grad[:, None, :, None], (size_x // 2, 2, size_y // 2, 2, size_z, chans)
    ).reshape(pre.shape)
    sig = jax.nn.sigmoid(pre)
    return 0.25 * wide * (sig * (1.0 + pre * (1.0 - sig)))


def local(level_input, weight_upper, weight_deep, deep_cotangent):
    tiles = lax.axis_size("gx") * lax.axis_size("gy")
    upper_scale = 1.0 / math.sqrt(
        level_input.shape[0] * level_input.shape[1] * level_input.shape[2] * tiles
    )
    deep_scale = 1.0 / math.sqrt(
        deep_cotangent.shape[0] * deep_cotangent.shape[1] * deep_cotangent.shape[2] * tiles
    )
    padded = pad_depth(extended(level_input, (("gx", 0), ("gy", 1)), 1))
    pre = conv_forward(padded, weight_upper)
    pooled = pool_relu(pre).astype(jnp.bfloat16)
    pooled_padded = pad_depth(extended(pooled, (("gx", 0), ("gy", 1)), 1))
    cotangent_padded = pad_depth(extended(deep_cotangent, (("gx", 0), ("gy", 1)), 1))
    deep_terms = kernel_grad(pooled_padded, deep_cotangent)
    pooled_grad = conv_transpose(cotangent_padded, weight_deep).astype(jnp.bfloat16)
    pre_grad = spread_back(pooled_grad.astype(jnp.float32), pre).astype(jnp.bfloat16)
    grad_padded = pad_depth(extended(pre_grad, (("gx", 0), ("gy", 1)), 1))
    input_grad = conv_transpose(grad_padded, weight_upper).astype(jnp.bfloat16)
    upper_terms = kernel_grad(padded, pre_grad)
    upper_total, deep_total = lax.psum((upper_terms, deep_terms), ("gx", "gy"))
    return (input_grad, upper_total * upper_scale, deep_total * deep_scale)


def solution(mesh):
    placed = (P("gx", "gy", None, None), P(), P(), P("gx", "gy", None, None))
    return jax.shard_map(
        local,
        mesh=mesh,
        in_specs=placed,
        out_specs=(P("gx", "gy", None, None), P(), P()),
        check_vma=False,
    )
```

profile of v0, /device:TPU:1, one launch (start us, length us, event | category | flops | bytes accessed | tf_op | source)
XLA Modules:
  0.0 371.8 jit_solution(17900548422133207353)
XLA Ops:
  8.6 4.6 %collective-permute-start.4 = (bf16[1,8,64,64]{2,3,1,0:T(8,128)(2,1)S(1)}, bf16[1,8,64,64]{2,3,1,0:T(8,128)(2,1)S(1)}, u32[]{:S(2)}, u32[]{:S(2)}) collective-permute-start(bf16[1,8,64,64]{2,3,1,0:T(8,128)(2,1)S(1)} %get-tuple-element.76), channel_id=1, source_target_pairs={{0,16},{16,32},{32,48},{48,64},{64,80},{80,96},{96,112},{1,17},{17... | collective-permute-start | bytes 196616 | tf_op jit(solution)/shard_map/ppermute | solution.py:17
  13.2 1.9 collective-permute-start.5
  15.2 3.6 collective-permute-start
  18.8 1.9 collective-permute-start.1
  20.8 3.5 collective-permute-start.6
  31.2 4.2 %collective-permute-start.2 = (bf16[4,1,64,128]{3,2,1,0:T(8,128)(2,1)}, bf16[4,1,64,128]{3,2,1,0:T(8,128)(2,1)S(1)}, u32[]{:S(2)}, u32[]{:S(2)}) collective-permute-start(bf16[4,1,64,128]{3,2,1,0:T(8,128)(2,1)} %get-tuple-element.107), channel_id=1, source_target_pairs={{0,1},{1,2},{2,3},{3,4},{4,5},{5,6},{6,7},{7,8},{8,9},{9,10},{10,1... | collective-permute-start | bytes 196616 | tf_op jit(solution)/shard_map/ppermute | solution.py:17
  40.9 4.4 %fusion.320 = (bf16[4,8,64,64]{2,3,1,0:T(8,128)(2,1)S(1)}, bf16[4,8,64,64]{2,3,1,0:T(8,128)(2,1)}, bf16[4,8,64,64]{2,3,1,0:T(8,128)(2,1)}, bf16[4,8,64,64]{2,3,1...) fusion(bf16[6,10,66,64]{2,3,1,0:T(8,128)(2,1)S(1)} %select_maxi, ...), kind=kLoop, calls=%fused_computation.500 | loop fusion | bytes 9437184 | tf_op jit(solution)/shard_map/slice | solution.py:36
  46.4 2.2 reshape.364
  48.6 2.2 copy.61
  50.8 2.2 reshape.366
  53.0 2.2 copy.62
  55.1 2.2 reshape.367
  58.6 2.2 reshape.369
  60.8 2.3 copy.66
  63.1 2.2 reshape.370
  66.4 2.3 reshape.371
  69.9 2.2 reshape.372
  72.1 2.2 copy.69
  74.3 2.2 reshape.373
  77.6 2.3 reshape.374
  81.0 2.2 reshape.375
  83.2 2.2 copy.72
  85.5 2.2 reshape.376
  88.8 2.2 reshape.378
  91.0 2.2 copy.74
  93.2 2.2 reshape.379
  96.6 2.3 reshape.380
  100.0 2.3 reshape.381
  102.3 2.2 copy.77
  104.6 2.2 reshape.382
  108.0 2.2 reshape.383
  110.1 2.2 copy.79
  112.4 2.2 reshape.384
  115.7 2.2 reshape.385
  117.9 2.2 copy.83
  120.2 2.2 reshape.387
  123.5 2.2 reshape.388
  145.2 3.2 fusion.71
  150.5 4.3 %collective-permute-start.12 = (bf16[1,4,64,64]{2,3,1,0:T(8,128)(2,1)}, bf16[1,4,64,64]{2,3,1,0:T(8,128)(2,1)}, u32[]{:S(2)}, u32[]{:S(2)}) collective-permute-start(bf16[1,4,64,64]{2,3,1,0:T(8,128)(2,1)} %get-tuple-element.109), channel_id=1, source_target_pairs={{0,16},{16,32},{32,48},{48,64},{64,80},{80,96},{96,112},{1,17},{17... | collective-permute-start | bytes 98312 | tf_op jit(solution)/shard_map/ppermute | solution.py:17
  154.8 1.9 collective-permute-start.13
  177.2 4.3 %collective-permute-start.14 = (bf16[4,1,64,64]{2,3,1,0:T(8,128)(2,1)S(1)}, bf16[4,1,64,64]{2,3,1,0:T(8,128)(2,1)S(1)}, u32[]{:S(2)}, u32[]{:S(2)}) collective-permute-start(bf16[4,1,64,64]{2,3,1,0:T(8,128)(2,1)S(1)} %get-tuple-element.102), channel_id=1, source_target_pairs={{0,1},{1,2},{2,3},{3,4},{4,5},{5,6},{6,7},{7,8},{8,9},{9,10},{10,1... | collective-permute-start | bytes 98312 | tf_op jit(solution)/shard_map/ppermute | solution.py:17
  183.5 3.9 %collective-permute-start.8 = (bf16[1,8,64,64]{3,2,1,0:T(8,128)(2,1)}, bf16[1,8,64,64]{3,2,1,0:T(8,128)(2,1)S(1)}, u32[]{:S(2)}, u32[]{:S(2)}) collective-permute-start(bf16[1,8,64,64]{3,2,1,0:T(8,128)(2,1)} %get-tuple-element.72), channel_id=1, source_target_pairs={{0,16},{16,32},{32,48},{48,64},{64,80},{80,96},{96,112},{1,17},{17... | collective-permute-start | bytes 196616 | tf_op jit(solution)/shard_map/ppermute | solution.py:17
  187.4 2.2 collective-permute-start.9
  205.3 4.3 %collective-permute-start.10 = (bf16[6,1,64,64]{3,2,1,0:T(8,128)(2,1)S(1)}, bf16[6,1,64,64]{3,2,1,0:T(8,128)(2,1)S(1)}, u32[]{:S(2)}, u32[]{:S(2)}) collective-permute-start(bf16[6,1,64,64]{3,2,1,0:T(8,128)(2,1)S(1)} %get-tuple-element.64), channel_id=1, source_target_pairs={{0,1},{1,2},{2,3},{3,4},{4,5},{5,6},{6,7},{7,8},{8,9},{9,10},{10,1... | collective-permute-start | bytes 147464 | tf_op jit(solution)/shard_map/ppermute | solution.py:17
  211.2 3.9 %collective-permute-done.11 = bf16[6,1,64,64]{3,2,1,0:T(8,128)(2,1)S(1)} collective-permute-done((bf16[6,1,64,64]{3,2,1,0:T(8,128)(2,1)S(1)}, bf16[6,1,64,64]{3,2,1,0:T(8,128)(2,1)S(1)}, u32[]{:S(2)}, u32[]{:S(2)}) %collective-permute-start.11) | collective-permute-done | bytes 49184 | tf_op jit(solution)/shard_map/ppermute | solution.py:19
  216.2 2.7 fusion.319
  229.1 132.1 %all-reduce.7.cloned.1.call-done = (f32[3,3,3,64,64]{4,3,2,1,0:T(8,128)}, f32[3,3,3,64,128]{4,3,2,1,0:T(8,128)}) async-done(((f32[3,3,3,64,64]{4,3,2,1,0:T(8,128)}, f32[3,3,3,64,128]{4,3,2,1,0:T(8,128)}), (f32[3,3,3,64,64]{4,3,2,1,0:T(8,128)}, f32[3,3,3,64,128]{4,3,2,1,0:T(8,128)})) %all-reduce.7.cloned.1.call-update) | async-done | bytes 1327120 | tf_op jit(solution)/shard_map/psum | solution.py:125
  361.2 2.3 broadcast_multiply_fusion
  (326 shorter events, 100.2 us)
Async XLA Ops:
  7.2 8.0 %copy-start = (bf16[2,4,64,128]{3,2,1,0:T(8,128)(2,1)S(1)}, bf16[2,4,64,128]{3,2,1,0:T(8,128)(2,1)}, u32[]{:S(2)}) copy-start(bf16[2,4,64,128]{3,2,1,0:T(8,128)(2,1)} %param.7) | copy-start | bytes 393220
  7.2 354.1 %all-reduce.7.cloned.1.call-start = ((), (), s32[]{:S(2)}) async-start(), calls=%async_computation | async-start | bytes 3538944 | tf_op jit(solution)/shard_map/psum | solution.py:125
  8.6 12.1 %collective-permute-start.4 = (bf16[1,8,64,64]{2,3,1,0:T(8,128)(2,1)S(1)}, bf16[1,8,64,64]{2,3,1,0:T(8,128)(2,1)S(1)}, u32[]{:S(2)}, u32[]{:S(2)}) collective-permute-start(bf16[1,8,64,64]{2,3,1,0:T(8,128)(2,1)S(1)} %get-tuple-element.76), channel_id=1, source_target_pairs={{0,16},{16,32},{32,48},{48,64},{64,80},{80,96},{96,112},{1,17},{17... | collective-permute-start | bytes 196616 | tf_op jit(solution)/shard_map/ppermute | solution.py:17
  13.2 7.5 %collective-permute-start.5 = (bf16[1,8,64,64]{2,3,1,0:T(8,128)(2,1)S(1)}, bf16[1,8,64,64]{2,3,1,0:T(8,128)(2,1)S(1)}, u32[]{:S(2)}, u32[]{:S(2)}) collective-permute-start(bf16[1,8,64,64]{2,3,1,0:T(8,128)(2,1)S(1)} %get-tuple-element.77), channel_id=1, source_target_pairs={{16,0},{32,16},{48,32},{64,48},{80,64},{96,80},{112,96},{17,1},{33... | collective-permute-start | bytes 196616 | tf_op jit(solution)/shard_map/ppermute | solution.py:19
  15.2 10.5 %collective-permute-start = (bf16[1,4,64,128]{3,2,1,0:T(8,128)(2,1)S(1)}, bf16[1,4,64,128]{3,2,1,0:T(8,128)(2,1)S(1)}, u32[]{:S(2)}, u32[]{:S(2)}) collective-permute-start(bf16[1,4,64,128]{3,2,1,0:T(8,128)(2,1)S(1)} %get-tuple-element.115), channel_id=1, source_target_pairs={{0,16},{16,32},{32,48},{48,64},{64,80},{80,96},{96,112},{1,17},{17... | collective-permute-start | bytes 196616 | tf_op jit(solution)/shard_map/ppermute | solution.py:17
  18.8 6.9 %collective-permute-start.1 = (bf16[1,4,64,128]{3,2,1,0:T(8,128)(2,1)S(1)}, bf16[1,4,64,128]{3,2,1,0:T(8,128)(2,1)S(1)}, u32[]{:S(2)}, u32[]{:S(2)}) collective-permute-start(bf16[1,4,64,128]{3,2,1,0:T(8,128)(2,1)S(1)} %get-tuple-element.114), channel_id=1, source_target_pairs={{16,0},{32,16},{48,32},{64,48},{80,64},{96,80},{112,96},{17,1},{33... | collective-permute-start | bytes 196616 | tf_op jit(solution)/shard_map/ppermute | solution.py:19
  20.8 19.5 %copy-start.15 = (bf16[1,8,64,64]{2,3,1,0:T(8,128)(2,1)}, bf16[1,8,64,64]{2,3,1,0:T(8,128)(2,1)S(1)}, u32[]{:S(2)}) copy-start(bf16[1,8,64,64]{2,3,1,0:T(8,128)(2,1)S(1)} %collective-permute-done.5) | copy-start | bytes 196612
  20.8 15.8 %collective-permute-start.6 = (bf16[6,1,64,64]{2,3,1,0:T(8,128)(2,1)S(1)}, bf16[6,1,64,64]{2,3,1,0:T(8,128)(2,1)S(1)}, u32[]{:S(2)}, u32[]{:S(2)}) collective-permute-start(bf16[6,1,64,64]{2,3,1,0:T(8,128)(2,1)S(1)} %get-tuple-element.68), channel_id=1, source_target_pairs={{0,1},{1,2},{2,3},{3,4},{4,5},{5,6},{6,7},{7,8},{8,9},{9,10},{10,1... | collective-permute-start | bytes 147464 | tf_op jit(solution)/shard_map/ppermute | solution.py:17
  24.4 12.3 %collective-permute-start.7 = (bf16[6,1,64,64]{2,3,1,0:T(8,128)(2,1)S(1)}, bf16[6,1,64,64]{2,3,1,0:T(8,128)(2,1)S(1)}, u32[]{:S(2)}, u32[]{:S(2)}) collective-permute-start(bf16[6,1,64,64]{2,3,1,0:T(8,128)(2,1)S(1)} %get-tuple-element.69), channel_id=1, source_target_pairs={{1,0},{2,1},{3,2},{4,3},{5,4},{6,5},{7,6},{8,7},{9,8},{10,9},{11,1... | collective-permute-start | bytes 147464 | tf_op jit(solution)/shard_map/ppermute | solution.py:19
  31.2 125.5 %collective-permute-start.2 = (bf16[4,1,64,128]{3,2,1,0:T(8,128)(2,1)}, bf16[4,1,64,128]{3,2,1,0:T(8,128)(2,1)S(1)}, u32[]{:S(2)}, u32[]{:S(2)}) collective-permute-start(bf16[4,1,64,128]{3,2,1,0:T(8,128)(2,1)} %get-tuple-element.107), channel_id=1, source_target_pairs={{0,1},{1,2},{2,3},{3,4},{4,5},{5,6},{6,7},{7,8},{8,9},{9,10},{10,1... | collective-permute-start | bytes 196616 | tf_op jit(solution)/shard_map/ppermute | solution.py:17
  35.3 121.4 %collective-permute-start.3 = (bf16[4,1,64,128]{3,2,1,0:T(8,128)(2,1)}, bf16[4,1,64,128]{3,2,1,0:T(8,128)(2,1)}, u32[]{:S(2)}, u32[]{:S(2)}) collective-permute-start(bf16[4,1,64,128]{3,2,1,0:T(8,128)(2,1)} %get-tuple-element.108), channel_id=1, source_target_pairs={{1,0},{2,1},{3,2},{4,3},{5,4},{6,5},{7,6},{8,7},{9,8},{10,9},{11,1... | collective-permute-start | bytes 196616 | tf_op jit(solution)/shard_map/ppermute | solution.py:19
  36.6 3.6 copy-start.54
  36.7 3.6 copy-start.52
  60.8 4.6 %copy-start.12 = (bf16[4,8,64,64]{2,3,1,0:T(8,128)(2,1)S(1)}, bf16[4,8,64,64]{2,3,1,0:T(8,128)(2,1)}, u32[]{:S(2)}) copy-start(bf16[4,8,64,64]{2,3,1,0:T(8,128)(2,1)} %get-tuple-element.58) | copy-start | bytes 786436
  66.4 2.3 copy-start.14
  72.1 4.4 %copy-start.10 = (bf16[4,8,64,64]{2,3,1,0:T(8,128)(2,1)S(1)}, bf16[4,8,64,64]{2,3,1,0:T(8,128)(2,1)}, u32[]{:S(2)}) copy-start(bf16[4,8,64,64]{2,3,1,0:T(8,128)(2,1)} %get-tuple-element.117) | copy-start | bytes 786436
  77.6 2.3 copy-start.13
  83.2 4.4 %copy-start.11 = (bf16[4,8,64,64]{2,3,1,0:T(8,128)(2,1)S(1)}, bf16[4,8,64,64]{2,3,1,0:T(8,128)(2,1)}, u32[]{:S(2)}) copy-start(bf16[4,8,64,64]{2,3,1,0:T(8,128)(2,1)} %get-tuple-element.40) | copy-start | bytes 786436
  91.0 4.4 %copy-start.7 = (bf16[4,8,64,64]{2,3,1,0:T(8,128)(2,1)S(1)}, bf16[4,8,64,64]{2,3,1,0:T(8,128)(2,1)}, u32[]{:S(2)}) copy-start(bf16[4,8,64,64]{2,3,1,0:T(8,128)(2,1)} %get-tuple-element.57) | copy-start | bytes 786436
  96.6 2.3 copy-start.9
  102.3 4.5 %copy-start.5 = (bf16[4,8,64,64]{2,3,1,0:T(8,128)(2,1)S(1)}, bf16[4,8,64,64]{2,3,1,0:T(8,128)(2,1)}, u32[]{:S(2)}) copy-start(bf16[4,8,64,64]{2,3,1,0:T(8,128)(2,1)} %get-tuple-element.118) | copy-start | bytes 786436
  110.1 4.5 %copy-start.8 = (bf16[4,8,64,64]{2,3,1,0:T(8,128)(2,1)S(1)}, bf16[4,8,64,64]{2,3,1,0:T(8,128)(2,1)}, u32[]{:S(2)}) copy-start(bf16[4,8,64,64]{2,3,1,0:T(8,128)(2,1)} %get-tuple-element.35) | copy-start | bytes 786436
  117.9 4.4 %copy-start.6 = (bf16[4,8,64,64]{2,3,1,0:T(8,128)(2,1)S(1)}, bf16[4,8,64,64]{2,3,1,0:T(8,128)(2,1)}, u32[]{:S(2)}) copy-start(bf16[4,8,64,64]{2,3,1,0:T(8,128)(2,1)} %get-tuple-element.33) | copy-start | bytes 786436
  127.2 1.5 copy-start.19
  128.8 2.5 copy-start.24
  130.0 1.6 copy-start.26
  131.6 1.0 copy-start.23
  135.5 1.1 copy-start.1
  136.4 1.0 copy-start.32
  136.5 1.1 copy-start.34
  140.6 1.0 copy-start.39
  148.5 8.3 %copy-start.18 = (bf16[4,4,64,128]{3,2,1,0:T(8,128)(2,1)S(1)}, bf16[4,4,64,128]{3,2,1,0:T(8,128)(2,1)}, u32[]{:S(2)}) copy-start(bf16[4,4,64,128]{3,2,1,0:T(8,128)(2,1)} %copy-done.17) | copy-start | bytes 786436
  150.5 25.8 %collective-permute-start.12 = (bf16[1,4,64,64]{2,3,1,0:T(8,128)(2,1)}, bf16[1,4,64,64]{2,3,1,0:T(8,128)(2,1)}, u32[]{:S(2)}, u32[]{:S(2)}) collective-permute-start(bf16[1,4,64,64]{2,3,1,0:T(8,128)(2,1)} %get-tuple-element.109), channel_id=1, source_target_pairs={{0,16},{16,32},{32,48},{48,64},{64,80},{80,96},{96,112},{1,17},{17... | collective-permute-start | bytes 98312 | tf_op jit(solution)/shard_map/ppermute | solution.py:17
  154.8 21.5 %collective-permute-start.13 = (bf16[1,4,64,64]{2,3,1,0:T(8,128)(2,1)}, bf16[1,4,64,64]{2,3,1,0:T(8,128)(2,1)}, u32[]{:S(2)}, u32[]{:S(2)}) collective-permute-start(bf16[1,4,64,64]{2,3,1,0:T(8,128)(2,1)} %get-tuple-element.110), channel_id=1, source_target_pairs={{16,0},{32,16},{48,32},{64,48},{80,64},{96,80},{112,96},{17,1},{33... | collective-permute-start | bytes 98312 | tf_op jit(solution)/shard_map/ppermute | solution.py:19
  157.7 1.0 copy-start.51
  159.6 1.4 copy-start.50
  164.8 1.2 copy-start.2
  175.8 13.8 %copy-start.4 = (f32[2,4,64,64]{2,1,0,3:T(4,128)S(1)}, f32[2,4,64,64]{2,1,0,3:T(4,128)}, u32[]{:S(2)}) copy-start(f32[2,4,64,64]{2,1,0,3:T(4,128)} %copy-done.3) | copy-start | bytes 393220
  176.2 11.2 %copy-start.47 = (f32[27,64,64]{2,1,0:T(8,128)}, f32[27,64,64]{2,1,0:T(8,128)S(1)}, u32[]{:S(2)}) copy-start(f32[27,64,64]{2,1,0:T(8,128)S(1)} %fusion.41) | copy-start | bytes 1327108
  177.2 14.5 %collective-permute-start.14 = (bf16[4,1,64,64]{2,3,1,0:T(8,128)(2,1)S(1)}, bf16[4,1,64,64]{2,3,1,0:T(8,128)(2,1)S(1)}, u32[]{:S(2)}, u32[]{:S(2)}) collective-permute-start(bf16[4,1,64,64]{2,3,1,0:T(8,128)(2,1)S(1)} %get-tuple-element.102), channel_id=1, source_target_pairs={{0,1},{1,2},{2,3},{3,4},{4,5},{5,6},{6,7},{7,8},{8,9},{9,10},{10,1... | collective-permute-start | bytes 98312 | tf_op jit(solution)/shard_map/ppermute | solution.py:17
  181.5 10.2 %collective-permute-start.15 = (bf16[4,1,64,64]{2,3,1,0:T(8,128)(2,1)S(1)}, bf16[4,1,64,64]{2,3,1,0:T(8,128)(2,1)S(1)}, u32[]{:S(2)}, u32[]{:S(2)}) collective-permute-start(bf16[4,1,64,64]{2,3,1,0:T(8,128)(2,1)S(1)} %get-tuple-element.103), channel_id=1, source_target_pairs={{1,0},{2,1},{3,2},{4,3},{5,4},{6,5},{7,6},{8,7},{9,8},{10,9},{11,1... | collective-permute-start | bytes 98312 | tf_op jit(solution)/shard_map/ppermute | solution.py:19
  183.5 21.7 %collective-permute-start.8 = (bf16[1,8,64,64]{3,2,1,0:T(8,128)(2,1)}, bf16[1,8,64,64]{3,2,1,0:T(8,128)(2,1)S(1)}, u32[]{:S(2)}, u32[]{:S(2)}) collective-permute-start(bf16[1,8,64,64]{3,2,1,0:T(8,128)(2,1)} %get-tuple-element.72), channel_id=1, source_target_pairs={{0,16},{16,32},{32,48},{48,64},{64,80},{80,96},{96,112},{1,17},{17... | collective-permute-start | bytes 196616 | tf_op jit(solution)/shard_map/ppermute | solution.py:17
  187.4 17.8 %collective-permute-start.9 = (bf16[1,8,64,64]{3,2,1,0:T(8,128)(2,1)S(1)}, bf16[1,8,64,64]{3,2,1,0:T(8,128)(2,1)S(1)}, u32[]{:S(2)}, u32[]{:S(2)}) collective-permute-start(bf16[1,8,64,64]{3,2,1,0:T(8,128)(2,1)S(1)} %get-tuple-element.73), channel_id=1, source_target_pairs={{16,0},{32,16},{48,32},{64,48},{80,64},{96,80},{112,96},{17,1},{33... | collective-permute-start | bytes 196616 | tf_op jit(solution)/shard_map/ppermute | solution.py:19
  205.3 5.9 %collective-permute-start.10 = (bf16[6,1,64,64]{3,2,1,0:T(8,128)(2,1)S(1)}, bf16[6,1,64,64]{3,2,1,0:T(8,128)(2,1)S(1)}, u32[]{:S(2)}, u32[]{:S(2)}) collective-permute-start(bf16[6,1,64,64]{3,2,1,0:T(8,128)(2,1)S(1)} %get-tuple-element.64), channel_id=1, source_target_pairs={{0,1},{1,2},{2,3},{3,4},{4,5},{5,6},{6,7},{7,8},{8,9},{9,10},{10,1... | collective-permute-start | bytes 147464 | tf_op jit(solution)/shard_map/ppermute | solution.py:17
  209.6 5.5 %collective-permute-start.11 = (bf16[6,1,64,64]{3,2,1,0:T(8,128)(2,1)S(1)}, bf16[6,1,64,64]{3,2,1,0:T(8,128)(2,1)S(1)}, u32[]{:S(2)}, u32[]{:S(2)}) collective-permute-start(bf16[6,1,64,64]{3,2,1,0:T(8,128)(2,1)S(1)} %get-tuple-element.65), channel_id=1, source_target_pairs={{1,0},{2,1},{3,2},{4,3},{5,4},{6,5},{7,6},{8,7},{9,8},{10,9},{11,1... | collective-permute-start | bytes 147464 | tf_op jit(solution)/shard_map/ppermute | solution.py:19
  216.2 2.7 copy-start.20
  223.1 1.1 copy-start.48
  361.2 2.3 copy-start.46
  (25 other events, 23.4 us)
Sparse Core Ops, SparseCore 0:
  205.3 155.8 all-reduce.6
where the time goes:
time: 379 us; the launch traced here: 372 us
  waiting for transfers between devices  136 us (36%)
  local copies, waits for them, and re-layouts  118 us (31%)
  starting transfers between devices  45.8 us (12%)
  matrix products  42.4 us (11%)
  between operations  15.7 us (4%)
  other arithmetic  13.8 us (4%)
    psum x1, waiting for transfers between devices, local(): upper_total, deep_total = lax.psum((upper_terms, deep_terms), ('gx', 'gy'))  132 us
    reshape x26, local copies, waits for them, and re-layouts, conv_forward(): window.reshape(-1, weight.shape[3])  52.4 us
    slice x28, local copies, waits for them, and re-layouts, conv_forward(): padded[shift_x:shift_x + size_x, shift_y:shift_y + size_y, shift_z:shift_...  41.7 us
    ppermute x8, starting transfers between devices, extended(): lax.ppermute(tail, axis, [(i, (i + 1) % count) for i in range(ends)])  32.7 us
    dot_general x54, matrix products, kernel_grad(): lax.dot_general(window.reshape(-1, padded.shape[3]), flat_grad, (((0,), (...  20.2 us
    ppermute x8, starting transfers between devices, extended(): lax.ppermute(head, axis, [((i + 1) % count, i) for i in range(ends)])  13.1 us
    dot_general x54, matrix products, conv_transpose(): jnp.dot(window.reshape(-1, weight.shape[4]), weight[shift_x, shift_y, shi...  12.8 us
    unnamed x116, local copies, waits for them, and re-layouts  12.6 us
  transfers between devices with their start and end apart: 17, of which 3 were waited for; matrix products, arithmetic and copies ran while one was open for 43% of the time, Pallas kernels for 0%

commit v1 on v0

v1 whole, which is shorter than its diff:
```python
import math

import jax
import jax.numpy as jnp
from jax import lax
from jax.experimental import pallas as pl
from jax.experimental.pallas import tpu as pltpu
from jax.sharding import PartitionSpec as P

F32 = jnp.float32
BF16 = jnp.bfloat16
VMEM_BYTES = 56 * 1024 * 1024

PAIR_ROW = 9 * 64
DEEP_ROW = 14 * 64
PAY_ROWS = 42 * 64

CORE = ("gx", 1, (0,))
Y_NEAR = ("gx", 2, (1, 2))
Y_FAR = ("gx", 6, (2,))
Z_NEAR = ("gy", 1, (0, 1))
Z_FAR = ("gy", 3, (1,))
X_NEAR = ("gy", 4, (2, 3))
X_FAR = ("gy", 12, (3,))


def depth_taps(row, gap):
    row = row.astype(F32)
    edge = jnp.zeros((1, row.shape[1]), F32)
    below = jnp.concatenate([edge, row[:-1]], axis=0)
    above = jnp.concatenate([row[1:], edge], axis=0)
    pieces = [below, row, above]
    if gap:
        pieces.append(jnp.zeros((row.shape[0], gap), F32))
    return jnp.concatenate(pieces, axis=1).astype(BF16)


def window(taps, at_x, at_y):
    return jnp.concatenate(
        [taps[2 * x + at_x, 2 * y + at_y] for x in range(2) for y in range(4)], axis=0
    )


def deep_window(taps, at_x, at_y):
    return jnp.concatenate(
        [taps[x + at_x, y + at_y] for x in range(2) for y in range(4)], axis=0
    )


def grads_kernel(
    own, x_lo, x_hi, y_lo, y_hi, cot, cx_lo, cx_hi, cy_lo, cy_hi, w_up, w_deep,
    payload, pre_grad, gx_lo, gx_hi, gy_lo, gy_hi,
    taps, cot_taps, blocks, sums,
):
    for x in range(6):
        for y in range(10):
            if y == 0:
                row = y_lo[x]
            elif y == 9:
                row = y_hi[x]
            elif x == 0:
                row = x_lo[y - 1]
            elif x == 5:
                row = x_hi[y - 1]
            else:
                row = own[x - 1, y - 1]
            taps[x, y] = depth_taps(row, 64)
    for x in range(4):
        for y in range(6):
            if y == 0:
                row = cy_lo[x]
            elif y == 5:
                row = cy_hi[x]
            elif x == 0:
                row = cx_lo[y - 1]
            elif x == 3:
                row = cx_hi[y - 1]
            else:
                row = cot[x - 1, y - 1]
            cot_taps[x, y] = depth_taps(row, 0)

    empty = jnp.zeros((192, 64), BF16)
    for x in range(3):
        for y in range(4):
            left = w_up[x, y].reshape(192, 64) if y < 3 else empty
            right = w_up[x, y - 1].reshape(192, 64) if y > 0 else empty
            pair = jnp.concatenate([left, right], axis=1)
            blocks[x, y, 0:192, 0:128] = pair
            blocks[x + 1, y, 0:192, 128:256] = pair
    for y in range(4):
        blocks[3, y, 0:192, 0:128] = jnp.zeros((192, 128), BF16)
        blocks[0, y, 0:192, 128:256] = jnp.zeros((192, 128), BF16)
        for x in range(4):
            blocks[x, y, 192:256, :] = jnp.zeros((64, 256), BF16)

    pre = jnp.zeros((512, 256), F32)
    for x in range(4):
        for y in range(4):
            pre = pre + jnp.dot(window(taps, x, y), blocks[x, y], preferred_element_type=F32)
    sig = 1.0 / (1.0 + jnp.exp(-pre))
    act = pre * sig
    half = act[:, :128] + act[:, 128:]
    pooled = 0.25 * (half[:, :64] + half[:, 64:])
    pooled_t = pooled.T.astype(BF16)

    pooled_grad = jnp.zeros((512, 64), F32)
    for a in range(3):
        for b in range(3):
            weight = jnp.concatenate([w_deep[2 - a, 2 - b, 2 - j] for j in range(3)], axis=1)
            pooled_grad = pooled_grad + lax.dot_general(
                deep_window(cot_taps, a, b), weight, (((1,), (1,)), ((), ())),
                preferred_element_type=F32,
            )
    wide = pooled_grad.astype(BF16).astype(F32)
    wide = jnp.concatenate([wide, wide], axis=1)
    wide = jnp.concatenate([wide, wide], axis=1)
    grad = 0.25 * wide * (sig * (1.0 + pre * (1.0 - sig)))
    grad_t = grad.T.astype(BF16)
    rounded = grad.astype(BF16)
    pre_grad[...] = rounded

    def column(x, y):
        at = (x % 2) * 128 + (y % 2) * 64
        top = ((x // 2) * 4 + y // 2) * 64
        return rounded[top : top + 64, at : at + 64]

    for y in range(8):
        gx_lo[y] = column(0, y)
        gx_hi[y] = column(3, y)
    for x in range(4):
        gy_lo[x] = column(x, 0)
        gy_hi[x] = column(x, 7)

    for a in range(3):
        for b in range(3):
            out = jnp.dot(
                pooled_t, deep_window(cot_taps, 2 - a, 2 - b), preferred_element_type=F32
            ).astype(BF16)
            for j in range(3):
                top = DEEP_ROW + ((a * 3 + b) * 3 + 2 - j) * 64
                payload[top : top + 64, :] = out[:, j * 128 : j * 128 + 128]

    for x in range(4):
        for y in range(4):
            part = jnp.dot(grad_t, window(taps, x, y), preferred_element_type=F32)
            for s in range(2):
                for t in range(2):
                    a, b = x - s, y - t
                    if 0 <= a < 3 and 0 <= b < 3:
                        top = (s * 2 + t) * 64
                        piece = part[top : top + 64]
                        if s == 0 and t == 0:
                            sums[a * 3 + b] = piece
                        else:
                            sums[a * 3 + b] = sums[a * 3 + b] + piece
    for k in range(9):
        payload[k * 64 : k * 64 + 64, :] = sums[k, :, 0:128].astype(BF16)
    for k in range(5):
        left = sums[2 * k, :, 128:192]
        right = sums[2 * k + 1, :, 128:192] if k < 4 else jnp.zeros((64, 64), F32)
        top = PAIR_ROW + k * 64
        payload[top : top + 64, :] = jnp.concatenate([left, right], axis=1).astype(BF16)
    payload[PAY_ROWS - 64 :, :] = jnp.zeros((64, 128), BF16)


def local_grads(own, x_lo, x_hi, y_lo, y_hi, cot, cx_lo, cx_hi, cy_lo, cy_hi, w_up, w_deep):
    return pl.pallas_call(
        grads_kernel,
        out_shape=[
            jax.ShapeDtypeStruct((PAY_ROWS, 128), BF16),
            jax.ShapeDtypeStruct((512, 256), BF16),
            jax.ShapeDtypeStruct((8, 64, 64), BF16),
            jax.ShapeDtypeStruct((8, 64, 64), BF16),
            jax.ShapeDtypeStruct((4, 64, 64), BF16),
            jax.ShapeDtypeStruct((4, 64, 64), BF16),
        ],
        scratch_shapes=[
            pltpu.VMEM((6, 10, 64, 256), BF16),
            pltpu.VMEM((4, 6, 64, 384), BF16),
            pltpu.VMEM((4, 4, 256, 256), BF16),
            pltpu.VMEM((9, 64, 256), F32),
        ],
        compiler_params=pltpu.CompilerParams(vmem_limit_bytes=VMEM_BYTES),
        cost_estimate=pl.CostEstimate(
            flops=4_000_000_000, bytes_accessed=4_000_000, transcendentals=131072
        ),
        name="local_grads",
    )(own, x_lo, x_hi, y_lo, y_hi, cot, cx_lo, cx_hi, cy_lo, cy_hi, w_up, w_deep)


def input_kernel(pre_grad, x_lo, x_hi, y_lo, y_hi, w_up, out, taps):
    for x in range(6):
        for y in range(10):
            if y == 0:
                row = y_lo[x]
            elif y == 9:
                row = y_hi[x]
            elif x == 0:
                row = x_lo[y - 1]
            elif x == 5:
                row = x_hi[y - 1]
            else:
                u, v = x - 1, y - 1
                at = (u % 2) * 128 + (v % 2) * 64
                top = ((u // 2) * 4 + v // 2) * 64
                row = pre_grad[top : top + 64, at : at + 64]
            taps[x, y] = depth_taps(row, 64)
    empty = jnp.zeros((64, 256), BF16)
    spare = jnp.zeros((64, 64), BF16)
    weights = {}
    for a in range(3):
        for b in range(3):
            weights[a, b] = jnp.concatenate(
                [w_up[a, b, 2], w_up[a, b, 1], w_up[a, b, 0], spare], axis=1
            )
    total = jnp.zeros((512, 256), F32)
    for x in range(4):
        for y in range(4):
            block = jnp.concatenate(
                [weights.get((s + 2 - x, t + 2 - y), empty) for s in range(2) for t in range(2)],
                axis=0,
            )
            total = total + lax.dot_general(
                window(taps, x, y), block, (((1,), (1,)), ((), ())), preferred_element_type=F32
            )
    total = total.astype(BF16)
    for x in range(4):
        for y in range(8):
            at = (x % 2) * 128 + (y % 2) * 64
            top = ((x // 2) * 4 + y // 2) * 64
            out[x, y] = total[top : top + 64, at : at + 64]


def local_input(pre_grad, x_lo, x_hi, y_lo, y_hi, w_up):
    return pl.pallas_call(
        input_kernel,
        out_shape=jax.ShapeDtypeStruct((4, 8, 64, 64), BF16),
        scratch_shapes=[pltpu.VMEM((6, 10, 64, 256), BF16)],
        compiler_params=pltpu.CompilerParams(vmem_limit_bytes=VMEM_BYTES),
        cost_estimate=pl.CostEstimate(
            flops=1_000_000_000, bytes_accessed=4_000_000, transcendentals=0
        ),
        name="local_input",
    )(pre_grad, x_lo, x_hi, y_lo, y_hi, w_up)


def unpack_kernel(up_scale, deep_scale, payload, up, deep):
    for k in range(9):
        a, b = k // 3, k % 3
        first = payload[k * 64 : k * 64 + 64, :].astype(F32).T * up_scale
        up[a, b, 0] = first[:64]
        up[a, b, 1] = first[64:]
    for k in range(5):
        top = PAIR_ROW + k * 64
        pair = payload[top : top + 64, :].astype(F32).T * up_scale
        up[2 * k // 3, 2 * k % 3, 2] = pair[:64]
        if k < 4:
            up[(2 * k + 1) // 3, (2 * k + 1) % 3, 2] = pair[64:]
    for k in range(27):
        top = DEEP_ROW + k * 64
        deep[k // 9, k // 3 % 3, k % 3] = payload[top : top + 64, :].astype(F32) * deep_scale


def unpack(payload, up_scale, deep_scale):
    def body(*refs):
        unpack_kernel(up_scale, deep_scale, *refs)

    return pl.pallas_call(
        body,
        out_shape=[
            jax.ShapeDtypeStruct((3, 3, 3, 64, 64), F32),
            jax.ShapeDtypeStruct((3, 3, 3, 64, 128), F32),
        ],
        compiler_params=pltpu.CompilerParams(vmem_limit_bytes=VMEM_BYTES),
        name="unpack",
    )(payload)


def side_bit(step):
    index = lax.axis_index(step[0])
    return sum(index >> bit for bit in step[2]) & 1


def swap(value, steps, which):
    masks = {"gx": 0, "gy": 0}
    for place, (axis, mask, _) in enumerate(steps):
        if (which >> place) & 1:
            masks[axis] ^= mask
    axes = [axis for axis in ("gx", "gy") if masks[axis]]
    if len(axes) == 1:
        axis = axes[0]
        count = lax.axis_size(axis)
        return lax.ppermute(value, axis, [(i, i ^ masks[axis]) for i in range(count)])
    rows, cols = lax.axis_size("gx"), lax.axis_size("gy")
    pairs = [
        (i * cols + j, (i ^ masks["gx"]) * cols + (j ^ masks["gy"]))
        for i in range(rows)
        for j in range(cols)
    ]
    return lax.ppermute(value, ("gx", "gy"), pairs)


def place_of(steps):
    return sum(side_bit(step) << place for place, step in enumerate(steps))


def tree_sum(values):
    values = [value.astype(F32) for value in values]
    while len(values) > 1:
        values = [values[i] + values[i + 1] for i in range(0, len(values), 2)]
    return values[0].astype(BF16)


def scatter_sum(value, steps):
    parts = 1 << len(steps)
    rows = value.shape[0] // parts
    me = place_of(steps)
    found = [lax.dynamic_slice_in_dim(value, me * rows, rows, 0)]
    for k in range(1, parts):
        piece = lax.dynamic_slice_in_dim(value, (me ^ k) * rows, rows, 0)
        found.append(swap(piece, steps, k))
    return tree_sum(found)


def swap_sum(value, steps):
    return tree_sum([value] + [swap(value, steps, k) for k in range(1, 1 << len(steps))])


def gather(value, steps):
    parts = 1 << len(steps)
    me = place_of(steps)
    found = [value] + [swap(value, steps, k) for k in range(1, parts)]
    for place in range(len(steps)):
        near = ((me >> place) & 1) == 0
        other = 1 << place
        found = [
            jnp.where(near, found[i & ~other], found[i | other])
            if not i & other
            else jnp.where(near, found[i | other], found[i & ~other])
            for i in range(parts)
        ]
    return jnp.concatenate(found)


def sum_everywhere(value):
    value = scatter_sum(value, (CORE,))
    value = scatter_sum(value, (Z_NEAR, X_NEAR))
    for step in (Z_FAR, X_FAR, Y_NEAR, Y_FAR):
        value = swap_sum(value, (step,))
    value = gather(value, (Z_NEAR, X_NEAR))
    return gather(value, (CORE,))


def neighbours(head, tail, axis):
    count = lax.axis_size(axis)
    before = lax.ppermute(tail, axis, [(i, i + 1) for i in range(count - 1)])
    after = lax.ppermute(head, axis, [(i + 1, i) for i in range(count - 1)])
    return before, after


def local(level_input, weight_upper, weight_deep, deep_cotangent):
    tiles = lax.axis_size("gx") * lax.axis_size("gy")
    up_scale = 1.0 / math.sqrt(math.prod(level_input.shape[:3]) * tiles)
    deep_scale = 1.0 / math.sqrt(math.prod(deep_cotangent.shape[:3]) * tiles)
    own, cot = level_input, deep_cotangent

    x_lo, x_hi = neighbours(own[0], own[3], "gx")
    cx_lo, cx_hi = neighbours(cot[0], cot[1], "gx")

    def side(lo, mid, hi, y):
        return jnp.concatenate([lo[None, y], mid[:, y], hi[None, y]])

    y_lo, y_hi = neighbours(side(x_lo, own, x_hi, 0), side(x_lo, own, x_hi, 7), "gy")
    cy_lo, cy_hi = neighbours(side(cx_lo, cot, cx_hi, 0), side(cx_lo, cot, cx_hi, 3), "gy")

    payload, pre_grad, gx_lo, gx_hi, gy_lo, gy_hi = local_grads(
        own, x_lo, x_hi, y_lo, y_hi, cot, cx_lo, cx_hi, cy_lo, cy_hi, weight_upper, weight_deep
    )
    gx_lo, gx_hi = neighbours(gx_lo, gx_hi, "gx")
    gy_lo, gy_hi = neighbours(
        jnp.concatenate([gx_lo[None, 0], gy_lo, gx_hi[None, 0]]),
        jnp.concatenate([gx_lo[None, 7], gy_hi, gx_hi[None, 7]]),
        "gy",
    )
    input_grad = local_input(pre_grad, gx_lo, gx_hi, gy_lo, gy_hi, weight_upper)
    total = sum_everywhere(payload)
    upper, deep = unpack(total, up_scale, deep_scale)
    return (input_grad, upper, deep)


def solution(mesh):
    placed = (P("gx", "gy", None, None), P(), P(), P("gx", "gy", None, None))
    return jax.shard_map(
        local,
        mesh=mesh,
        in_specs=placed,
        out_specs=(P("gx", "gy", None, None), P(), P()),
        check_vma=False,
    )
```

time: 379 us -> 105 us (0.28); the launches traced: 372 us -> 105 us
  local copies, waits for them, and re-layouts: 118 us -> 5.86 us
  waiting for transfers between devices: 136 us -> 27.2 us
  matrix products: 42.4 us -> 0 us
  Pallas kernels: 0 us -> 14.8 us
  between operations: 15.7 us -> 1.13 us
  other arithmetic: 13.8 us -> 1.52 us
  starting transfers between devices: 45.8 us -> 54.1 us
    psum x1 -> x0, waiting for transfers between devices: 132 us -> none  [local(): upper_total, deep_total = lax.psum((upper_terms, deep_terms), ('gx', 'gy'))]
    reshape x28 -> x0, local copies, waits for them, and re-layouts: 55.5 us -> none  [the longest x26 52.4 us: conv_forward(): window.reshape(-1, weight.shape[3])]
    slice x37 -> x6, local copies, waits for them, and re-layouts: 47.5 us -> 0.03 us  [the longest x4 0.02 us: side(): return jnp.concatenate([lo[None, y], mid[:, y], hi[None, y]])]
    dot_general x135 -> x0, matrix products: 42.4 us -> none  [the longest x54 20.2 us: kernel_grad(): lax.dot_general(window.reshape(-1, padded.shape[3]), flat_grad, (((0,), (...]
    ppermute x16 -> x24, waiting for transfers between devices: 4.07 us -> 27.2 us  [the longest x12 16.1 us: swap(): lax.ppermute(value, axis, [(i, i ^ masks[axis]) for i in range(count)])]
    pallas_call x0 -> x3, Pallas kernels: none -> 14.8 us  [the longest x1 8.79 us: local_grads(): pl.pallas_call(grads_kernel, out_shape=[jax.ShapeDtypeStruct((PAY_ROWS, 1...]
    unnamed x116 -> x36, local copies, waits for them, and re-layouts: 12.6 us -> 1.93 us
    ppermute x16 -> x24, starting transfers between devices: 45.8 us -> 54.1 us  [the longest x6 23.2 us: neighbours(): before = lax.ppermute(tail, axis, [(i, i + 1) for i in range(count - 1)])]
  transfers between devices with their start and end apart: 17 -> 24, of which waited for: 3 -> 12; matrix products, arithmetic and copies ran while one was open for 43% -> 2% of each run, Pallas kernels for 0% -> 3%
where the time goes in v1:
time: 105 us
  starting transfers between devices  54.1 us (52%)
  waiting for transfers between devices  27.2 us (26%)
  Pallas kernels  14.8 us (14%)
  local copies, waits for them, and re-layouts  5.86 us (6%)
  other arithmetic  1.52 us (1%)
  between operations  1.13 us (1%)
    ppermute x6, starting transfers between devices, neighbours(): before = lax.ppermute(tail, axis, [(i, i + 1) for i in range(count - 1)])  23.2 us
    ppermute x12, starting transfers between devices, swap(): lax.ppermute(value, axis, [(i, i ^ masks[axis]) for i in range(count)])  19.8 us
    ppermute x12, waiting for transfers between devices, swap(): lax.ppermute(value, axis, [(i, i ^ masks[axis]) for i in range(count)])  16.1 us
    ppermute x6, starting transfers between devices, neighbours(): after = lax.ppermute(head, axis, [(i + 1, i) for i in range(count - 1)])  11 us
    ppermute x6, waiting for transfers between devices, neighbours(): after = lax.ppermute(head, axis, [(i + 1, i) for i in range(count - 1)])  9.39 us
    pallas_call x1, Pallas kernels, local_grads(): pl.pallas_call(grads_kernel, out_shape=[jax.ShapeDtypeStruct((PAY_ROWS, 1...  8.79 us
    pallas_call x1, Pallas kernels, local_input(): pl.pallas_call(input_kernel, out_shape=jax.ShapeDtypeStruct((4, 8, 64, 64...  3.52 us
    pallas_call x1, Pallas kernels, unpack(): pl.pallas_call(body, out_shape=[jax.ShapeDtypeStruct((3, 3, 3, 64, 64), F...  2.51 us
  transfers between devices with their start and end apart: 24, of which 12 were waited for; matrix products, arithmetic and copies ran while one was open for 2% of the time, Pallas kernels for 3%

profile of v1, /device:TPU:1, one launch (start us, length us, event | category | flops | bytes accessed | tf_op | source)
XLA Modules:
  0.0 104.6 jit_solution(3708823852233290147)
XLA Ops:
  0.6 0.9 slice_bitcast_fusion.2
  1.6 3.3 %collective-permute-start.5 = (bf16[4,64,128]{2,1,0:T(8,128)(2,1)S(1)}, bf16[4,64,128]{2,1,0:T(8,128)(2,1)S(1)}, u32[]{:S(2)}, u32[]{:S(2)}) collective-permute-start(bf16[4,64,128]{2,1,0:T(8,128)(2,1)S(1)} %get-tuple-element.38), channel_id=1, source_target_pairs={{16,0},{32,16},{48,32},{64,48},{80,64},{96,80},{112,96},{17,1},{33... | collective-permute-start | bytes 196616 | tf_op jit(solution)/shard_map/ppermute | solution.py:357
  4.9 3.2 %collective-permute-start.4 = (bf16[4,64,128]{2,1,0:T(8,128)(2,1)S(1)}, bf16[4,64,128]{2,1,0:T(8,128)(2,1)S(1)}, u32[]{:S(2)}, u32[]{:S(2)}) collective-permute-start(bf16[4,64,128]{2,1,0:T(8,128)(2,1)S(1)} %get-tuple-element.39), channel_id=1, source_target_pairs={{0,16},{16,32},{32,48},{48,64},{64,80},{80,96},{96,112},{1,17},{17... | collective-permute-start | bytes 196616 | tf_op jit(solution)/shard_map/ppermute | solution.py:356
  8.1 1.0 slice_bitcast_fusion
  9.1 1.9 %collective-permute-start.1 = (bf16[8,64,64]{2,1,0:T(8,128)(2,1)S(1)}, bf16[8,64,64]{2,1,0:T(8,128)(2,1)S(1)}, u32[]{:S(2)}, u32[]{:S(2)}) collective-permute-start(bf16[8,64,64]{2,1,0:T(8,128)(2,1)S(1)} %get-tuple-element.23), channel_id=1, source_target_pairs={{16,0},{32,16},{48,32},{64,48},{80,64},{96,80},{112,96},{17,1},{33... | collective-permute-start | bytes 196616 | tf_op jit(solution)/shard_map/ppermute | solution.py:357
  11.0 3.6 %collective-permute-start = (bf16[8,64,64]{2,1,0:T(8,128)(2,1)S(1)}, bf16[8,64,64]{2,1,0:T(8,128)(2,1)S(1)}, u32[]{:S(2)}, u32[]{:S(2)}) collective-permute-start(bf16[8,64,64]{2,1,0:T(8,128)(2,1)S(1)} %get-tuple-element.24), channel_id=1, source_target_pairs={{0,16},{16,32},{32,48},{48,64},{64,80},{80,96},{96,112},{1,17},{17... | collective-permute-start | bytes 196616 | tf_op jit(solution)/shard_map/ppermute | solution.py:356
  14.7 0.9 slice_bitcast_fusion.4
  15.7 3.5 %collective-permute-start.6 = (bf16[4,64,128]{2,1,0:T(8,128)(2,1)S(1)}, bf16[4,64,128]{2,1,0:T(8,128)(2,1)S(1)}, u32[]{:S(2)}, u32[]{:S(2)}) collective-permute-start(bf16[4,64,128]{2,1,0:T(8,128)(2,1)S(1)} %pad_maximum_fusion.6), channel_id=1, source_target_pairs={{0,1},{1,2},{2,3},{3,4},{4,5},{5,6},{6,7},{7,8},{8,9},{9,10},{10,1... | collective-permute-start | bytes 196616 | tf_op jit(solution)/shard_map/ppermute | solution.py:356
  19.2 1.3 %collective-permute-start.7 = (bf16[4,64,128]{2,1,0:T(8,128)(2,1)S(1)}, bf16[4,64,128]{2,1,0:T(8,128)(2,1)S(1)}, u32[]{:S(2)}, u32[]{:S(2)}) collective-permute-start(bf16[4,64,128]{2,1,0:T(8,128)(2,1)S(1)} %pad_maximum_fusion.7), channel_id=1, source_target_pairs={{1,0},{2,1},{3,2},{4,3},{5,4},{6,5},{7,6},{8,7},{9,8},{10,9},{11,1... | collective-permute-start | bytes 196616 | tf_op jit(solution)/shard_map/ppermute | solution.py:357
  20.6 4.2 %collective-permute-start.2 = (bf16[6,64,64]{2,1,0:T(8,128)(2,1)S(1)}, bf16[6,64,64]{2,1,0:T(8,128)(2,1)S(1)}, u32[]{:S(2)}, u32[]{:S(2)}) collective-permute-start(bf16[6,64,64]{2,1,0:T(8,128)(2,1)S(1)} %pad_maximum_fusion.2), channel_id=1, source_target_pairs={{0,1},{1,2},{2,3},{3,4},{4,5},{5,6},{6,7},{7,8},{8,9},{9,10},{10,1... | collective-permute-start | bytes 147464 | tf_op jit(solution)/shard_map/ppermute | solution.py:356
  24.9 1.3 %collective-permute-start.3 = (bf16[6,64,64]{2,1,0:T(8,128)(2,1)S(1)}, bf16[6,64,64]{2,1,0:T(8,128)(2,1)S(1)}, u32[]{:S(2)}, u32[]{:S(2)}) collective-permute-start(bf16[6,64,64]{2,1,0:T(8,128)(2,1)S(1)} %pad_maximum_fusion.3), channel_id=1, source_target_pairs={{1,0},{2,1},{3,2},{4,3},{5,4},{6,5},{7,6},{8,7},{9,8},{10,9},{11,1... | collective-permute-start | bytes 147464 | tf_op jit(solution)/shard_map/ppermute | solution.py:357
  26.2 0.9 collective-permute-done.2.y_lo
  27.0 4.3 %collective-permute-done.3.y_hi = bf16[6,64,64]{2,1,0:T(8,128)(2,1)S(1)} collective-permute-done((bf16[6,64,64]{2,1,0:T(8,128)(2,1)S(1)}, bf16[6,64,64]{2,1,0:T(8,128)(2,1)S(1)}, u32[]{:S(2)}, u32[]{:S(2)}) %collective-permute-start.3) | collective-permute-done | bytes 49184 | tf_op jit(solution)/shard_map/ppermute | solution.py:357
  31.4 0.6 copy-done.13
  32.0 0.6 copy-done.17
  32.6 8.8 %local_grads.1 = (bf16[2688,128]{1,0:T(8,128)(2,1)}, bf16[512,256]{1,0:T(8,128)(2,1)}, bf16[8,64,64]{2,1,0:T(8,128)(2,1)}, bf16[8,64,64]{2,1,0:T(8,128)(2,1)}, b...) custom-call(bf16[4,8,64,64]{3,2,1,0:T(8,128)(2,1)} %own.1, bf16[8,64,64]{2,1,0:T(8,128)(2,1)} %copy-done.7, ...), custom_call_target="tpu_custom_call" | custom-call | flops 4000000000 | bytes 4000000 | tf_op jit(solution)/shard_map/local_grads/pallas_call | solution.py:167
  41.5 1.1 %constant_dynamic-slice_fusion.3 = bf16[1344,128]{1,0:T(8,128)(2,1)S(1)} fusion(bf16[2688,128]{1,0:T(8,128)(2,1)} %get-tuple-element.16, s32[]{:T(128)S(6)} %select_n.72), kind=kLoop, calls=%fused_computation.35 | loop fusion | bytes 688132 | tf_op jit(solution)/shard_map/dynamic_slice | solution.py:320
  42.5 0.5 collective-permute-start.12
  43.0 1.3 %collective-permute-done.12 = bf16[1344,128]{1,0:T(8,128)(2,1)S(1)} collective-permute-done((bf16[1344,128]{1,0:T(8,128)(2,1)S(1)}, bf16[1344,128]{1,0:T(8,128)(2,1)S(1)}, u32[]{:S(2)}, u32[]{:S(2)}) %collective-permute-start.12) | collective-permute-done | bytes 344096 | tf_op jit(solution)/shard_map/ppermute | solution.py:293
  44.3 0.1 add_convert_fusion
  44.4 1.7 %collective-permute-start.13 = (bf16[336,128]{1,0:T(8,128)(2,1)S(1)}, bf16[336,128]{1,0:T(8,128)(2,1)S(1)}, u32[]{:S(2)}, u32[]{:S(2)}) collective-permute-start(bf16[336,128]{1,0:T(8,128)(2,1)S(1)} %get-tuple-element.29), channel_id=1, source_target_pairs={{0,1},{1,0},{2,3},{3,2},{4,5},{5,4},{6,7},{7,6},{8,9},{9,8},{10,11... | collective-permute-start | bytes 258056 | tf_op jit(solution)/shard_map/ppermute | solution.py:293
  46.2 2.8 %collective-permute-start.15 = (bf16[336,128]{1,0:T(8,128)(2,1)S(1)}, bf16[336,128]{1,0:T(8,128)(2,1)S(1)}, u32[]{:S(2)}, u32[]{:S(2)}) collective-permute-start(bf16[336,128]{1,0:T(8,128)(2,1)S(1)} %get-tuple-element.30), channel_id=1, source_target_pairs={{0,5},{1,4},{2,7},{3,6},{4,1},{5,0},{6,3},{7,2},{8,13},{9,12},{10,... | collective-permute-start | bytes 258056 | tf_op jit(solution)/shard_map/ppermute | solution.py:293
  48.9 2.4 %collective-permute-done.15 = bf16[336,128]{1,0:T(8,128)(2,1)S(1)} collective-permute-done((bf16[336,128]{1,0:T(8,128)(2,1)S(1)}, bf16[336,128]{1,0:T(8,128)(2,1)S(1)}, u32[]{:S(2)}, u32[]{:S(2)}) %collective-permute-start.15) | collective-permute-done | bytes 86048 | tf_op jit(solution)/shard_map/ppermute | solution.py:293
  51.3 1.2 %collective-permute-done.14 = bf16[336,128]{1,0:T(8,128)(2,1)S(1)} collective-permute-done((bf16[336,128]{1,0:T(8,128)(2,1)S(1)}, bf16[336,128]{1,0:T(8,128)(2,1)S(1)}, u32[]{:S(2)}, u32[]{:S(2)}) %collective-permute-start.14) | collective-permute-done | bytes 86048 | tf_op jit(solution)/shard_map/ppermute | solution.py:293
  52.6 5.2 %collective-permute-start.16 = (bf16[336,128]{1,0:T(8,128)(2,1)S(1)}, bf16[336,128]{1,0:T(8,128)(2,1)S(1)}, u32[]{:S(2)}, u32[]{:S(2)}) collective-permute-start(bf16[336,128]{1,0:T(8,128)(2,1)S(1)} %add_convert_fusion.5), channel_id=1, source_target_pairs={{0,3},{1,2},{2,1},{3,0},{4,7},{5,6},{6,5},{7,4},{8,11},{9,10},{10,... | collective-permute-start | bytes 258056 | tf_op jit(solution)/shard_map/ppermute | solution.py:293
  57.8 1.9 %collective-permute-done.16 = bf16[336,128]{1,0:T(8,128)(2,1)S(1)} collective-permute-done((bf16[336,128]{1,0:T(8,128)(2,1)S(1)}, bf16[336,128]{1,0:T(8,128)(2,1)S(1)}, u32[]{:S(2)}, u32[]{:S(2)}) %collective-permute-start.16) | collective-permute-done | bytes 86048 | tf_op jit(solution)/shard_map/ppermute | solution.py:293
  59.7 0.7 collective-permute-start.17
  60.5 3.9 %collective-permute-done.17 = bf16[336,128]{1,0:T(8,128)(2,1)S(1)} collective-permute-done((bf16[336,128]{1,0:T(8,128)(2,1)S(1)}, bf16[336,128]{1,0:T(8,128)(2,1)S(1)}, u32[]{:S(2)}, u32[]{:S(2)}) %collective-permute-start.17) | collective-permute-done | bytes 86048 | tf_op jit(solution)/shard_map/ppermute | solution.py:293
  64.4 1.5 %collective-permute-start.18 = (bf16[336,128]{1,0:T(8,128)(2,1)S(1)}, bf16[336,128]{1,0:T(8,128)(2,1)S(1)}, u32[]{:S(2)}, u32[]{:S(2)}) collective-permute-start(bf16[336,128]{1,0:T(8,128)(2,1)S(1)} %add_convert_fusion.3), channel_id=1, source_target_pairs={{0,32},{16,48},{32,0},{48,16},{64,96},{80,112},{96,64},{112,80},{1... | collective-permute-start | bytes 258056 | tf_op jit(solution)/shard_map/ppermute | solution.py:293
  65.8 5.4 %collective-permute-start.8 = (bf16[8,64,64]{2,1,0:T(8,128)(2,1)S(1)}, bf16[8,64,64]{2,1,0:T(8,128)(2,1)S(1)}, u32[]{:S(2)}, u32[]{:S(2)}) collective-permute-start(bf16[8,64,64]{2,1,0:T(8,128)(2,1)S(1)} %copy-done.11), channel_id=1, source_target_pairs={{0,16},{16,32},{32,48},{48,64},{64,80},{80,96},{96,112},{1,17},{17... | collective-permute-start | bytes 196616 | tf_op jit(solution)/shard_map/ppermute | solution.py:356
  71.2 1.9 %collective-permute-start.9 = (bf16[8,64,64]{2,1,0:T(8,128)(2,1)S(1)}, bf16[8,64,64]{2,1,0:T(8,128)(2,1)S(1)}, u32[]{:S(2)}, u32[]{:S(2)}) collective-permute-start(bf16[8,64,64]{2,1,0:T(8,128)(2,1)S(1)} %copy-done.10), channel_id=1, source_target_pairs={{16,0},{32,16},{48,32},{64,48},{80,64},{96,80},{112,96},{17,1},{33... | collective-permute-start | bytes 196616 | tf_op jit(solution)/shard_map/ppermute | solution.py:357
  73.2 2.0 %collective-permute-start.19 = (bf16[336,128]{1,0:T(8,128)(2,1)S(1)}, bf16[336,128]{1,0:T(8,128)(2,1)S(1)}, u32[]{:S(2)}, u32[]{:S(2)}) collective-permute-start(bf16[336,128]{1,0:T(8,128)(2,1)S(1)} %add_convert_fusion.2), channel_id=1, source_target_pairs={{0,96},{16,112},{32,64},{48,80},{64,32},{80,48},{96,0},{112,16},{1... | collective-permute-start | bytes 258056 | tf_op jit(solution)/shard_map/ppermute | solution.py:293
  75.2 2.7 %collective-permute-done.19 = bf16[336,128]{1,0:T(8,128)(2,1)S(1)} collective-permute-done((bf16[336,128]{1,0:T(8,128)(2,1)S(1)}, bf16[336,128]{1,0:T(8,128)(2,1)S(1)}, u32[]{:S(2)}, u32[]{:S(2)}) %collective-permute-start.19) | collective-permute-done | bytes 86048 | tf_op jit(solution)/shard_map/ppermute | solution.py:293
  77.9 0.1 collective-permute-start.22
  78.0 0.7 collective-permute-start.21
  78.7 1.9 %collective-permute-start.20 = (bf16[336,128]{1,0:T(8,128)(2,1)S(1)}, bf16[336,128]{1,0:T(8,128)(2,1)S(1)}, u32[]{:S(2)}, u32[]{:S(2)}) collective-permute-start(bf16[336,128]{1,0:T(8,128)(2,1)S(1)} %add_convert_fusion.1), channel_id=1, source_target_pairs={{0,1},{1,0},{2,3},{3,2},{4,5},{5,4},{6,7},{7,6},{8,9},{9,8},{10,11... | collective-permute-start | bytes 258056 | tf_op jit(solution)/shard_map/ppermute | solution.py:293
  80.6 1.6 %collective-permute-done.22 = bf16[336,128]{1,0:T(8,128)(2,1)S(1)} collective-permute-done((bf16[336,128]{1,0:T(8,128)(2,1)S(1)}, bf16[336,128]{1,0:T(8,128)(2,1)S(1)}, u32[]{:S(2)}, u32[]{:S(2)}) %collective-permute-start.22) | collective-permute-done | bytes 86048 | tf_op jit(solution)/shard_map/ppermute | solution.py:293
  82.3 1.1 %collective-permute-done.20 = bf16[336,128]{1,0:T(8,128)(2,1)S(1)} collective-permute-done((bf16[336,128]{1,0:T(8,128)(2,1)S(1)}, bf16[336,128]{1,0:T(8,128)(2,1)S(1)}, u32[]{:S(2)}, u32[]{:S(2)}) %collective-permute-start.20) | collective-permute-done | bytes 86048 | tf_op jit(solution)/shard_map/ppermute | solution.py:293
  83.5 2.7 %collective-permute-start.23 = (bf16[1344,128]{1,0:T(8,128)(2,1)S(1)}, bf16[1344,128]{1,0:T(8,128)(2,1)S(1)}, u32[]{:S(2)}, u32[]{:S(2)}) collective-permute-start(bf16[1344,128]{1,0:T(8,128)(2,1)S(1)} %pad_maximum_fusion.1), channel_id=1, source_target_pairs={{0,16},{16,0},{32,48},{48,32},{64,80},{80,64},{96,112},{112,96},{1... | collective-permute-start | bytes 1032200 | tf_op jit(solution)/shard_map/ppermute | solution.py:293
  86.3 3.3 %collective-permute-start.10 = (bf16[6,64,64]{2,1,0:T(8,128)(2,1)S(1)}, bf16[6,64,64]{2,1,0:T(8,128)(2,1)S(1)}, u32[]{:S(2)}, u32[]{:S(2)}) collective-permute-start(bf16[6,64,64]{2,1,0:T(8,128)(2,1)S(1)} %pad_maximum_fusion.4), channel_id=1, source_target_pairs={{0,1},{1,2},{2,3},{3,4},{4,5},{5,6},{6,7},{7,8},{8,9},{9,10},{10,1... | collective-permute-start | bytes 147464 | tf_op jit(solution)/shard_map/ppermute | solution.py:356
  89.6 1.3 %collective-permute-start.11 = (bf16[6,64,64]{2,1,0:T(8,128)(2,1)S(1)}, bf16[6,64,64]{2,1,0:T(8,128)(2,1)S(1)}, u32[]{:S(2)}, u32[]{:S(2)}) collective-permute-start(bf16[6,64,64]{2,1,0:T(8,128)(2,1)S(1)} %pad_maximum_fusion.5), channel_id=1, source_target_pairs={{1,0},{2,1},{3,2},{4,3},{5,4},{6,5},{7,6},{8,7},{9,8},{10,9},{11,1... | collective-permute-start | bytes 147464 | tf_op jit(solution)/shard_map/ppermute | solution.py:357
  90.9 0.8 collective-permute-done.10.y_lo
  91.8 5.1 %collective-permute-done.11.y_hi = bf16[6,64,64]{2,1,0:T(8,128)(2,1)S(1)} collective-permute-done((bf16[6,64,64]{2,1,0:T(8,128)(2,1)S(1)}, bf16[6,64,64]{2,1,0:T(8,128)(2,1)S(1)}, u32[]{:S(2)}, u32[]{:S(2)}) %collective-permute-start.11) | collective-permute-done | bytes 49184 | tf_op jit(solution)/shard_map/ppermute | solution.py:357
  96.8 0.6 copy-done.15
  97.5 3.5 %local_input.1 = bf16[4,8,64,64]{3,2,1,0:T(8,128)(2,1)} custom-call(bf16[512,256]{1,0:T(8,128)(2,1)} %get-tuple-element.11.pre_grad, bf16[8,64,64]{2,1,0:T(8,128)(2,1)} %copy-done.8, bf16[8,64,64]{2,1,0:T(8,128)(2,1)} %copy-done.9, bf16[6,64,64]{2,1,0:T(8,128)(2,1)} %copy-done.14, bf16[6,64,64]{2,1,0:T(8,128)(2,1)} %copy-done.15, bf16[3,3,3,64,64]{4,3,2,1,0:T(8,128)(2,1)} %w_up.3), custom_call_target="tpu_custom_call" | custom-call | flops 1000000000 | bytes 4000000 | tf_op jit(solution)/shard_map/local_input/pallas_call | solution.py:235
  101.0 0.2 broadcast_select_fusion.1
  101.2 0.9 pad_maximum_fusion.refs_0_
  102.1 2.5 %unpack.1 = (f32[3,3,3,64,64]{4,3,2,1,0:T(8,128)}, f32[3,3,3,64,128]{4,3,2,1,0:T(8,128)}) custom-call(bf16[2688,128]{1,0:T(8,128)(2,1)} %pad_maximum_fusion.refs_0_), custom_call_target="tpu_custom_call" | custom-call | tf_op jit(solution)/shard_map/unpack/pallas_call | solution.py:268
  (67 shorter events, 0.6 us)
Async XLA Ops:
  0.6 14.9 %copy-start.1 = (bf16[2,4,64,128]{3,2,1,0:T(8,128)(2,1)S(1)}, bf16[2,4,64,128]{3,2,1,0:T(8,128)(2,1)}, u32[]{:S(2)}) copy-start(bf16[2,4,64,128]{3,2,1,0:T(8,128)(2,1)} %cot.1) | copy-start | bytes 393220
  1.6 14.0 %collective-permute-start.5 = (bf16[4,64,128]{2,1,0:T(8,128)(2,1)S(1)}, bf16[4,64,128]{2,1,0:T(8,128)(2,1)S(1)}, u32[]{:S(2)}, u32[]{:S(2)}) collective-permute-start(bf16[4,64,128]{2,1,0:T(8,128)(2,1)S(1)} %get-tuple-element.38), channel_id=1, source_target_pairs={{16,0},{32,16},{48,32},{64,48},{80,64},{96,80},{112,96},{17,1},{33... | collective-permute-start | bytes 196616 | tf_op jit(solution)/shard_map/ppermute | solution.py:357
  4.9 10.7 %collective-permute-start.4 = (bf16[4,64,128]{2,1,0:T(8,128)(2,1)S(1)}, bf16[4,64,128]{2,1,0:T(8,128)(2,1)S(1)}, u32[]{:S(2)}, u32[]{:S(2)}) collective-permute-start(bf16[4,64,128]{2,1,0:T(8,128)(2,1)S(1)} %get-tuple-element.39), channel_id=1, source_target_pairs={{0,16},{16,32},{32,48},{48,64},{64,80},{80,96},{96,112},{1,17},{17... | collective-permute-start | bytes 196616 | tf_op jit(solution)/shard_map/ppermute | solution.py:356
  9.1 11.5 %collective-permute-start.1 = (bf16[8,64,64]{2,1,0:T(8,128)(2,1)S(1)}, bf16[8,64,64]{2,1,0:T(8,128)(2,1)S(1)}, u32[]{:S(2)}, u32[]{:S(2)}) collective-permute-start(bf16[8,64,64]{2,1,0:T(8,128)(2,1)S(1)} %get-tuple-element.23), channel_id=1, source_target_pairs={{16,0},{32,16},{48,32},{64,48},{80,64},{96,80},{112,96},{17,1},{33... | collective-permute-start | bytes 196616 | tf_op jit(solution)/shard_map/ppermute | solution.py:357
  11.0 9.6 %collective-permute-start = (bf16[8,64,64]{2,1,0:T(8,128)(2,1)S(1)}, bf16[8,64,64]{2,1,0:T(8,128)(2,1)S(1)}, u32[]{:S(2)}, u32[]{:S(2)}) collective-permute-start(bf16[8,64,64]{2,1,0:T(8,128)(2,1)S(1)} %get-tuple-element.24), channel_id=1, source_target_pairs={{0,16},{16,32},{32,48},{48,64},{64,80},{80,96},{96,112},{1,17},{17... | collective-permute-start | bytes 196616 | tf_op jit(solution)/shard_map/ppermute | solution.py:356
  15.6 15.8 %copy-start.4 = (bf16[4,64,128]{2,1,0:T(8,128)(2,1)}, bf16[4,64,128]{2,1,0:T(8,128)(2,1)S(1)}, u32[]{:S(2)}) copy-start(bf16[4,64,128]{2,1,0:T(8,128)(2,1)S(1)} %collective-permute-done.5.cx_hi) | copy-start | bytes 196612
  15.6 15.8 %copy-start.5 = (bf16[4,64,128]{2,1,0:T(8,128)(2,1)}, bf16[4,64,128]{2,1,0:T(8,128)(2,1)S(1)}, u32[]{:S(2)}) copy-start(bf16[4,64,128]{2,1,0:T(8,128)(2,1)S(1)} %collective-permute-done.4.cx_lo) | copy-start | bytes 196612
  15.7 15.7 %collective-permute-start.6 = (bf16[4,64,128]{2,1,0:T(8,128)(2,1)S(1)}, bf16[4,64,128]{2,1,0:T(8,128)(2,1)S(1)}, u32[]{:S(2)}, u32[]{:S(2)}) collective-permute-start(bf16[4,64,128]{2,1,0:T(8,128)(2,1)S(1)} %pad_maximum_fusion.6), channel_id=1, source_target_pairs={{0,1},{1,2},{2,3},{3,4},{4,5},{5,6},{6,7},{7,8},{8,9},{9,10},{10,1... | collective-permute-start | bytes 196616 | tf_op jit(solution)/shard_map/ppermute | solution.py:356
  19.2 12.1 %collective-permute-start.7 = (bf16[4,64,128]{2,1,0:T(8,128)(2,1)S(1)}, bf16[4,64,128]{2,1,0:T(8,128)(2,1)S(1)}, u32[]{:S(2)}, u32[]{:S(2)}) collective-permute-start(bf16[4,64,128]{2,1,0:T(8,128)(2,1)S(1)} %pad_maximum_fusion.7), channel_id=1, source_target_pairs={{1,0},{2,1},{3,2},{4,3},{5,4},{6,5},{7,6},{8,7},{9,8},{10,9},{11,1... | collective-permute-start | bytes 196616 | tf_op jit(solution)/shard_map/ppermute | solution.py:357
  20.5 10.8 %copy-start.6 = (bf16[8,64,64]{2,1,0:T(8,128)(2,1)}, bf16[8,64,64]{2,1,0:T(8,128)(2,1)S(1)}, u32[]{:S(2)}) copy-start(bf16[8,64,64]{2,1,0:T(8,128)(2,1)S(1)} %collective-permute-done.1.x_hi) | copy-start | bytes 196612
  20.6 10.8 %copy-start.7 = (bf16[8,64,64]{2,1,0:T(8,128)(2,1)}, bf16[8,64,64]{2,1,0:T(8,128)(2,1)S(1)}, u32[]{:S(2)}) copy-start(bf16[8,64,64]{2,1,0:T(8,128)(2,1)S(1)} %collective-permute-done.x_lo) | copy-start | bytes 196612
  20.6 6.4 %collective-permute-start.2 = (bf16[6,64,64]{2,1,0:T(8,128)(2,1)S(1)}, bf16[6,64,64]{2,1,0:T(8,128)(2,1)S(1)}, u32[]{:S(2)}, u32[]{:S(2)}) collective-permute-start(bf16[6,64,64]{2,1,0:T(8,128)(2,1)S(1)} %pad_maximum_fusion.2), channel_id=1, source_target_pairs={{0,1},{1,2},{2,3},{3,4},{4,5},{5,6},{6,7},{7,8},{8,9},{9,10},{10,1... | collective-permute-start | bytes 147464 | tf_op jit(solution)/shard_map/ppermute | solution.py:356
  24.9 6.5 %collective-permute-start.3 = (bf16[6,64,64]{2,1,0:T(8,128)(2,1)S(1)}, bf16[6,64,64]{2,1,0:T(8,128)(2,1)S(1)}, u32[]{:S(2)}, u32[]{:S(2)}) collective-permute-start(bf16[6,64,64]{2,1,0:T(8,128)(2,1)S(1)} %pad_maximum_fusion.3), channel_id=1, source_target_pairs={{1,0},{2,1},{3,2},{4,3},{5,4},{6,5},{7,6},{8,7},{9,8},{10,9},{11,1... | collective-permute-start | bytes 147464 | tf_op jit(solution)/shard_map/ppermute | solution.py:357
  27.0 4.4 %copy-start.12 = (bf16[6,64,64]{2,1,0:T(8,128)(2,1)}, bf16[6,64,64]{2,1,0:T(8,128)(2,1)S(1)}, u32[]{:S(2)}) copy-start(bf16[6,64,64]{2,1,0:T(8,128)(2,1)S(1)} %collective-permute-done.2.y_lo) | copy-start | bytes 147460
  31.4 0.6 copy-start.13
  31.4 0.7 copy-start.16
  32.0 0.6 copy-start.17
  41.4 2.8 %copy-start = (bf16[2688,128]{1,0:T(8,128)(2,1)S(1)}, bf16[2688,128]{1,0:T(8,128)(2,1)}, u32[]{:S(2)}) copy-start(bf16[2688,128]{1,0:T(8,128)(2,1)} %get-tuple-element.16) | copy-start | bytes 2064388
  42.5 1.8 %collective-permute-start.12 = (bf16[1344,128]{1,0:T(8,128)(2,1)S(1)}, bf16[1344,128]{1,0:T(8,128)(2,1)S(1)}, u32[]{:S(2)}, u32[]{:S(2)}) collective-permute-start(bf16[1344,128]{1,0:T(8,128)(2,1)S(1)} %constant_dynamic-slice_fusion.3), channel_id=1, source_target_pairs={{0,16},{16,0},{32,48},{48,32},{64,80},{80,64},{96,112},{112,96},{1... | collective-permute-start | bytes 1032200 | tf_op jit(solution)/shard_map/ppermute | solution.py:293
  44.4 21.5 %copy-start.11 = (bf16[8,64,64]{2,1,0:T(8,128)(2,1)S(1)}, bf16[8,64,64]{2,1,0:T(8,128)(2,1)}, u32[]{:S(2)}) copy-start(bf16[8,64,64]{2,1,0:T(8,128)(2,1)} %get-tuple-element.12) | copy-start | bytes 196612
  44.4 26.8 %copy-start.10 = (bf16[8,64,64]{2,1,0:T(8,128)(2,1)S(1)}, bf16[8,64,64]{2,1,0:T(8,128)(2,1)}, u32[]{:S(2)}) copy-start(bf16[8,64,64]{2,1,0:T(8,128)(2,1)} %get-tuple-element.13) | copy-start | bytes 196612
  44.4 4.5 %collective-permute-start.13 = (bf16[336,128]{1,0:T(8,128)(2,1)S(1)}, bf16[336,128]{1,0:T(8,128)(2,1)S(1)}, u32[]{:S(2)}, u32[]{:S(2)}) collective-permute-start(bf16[336,128]{1,0:T(8,128)(2,1)S(1)} %get-tuple-element.29), channel_id=1, source_target_pairs={{0,1},{1,0},{2,3},{3,2},{4,5},{5,4},{6,7},{7,6},{8,9},{9,8},{10,11... | collective-permute-start | bytes 258056 | tf_op jit(solution)/shard_map/ppermute | solution.py:293
  46.2 5.2 %collective-permute-start.15 = (bf16[336,128]{1,0:T(8,128)(2,1)S(1)}, bf16[336,128]{1,0:T(8,128)(2,1)S(1)}, u32[]{:S(2)}, u32[]{:S(2)}) collective-permute-start(bf16[336,128]{1,0:T(8,128)(2,1)S(1)} %get-tuple-element.30), channel_id=1, source_target_pairs={{0,5},{1,4},{2,7},{3,6},{4,1},{5,0},{6,3},{7,2},{8,13},{9,12},{10,... | collective-permute-start | bytes 258056 | tf_op jit(solution)/shard_map/ppermute | solution.py:293
  48.9 3.6 %collective-permute-start.14 = (bf16[336,128]{1,0:T(8,128)(2,1)S(1)}, bf16[336,128]{1,0:T(8,128)(2,1)S(1)}, u32[]{:S(2)}, u32[]{:S(2)}) collective-permute-start(bf16[336,128]{1,0:T(8,128)(2,1)S(1)} %get-tuple-element.31), channel_id=1, source_target_pairs={{0,4},{1,5},{2,6},{3,7},{4,0},{5,1},{6,2},{7,3},{8,12},{9,13},{10,... | collective-permute-start | bytes 258056 | tf_op jit(solution)/shard_map/ppermute | solution.py:293
  52.6 7.1 %collective-permute-start.16 = (bf16[336,128]{1,0:T(8,128)(2,1)S(1)}, bf16[336,128]{1,0:T(8,128)(2,1)S(1)}, u32[]{:S(2)}, u32[]{:S(2)}) collective-permute-start(bf16[336,128]{1,0:T(8,128)(2,1)S(1)} %add_convert_fusion.5), channel_id=1, source_target_pairs={{0,3},{1,2},{2,1},{3,0},{4,7},{5,6},{6,5},{7,4},{8,11},{9,10},{10,... | collective-permute-start | bytes 258056 | tf_op jit(solution)/shard_map/ppermute | solution.py:293
  59.7 4.6 %collective-permute-start.17 = (bf16[336,128]{1,0:T(8,128)(2,1)S(1)}, bf16[336,128]{1,0:T(8,128)(2,1)S(1)}, u32[]{:S(2)}, u32[]{:S(2)}) collective-permute-start(bf16[336,128]{1,0:T(8,128)(2,1)S(1)} %add_convert_fusion.4), channel_id=1, source_target_pairs={{0,12},{1,13},{2,14},{3,15},{4,8},{5,9},{6,10},{7,11},{8,4},{9,5},... | collective-permute-start | bytes 258056 | tf_op jit(solution)/shard_map/ppermute | solution.py:293
  64.4 8.8 %collective-permute-start.18 = (bf16[336,128]{1,0:T(8,128)(2,1)S(1)}, bf16[336,128]{1,0:T(8,128)(2,1)S(1)}, u32[]{:S(2)}, u32[]{:S(2)}) collective-permute-start(bf16[336,128]{1,0:T(8,128)(2,1)S(1)} %add_convert_fusion.3), channel_id=1, source_target_pairs={{0,32},{16,48},{32,0},{48,16},{64,96},{80,112},{96,64},{112,80},{1... | collective-permute-start | bytes 258056 | tf_op jit(solution)/shard_map/ppermute | solution.py:293
  65.8 9.3 %collective-permute-start.8 = (bf16[8,64,64]{2,1,0:T(8,128)(2,1)S(1)}, bf16[8,64,64]{2,1,0:T(8,128)(2,1)S(1)}, u32[]{:S(2)}, u32[]{:S(2)}) collective-permute-start(bf16[8,64,64]{2,1,0:T(8,128)(2,1)S(1)} %copy-done.11), channel_id=1, source_target_pairs={{0,16},{16,32},{32,48},{48,64},{64,80},{80,96},{96,112},{1,17},{17... | collective-permute-start | bytes 196616 | tf_op jit(solution)/shard_map/ppermute | solution.py:356
  71.2 9.4 %collective-permute-start.9 = (bf16[8,64,64]{2,1,0:T(8,128)(2,1)S(1)}, bf16[8,64,64]{2,1,0:T(8,128)(2,1)S(1)}, u32[]{:S(2)}, u32[]{:S(2)}) collective-permute-start(bf16[8,64,64]{2,1,0:T(8,128)(2,1)S(1)} %copy-done.10), channel_id=1, source_target_pairs={{16,0},{32,16},{48,32},{64,48},{80,64},{96,80},{112,96},{17,1},{33... | collective-permute-start | bytes 196616 | tf_op jit(solution)/shard_map/ppermute | solution.py:357
  73.2 13.0 %copy-start.3 = (bf16[4,64,64]{2,1,0:T(8,128)(2,1)S(1)}, bf16[4,64,64]{2,1,0:T(8,128)(2,1)}, u32[]{:S(2)}) copy-start(bf16[4,64,64]{2,1,0:T(8,128)(2,1)} %get-tuple-element.14) | copy-start | bytes 98308
  73.2 4.6 %collective-permute-start.19 = (bf16[336,128]{1,0:T(8,128)(2,1)S(1)}, bf16[336,128]{1,0:T(8,128)(2,1)S(1)}, u32[]{:S(2)}, u32[]{:S(2)}) collective-permute-start(bf16[336,128]{1,0:T(8,128)(2,1)S(1)} %add_convert_fusion.2), channel_id=1, source_target_pairs={{0,96},{16,112},{32,64},{48,80},{64,32},{80,48},{96,0},{112,16},{1... | collective-permute-start | bytes 258056 | tf_op jit(solution)/shard_map/ppermute | solution.py:293
  75.2 8.3 %copy-start.8 = (bf16[8,64,64]{2,1,0:T(8,128)(2,1)}, bf16[8,64,64]{2,1,0:T(8,128)(2,1)S(1)}, u32[]{:S(2)}) copy-start(bf16[8,64,64]{2,1,0:T(8,128)(2,1)S(1)} %collective-permute-done.8.x_lo) | copy-start | bytes 196612
  77.9 11.7 %copy-start.2 = (bf16[4,64,64]{2,1,0:T(8,128)(2,1)S(1)}, bf16[4,64,64]{2,1,0:T(8,128)(2,1)}, u32[]{:S(2)}) copy-start(bf16[4,64,64]{2,1,0:T(8,128)(2,1)} %get-tuple-element.15) | copy-start | bytes 98308
  77.9 4.4 %collective-permute-start.22 = (bf16[336,128]{1,0:T(8,128)(2,1)S(1)}, bf16[336,128]{1,0:T(8,128)(2,1)S(1)}, u32[]{:S(2)}, u32[]{:S(2)}) collective-permute-start(bf16[336,128]{1,0:T(8,128)(2,1)S(1)} %add_convert_fusion.1), channel_id=1, source_target_pairs={{0,5},{1,4},{2,7},{3,6},{4,1},{5,0},{6,3},{7,2},{8,13},{9,12},{10,... | collective-permute-start | bytes 258056 | tf_op jit(solution)/shard_map/ppermute | solution.py:293
  78.0 4.3 %collective-permute-start.21 = (bf16[336,128]{1,0:T(8,128)(2,1)S(1)}, bf16[336,128]{1,0:T(8,128)(2,1)S(1)}, u32[]{:S(2)}, u32[]{:S(2)}) collective-permute-start(bf16[336,128]{1,0:T(8,128)(2,1)S(1)} %add_convert_fusion.1), channel_id=1, source_target_pairs={{0,4},{1,5},{2,6},{3,7},{4,0},{5,1},{6,2},{7,3},{8,12},{9,13},{10,... | collective-permute-start | bytes 258056 | tf_op jit(solution)/shard_map/ppermute | solution.py:293
  78.7 4.7 %collective-permute-start.20 = (bf16[336,128]{1,0:T(8,128)(2,1)S(1)}, bf16[336,128]{1,0:T(8,128)(2,1)S(1)}, u32[]{:S(2)}, u32[]{:S(2)}) collective-permute-start(bf16[336,128]{1,0:T(8,128)(2,1)S(1)} %add_convert_fusion.1), channel_id=1, source_target_pairs={{0,1},{1,0},{2,3},{3,2},{4,5},{5,4},{6,7},{7,6},{8,9},{9,8},{10,11... | collective-permute-start | bytes 258056 | tf_op jit(solution)/shard_map/ppermute | solution.py:293
  80.6 9.0 %copy-start.9 = (bf16[8,64,64]{2,1,0:T(8,128)(2,1)}, bf16[8,64,64]{2,1,0:T(8,128)(2,1)S(1)}, u32[]{:S(2)}) copy-start(bf16[8,64,64]{2,1,0:T(8,128)(2,1)S(1)} %collective-permute-done.9.x_hi) | copy-start | bytes 196612
  83.5 17.5 %collective-permute-start.23 = (bf16[1344,128]{1,0:T(8,128)(2,1)S(1)}, bf16[1344,128]{1,0:T(8,128)(2,1)S(1)}, u32[]{:S(2)}, u32[]{:S(2)}) collective-permute-start(bf16[1344,128]{1,0:T(8,128)(2,1)S(1)} %pad_maximum_fusion.1), channel_id=1, source_target_pairs={{0,16},{16,0},{32,48},{48,32},{64,80},{80,64},{96,112},{112,96},{1... | collective-permute-start | bytes 1032200 | tf_op jit(solution)/shard_map/ppermute | solution.py:293
  86.3 5.5 %collective-permute-start.10 = (bf16[6,64,64]{2,1,0:T(8,128)(2,1)S(1)}, bf16[6,64,64]{2,1,0:T(8,128)(2,1)S(1)}, u32[]{:S(2)}, u32[]{:S(2)}) collective-permute-start(bf16[6,64,64]{2,1,0:T(8,128)(2,1)S(1)} %pad_maximum_fusion.4), channel_id=1, source_target_pairs={{0,1},{1,2},{2,3},{3,4},{4,5},{5,6},{6,7},{7,8},{8,9},{9,10},{10,1... | collective-permute-start | bytes 147464 | tf_op jit(solution)/shard_map/ppermute | solution.py:356
  89.6 7.2 %collective-permute-start.11 = (bf16[6,64,64]{2,1,0:T(8,128)(2,1)S(1)}, bf16[6,64,64]{2,1,0:T(8,128)(2,1)S(1)}, u32[]{:S(2)}, u32[]{:S(2)}) collective-permute-start(bf16[6,64,64]{2,1,0:T(8,128)(2,1)S(1)} %pad_maximum_fusion.5), channel_id=1, source_target_pairs={{1,0},{2,1},{3,2},{4,3},{5,4},{6,5},{7,6},{8,7},{9,8},{10,9},{11,1... | collective-permute-start | bytes 147464 | tf_op jit(solution)/shard_map/ppermute | solution.py:357
  91.8 5.1 %copy-start.14 = (bf16[6,64,64]{2,1,0:T(8,128)(2,1)}, bf16[6,64,64]{2,1,0:T(8,128)(2,1)S(1)}, u32[]{:S(2)}) copy-start(bf16[6,64,64]{2,1,0:T(8,128)(2,1)S(1)} %collective-permute-done.10.y_lo) | copy-start | bytes 147460
  96.8 0.6 copy-start.15

commit v2 on v1

--- a/solution.py
+++ b/solution.py
@@ -1,3 +1,4 @@
+import functools
 import math
 
 import jax
@@ -9,11 +10,12 @@
 
 F32 = jnp.float32
 BF16 = jnp.bfloat16
-VMEM_BYTES = 56 * 1024 * 1024
+VMEM_BYTES = 28 * 1024 * 1024
 
 PAIR_ROW = 9 * 64
 DEEP_ROW = 14 * 64
 PAY_ROWS = 42 * 64
+HALF_ROWS = PAY_ROWS // 2
 
 CORE = ("gx", 1, (0,))
 Y_NEAR = ("gx", 2, (1, 2))
@@ -47,34 +49,84 @@
     )
 
 
+def faces_kernel(odd, own, cot, to_core, to_chip, y_head, y_tail):
+    swapped = odd[0] == 1
+    for k in range(4):
+        head = jnp.concatenate([own[0, 2 * k + 1], own[0, 2 * k]], axis=1)
+        tail = jnp.concatenate([own[3, 2 * k], own[3, 2 * k + 1]], axis=1)
+        to_core[k] = jnp.where(swapped, head, tail)
+        to_chip[k] = jnp.where(swapped, tail, head)
+        to_core[4 + k] = jnp.where(swapped, cot[0, k], cot[1, k])
+        to_chip[4 + k] = jnp.where(swapped, cot[1, k], cot[0, k])
+    for k in range(2):
+        y_head[k] = jnp.concatenate([own[2 * k, 0], own[2 * k + 1, 0]], axis=1)
+        y_tail[k] = jnp.concatenate([own[2 * k, 7], own[2 * k + 1, 7]], axis=1)
+        y_head[2 + k] = cot[k, 0]
+        y_tail[2 + k] = cot[k, 3]
+
+
+def faces(odd, own, cot):
+    vmem = pl.BlockSpec(memory_space=pltpu.VMEM)
+    return pl.pallas_call(
+        faces_kernel,
+        in_specs=[pl.BlockSpec(memory_space=pltpu.SMEM), vmem, vmem],
+        out_shape=[jax.ShapeDtypeStruct((8, 64, 128), BF16)] * 2
+        + [jax.ShapeDtypeStruct((4, 64, 128), BF16)] * 2,
+        name="faces",
+    )(odd, own, cot)
+
+
+def level_column(x, y, own, x_lo, x_hi, y_lo, y_hi):
+    if y == 0 or y == 9:
+        pairs = y_lo if y == 0 else y_hi
+        if 1 <= x <= 4:
+            return half(pairs(((x - 1) // 2)), (x - 1) % 2)
+        return half(pairs(2), int((x == 5) == (y == 9)))
+    if x == 0:
+        return half(x_lo((y - 1) // 2), (y - 1) % 2)
+    if x == 5:
+        return half(x_hi((y - 1) // 2), 1 - (y - 1) % 2)
+    return own(x - 1, y - 1)
+
+
+def half(value, which):
+    return value[:, which * 64 : which * 64 + 64]
+
+
 def grads_kernel(
-    own, x_lo, x_hi, y_lo, y_hi, cot, cx_lo, cx_hi, cy_lo, cy_hi, w_up, w_deep,
-    payload, pre_grad, gx_lo, gx_hi, gy_lo, gy_hi,
-    taps, cot_taps, blocks, sums,
+    odd_x, odd_y, own, cot, core, chip, near, far, w_up, w_deep,
+    keep, send, pre_grad, to_core, to_chip, gy_head, gy_tail,
+    taps, cot_taps, blocks, sums, payload,
 ):
+    swap_x = odd_x[0] == 1
+    swap_y = odd_y[0] == 1
+
+    def x_lo(k):
+        return jnp.where(swap_x, core[k], chip[k])
+
+    def x_hi(k):
+        return jnp.where(swap_x, chip[k], core[k])
+
+    def y_lo(k):
+        return jnp.where(swap_y, near[k], far[k])
+
+    def y_hi(k):
+        return jnp.where(swap_y, far[k], near[k])
+
     for x in range(6):
         for y in range(10):
-            if y == 0:
-                row = y_lo[x]
-            elif y == 9:
-                row = y_hi[x]
-            elif x == 0:
-                row = x_lo[y - 1]
-            elif x == 5:
-                row = x_hi[y - 1]
-            else:
-                row = own[x - 1, y - 1]
+            row = level_column(x, y, lambda u, v: own[u, v], x_lo, x_hi, y_lo, y_hi)
             taps[x, y] = depth_taps(row, 64)
     for x in range(4):
         for y in range(6):
             if y == 0:
-                row = cy_lo[x]
+                row = y_lo(3 + x)
             elif y == 5:
-                row = cy_hi[x]
+                row = y_hi(3 + x)
             elif x == 0:
-                row = cx_lo[y - 1]
+                row = x_lo(3 + y)
             elif x == 3:
-                row = cx_hi[y - 1]
+                row = x_hi(3 + y)
             else:
                 row = cot[x - 1, y - 1]
             cot_taps[x, y] = depth_taps(row, 0)
@@ -99,8 +151,8 @@
             pre = pre + jnp.dot(window(taps, x, y), blocks[x, y], preferred_element_type=F32)
     sig = 1.0 / (1.0 + jnp.exp(-pre))
     act = pre * sig
-    half = act[:, :128] + act[:, 128:]
-    pooled = 0.25 * (half[:, :64] + half[:, 64:])
+    summed = act[:, :128] + act[:, 128:]
+    pooled = 0.25 * (summed[:, :64] + summed[:, 64:])
     pooled_t = pooled.T.astype(BF16)
 
     pooled_grad = jnp.zeros((512, 64), F32)
@@ -119,17 +171,17 @@
     rounded = grad.astype(BF16)
     pre_grad[...] = rounded
 
-    def column(x, y):
-        at = (x % 2) * 128 + (y % 2) * 64
-        top = ((x // 2) * 4 + y // 2) * 64
-        return rounded[top : top + 64, at : at + 64]
-
-    for y in range(8):
-        gx_lo[y] = column(0, y)
-        gx_hi[y] = column(3, y)
-    for x in range(4):
-        gy_lo[x] = column(x, 0)
-        gy_hi[x] = column(x, 7)
+    for k in range(4):
+        head = rounded[k * 64 : k * 64 + 64, 0:128]
+        head = jnp.concatenate([half(head, 1), half(head, 0)], axis=1)
+        tail = rounded[256 + k * 64 : 320 + k * 64, 128:256]
+        to_core[k] = jnp.where(swap_x, head, tail)
+        to_chip[k] = jnp.where(swap_x, tail, head)
+    for k in range(2):
+        first = rounded[k * 256 : k * 256 + 64]
+        last = rounded[k * 256 + 192 : k * 256 + 256]
+        gy_head[k] = jnp.concatenate([first[:, 0:64], first[:, 128:192]], axis=1)
+        gy_tail[k] = jnp.concatenate([last[:, 64:128], last[:, 192:256]], axis=1)
 
     for a in range(3):
         for b in range(3):
@@ -161,50 +213,65 @@
         top = PAIR_ROW + k * 64
         payload[top : top + 64, :] = jnp.concatenate([left, right], axis=1).astype(BF16)
     payload[PAY_ROWS - 64 :, :] = jnp.zeros((64, 128), BF16)
-
-
-def local_grads(own, x_lo, x_hi, y_lo, y_hi, cot, cx_lo, cx_hi, cy_lo, cy_hi, w_up, w_deep):
+    mine = pl.multiple_of(odd_x[0] * HALF_ROWS, HALF_ROWS)
+    keep[...] = payload[pl.ds(mine, HALF_ROWS), :]
+    send[...] = payload[pl.ds(HALF_ROWS - mine, HALF_ROWS), :]
+
+
+def local_grads(odd_x, odd_y, own, cot, core, chip, near, far, w_up, w_deep):
+    smem = pl.BlockSpec(memory_space=pltpu.SMEM)
+    vmem = pl.BlockSpec(memory_space=pltpu.VMEM)
     return pl.pallas_call(
         grads_kernel,
+        in_specs=[smem, smem] + [vmem] * 8,
         out_shape=[
-            jax.ShapeDtypeStruct((PAY_ROWS, 128), BF16),
+            jax.ShapeDtypeStruct((HALF_ROWS, 128), BF16),
+            jax.ShapeDtypeStruct((HALF_ROWS, 128), BF16),
             jax.ShapeDtypeStruct((512, 256), BF16),
-            jax.ShapeDtypeStruct((8, 64, 64), BF16),
-            jax.ShapeDtypeStruct((8, 64, 64), BF16),
-            jax.ShapeDtypeStruct((4, 64, 64), BF16),
-            jax.ShapeDtypeStruct((4, 64, 64), BF16),
+            jax.ShapeDtypeStruct((4, 64, 128), BF16),
+            jax.ShapeDtypeStruct((4, 64, 128), BF16),
+            jax.ShapeDtypeStruct((2, 64, 128), BF16),
+            jax.ShapeDtypeStruct((2, 64, 128), BF16),
         ],
         scratch_shapes=[
             pltpu.VMEM((6, 10, 64, 256), BF16),
             pltpu.VMEM((4, 6, 64, 384), BF16),
             pltpu.VMEM((4, 4, 256, 256), BF16),
             pltpu.VMEM((9, 64, 256), F32),
+            pltpu.VMEM((PAY_ROWS, 128), BF16),
         ],
         compiler_params=pltpu.CompilerParams(vmem_limit_bytes=VMEM_BYTES),
         cost_estimate=pl.CostEstimate(
             flops=4_000_000_000, bytes_accessed=4_000_000, transcendentals=131072
         ),
         name="local_grads",
-    )(own, x_lo, x_hi, y_lo, y_hi, cot, cx_lo, cx_hi, cy_lo, cy_hi, w_up, w_deep)
-
-
-def input_kernel(pre_grad, x_lo, x_hi, y_lo, y_hi, w_up, out, taps):
+    )(odd_x, odd_y, own, cot, core, chip, near, far, w_up, w_deep)
+
+
+def input_kernel(odd_x, odd_y, pre_grad, core, chip, near, far, w_up, out, taps):
+    swap_x = odd_x[0] == 1
+    swap_y = odd_y[0] == 1
+
+    def x_lo(k):
+        return jnp.where(swap_x, core[k], chip[k])
+
+    def x_hi(k):
+        return jnp.where(swap_x, chip[k], core[k])
+
+    def y_lo(k):
+        return jnp.where(swap_y, near[k], far[k])
+
+    def y_hi(k):
+        return jnp.where(swap_y, far[k], near[k])
+
+    def own(u, v):
+        at = (u % 2) * 128 + (v % 2) * 64
+        top = ((u // 2) * 4 + v // 2) * 64
+        return pre_grad[top : top + 64, at : at + 64]
+
     for x in range(6):
         for y in range(10):
-            if y == 0:
-                row = y_lo[x]
-            elif y == 9:
-                row = y_hi[x]
-            elif x == 0:
-                row = x_lo[y - 1]
-            elif x == 5:
-                row = x_hi[y - 1]
-            else:
-                u, v = x - 1, y - 1
-                at = (u % 2) * 128 + (v % 2) * 64
-                top = ((u // 2) * 4 + v // 2) * 64
-                row = pre_grad[top : top + 64, at : at + 64]
-            taps[x, y] = depth_taps(row, 64)
+            taps[x, y] = depth_taps(level_column(x, y, own, x_lo, x_hi, y_lo, y_hi), 64)
     empty = jnp.zeros((64, 256), BF16)
     spare = jnp.zeros((64, 64), BF16)
     weights = {}
@@ -231,9 +298,12 @@
             out[x, y] = total[top : top + 64, at : at + 64]
 
 
-def local_input(pre_grad, x_lo, x_hi, y_lo, y_hi, w_up):
+def local_input(odd_x, odd_y, pre_grad, core, chip, near, far, w_up):
+    smem = pl.BlockSpec(memory_space=pltpu.SMEM)
+    vmem = pl.BlockSpec(memory_space=pltpu.VMEM)
     return pl.pallas_call(
         input_kernel,
+        in_specs=[smem, smem] + [vmem] * 6,
         out_shape=jax.ShapeDtypeStruct((4, 8, 64, 64), BF16),
         scratch_shapes=[pltpu.VMEM((6, 10, 64, 256), BF16)],
         compiler_params=pltpu.CompilerParams(vmem_limit_bytes=VMEM_BYTES),
@@ -241,15 +311,18 @@
             flops=1_000_000_000, bytes_accessed=4_000_000, transcendentals=0
         ),
         name="local_input",
-    )(pre_grad, x_lo, x_hi, y_lo, y_hi, w_up)
-
-
-def unpack_kernel(up_scale, deep_scale, payload, up, deep):
+    )(odd_x, odd_y, pre_grad, core, chip, near, far, w_up)
+
+
+def unpack_kernel(up_scale, deep_scale, odd, mine, other, up, deep, payload):
+    first = pl.multiple_of(odd[0] * HALF_ROWS, HALF_ROWS)
+    payload[pl.ds(first, HALF_ROWS), :] = mine[...]
+    payload[pl.ds(HALF_ROWS - first, HALF_ROWS), :] = other[...]
     for k in range(9):
         a, b = k // 3, k % 3
-        first = payload[k * 64 : k * 64 + 64, :].astype(F32).T * up_scale
-        up[a, b, 0] = first[:64]
-        up[a, b, 1] = first[64:]
+        pair = payload[k * 64 : k * 64 + 64, :].astype(F32).T * up_scale
+        up[a, b, 0] = pair[:64]
+        up[a, b, 1] = pair[64:]
     for k in range(5):
         top = PAIR_ROW + k * 64
         pair = payload[top : top + 64, :].astype(F32).T * up_scale
@@ -261,19 +334,19 @@
         deep[k // 9, k // 3 % 3, k % 3] = payload[top : top + 64, :].astype(F32) * deep_scale
 
 
-def unpack(payload, up_scale, deep_scale):
-    def body(*refs):
-        unpack_kernel(up_scale, deep_scale, *refs)
-
+def unpack(odd, mine, other, up_scale, deep_scale):
+    vmem = pl.BlockSpec(memory_space=pltpu.VMEM)
     return pl.pallas_call(
-        body,
+        functools.partial(unpack_kernel, up_scale, deep_scale),
+        in_specs=[pl.BlockSpec(memory_space=pltpu.SMEM), vmem, vmem],
         out_shape=[
             jax.ShapeDtypeStruct((3, 3, 3, 64, 64), F32),
             jax.ShapeDtypeStruct((3, 3, 3, 64, 128), F32),
         ],
+        scratch_shapes=[pltpu.VMEM((PAY_ROWS, 128), BF16)],
         compiler_params=pltpu.CompilerParams(vmem_limit_bytes=VMEM_BYTES),
         name="unpack",
-    )(payload)
+    )(odd, mine, other)
 
 
 def side_bit(step):
@@ -342,49 +415,67 @@
     return jnp.concatenate(found)
 
 
-def sum_everywhere(value):
-    value = scatter_sum(value, (CORE,))
-    value = scatter_sum(value, (Z_NEAR, X_NEAR))
-    for step in (Z_FAR, X_FAR, Y_NEAR, Y_FAR):
-        value = swap_sum(value, (step,))
-    value = gather(value, (Z_NEAR, X_NEAR))
-    return gather(value, (CORE,))
-
-
-def neighbours(head, tail, axis):
-    count = lax.axis_size(axis)
-    before = lax.ppermute(tail, axis, [(i, i + 1) for i in range(count - 1)])
-    after = lax.ppermute(head, axis, [(i + 1, i) for i in range(count - 1)])
-    return before, after
+def pairs_of(axis, first):
+    found = []
+    for i in range(first, lax.axis_size(axis) - 1, 2):
+        found += [(i, i + 1), (i + 1, i)]
+    return found
+
+
+def both_sides(first, second, axis):
+    return (
+        lax.ppermute(first, axis, pairs_of(axis, 0)),
+        lax.ppermute(second, axis, pairs_of(axis, 1)),
+    )
+
+
+def column_ends(odd_x, odd_y, core, chip, head, tail, level_rows):
+    lo = jnp.where(odd_x == 1, core, chip)
+    hi = jnp.where(odd_x == 1, chip, core)
+    left = lax.broadcasted_iota(jnp.int32, (1, 64, 128), 2) < 64
+    head = [head[:2], jnp.where(left, lo[0:1], hi[0:1])] + (
+        [lo[4:5], head[2:], hi[4:5]] if level_rows else []
+    )
+    tail = [tail[:2], jnp.where(left, hi[3:4], lo[3:4])] + (
+        [lo[7:8], tail[2:], hi[7:8]] if level_rows else []
+    )
+    head, tail = jnp.concatenate(head), jnp.concatenate(tail)
+    return jnp.where(odd_y == 1, head, tail), jnp.where(odd_y == 1, tail, head)
 
 
 def local(level_input, weight_upper, weight_deep, deep_cotangent):
     tiles = lax.axis_size("gx") * lax.axis_size("gy")
     up_scale = 1.0 / math.sqrt(math.prod(level_input.shape[:3]) * tiles)
     deep_scale = 1.0 / math.sqrt(math.prod(deep_cotangent.shape[:3]) * tiles)
-    own, cot = level_input, deep_cotangent
-
-    x_lo, x_hi = neighbours(own[0], own[3], "gx")
-    cx_lo, cx_hi = neighbours(cot[0], cot[1], "gx")
-
-    def side(lo, mid, hi, y):
-        return jnp.concatenate([lo[None, y], mid[:, y], hi[None, y]])
-
-    y_lo, y_hi = neighbours(side(x_lo, own, x_hi, 0), side(x_lo, own, x_hi, 7), "gy")
-    cy_lo, cy_hi = neighbours(side(cx_lo, cot, cx_hi, 0), side(cx_lo, cot, cx_hi, 3), "gy")
-
-    payload, pre_grad, gx_lo, gx_hi, gy_lo, gy_hi = local_grads(
-        own, x_lo, x_hi, y_lo, y_hi, cot, cx_lo, cx_hi, cy_lo, cy_hi, weight_upper, weight_deep
-    )
-    gx_lo, gx_hi = neighbours(gx_lo, gx_hi, "gx")
-    gy_lo, gy_hi = neighbours(
-        jnp.concatenate([gx_lo[None, 0], gy_lo, gx_hi[None, 0]]),
-        jnp.concatenate([gx_lo[None, 7], gy_hi, gx_hi[None, 7]]),
-        "gy",
-    )
-    input_grad = local_input(pre_grad, gx_lo, gx_hi, gy_lo, gy_hi, weight_upper)
-    total = sum_everywhere(payload)
-    upper, deep = unpack(total, up_scale, deep_scale)
+    odd_x = (lax.axis_index("gx") & 1).astype(jnp.int32)
+    odd_y = (lax.axis_index("gy") & 1).astype(jnp.int32)
+    flag_x, flag_y = odd_x.reshape(1), odd_y.reshape(1)
+
+    to_core, to_chip, y_head, y_tail = faces(flag_x, level_input, deep_cotangent)
+    core, chip = both_sides(to_core, to_chip, "gx")
+    to_near, to_far = column_ends(odd_x, odd_y, core, chip, y_head, y_tail, True)
+    near, far = both_sides(to_near, to_far, "gy")
+
+    keep, send, pre_grad, to_core, to_chip, y_head, y_tail = local_grads(
+        flag_x, flag_y, level_input, deep_cotangent, core, chip, near, far,
+        weight_upper, weight_deep,
+    )
+    total = tree_sum([keep, swap(send, (CORE,), 1)])
+    core, chip = both_sides(to_core, to_chip, "gx")
+    total = scatter_sum(total, (Z_NEAR, X_NEAR))
+    total, core, chip = lax.optimization_barrier((total, core, chip))
+    to_near, to_far = column_ends(odd_x, odd_y, core, chip, y_head, y_tail, False)
+    near, far = both_sides(to_near, to_far, "gy")
+    total = swap_sum(total, (Z_FAR,))
+    total, near, far = lax.optimization_barrier((total, near, far))
+    input_grad = local_input(
+        flag_x, flag_y, pre_grad, core, chip, near, far, weight_upper
+    )
+    for step in (X_FAR, Y_NEAR, Y_FAR):
+        total = swap_sum(total, (step,))
+    total = gather(total, (Z_NEAR, X_NEAR))
+    other = swap(total, (CORE,), 1)
+    upper, deep = unpack(flag_x, total, other, up_scale, deep_scale)
     return (input_grad, upper, deep)
 
 

time: 105 us -> 76.5 us (0.73)
  starting transfers between devices: 54.1 us -> 40.2 us
  waiting for transfers between devices: 27.2 us -> 21.2 us
  local copies, waits for them, and re-layouts: 5.86 us -> 1.61 us
  Pallas kernels: 14.8 us -> 11.9 us
  other arithmetic: 1.52 us -> 0.42 us
    ppermute x12 -> x8, starting transfers between devices: 34.3 us -> 13.2 us  [the longest x4 9.18 us: both_sides(): lax.ppermute(second, axis, pairs_of(axis, 1))]
    ppermute x12, starting transfers between devices: 19.8 us -> 27 us  [swap(): lax.ppermute(value, axis, [(i, i ^ masks[axis]) for i in range(count)])]
    ppermute x12 -> x8, waiting for transfers between devices: 11.1 us -> 7.21 us  [the longest x4 4.51 us: both_sides(): lax.ppermute(second, axis, pairs_of(axis, 1))]
    pallas_call x3 -> x4, Pallas kernels: 14.8 us -> 11.9 us  [the longest x1 6.31 us: local_grads(): pl.pallas_call(grads_kernel, in_specs=[smem, smem] + [vmem] * 8, out_shap...]
    squeeze x4 -> x0, local copies, waits for them, and re-layouts: 2.8 us -> none  [the longest x1 0.99 us: local(): x_lo, x_hi = neighbours(own[0], own[3], 'gx')]
    ppermute x12, waiting for transfers between devices: 16.1 us -> 14 us  [swap(): lax.ppermute(value, axis, [(i, i ^ masks[axis]) for i in range(count)])]
    dynamic_slice x2 -> x1, local copies, waits for them, and re-layouts: 1.1 us -> 0.03 us  [scatter_sum(): piece = lax.dynamic_slice_in_dim(value, (me ^ k) * rows, rows, 0)]
  transfers between devices with their start and end apart: 24 -> 20, of which waited for: 12 -> 12; matrix products, arithmetic and copies ran while one was open for 2% -> 1% of each run, Pallas kernels for 3% -> 3%
where the time goes in v2:
time: 76.5 us; the launch traced here: 76.2 us
  starting transfers between devices  40.2 us (53%)
  waiting for transfers between devices  21.2 us (28%)
  Pallas kernels  11.9 us (16%)
  local copies, waits for them, and re-layouts  1.61 us (2%)
  between operations  0.92 us (1%)
    ppermute x12, starting transfers between devices, swap(): lax.ppermute(value, axis, [(i, i ^ masks[axis]) for i in range(count)])  27 us
    ppermute x12, waiting for transfers between devices, swap(): lax.ppermute(value, axis, [(i, i ^ masks[axis]) for i in range(count)])  14 us
    ppermute x4, starting transfers between devices, both_sides(): lax.ppermute(second, axis, pairs_of(axis, 1))  9.18 us
    pallas_call x1, Pallas kernels, local_grads(): pl.pallas_call(grads_kernel, in_specs=[smem, smem] + [vmem] * 8, out_shap...  6.31 us
    ppermute x4, waiting for transfers between devices, both_sides(): lax.ppermute(second, axis, pairs_of(axis, 1))  4.51 us
    ppermute x4, starting transfers between devices, both_sides(): lax.ppermute(first, axis, pairs_of(axis, 0))  4.02 us
    ppermute x4, waiting for transfers between devices, both_sides(): lax.ppermute(first, axis, pairs_of(axis, 0))  2.7 us
    pallas_call x1, Pallas kernels, local_input(): pl.pallas_call(input_kernel, in_specs=[smem, smem] + [vmem] * 6, out_shap...  2.18 us
  transfers between devices with their start and end apart: 20, of which 12 were waited for; matrix products, arithmetic and copies ran while one was open for 1% of the time, Pallas kernels for 3%

profile of v2, /device:TPU:1, one launch (start us, length us, event | category | flops | bytes accessed | tf_op | source)
XLA Modules:
  0.0 76.2 jit_solution(1854935416433232266)
XLA Ops:
  0.6 1.9 %faces.1 = (bf16[8,64,128]{2,1,0:T(8,128)(2,1)}, bf16[8,64,128]{2,1,0:T(8,128)(2,1)}, bf16[4,64,128]{2,1,0:T(8,128)(2,1)}, bf16[4,64,128]{2,1,0:T(8,128)(2,1)}) custom-call(s32[1]{0:T(128)} %bitcast.odd.odd_x, bf16[4,8,64,64]{3,2,1,0:T(8,128)(2,1)} %own.3, bf16[2,4,64,128]{3,2,1,0:T(8,128)(2,1)} %cot.3), custom_call_target="tpu_custom_call" | custom-call | tf_op jit(solution)/shard_map/faces/pallas_call | solution.py:70
  2.6 1.4 %collective-permute-start = (bf16[8,64,128]{2,1,0:T(8,128)(2,1)}, bf16[8,64,128]{2,1,0:T(8,128)(2,1)S(1)}, u32[]{:S(2)}, u32[]{:S(2)}) collective-permute-start(bf16[8,64,128]{2,1,0:T(8,128)(2,1)} %get-tuple-element.22), channel_id=1, source_target_pairs={{0,16},{16,0},{32,48},{48,32},{64,80},{80,64},{96,112},{112,96},{1... | collective-permute-start | bytes 393224 | tf_op jit(solution)/shard_map/ppermute | solution.py:427
  4.0 3.3 %collective-permute-start.1 = (bf16[8,64,128]{2,1,0:T(8,128)(2,1)}, bf16[8,64,128]{2,1,0:T(8,128)(2,1)S(1)}, u32[]{:S(2)}, u32[]{:S(2)}) collective-permute-start(bf16[8,64,128]{2,1,0:T(8,128)(2,1)} %get-tuple-element.23), channel_id=1, source_target_pairs={{16,32},{32,16},{48,64},{64,48},{80,96},{96,80},{17,33},{33,17},{4... | collective-permute-start | bytes 393224 | tf_op jit(solution)/shard_map/ppermute | solution.py:428
  7.3 0.8 slice_dynamic-update-slice_fusion.1
  8.1 0.0 collective-permute-done.core
  8.1 2.7 %collective-permute-done.1.chip = bf16[8,64,128]{2,1,0:T(8,128)(2,1)S(1)} collective-permute-done((bf16[8,64,128]{2,1,0:T(8,128)(2,1)}, bf16[8,64,128]{2,1,0:T(8,128)(2,1)S(1)}, u32[]{:S(2)}, u32[]{:S(2)}) %collective-permute-start.1) | collective-permute-done | bytes 131104 | tf_op jit(solution)/shard_map/ppermute | solution.py:428
  10.8 0.0 copy-start
  10.9 0.8 copy-done.5
  11.7 0.0 copy-start.1
  11.7 1.8 %collective-permute-start.2 = (bf16[7,64,128]{2,1,0:T(8,128)(2,1)S(1)}, bf16[7,64,128]{2,1,0:T(8,128)(2,1)S(1)}, u32[]{:S(2)}, u32[]{:S(2)}) collective-permute-start(bf16[7,64,128]{2,1,0:T(8,128)(2,1)S(1)} %get-tuple-element.53), channel_id=1, source_target_pairs={{0,1},{1,0},{2,3},{3,2},{4,5},{5,4},{6,7},{7,6},{8,9},{9,8},{10,11... | collective-permute-start | bytes 344072 | tf_op jit(solution)/shard_map/ppermute | solution.py:427
  13.5 0.7 collective-permute-start.3
  14.2 1.5 %collective-permute-done.2.near = bf16[7,64,128]{2,1,0:T(8,128)(2,1)S(1)} collective-permute-done((bf16[7,64,128]{2,1,0:T(8,128)(2,1)S(1)}, bf16[7,64,128]{2,1,0:T(8,128)(2,1)S(1)}, u32[]{:S(2)}, u32[]{:S(2)}) %collective-permute-start.2) | collective-permute-done | bytes 114720 | tf_op jit(solution)/shard_map/ppermute | solution.py:427
  15.7 0.0 collective-permute-done.3.far
  15.7 6.3 %local_grads.1 = (bf16[1344,128]{1,0:T(8,128)(2,1)S(1)}, bf16[1344,128]{1,0:T(8,128)(2,1)S(1)}, bf16[512,256]{1,0:T(8,128)(2,1)S(1)}, bf16[4,64,128]{2,1,0:T(8,1...) custom-call(s32[1]{0:T(128)} %bitcast.odd.odd_x, ...), custom_call_target="tpu_custom_call" | custom-call | flops 4000000000 | bytes 4000000 | tf_op jit(solution)/shard_map/local_grads/pallas_call | solution.py:224
  22.0 0.1 collective-permute-start.4
  22.2 1.6 %collective-permute-done.4 = bf16[1344,128]{1,0:T(8,128)(2,1)S(1)} collective-permute-done((bf16[1344,128]{1,0:T(8,128)(2,1)S(1)}, bf16[1344,128]{1,0:T(8,128)(2,1)S(1)}, u32[]{:S(2)}, u32[]{:S(2)}) %collective-permute-start.4) | collective-permute-done | bytes 344096 | tf_op jit(solution)/shard_map/ppermute | solution.py:366
  23.8 0.1 add_convert_fusion
  23.9 4.9 %collective-permute-start.5 = (bf16[336,128]{1,0:T(8,128)(2,1)S(1)}, bf16[336,128]{1,0:T(8,128)(2,1)S(1)}, u32[]{:S(2)}, u32[]{:S(2)}) collective-permute-start(bf16[336,128]{1,0:T(8,128)(2,1)S(1)} %get-tuple-element.45), channel_id=1, source_target_pairs={{0,1},{1,0},{2,3},{3,2},{4,5},{5,4},{6,7},{7,6},{8,9},{9,8},{10,11... | collective-permute-start | bytes 258056 | tf_op jit(solution)/shard_map/ppermute | solution.py:366
  28.8 1.9 %collective-permute-start.6 = (bf16[336,128]{1,0:T(8,128)(2,1)S(1)}, bf16[336,128]{1,0:T(8,128)(2,1)S(1)}, u32[]{:S(2)}, u32[]{:S(2)}) collective-permute-start(bf16[336,128]{1,0:T(8,128)(2,1)S(1)} %get-tuple-element.47), channel_id=1, source_target_pairs={{0,4},{1,5},{2,6},{3,7},{4,0},{5,1},{6,2},{7,3},{8,12},{9,13},{10,... | collective-permute-start | bytes 258056 | tf_op jit(solution)/shard_map/ppermute | solution.py:366
  30.7 1.1 %collective-permute-start.7 = (bf16[336,128]{1,0:T(8,128)(2,1)S(1)}, bf16[336,128]{1,0:T(8,128)(2,1)S(1)}, u32[]{:S(2)}, u32[]{:S(2)}) collective-permute-start(bf16[336,128]{1,0:T(8,128)(2,1)S(1)} %get-tuple-element.46), channel_id=1, source_target_pairs={{0,5},{1,4},{2,7},{3,6},{4,1},{5,0},{6,3},{7,2},{8,13},{9,12},{10,... | collective-permute-start | bytes 258056 | tf_op jit(solution)/shard_map/ppermute | solution.py:366
  31.8 0.7 collective-permute-start.8
  32.5 4.6 %collective-permute-start.9 = (bf16[4,64,128]{2,1,0:T(8,128)(2,1)S(1)}, bf16[4,64,128]{2,1,0:T(8,128)(2,1)S(1)}, u32[]{:S(2)}, u32[]{:S(2)}) collective-permute-start(bf16[4,64,128]{2,1,0:T(8,128)(2,1)S(1)} %get-tuple-element.30), channel_id=1, source_target_pairs={{16,32},{32,16},{48,64},{64,48},{80,96},{96,80},{17,33},{33,17},{4... | collective-permute-start | bytes 196616 | tf_op jit(solution)/shard_map/ppermute | solution.py:428
  37.1 0.0 collective-permute-done.5
  37.1 0.0 collective-permute-done.6
  37.1 0.0 collective-permute-done.7
  37.1 0.1 add_convert_fusion.5
  37.2 1.8 %collective-permute-done.9.chip = bf16[4,64,128]{2,1,0:T(8,128)(2,1)S(1)} collective-permute-done((bf16[4,64,128]{2,1,0:T(8,128)(2,1)S(1)}, bf16[4,64,128]{2,1,0:T(8,128)(2,1)S(1)}, u32[]{:S(2)}, u32[]{:S(2)}) %collective-permute-start.9) | collective-permute-done | bytes 65568 | tf_op jit(solution)/shard_map/ppermute | solution.py:428
  39.0 2.8 %collective-permute-start.10 = (bf16[336,128]{1,0:T(8,128)(2,1)S(1)}, bf16[336,128]{1,0:T(8,128)(2,1)S(1)}, u32[]{:S(2)}, u32[]{:S(2)}) collective-permute-start(bf16[336,128]{1,0:T(8,128)(2,1)S(1)} %add_convert_fusion.5), channel_id=1, source_target_pairs={{0,3},{1,2},{2,1},{3,0},{4,7},{5,6},{6,5},{7,4},{8,11},{9,10},{10,... | collective-permute-start | bytes 258056 | tf_op jit(solution)/shard_map/ppermute | solution.py:366
  41.9 0.1 collective-permute-start.11
  42.0 0.7 collective-permute-start.12
  42.6 1.1 %collective-permute-done.10 = bf16[336,128]{1,0:T(8,128)(2,1)S(1)} collective-permute-done((bf16[336,128]{1,0:T(8,128)(2,1)S(1)}, bf16[336,128]{1,0:T(8,128)(2,1)S(1)}, u32[]{:S(2)}, u32[]{:S(2)}) %collective-permute-start.10) | collective-permute-done | bytes 86048 | tf_op jit(solution)/shard_map/ppermute | solution.py:366
  43.7 1.2 %collective-permute-done.11.near = bf16[3,64,128]{2,1,0:T(8,128)(2,1)S(1)} collective-permute-done((bf16[3,64,128]{2,1,0:T(8,128)(2,1)S(1)}, bf16[3,64,128]{2,1,0:T(8,128)(2,1)S(1)}, u32[]{:S(2)}, u32[]{:S(2)}) %collective-permute-start.11) | collective-permute-done | bytes 49184 | tf_op jit(solution)/shard_map/ppermute | solution.py:427
  44.9 0.0 collective-permute-done.12.far
  44.9 5.5 %collective-permute-start.13 = (bf16[336,128]{1,0:T(8,128)(2,1)S(1)}, bf16[336,128]{1,0:T(8,128)(2,1)S(1)}, u32[]{:S(2)}, u32[]{:S(2)}) collective-permute-start(bf16[336,128]{1,0:T(8,128)(2,1)S(1)} %add_convert_fusion.4), channel_id=1, source_target_pairs={{0,12},{1,13},{2,14},{3,15},{4,8},{5,9},{6,10},{7,11},{8,4},{9,5},... | collective-permute-start | bytes 258056 | tf_op jit(solution)/shard_map/ppermute | solution.py:366
  50.4 2.6 %collective-permute-done.13 = bf16[336,128]{1,0:T(8,128)(2,1)S(1)} collective-permute-done((bf16[336,128]{1,0:T(8,128)(2,1)S(1)}, bf16[336,128]{1,0:T(8,128)(2,1)S(1)}, u32[]{:S(2)}, u32[]{:S(2)}) %collective-permute-start.13) | collective-permute-done | bytes 86048 | tf_op jit(solution)/shard_map/ppermute | solution.py:366
  53.0 1.0 %collective-permute-start.14 = (bf16[336,128]{1,0:T(8,128)(2,1)S(1)}, bf16[336,128]{1,0:T(8,128)(2,1)S(1)}, u32[]{:S(2)}, u32[]{:S(2)}) collective-permute-start(bf16[336,128]{1,0:T(8,128)(2,1)S(1)} %add_convert_fusion.3), channel_id=1, source_target_pairs={{0,32},{16,48},{32,0},{48,16},{64,96},{80,112},{96,64},{112,80},{1... | collective-permute-start | bytes 258056 | tf_op jit(solution)/shard_map/ppermute | solution.py:366
  54.0 2.4 %collective-permute-done.14 = bf16[336,128]{1,0:T(8,128)(2,1)S(1)} collective-permute-done((bf16[336,128]{1,0:T(8,128)(2,1)S(1)}, bf16[336,128]{1,0:T(8,128)(2,1)S(1)}, u32[]{:S(2)}, u32[]{:S(2)}) %collective-permute-start.14) | collective-permute-done | bytes 86048 | tf_op jit(solution)/shard_map/ppermute | solution.py:366
  56.5 1.4 %collective-permute-start.15 = (bf16[336,128]{1,0:T(8,128)(2,1)S(1)}, bf16[336,128]{1,0:T(8,128)(2,1)S(1)}, u32[]{:S(2)}, u32[]{:S(2)}) collective-permute-start(bf16[336,128]{1,0:T(8,128)(2,1)S(1)} %add_convert_fusion.2), channel_id=1, source_target_pairs={{0,96},{16,112},{32,64},{48,80},{64,32},{80,48},{96,0},{112,16},{1... | collective-permute-start | bytes 258056 | tf_op jit(solution)/shard_map/ppermute | solution.py:366
  57.9 3.2 %collective-permute-done.15 = bf16[336,128]{1,0:T(8,128)(2,1)S(1)} collective-permute-done((bf16[336,128]{1,0:T(8,128)(2,1)S(1)}, bf16[336,128]{1,0:T(8,128)(2,1)S(1)}, u32[]{:S(2)}, u32[]{:S(2)}) %collective-permute-start.15) | collective-permute-done | bytes 86048 | tf_op jit(solution)/shard_map/ppermute | solution.py:366
  61.1 0.9 %collective-permute-start.16 = (bf16[336,128]{1,0:T(8,128)(2,1)S(1)}, bf16[336,128]{1,0:T(8,128)(2,1)S(1)}, u32[]{:S(2)}, u32[]{:S(2)}) collective-permute-start(bf16[336,128]{1,0:T(8,128)(2,1)S(1)} %add_convert_fusion.1), channel_id=1, source_target_pairs={{0,1},{1,0},{2,3},{3,2},{4,5},{5,4},{6,7},{7,6},{8,9},{9,8},{10,11... | collective-permute-start | bytes 258056 | tf_op jit(solution)/shard_map/ppermute | solution.py:366
  62.0 0.7 collective-permute-start.17
  62.7 1.1 %collective-permute-start.18 = (bf16[336,128]{1,0:T(8,128)(2,1)S(1)}, bf16[336,128]{1,0:T(8,128)(2,1)S(1)}, u32[]{:S(2)}, u32[]{:S(2)}) collective-permute-start(bf16[336,128]{1,0:T(8,128)(2,1)S(1)} %add_convert_fusion.1), channel_id=1, source_target_pairs={{0,5},{1,4},{2,7},{3,6},{4,1},{5,0},{6,3},{7,2},{8,13},{9,12},{10,... | collective-permute-start | bytes 258056 | tf_op jit(solution)/shard_map/ppermute | solution.py:366
  63.9 0.7 collective-permute-done.16
  64.5 0.8 %collective-permute-done.17 = bf16[336,128]{1,0:T(8,128)(2,1)S(1)} collective-permute-done((bf16[336,128]{1,0:T(8,128)(2,1)S(1)}, bf16[336,128]{1,0:T(8,128)(2,1)S(1)}, u32[]{:S(2)}, u32[]{:S(2)}) %collective-permute-start.17) | collective-permute-done | bytes 86048 | tf_op jit(solution)/shard_map/ppermute | solution.py:366
  65.4 1.6 %collective-permute-done.18 = bf16[336,128]{1,0:T(8,128)(2,1)S(1)} collective-permute-done((bf16[336,128]{1,0:T(8,128)(2,1)S(1)}, bf16[336,128]{1,0:T(8,128)(2,1)S(1)}, u32[]{:S(2)}, u32[]{:S(2)}) %collective-permute-start.18) | collective-permute-done | bytes 86048 | tf_op jit(solution)/shard_map/ppermute | solution.py:366
  67.0 5.5 %collective-permute-start.19 = (bf16[1344,128]{1,0:T(8,128)(2,1)S(1)}, bf16[1344,128]{1,0:T(8,128)(2,1)S(1)}, u32[]{:S(2)}, u32[]{:S(2)}) collective-permute-start(bf16[1344,128]{1,0:T(8,128)(2,1)S(1)} %pad_maximum_fusion.mine), channel_id=1, source_target_pairs={{0,16},{16,0},{32,48},{48,32},{64,80},{80,64},{96,112},{112,96},{1... | collective-permute-start | bytes 1032200 | tf_op jit(solution)/shard_map/ppermute | solution.py:366
  72.6 2.2 %local_input.1 = bf16[4,8,64,64]{3,2,1,0:T(8,128)(2,1)} custom-call(s32[1]{0:T(128)} %bitcast.odd.odd_x, s32[1]{0:T(128)} %bitcast.1.odd_y, bf16[512,256]{1,0:T(8,128)(2,1)S(1)} %get-tuple-element.26.pre_grad, bf16[4,64,128]{2,1,0:T(8,128)(2,1)S(1)} %collective-permute-done.8.core, bf16[4,64,128]{2,1,0:T(8,128)(2,1)S(1)} %collective-permute-done.9.chip, ...), custom_call_target="tpu_custom_call" | custom-call | flops 1000000000 | bytes 4000000 | tf_op jit(solution)/shard_map/local_input/pallas_call | solution.py:304
  74.7 1.5 %unpack.1 = (f32[3,3,3,64,64]{4,3,2,1,0:T(8,128)}, f32[3,3,3,64,128]{4,3,2,1,0:T(8,128)}) custom-call(s32[1]{0:T(128)} %bitcast.odd.odd_x, bf16[1344,128]{1,0:T(8,128)(2,1)S(1)} %pad_maximum_fusion.mine, bf16[1344,128]{1,0:T(8,128)(2,1)S(1)} %collective-permute-done.19.other), custom_call_target="tpu_custom_call" | custom-call | tf_op jit(solution)/shard_map/unpack/pallas_call | solution.py:339
  (29 shorter events, 0.4 us)
Async XLA Ops:
  0.6 15.1 %copy-start.3 = (bf16[3,3,3,64,64]{4,3,2,1,0:T(8,128)(2,1)S(1)}, bf16[3,3,3,64,64]{4,3,2,1,0:T(8,128)(2,1)}, u32[]{:S(2)}) copy-start(bf16[3,3,3,64,64]{4,3,2,1,0:T(8,128)(2,1)} %w_up.3) | copy-start | bytes 663556
  2.6 5.5 %copy-start.4 = (bf16[4,64,128]{2,1,0:T(8,128)(2,1)S(1)}, bf16[4,64,128]{2,1,0:T(8,128)(2,1)}, u32[]{:S(2)}) copy-start(bf16[4,64,128]{2,1,0:T(8,128)(2,1)} %get-tuple-element.24) | copy-start | bytes 196612
  2.6 5.5 %collective-permute-start = (bf16[8,64,128]{2,1,0:T(8,128)(2,1)}, bf16[8,64,128]{2,1,0:T(8,128)(2,1)S(1)}, u32[]{:S(2)}, u32[]{:S(2)}) collective-permute-start(bf16[8,64,128]{2,1,0:T(8,128)(2,1)} %get-tuple-element.22), channel_id=1, source_target_pairs={{0,16},{16,0},{32,48},{48,32},{64,80},{80,64},{96,112},{112,96},{1... | collective-permute-start | bytes 393224 | tf_op jit(solution)/shard_map/ppermute | solution.py:427
  4.0 6.8 %collective-permute-start.1 = (bf16[8,64,128]{2,1,0:T(8,128)(2,1)}, bf16[8,64,128]{2,1,0:T(8,128)(2,1)S(1)}, u32[]{:S(2)}, u32[]{:S(2)}) collective-permute-start(bf16[8,64,128]{2,1,0:T(8,128)(2,1)} %get-tuple-element.23), channel_id=1, source_target_pairs={{16,32},{32,16},{48,64},{64,48},{80,96},{96,80},{17,33},{33,17},{4... | collective-permute-start | bytes 393224 | tf_op jit(solution)/shard_map/ppermute | solution.py:428
  10.8 0.8 %copy-start.5 = (bf16[4,64,128]{2,1,0:T(8,128)(2,1)S(1)}, bf16[4,64,128]{2,1,0:T(8,128)(2,1)}, u32[]{:S(2)}) copy-start(bf16[4,64,128]{2,1,0:T(8,128)(2,1)} %get-tuple-element.25) | copy-start | bytes 196612
  10.8 4.9 %copy-start.2 = (bf16[3,3,3,64,128]{4,3,2,1,0:T(8,128)(2,1)S(1)}, bf16[3,3,3,64,128]{4,3,2,1,0:T(8,128)(2,1)}, u32[]{:S(2)}) copy-start(bf16[3,3,3,64,128]{4,3,2,1,0:T(8,128)(2,1)} %w_deep.1) | copy-start | bytes 1327108
  10.8 4.9 %copy-start = (bf16[4,8,64,64]{3,2,1,0:T(8,128)(2,1)S(1)}, bf16[4,8,64,64]{3,2,1,0:T(8,128)(2,1)}, u32[]{:S(2)}) copy-start(bf16[4,8,64,64]{3,2,1,0:T(8,128)(2,1)} %own.3) | copy-start | bytes 786436
  11.7 4.0 %copy-start.1 = (bf16[2,4,64,128]{3,2,1,0:T(8,128)(2,1)S(1)}, bf16[2,4,64,128]{3,2,1,0:T(8,128)(2,1)}, u32[]{:S(2)}) copy-start(bf16[2,4,64,128]{3,2,1,0:T(8,128)(2,1)} %cot.3) | copy-start | bytes 393220
  11.7 4.0 %collective-permute-start.2 = (bf16[7,64,128]{2,1,0:T(8,128)(2,1)S(1)}, bf16[7,64,128]{2,1,0:T(8,128)(2,1)S(1)}, u32[]{:S(2)}, u32[]{:S(2)}) collective-permute-start(bf16[7,64,128]{2,1,0:T(8,128)(2,1)S(1)} %get-tuple-element.53), channel_id=1, source_target_pairs={{0,1},{1,0},{2,3},{3,2},{4,5},{5,4},{6,7},{7,6},{8,9},{9,8},{10,11... | collective-permute-start | bytes 344072 | tf_op jit(solution)/shard_map/ppermute | solution.py:427
  13.5 2.2 %collective-permute-start.3 = (bf16[7,64,128]{2,1,0:T(8,128)(2,1)S(1)}, bf16[7,64,128]{2,1,0:T(8,128)(2,1)S(1)}, u32[]{:S(2)}, u32[]{:S(2)}) collective-permute-start(bf16[7,64,128]{2,1,0:T(8,128)(2,1)S(1)} %get-tuple-element.52), channel_id=1, source_target_pairs={{1,2},{2,1},{3,4},{4,3},{5,6},{6,5},{7,8},{8,7},{9,10},{10,9},{11,... | collective-permute-start | bytes 344072 | tf_op jit(solution)/shard_map/ppermute | solution.py:428
  22.0 1.7 %collective-permute-start.4 = (bf16[1344,128]{1,0:T(8,128)(2,1)S(1)}, bf16[1344,128]{1,0:T(8,128)(2,1)S(1)}, u32[]{:S(2)}, u32[]{:S(2)}) collective-permute-start(bf16[1344,128]{1,0:T(8,128)(2,1)S(1)} %get-tuple-element.28), channel_id=1, source_target_pairs={{0,16},{16,0},{32,48},{48,32},{64,80},{80,64},{96,112},{112,96},{1... | collective-permute-start | bytes 1032200 | tf_op jit(solution)/shard_map/ppermute | solution.py:366
  23.9 13.2 %collective-permute-start.5 = (bf16[336,128]{1,0:T(8,128)(2,1)S(1)}, bf16[336,128]{1,0:T(8,128)(2,1)S(1)}, u32[]{:S(2)}, u32[]{:S(2)}) collective-permute-start(bf16[336,128]{1,0:T(8,128)(2,1)S(1)} %get-tuple-element.45), channel_id=1, source_target_pairs={{0,1},{1,0},{2,3},{3,2},{4,5},{5,4},{6,7},{7,6},{8,9},{9,8},{10,11... | collective-permute-start | bytes 258056 | tf_op jit(solution)/shard_map/ppermute | solution.py:366
  28.8 8.3 %collective-permute-start.6 = (bf16[336,128]{1,0:T(8,128)(2,1)S(1)}, bf16[336,128]{1,0:T(8,128)(2,1)S(1)}, u32[]{:S(2)}, u32[]{:S(2)}) collective-permute-start(bf16[336,128]{1,0:T(8,128)(2,1)S(1)} %get-tuple-element.47), channel_id=1, source_target_pairs={{0,4},{1,5},{2,6},{3,7},{4,0},{5,1},{6,2},{7,3},{8,12},{9,13},{10,... | collective-permute-start | bytes 258056 | tf_op jit(solution)/shard_map/ppermute | solution.py:366
  30.7 6.4 %collective-permute-start.7 = (bf16[336,128]{1,0:T(8,128)(2,1)S(1)}, bf16[336,128]{1,0:T(8,128)(2,1)S(1)}, u32[]{:S(2)}, u32[]{:S(2)}) collective-permute-start(bf16[336,128]{1,0:T(8,128)(2,1)S(1)} %get-tuple-element.46), channel_id=1, source_target_pairs={{0,5},{1,4},{2,7},{3,6},{4,1},{5,0},{6,3},{7,2},{8,13},{9,12},{10,... | collective-permute-start | bytes 258056 | tf_op jit(solution)/shard_map/ppermute | solution.py:366
  31.8 5.4 %collective-permute-start.8 = (bf16[4,64,128]{2,1,0:T(8,128)(2,1)S(1)}, bf16[4,64,128]{2,1,0:T(8,128)(2,1)S(1)}, u32[]{:S(2)}, u32[]{:S(2)}) collective-permute-start(bf16[4,64,128]{2,1,0:T(8,128)(2,1)S(1)} %get-tuple-element.29), channel_id=1, source_target_pairs={{0,16},{16,0},{32,48},{48,32},{64,80},{80,64},{96,112},{112,96},{1... | collective-permute-start | bytes 196616 | tf_op jit(solution)/shard_map/ppermute | solution.py:427
  32.5 6.5 %collective-permute-start.9 = (bf16[4,64,128]{2,1,0:T(8,128)(2,1)S(1)}, bf16[4,64,128]{2,1,0:T(8,128)(2,1)S(1)}, u32[]{:S(2)}, u32[]{:S(2)}) collective-permute-start(bf16[4,64,128]{2,1,0:T(8,128)(2,1)S(1)} %get-tuple-element.30), channel_id=1, source_target_pairs={{16,32},{32,16},{48,64},{64,48},{80,96},{96,80},{17,33},{33,17},{4... | collective-permute-start | bytes 196616 | tf_op jit(solution)/shard_map/ppermute | solution.py:428
  39.0 4.6 %collective-permute-start.10 = (bf16[336,128]{1,0:T(8,128)(2,1)S(1)}, bf16[336,128]{1,0:T(8,128)(2,1)S(1)}, u32[]{:S(2)}, u32[]{:S(2)}) collective-permute-start(bf16[336,128]{1,0:T(8,128)(2,1)S(1)} %add_convert_fusion.5), channel_id=1, source_target_pairs={{0,3},{1,2},{2,1},{3,0},{4,7},{5,6},{6,5},{7,4},{8,11},{9,10},{10,... | collective-permute-start | bytes 258056 | tf_op jit(solution)/shard_map/ppermute | solution.py:366
  41.9 3.0 %collective-permute-start.11 = (bf16[3,64,128]{2,1,0:T(8,128)(2,1)S(1)}, bf16[3,64,128]{2,1,0:T(8,128)(2,1)S(1)}, u32[]{:S(2)}, u32[]{:S(2)}) collective-permute-start(bf16[3,64,128]{2,1,0:T(8,128)(2,1)S(1)} %get-tuple-element.63), channel_id=1, source_target_pairs={{0,1},{1,0},{2,3},{3,2},{4,5},{5,4},{6,7},{7,6},{8,9},{9,8},{10,11... | collective-permute-start | bytes 147464 | tf_op jit(solution)/shard_map/ppermute | solution.py:427
  42.0 2.9 %collective-permute-start.12 = (bf16[3,64,128]{2,1,0:T(8,128)(2,1)S(1)}, bf16[3,64,128]{2,1,0:T(8,128)(2,1)S(1)}, u32[]{:S(2)}, u32[]{:S(2)}) collective-permute-start(bf16[3,64,128]{2,1,0:T(8,128)(2,1)S(1)} %get-tuple-element.62), channel_id=1, source_target_pairs={{1,2},{2,1},{3,4},{4,3},{5,6},{6,5},{7,8},{8,7},{9,10},{10,9},{11,... | collective-permute-start | bytes 147464 | tf_op jit(solution)/shard_map/ppermute | solution.py:428
  44.9 8.1 %collective-permute-start.13 = (bf16[336,128]{1,0:T(8,128)(2,1)S(1)}, bf16[336,128]{1,0:T(8,128)(2,1)S(1)}, u32[]{:S(2)}, u32[]{:S(2)}) collective-permute-start(bf16[336,128]{1,0:T(8,128)(2,1)S(1)} %add_convert_fusion.4), channel_id=1, source_target_pairs={{0,12},{1,13},{2,14},{3,15},{4,8},{5,9},{6,10},{7,11},{8,4},{9,5},... | collective-permute-start | bytes 258056 | tf_op jit(solution)/shard_map/ppermute | solution.py:366
  53.0 3.4 %collective-permute-start.14 = (bf16[336,128]{1,0:T(8,128)(2,1)S(1)}, bf16[336,128]{1,0:T(8,128)(2,1)S(1)}, u32[]{:S(2)}, u32[]{:S(2)}) collective-permute-start(bf16[336,128]{1,0:T(8,128)(2,1)S(1)} %add_convert_fusion.3), channel_id=1, source_target_pairs={{0,32},{16,48},{32,0},{48,16},{64,96},{80,112},{96,64},{112,80},{1... | collective-permute-start | bytes 258056 | tf_op jit(solution)/shard_map/ppermute | solution.py:366
  56.5 4.6 %collective-permute-start.15 = (bf16[336,128]{1,0:T(8,128)(2,1)S(1)}, bf16[336,128]{1,0:T(8,128)(2,1)S(1)}, u32[]{:S(2)}, u32[]{:S(2)}) collective-permute-start(bf16[336,128]{1,0:T(8,128)(2,1)S(1)} %add_convert_fusion.2), channel_id=1, source_target_pairs={{0,96},{16,112},{32,64},{48,80},{64,32},{80,48},{96,0},{112,16},{1... | collective-permute-start | bytes 258056 | tf_op jit(solution)/shard_map/ppermute | solution.py:366
  61.1 3.4 %collective-permute-start.16 = (bf16[336,128]{1,0:T(8,128)(2,1)S(1)}, bf16[336,128]{1,0:T(8,128)(2,1)S(1)}, u32[]{:S(2)}, u32[]{:S(2)}) collective-permute-start(bf16[336,128]{1,0:T(8,128)(2,1)S(1)} %add_convert_fusion.1), channel_id=1, source_target_pairs={{0,1},{1,0},{2,3},{3,2},{4,5},{5,4},{6,7},{7,6},{8,9},{9,8},{10,11... | collective-permute-start | bytes 258056 | tf_op jit(solution)/shard_map/ppermute | solution.py:366
  62.0 3.3 %collective-permute-start.17 = (bf16[336,128]{1,0:T(8,128)(2,1)S(1)}, bf16[336,128]{1,0:T(8,128)(2,1)S(1)}, u32[]{:S(2)}, u32[]{:S(2)}) collective-permute-start(bf16[336,128]{1,0:T(8,128)(2,1)S(1)} %add_convert_fusion.1), channel_id=1, source_target_pairs={{0,4},{1,5},{2,6},{3,7},{4,0},{5,1},{6,2},{7,3},{8,12},{9,13},{10,... | collective-permute-start | bytes 258056 | tf_op jit(solution)/shard_map/ppermute | solution.py:366
  62.7 4.2 %collective-permute-start.18 = (bf16[336,128]{1,0:T(8,128)(2,1)S(1)}, bf16[336,128]{1,0:T(8,128)(2,1)S(1)}, u32[]{:S(2)}, u32[]{:S(2)}) collective-permute-start(bf16[336,128]{1,0:T(8,128)(2,1)S(1)} %add_convert_fusion.1), channel_id=1, source_target_pairs={{0,5},{1,4},{2,7},{3,6},{4,1},{5,0},{6,3},{7,2},{8,13},{9,12},{10,... | collective-permute-start | bytes 258056 | tf_op jit(solution)/shard_map/ppermute | solution.py:366
  67.0 7.7 %collective-permute-start.19 = (bf16[1344,128]{1,0:T(8,128)(2,1)S(1)}, bf16[1344,128]{1,0:T(8,128)(2,1)S(1)}, u32[]{:S(2)}, u32[]{:S(2)}) collective-permute-start(bf16[1344,128]{1,0:T(8,128)(2,1)S(1)} %pad_maximum_fusion.mine), channel_id=1, source_target_pairs={{0,16},{16,0},{32,48},{48,32},{64,80},{80,64},{96,112},{112,96},{1... | collective-permute-start | bytes 1032200 | tf_op jit(solution)/shard_map/ppermute | solution.py:366

commit v3 on v2

--- a/solution.py
+++ b/solution.py
@@ -37,16 +37,18 @@
     return jnp.concatenate(pieces, axis=1).astype(BF16)
 
 
-def window(taps, at_x, at_y):
+INNER = (1, 2)
+OUTER = (0, 3)
+
+
+def window(taps, at_x, at_y, ys):
     return jnp.concatenate(
-        [taps[2 * x + at_x, 2 * y + at_y] for x in range(2) for y in range(4)], axis=0
-    )
-
-
-def deep_window(taps, at_x, at_y):
-    return jnp.concatenate(
-        [taps[x + at_x, y + at_y] for x in range(2) for y in range(4)], axis=0
-    )
+        [taps[2 * x + at_x, 2 * y + at_y] for x in range(2) for y in ys], axis=0
+    )
+
+
+def deep_window(taps, at_x, at_y, ys):
+    return jnp.concatenate([taps[x + at_x, y + at_y] for x in range(2) for y in ys], axis=0)
 
 
 def faces_kernel(odd, own, cot, to_core, to_chip, y_head, y_tail):
@@ -72,6 +74,7 @@
         in_specs=[pl.BlockSpec(memory_space=pltpu.SMEM), vmem, vmem],
         out_shape=[jax.ShapeDtypeStruct((8, 64, 128), BF16)] * 2
         + [jax.ShapeDtypeStruct((4, 64, 128), BF16)] * 2,
+        compiler_params=pltpu.CompilerParams(vmem_limit_bytes=6 * 1024 * 1024),
         name="faces",
     )(odd, own, cot)
 
@@ -93,9 +96,129 @@
     return value[:, which * 64 : which * 64 + 64]
 
 
-def grads_kernel(
-    odd_x, odd_y, own, cot, core, chip, near, far, w_up, w_deep,
-    keep, send, pre_grad, to_core, to_chip, gy_head, gy_tail,
+def build_blocks(w_up, blocks):
+    empty = jnp.zeros((192, 64), BF16)
+    for x in range(3):
+        for y in range(4):
+            left = w_up[x, y].reshape(192, 64) if y < 3 else empty
+            right = w_up[x, y - 1].reshape(192, 64) if y > 0 else empty
+            pair = jnp.concatenate([left, right], axis=1)
+            blocks[x, y, 0:192, 0:128] = pair
+            blocks[x + 1, y, 0:192, 128:256] = pair
+    for y in range(4):
+        blocks[3, y, 0:192, 0:128] = jnp.zeros((192, 128), BF16)
+        blocks[0, y, 0:192, 128:256] = jnp.zeros((192, 128), BF16)
+        for x in range(4):
+            blocks[x, y, 192:256, :] = jnp.zeros((64, 256), BF16)
+
+
+def column_grads(ys, taps, cot_taps, blocks, w_deep, sums, deep):
+    rows = 2 * len(ys) * 64
+    pre = jnp.zeros((rows, 256), F32)
+    for x in range(4):
+        for y in range(4):
+            pre = pre + jnp.dot(
+                window(taps, x, y, ys), blocks[x, y], preferred_element_type=F32
+            )
+    sig = 1.0 / (1.0 + jnp.exp(-pre))
+    act = pre * sig
+    summed = act[:, :128] + act[:, 128:]
+    pooled = 0.25 * (summed[:, :64] + summed[:, 64:])
+    pooled_t = pooled.T.astype(BF16)
+
+    pooled_grad = jnp.zeros((rows, 64), F32)
+    for a in range(3):
+        for b in range(3):
+            weight = jnp.concatenate([w_deep[2 - a, 2 - b, 2 - j] for j in range(3)], axis=1)
+            pooled_grad = pooled_grad + lax.dot_general(
+                deep_window(cot_taps, a, b, ys), weight, (((1,), (1,)), ((), ())),
+                preferred_element_type=F32,
+            )
+    wide = pooled_grad.astype(BF16).astype(F32)
+    wide = jnp.concatenate([wide, wide], axis=1)
+    wide = jnp.concatenate([wide, wide], axis=1)
+    grad = 0.25 * wide * (sig * (1.0 + pre * (1.0 - sig)))
+    grad_t = grad.T.astype(BF16)
+
+    for a in range(3):
+        for b in range(3):
+            out = jnp.dot(
+                pooled_t, deep_window(cot_taps, 2 - a, 2 - b, ys), preferred_element_type=F32
+            )
+            for j in range(3):
+                deep((a * 3 + b) * 3 + 2 - j, out[:, j * 128 : j * 128 + 128])
+    for x in range(4):
+        for y in range(4):
+            part = jnp.dot(grad_t, window(taps, x, y, ys), preferred_element_type=F32)
+            for s in range(2):
+                for t in range(2):
+                    a, b = x - s, y - t
+                    if 0 <= a < 3 and 0 <= b < 3:
+                        top = (s * 2 + t) * 64
+                        sums(a * 3 + b, part[top : top + 64], s == 0 and t == 0)
+    return grad.astype(BF16)
+
+
+def inner_kernel(odd_x, own, cot, core, chip, w_up, w_deep, sums, deep, inner, taps, cot_taps, blocks):
+    swap_x = odd_x[0] == 1
+
+    def x_lo(k):
+        return jnp.where(swap_x, core[k], chip[k])
+
+    def x_hi(k):
+        return jnp.where(swap_x, chip[k], core[k])
+
+    for x in range(6):
+        for y in range(2, 8):
+            row = level_column(x, y, lambda u, v: own[u, v], x_lo, x_hi, None, None)
+            taps[x, y] = depth_taps(row, 64)
+    for x in range(4):
+        for y in range(1, 5):
+            if x == 0:
+                row = x_lo(3 + y)
+            elif x == 3:
+                row = x_hi(3 + y)
+            else:
+                row = cot[x - 1, y - 1]
+            cot_taps[x, y] = depth_taps(row, 0)
+    build_blocks(w_up, blocks)
+
+    def add_sum(k, piece, first):
+        sums[k] = piece if first else sums[k] + piece
+
+    def add_deep(k, piece):
+        deep[k] = piece
+
+    inner[...] = column_grads(INNER, taps, cot_taps, blocks, w_deep, add_sum, add_deep)
+
+
+def inner_grads(odd_x, own, cot, core, chip, w_up, w_deep):
+    smem = pl.BlockSpec(memory_space=pltpu.SMEM)
+    vmem = pl.BlockSpec(memory_space=pltpu.VMEM)
+    return pl.pallas_call(
+        inner_kernel,
+        in_specs=[smem] + [vmem] * 6,
+        out_shape=[
+            jax.ShapeDtypeStruct((9, 64, 256), F32),
+            jax.ShapeDtypeStruct((27, 64, 128), F32),
+            jax.ShapeDtypeStruct((256, 256), BF16),
+        ],
+        scratch_shapes=[
+            pltpu.VMEM((6, 10, 64, 256), BF16),
+            pltpu.VMEM((4, 6, 64, 384), BF16),
+            pltpu.VMEM((4, 4, 256, 256), BF16),
+        ],
+        compiler_params=pltpu.CompilerParams(vmem_limit_bytes=VMEM_BYTES),
+        cost_estimate=pl.CostEstimate(
+            flops=2_000_000_000, bytes_accessed=4_000_000, transcendentals=65536
+        ),
+        name="inner_grads",
+    )(odd_x, own, cot, core, chip, w_up, w_deep)
+
+
+def outer_kernel(
+    odd_x, odd_y, own, cot, core, chip, near, far, w_up, w_deep, sums_in, deep_in, inner,
+    keep, send, outer, to_core, to_chip, gy_head, gy_tail,
     taps, cot_taps, blocks, sums, payload,
 ):
     swap_x = odd_x[0] == 1
@@ -114,7 +237,7 @@
         return jnp.where(swap_y, far[k], near[k])
 
     for x in range(6):
-        for y in range(10):
+        for y in (0, 1, 2, 3, 6, 7, 8, 9):
             row = level_column(x, y, lambda u, v: own[u, v], x_lo, x_hi, y_lo, y_hi)
             taps[x, y] = depth_taps(row, 64)
     for x in range(4):
@@ -130,81 +253,33 @@
             else:
                 row = cot[x - 1, y - 1]
             cot_taps[x, y] = depth_taps(row, 0)
-
-    empty = jnp.zeros((192, 64), BF16)
-    for x in range(3):
-        for y in range(4):
-            left = w_up[x, y].reshape(192, 64) if y < 3 else empty
-            right = w_up[x, y - 1].reshape(192, 64) if y > 0 else empty
-            pair = jnp.concatenate([left, right], axis=1)
-            blocks[x, y, 0:192, 0:128] = pair
-            blocks[x + 1, y, 0:192, 128:256] = pair
-    for y in range(4):
-        blocks[3, y, 0:192, 0:128] = jnp.zeros((192, 128), BF16)
-        blocks[0, y, 0:192, 128:256] = jnp.zeros((192, 128), BF16)
-        for x in range(4):
-            blocks[x, y, 192:256, :] = jnp.zeros((64, 256), BF16)
-
-    pre = jnp.zeros((512, 256), F32)
-    for x in range(4):
-        for y in range(4):
-            pre = pre + jnp.dot(window(taps, x, y), blocks[x, y], preferred_element_type=F32)
-    sig = 1.0 / (1.0 + jnp.exp(-pre))
-    act = pre * sig
-    summed = act[:, :128] + act[:, 128:]
-    pooled = 0.25 * (summed[:, :64] + summed[:, 64:])
-    pooled_t = pooled.T.astype(BF16)
-
-    pooled_grad = jnp.zeros((512, 64), F32)
-    for a in range(3):
-        for b in range(3):
-            weight = jnp.concatenate([w_deep[2 - a, 2 - b, 2 - j] for j in range(3)], axis=1)
-            pooled_grad = pooled_grad + lax.dot_general(
-                deep_window(cot_taps, a, b), weight, (((1,), (1,)), ((), ())),
-                preferred_element_type=F32,
-            )
-    wide = pooled_grad.astype(BF16).astype(F32)
-    wide = jnp.concatenate([wide, wide], axis=1)
-    wide = jnp.concatenate([wide, wide], axis=1)
-    grad = 0.25 * wide * (sig * (1.0 + pre * (1.0 - sig)))
-    grad_t = grad.T.astype(BF16)
-    rounded = grad.astype(BF16)
-    pre_grad[...] = rounded
+    build_blocks(w_up, blocks)
+
+    def add_sum(k, piece, first):
+        sums[k] = (sums_in[k] if first else sums[k]) + piece
+
+    def add_deep(k, piece):
+        top = DEEP_ROW + k * 64
+        payload[top : top + 64, :] = (deep_in[k] + piece).astype(BF16)
+
+    rounded = column_grads(OUTER, taps, cot_taps, blocks, w_deep, add_sum, add_deep)
+    outer[...] = rounded
+
+    def block(x, y):
+        top = (x * 2 + (y in (2, 3))) * 64
+        return (inner if y in INNER else rounded)[top : top + 64]
 
     for k in range(4):
-        head = rounded[k * 64 : k * 64 + 64, 0:128]
+        head = block(0, k)[:, 0:128]
         head = jnp.concatenate([half(head, 1), half(head, 0)], axis=1)
-        tail = rounded[256 + k * 64 : 320 + k * 64, 128:256]
+        tail = block(1, k)[:, 128:256]
         to_core[k] = jnp.where(swap_x, head, tail)
         to_chip[k] = jnp.where(swap_x, tail, head)
     for k in range(2):
-        first = rounded[k * 256 : k * 256 + 64]
-        last = rounded[k * 256 + 192 : k * 256 + 256]
+        first, last = block(k, 0), block(k, 3)
         gy_head[k] = jnp.concatenate([first[:, 0:64], first[:, 128:192]], axis=1)
         gy_tail[k] = jnp.concatenate([last[:, 64:128], last[:, 192:256]], axis=1)
 
-    for a in range(3):
-        for b in range(3):
-            out = jnp.dot(
-                pooled_t, deep_window(cot_taps, 2 - a, 2 - b), preferred_element_type=F32
-            ).astype(BF16)
-            for j in range(3):
-                top = DEEP_ROW + ((a * 3 + b) * 3 + 2 - j) * 64
-                payload[top : top + 64, :] = out[:, j * 128 : j * 128 + 128]
-
-    for x in range(4):
-        for y in range(4):
-            part = jnp.dot(grad_t, window(taps, x, y), preferred_element_type=F32)
-            for s in range(2):
-                for t in range(2):
-                    a, b = x - s, y - t
-                    if 0 <= a < 3 and 0 <= b < 3:
-                        top = (s * 2 + t) * 64
-                        piece = part[top : top + 64]
-                        if s == 0 and t == 0:
-                            sums[a * 3 + b] = piece
-                        else:
-                            sums[a * 3 + b] = sums[a * 3 + b] + piece
     for k in range(9):
         payload[k * 64 : k * 64 + 64, :] = sums[k, :, 0:128].astype(BF16)
     for k in range(5):
@@ -218,16 +293,16 @@
     send[...] = payload[pl.ds(HALF_ROWS - mine, HALF_ROWS), :]
 
 
-def local_grads(odd_x, odd_y, own, cot, core, chip, near, far, w_up, w_deep):
+def outer_grads(odd_x, odd_y, own, cot, core, chip, near, far, w_up, w_deep, sums, deep, inner):
     smem = pl.BlockSpec(memory_space=pltpu.SMEM)
     vmem = pl.BlockSpec(memory_space=pltpu.VMEM)
     return pl.pallas_call(
-        grads_kernel,
-        in_specs=[smem, smem] + [vmem] * 8,
+        outer_kernel,
+        in_specs=[smem, smem] + [vmem] * 11,
         out_shape=[
             jax.ShapeDtypeStruct((HALF_ROWS, 128), BF16),
             jax.ShapeDtypeStruct((HALF_ROWS, 128), BF16),
-            jax.ShapeDtypeStruct((512, 256), BF16),
+            jax.ShapeDtypeStruct((256, 256), BF16),
             jax.ShapeDtypeStruct((4, 64, 128), BF16),
             jax.ShapeDtypeStruct((4, 64, 128), BF16),
             jax.ShapeDtypeStruct((2, 64, 128), BF16),
@@ -242,13 +317,13 @@
         ],
         compiler_params=pltpu.CompilerParams(vmem_limit_bytes=VMEM_BYTES),
         cost_estimate=pl.CostEstimate(
-            flops=4_000_000_000, bytes_accessed=4_000_000, transcendentals=131072
+            flops=2_000_000_000, bytes_accessed=4_000_000, transcendentals=65536
         ),
-        name="local_grads",
-    )(odd_x, odd_y, own, cot, core, chip, near, far, w_up, w_deep)
-
-
-def input_kernel(odd_x, odd_y, pre_grad, core, chip, near, far, w_up, out, taps):
+        name="outer_grads",
+    )(odd_x, odd_y, own, cot, core, chip, near, far, w_up, w_deep, sums, deep, inner)
+
+
+def input_kernel(odd_x, odd_y, inner, outer, core, chip, near, far, w_up, out, taps):
     swap_x = odd_x[0] == 1
     swap_y = odd_y[0] == 1
 
@@ -266,8 +341,8 @@
 
     def own(u, v):
         at = (u % 2) * 128 + (v % 2) * 64
-        top = ((u // 2) * 4 + v // 2) * 64
-        return pre_grad[top : top + 64, at : at + 64]
+        top = ((u // 2) * 2 + (v // 2 in (2, 3))) * 64
+        return (inner if v // 2 in INNER else outer)[top : top + 64, at : at + 64]
 
     for x in range(6):
         for y in range(10):
@@ -288,7 +363,7 @@
                 axis=0,
             )
             total = total + lax.dot_general(
-                window(taps, x, y), block, (((1,), (1,)), ((), ())), preferred_element_type=F32
+                window(taps, x, y, range(4)), block, (((1,), (1,)), ((), ())), preferred_element_type=F32
             )
     total = total.astype(BF16)
     for x in range(4):
@@ -298,12 +373,12 @@
             out[x, y] = total[top : top + 64, at : at + 64]
 
 
-def local_input(odd_x, odd_y, pre_grad, core, chip, near, far, w_up):
+def local_input(odd_x, odd_y, inner, outer, core, chip, near, far, w_up):
     smem = pl.BlockSpec(memory_space=pltpu.SMEM)
     vmem = pl.BlockSpec(memory_space=pltpu.VMEM)
     return pl.pallas_call(
         input_kernel,
-        in_specs=[smem, smem] + [vmem] * 6,
+        in_specs=[smem, smem] + [vmem] * 7,
         out_shape=jax.ShapeDtypeStruct((4, 8, 64, 64), BF16),
         scratch_shapes=[pltpu.VMEM((6, 10, 64, 256), BF16)],
         compiler_params=pltpu.CompilerParams(vmem_limit_bytes=VMEM_BYTES),
@@ -311,7 +386,7 @@
             flops=1_000_000_000, bytes_accessed=4_000_000, transcendentals=0
         ),
         name="local_input",
-    )(odd_x, odd_y, pre_grad, core, chip, near, far, w_up)
+    )(odd_x, odd_y, inner, outer, core, chip, near, far, w_up)
 
 
 def unpack_kernel(up_scale, deep_scale, odd, mine, other, up, deep, payload):
@@ -456,23 +531,33 @@
     to_near, to_far = column_ends(odd_x, odd_y, core, chip, y_head, y_tail, True)
     near, far = both_sides(to_near, to_far, "gy")
 
-    keep, send, pre_grad, to_core, to_chip, y_head, y_tail = local_grads(
+    sums, deep, inner = inner_grads(
+        flag_x, level_input, deep_cotangent, core, chip, weight_upper, weight_deep
+    )
+    keep, send, outer, to_core, to_chip, y_head, y_tail = outer_grads(
         flag_x, flag_y, level_input, deep_cotangent, core, chip, near, far,
-        weight_upper, weight_deep,
+        weight_upper, weight_deep, sums, deep, inner,
     )
     total = tree_sum([keep, swap(send, (CORE,), 1)])
-    core, chip = both_sides(to_core, to_chip, "gx")
+    core = lax.ppermute(to_core, "gx", pairs_of("gx", 0))
+    total, core = lax.optimization_barrier((total, core))
     total = scatter_sum(total, (Z_NEAR, X_NEAR))
-    total, core, chip = lax.optimization_barrier((total, core, chip))
+    total, to_chip = lax.optimization_barrier((total, to_chip))
+    total = swap_sum(total, (Z_FAR,))
+    chip = lax.ppermute(to_chip, "gx", pairs_of("gx", 1))
+    total, chip = lax.optimization_barrier((total, chip))
     to_near, to_far = column_ends(odd_x, odd_y, core, chip, y_head, y_tail, False)
-    near, far = both_sides(to_near, to_far, "gy")
-    total = swap_sum(total, (Z_FAR,))
-    total, near, far = lax.optimization_barrier((total, near, far))
+    total = swap_sum(total, (X_FAR,))
+    near = lax.ppermute(to_near, "gy", pairs_of("gy", 0))
+    total, near, to_far = lax.optimization_barrier((total, near, to_far))
+    total = swap_sum(total, (Y_NEAR,))
+    far = lax.ppermute(to_far, "gy", pairs_of("gy", 1))
+    total, far = lax.optimization_barrier((total, far))
     input_grad = local_input(
-        flag_x, flag_y, pre_grad, core, chip, near, far, weight_upper
-    )
-    for step in (X_FAR, Y_NEAR, Y_FAR):
-        total = swap_sum(total, (step,))
+        flag_x, flag_y, inner, outer, core, chip, near, far, weight_upper
+    )
+    total = swap_sum(total, (Y_FAR,))
+    total, input_grad = lax.optimization_barrier((total, input_grad))
     total = gather(total, (Z_NEAR, X_NEAR))
     other = swap(total, (CORE,), 1)
     upper, deep = unpack(flag_x, total, other, up_scale, deep_scale)

time: 76.5 us -> 74.4 us (0.973)
  waiting for transfers between devices: 21.2 us -> 19.3 us
  Pallas kernels: 11.9 us -> 10.3 us
  starting transfers between devices: 40.2 us -> 41.2 us
    ppermute x0 -> x4, starting transfers between devices: none -> 8.09 us  [the longest x1 6.22 us: local(): chip = lax.ppermute(to_chip, 'gx', pairs_of('gx', 1))]
    ppermute x4 -> x2, starting transfers between devices: 9.18 us -> 3.84 us  [both_sides(): lax.ppermute(second, axis, pairs_of(axis, 1))]
    ppermute x4 -> x2, waiting for transfers between devices: 2.7 us -> 0.01 us  [both_sides(): lax.ppermute(first, axis, pairs_of(axis, 0))]
    ppermute x0 -> x4, waiting for transfers between devices: none -> 1.9 us  [the longest x1 1.89 us: local(): chip = lax.ppermute(to_chip, 'gx', pairs_of('gx', 1))]
    pallas_call x1, Pallas kernels: 1.95 us -> 0.12 us  [faces(): pl.pallas_call(faces_kernel, in_specs=[pl.BlockSpec(memory_space=pltpu.SM...]
    ppermute x4 -> x2, waiting for transfers between devices: 4.51 us -> 3.03 us  [both_sides(): lax.ppermute(second, axis, pairs_of(axis, 1))]
    ppermute x12, starting transfers between devices: 27 us -> 25.9 us  [swap(): lax.ppermute(value, axis, [(i, i ^ masks[axis]) for i in range(count)])]
    ppermute x4 -> x2, starting transfers between devices: 4.02 us -> 3.3 us  [both_sides(): lax.ppermute(first, axis, pairs_of(axis, 0))]
  transfers between devices with their start and end apart: 20 -> 20, of which waited for: 12 -> 12; matrix products, arithmetic and copies ran while one was open for 1% -> 0% of each run, Pallas kernels for 3% -> 7%
where the time goes in v3:
time: 74.4 us; the launch traced here: 74.2 us
  starting transfers between devices  41.2 us (55%)
  waiting for transfers between devices  19.3 us (26%)
  Pallas kernels  10.3 us (14%)
  local copies, waits for them, and re-layouts  2.04 us (3%)
  between operations  0.97 us (1%)
    ppermute x12, starting transfers between devices, swap(): lax.ppermute(value, axis, [(i, i ^ masks[axis]) for i in range(count)])  25.9 us
    ppermute x12, waiting for transfers between devices, swap(): lax.ppermute(value, axis, [(i, i ^ masks[axis]) for i in range(count)])  14.3 us
    ppermute x1, starting transfers between devices, local(): chip = lax.ppermute(to_chip, 'gx', pairs_of('gx', 1))  6.22 us
    ppermute x2, starting transfers between devices, both_sides(): lax.ppermute(second, axis, pairs_of(axis, 1))  3.84 us
    pallas_call x1, Pallas kernels, outer_grads(): pl.pallas_call(outer_kernel, in_specs=[smem, smem] + [vmem] * 11, out_sha...  3.33 us
    ppermute x2, starting transfers between devices, both_sides(): lax.ppermute(first, axis, pairs_of(axis, 0))  3.3 us
    pallas_call x1, Pallas kernels, inner_grads(): pl.pallas_call(inner_kernel, in_specs=[smem] + [vmem] * 6, out_shape=[jax...  3.2 us
    ppermute x2, waiting for transfers between devices, both_sides(): lax.ppermute(second, axis, pairs_of(axis, 1))  3.03 us
  transfers between devices with their start and end apart: 20, of which 12 were waited for; matrix products, arithmetic and copies ran while one was open for 0% of the time, Pallas kernels for 7%

profile of v3, /device:TPU:1, one launch (start us, length us, event | category | flops | bytes accessed | tf_op | source)
XLA Modules:
  0.0 74.2 jit_solution(16960289252341288372)
XLA Ops:
  0.6 0.0 copy-start
  0.6 1.0 %copy-done = bf16[4,8,64,64]{3,2,1,0:T(8,128)(2,1)S(1)} copy-done((bf16[4,8,64,64]{3,2,1,0:T(8,128)(2,1)S(1)}, bf16[4,8,64,64]{3,2,1,0:T(8,128)(2,1)}, u32[]{:S(2)}) %copy-start) | copy-done | bytes 262168
  1.7 0.9 %copy-done.2 = bf16[2,4,64,128]{3,2,1,0:T(8,128)(2,1)S(1)} copy-done((bf16[2,4,64,128]{3,2,1,0:T(8,128)(2,1)S(1)}, bf16[2,4,64,128]{3,2,1,0:T(8,128)(2,1)}, u32[]{:S(2)}) %copy-start.2) | copy-done | bytes 131096
  2.6 0.1 faces.1
  2.7 1.5 %collective-permute-start = (bf16[8,64,128]{2,1,0:T(8,128)(2,1)S(1)}, bf16[8,64,128]{2,1,0:T(8,128)(2,1)S(1)}, u32[]{:S(2)}, u32[]{:S(2)}) collective-permute-start(bf16[8,64,128]{2,1,0:T(8,128)(2,1)S(1)} %get-tuple-element.32), channel_id=1, source_target_pairs={{0,16},{16,0},{32,48},{48,32},{64,80},{80,64},{96,112},{112,96},{1... | collective-permute-start | bytes 393224 | tf_op jit(solution)/shard_map/ppermute | solution.py:502
  4.2 3.2 %collective-permute-start.1 = (bf16[8,64,128]{2,1,0:T(8,128)(2,1)S(1)}, bf16[8,64,128]{2,1,0:T(8,128)(2,1)S(1)}, u32[]{:S(2)}, u32[]{:S(2)}) collective-permute-start(bf16[8,64,128]{2,1,0:T(8,128)(2,1)S(1)} %get-tuple-element.33), channel_id=1, source_target_pairs={{16,32},{32,16},{48,64},{64,48},{80,96},{96,80},{17,33},{33,17},{4... | collective-permute-start | bytes 393224 | tf_op jit(solution)/shard_map/ppermute | solution.py:503
  7.4 0.0 collective-permute-done.core
  7.5 3.0 %collective-permute-done.1.chip = bf16[8,64,128]{2,1,0:T(8,128)(2,1)S(1)} collective-permute-done((bf16[8,64,128]{2,1,0:T(8,128)(2,1)S(1)}, bf16[8,64,128]{2,1,0:T(8,128)(2,1)S(1)}, u32[]{:S(2)}, u32[]{:S(2)}) %collective-permute-start.1) | collective-permute-done | bytes 131104 | tf_op jit(solution)/shard_map/ppermute | solution.py:503
  10.5 0.0 copy-start.1
  10.6 0.0 copy-start.3
  10.6 1.8 %collective-permute-start.2 = (bf16[7,64,128]{2,1,0:T(8,128)(2,1)S(1)}, bf16[7,64,128]{2,1,0:T(8,128)(2,1)S(1)}, u32[]{:S(2)}, u32[]{:S(2)}) collective-permute-start(bf16[7,64,128]{2,1,0:T(8,128)(2,1)S(1)} %get-tuple-element.73), channel_id=1, source_target_pairs={{0,1},{1,0},{2,3},{3,2},{4,5},{5,4},{6,7},{7,6},{8,9},{9,8},{10,11... | collective-permute-start | bytes 344072 | tf_op jit(solution)/shard_map/ppermute | solution.py:502
  12.4 0.7 collective-permute-start.3
  13.2 3.2 %inner_grads.1 = (f32[9,64,256]{2,1,0:T(8,128)S(1)}, f32[27,64,128]{2,1,0:T(8,128)S(1)}, bf16[256,256]{1,0:T(8,128)(2,1)S(1)}) custom-call(s32[1]{0:T(128)} %bitcast.odd.odd_x, bf16[4,8,64,64]{3,2,1,0:T(8,128)(2,1)S(1)} %copy-done.1, bf16[2,4,64,128]{3,2,1,0:T(8,128)(2,1)S(1)} %copy-done.3, bf16[8,64,128]{2,1,0:T(8,128)(2,1)S(1)} %collective-permute-done.core, ...), custom_call_target="tpu_custom_call" | custom-call | flops 2000000000 | bytes 4000000 | tf_op jit(solution)/shard_map/inner_grads/pallas_call | solution.py:198
  16.4 0.0 collective-permute-done.2.near
  16.4 0.0 collective-permute-done.3.far
  16.4 3.3 %outer_grads.1 = (bf16[1344,128]{1,0:T(8,128)(2,1)S(1)}, bf16[1344,128]{1,0:T(8,128)(2,1)S(1)}, bf16[256,256]{1,0:T(8,128)(2,1)S(1)}, bf16[4,64,128]{2,1,0:T(8,1...) custom-call(s32[1]{0:T(128)} %bitcast.odd.odd_x, ...), custom_call_target="tpu_custom_call" | custom-call | flops 2000000000 | bytes 4000000 | tf_op jit(solution)/shard_map/outer_grads/pallas_call | solution.py:299
  19.7 0.1 collective-permute-start.4
  19.8 0.5 collective-permute-start.5
  20.3 1.1 %collective-permute-done.4 = bf16[1344,128]{1,0:T(8,128)(2,1)S(1)} collective-permute-done((bf16[1344,128]{1,0:T(8,128)(2,1)S(1)}, bf16[1344,128]{1,0:T(8,128)(2,1)S(1)}, u32[]{:S(2)}, u32[]{:S(2)}) %collective-permute-start.4) | collective-permute-done | bytes 344096 | tf_op jit(solution)/shard_map/ppermute | solution.py:441
  21.4 0.1 add_convert_fusion
  21.5 0.0 collective-permute-done.5.core
  21.6 4.3 %collective-permute-start.6 = (bf16[336,128]{1,0:T(8,128)(2,1)S(1)}, bf16[336,128]{1,0:T(8,128)(2,1)S(1)}, u32[]{:S(2)}, u32[]{:S(2)}) collective-permute-start(bf16[336,128]{1,0:T(8,128)(2,1)S(1)} %get-tuple-element.65), channel_id=1, source_target_pairs={{0,1},{1,0},{2,3},{3,2},{4,5},{5,4},{6,7},{7,6},{8,9},{9,8},{10,11... | collective-permute-start | bytes 258056 | tf_op jit(solution)/shard_map/ppermute | solution.py:441
  25.9 1.2 %collective-permute-start.7 = (bf16[336,128]{1,0:T(8,128)(2,1)S(1)}, bf16[336,128]{1,0:T(8,128)(2,1)S(1)}, u32[]{:S(2)}, u32[]{:S(2)}) collective-permute-start(bf16[336,128]{1,0:T(8,128)(2,1)S(1)} %get-tuple-element.67), channel_id=1, source_target_pairs={{0,4},{1,5},{2,6},{3,7},{4,0},{5,1},{6,2},{7,3},{8,12},{9,13},{10,... | collective-permute-start | bytes 258056 | tf_op jit(solution)/shard_map/ppermute | solution.py:441
  27.1 0.7 collective-permute-start.8
  27.8 0.9 %collective-permute-done.6 = bf16[336,128]{1,0:T(8,128)(2,1)S(1)} collective-permute-done((bf16[336,128]{1,0:T(8,128)(2,1)S(1)}, bf16[336,128]{1,0:T(8,128)(2,1)S(1)}, u32[]{:S(2)}, u32[]{:S(2)}) %collective-permute-start.6) | collective-permute-done | bytes 86048 | tf_op jit(solution)/shard_map/ppermute | solution.py:441
  28.7 0.9 %collective-permute-done.7 = bf16[336,128]{1,0:T(8,128)(2,1)S(1)} collective-permute-done((bf16[336,128]{1,0:T(8,128)(2,1)S(1)}, bf16[336,128]{1,0:T(8,128)(2,1)S(1)}, u32[]{:S(2)}, u32[]{:S(2)}) %collective-permute-start.7) | collective-permute-done | bytes 86048 | tf_op jit(solution)/shard_map/ppermute | solution.py:441
  29.6 1.9 %collective-permute-done.8 = bf16[336,128]{1,0:T(8,128)(2,1)S(1)} collective-permute-done((bf16[336,128]{1,0:T(8,128)(2,1)S(1)}, bf16[336,128]{1,0:T(8,128)(2,1)S(1)}, u32[]{:S(2)}, u32[]{:S(2)}) %collective-permute-start.8) | collective-permute-done | bytes 86048 | tf_op jit(solution)/shard_map/ppermute | solution.py:441
  31.5 3.0 %collective-permute-start.9 = (bf16[336,128]{1,0:T(8,128)(2,1)S(1)}, bf16[336,128]{1,0:T(8,128)(2,1)S(1)}, u32[]{:S(2)}, u32[]{:S(2)}) collective-permute-start(bf16[336,128]{1,0:T(8,128)(2,1)S(1)} %add_convert_fusion.5), channel_id=1, source_target_pairs={{0,3},{1,2},{2,1},{3,0},{4,7},{5,6},{6,5},{7,4},{8,11},{9,10},{10,... | collective-permute-start | bytes 258056 | tf_op jit(solution)/shard_map/ppermute | solution.py:441
  34.5 6.2 %collective-permute-start.10 = (bf16[4,64,128]{2,1,0:T(8,128)(2,1)S(1)}, bf16[4,64,128]{2,1,0:T(8,128)(2,1)S(1)}, u32[]{:S(2)}, u32[]{:S(2)}) collective-permute-start(bf16[4,64,128]{2,1,0:T(8,128)(2,1)S(1)} %get-tuple-element.45), channel_id=1, source_target_pairs={{16,32},{32,16},{48,64},{64,48},{80,96},{96,80},{17,33},{33,17},{4... | collective-permute-start | bytes 196616 | tf_op jit(solution)/shard_map/ppermute | solution.py:547
  40.8 1.9 %collective-permute-done.10.chip = bf16[4,64,128]{2,1,0:T(8,128)(2,1)S(1)} collective-permute-done((bf16[4,64,128]{2,1,0:T(8,128)(2,1)S(1)}, bf16[4,64,128]{2,1,0:T(8,128)(2,1)S(1)}, u32[]{:S(2)}, u32[]{:S(2)}) %collective-permute-start.10) | collective-permute-done | bytes 65568 | tf_op jit(solution)/shard_map/ppermute | solution.py:547
  42.7 1.5 %collective-permute-start.11 = (bf16[336,128]{1,0:T(8,128)(2,1)S(1)}, bf16[336,128]{1,0:T(8,128)(2,1)S(1)}, u32[]{:S(2)}, u32[]{:S(2)}) collective-permute-start(bf16[336,128]{1,0:T(8,128)(2,1)S(1)} %add_convert_fusion.4), channel_id=1, source_target_pairs={{0,12},{1,13},{2,14},{3,15},{4,8},{5,9},{6,10},{7,11},{8,4},{9,5},... | collective-permute-start | bytes 258056 | tf_op jit(solution)/shard_map/ppermute | solution.py:441
  44.2 0.8 %collective-permute-start.12 = (bf16[3,64,128]{2,1,0:T(8,128)(2,1)S(1)}, bf16[3,64,128]{2,1,0:T(8,128)(2,1)S(1)}, u32[]{:S(2)}, u32[]{:S(2)}) collective-permute-start(bf16[3,64,128]{2,1,0:T(8,128)(2,1)S(1)} %get-tuple-element.83), channel_id=1, source_target_pairs={{0,1},{1,0},{2,3},{3,2},{4,5},{5,4},{6,7},{7,6},{8,9},{9,8},{10,11... | collective-permute-start | bytes 147464 | tf_op jit(solution)/shard_map/ppermute | solution.py:551
  44.9 2.3 %collective-permute-done.11 = bf16[336,128]{1,0:T(8,128)(2,1)S(1)} collective-permute-done((bf16[336,128]{1,0:T(8,128)(2,1)S(1)}, bf16[336,128]{1,0:T(8,128)(2,1)S(1)}, u32[]{:S(2)}, u32[]{:S(2)}) %collective-permute-start.11) | collective-permute-done | bytes 86048 | tf_op jit(solution)/shard_map/ppermute | solution.py:441
  47.2 1.9 %collective-permute-start.13 = (bf16[336,128]{1,0:T(8,128)(2,1)S(1)}, bf16[336,128]{1,0:T(8,128)(2,1)S(1)}, u32[]{:S(2)}, u32[]{:S(2)}) collective-permute-start(bf16[336,128]{1,0:T(8,128)(2,1)S(1)} %add_convert_fusion.3), channel_id=1, source_target_pairs={{0,32},{16,48},{32,0},{48,16},{64,96},{80,112},{96,64},{112,80},{1... | collective-permute-start | bytes 258056 | tf_op jit(solution)/shard_map/ppermute | solution.py:441
  49.2 0.7 collective-permute-start.14
  49.8 1.2 %collective-permute-done.13 = bf16[336,128]{1,0:T(8,128)(2,1)S(1)} collective-permute-done((bf16[336,128]{1,0:T(8,128)(2,1)S(1)}, bf16[336,128]{1,0:T(8,128)(2,1)S(1)}, u32[]{:S(2)}, u32[]{:S(2)}) %collective-permute-start.13) | collective-permute-done | bytes 86048 | tf_op jit(solution)/shard_map/ppermute | solution.py:441
  51.1 0.0 collective-permute-done.14.far
  51.1 1.0 %collective-permute-start.15 = (bf16[336,128]{1,0:T(8,128)(2,1)S(1)}, bf16[336,128]{1,0:T(8,128)(2,1)S(1)}, u32[]{:S(2)}, u32[]{:S(2)}) collective-permute-start(bf16[336,128]{1,0:T(8,128)(2,1)S(1)} %add_convert_fusion.2), channel_id=1, source_target_pairs={{0,96},{16,112},{32,64},{48,80},{64,32},{80,48},{96,0},{112,16},{1... | collective-permute-start | bytes 258056 | tf_op jit(solution)/shard_map/ppermute | solution.py:441
  52.1 2.2 %local_input.1 = bf16[4,8,64,64]{3,2,1,0:T(8,128)(2,1)} custom-call(s32[1]{0:T(128)} %bitcast.odd.odd_x, s32[1]{0:T(128)} %bitcast.1.odd_y, bf16[256,256]{1,0:T(8,128)(2,1)S(1)} %get-tuple-element.38.inner, bf16[256,256]{1,0:T(8,128)(2,1)S(1)} %get-tuple-element.54.outer, bf16[4,64,128]{2,1,0:T(8,128)(2,1)S(1)} %collective-permute-done.5.core, ...), custom_call_target="tpu_custom_call" | custom-call | flops 1000000000 | bytes 4000000 | tf_op jit(solution)/shard_map/local_input/pallas_call | solution.py:379
  54.2 1.5 %collective-permute-done.15 = bf16[336,128]{1,0:T(8,128)(2,1)S(1)} collective-permute-done((bf16[336,128]{1,0:T(8,128)(2,1)S(1)}, bf16[336,128]{1,0:T(8,128)(2,1)S(1)}, u32[]{:S(2)}, u32[]{:S(2)}) %collective-permute-start.15) | collective-permute-done | bytes 86048 | tf_op jit(solution)/shard_map/ppermute | solution.py:441
  55.7 3.4 %collective-permute-start.16 = (bf16[336,128]{1,0:T(8,128)(2,1)S(1)}, bf16[336,128]{1,0:T(8,128)(2,1)S(1)}, u32[]{:S(2)}, u32[]{:S(2)}) collective-permute-start(bf16[336,128]{1,0:T(8,128)(2,1)S(1)} %add_convert_fusion.1), channel_id=1, source_target_pairs={{0,1},{1,0},{2,3},{3,2},{4,5},{5,4},{6,7},{7,6},{8,9},{9,8},{10,11... | collective-permute-start | bytes 258056 | tf_op jit(solution)/shard_map/ppermute | solution.py:441
  59.1 2.4 %collective-permute-start.17 = (bf16[336,128]{1,0:T(8,128)(2,1)S(1)}, bf16[336,128]{1,0:T(8,128)(2,1)S(1)}, u32[]{:S(2)}, u32[]{:S(2)}) collective-permute-start(bf16[336,128]{1,0:T(8,128)(2,1)S(1)} %add_convert_fusion.1), channel_id=1, source_target_pairs={{0,4},{1,5},{2,6},{3,7},{4,0},{5,1},{6,2},{7,3},{8,12},{9,13},{10,... | collective-permute-start | bytes 258056 | tf_op jit(solution)/shard_map/ppermute | solution.py:441
  61.5 1.1 %collective-permute-start.18 = (bf16[336,128]{1,0:T(8,128)(2,1)S(1)}, bf16[336,128]{1,0:T(8,128)(2,1)S(1)}, u32[]{:S(2)}, u32[]{:S(2)}) collective-permute-start(bf16[336,128]{1,0:T(8,128)(2,1)S(1)} %add_convert_fusion.1), channel_id=1, source_target_pairs={{0,5},{1,4},{2,7},{3,6},{4,1},{5,0},{6,3},{7,2},{8,13},{9,12},{10,... | collective-permute-start | bytes 258056 | tf_op jit(solution)/shard_map/ppermute | solution.py:441
  62.6 0.8 %collective-permute-done.17 = bf16[336,128]{1,0:T(8,128)(2,1)S(1)} collective-permute-done((bf16[336,128]{1,0:T(8,128)(2,1)S(1)}, bf16[336,128]{1,0:T(8,128)(2,1)S(1)}, u32[]{:S(2)}, u32[]{:S(2)}) %collective-permute-start.17) | collective-permute-done | bytes 86048 | tf_op jit(solution)/shard_map/ppermute | solution.py:441
  63.3 2.5 %collective-permute-done.18 = bf16[336,128]{1,0:T(8,128)(2,1)S(1)} collective-permute-done((bf16[336,128]{1,0:T(8,128)(2,1)S(1)}, bf16[336,128]{1,0:T(8,128)(2,1)S(1)}, u32[]{:S(2)}, u32[]{:S(2)}) %collective-permute-start.18) | collective-permute-done | bytes 86048 | tf_op jit(solution)/shard_map/ppermute | solution.py:441
  65.9 5.5 %collective-permute-start.19 = (bf16[1344,128]{1,0:T(8,128)(2,1)S(1)}, bf16[1344,128]{1,0:T(8,128)(2,1)S(1)}, u32[]{:S(2)}, u32[]{:S(2)}) collective-permute-start(bf16[1344,128]{1,0:T(8,128)(2,1)S(1)} %pad_maximum_fusion.mine), channel_id=1, source_target_pairs={{0,16},{16,0},{32,48},{48,32},{64,80},{80,64},{96,112},{112,96},{1... | collective-permute-start | bytes 1032200 | tf_op jit(solution)/shard_map/ppermute | solution.py:441
  71.4 1.3 %collective-permute-done.19.other = bf16[1344,128]{1,0:T(8,128)(2,1)S(1)} collective-permute-done((bf16[1344,128]{1,0:T(8,128)(2,1)S(1)}, bf16[1344,128]{1,0:T(8,128)(2,1)S(1)}, u32[]{:S(2)}, u32[]{:S(2)}) %collective-permute-start.19) | collective-permute-done | bytes 344096 | tf_op jit(solution)/shard_map/ppermute | solution.py:441
  72.7 1.5 %unpack.1 = (f32[3,3,3,64,64]{4,3,2,1,0:T(8,128)}, f32[3,3,3,64,128]{4,3,2,1,0:T(8,128)}) custom-call(s32[1]{0:T(128)} %bitcast.odd.odd_x, bf16[1344,128]{1,0:T(8,128)(2,1)S(1)} %pad_maximum_fusion.mine, bf16[1344,128]{1,0:T(8,128)(2,1)S(1)} %collective-permute-done.19.other), custom_call_target="tpu_custom_call" | custom-call | tf_op jit(solution)/shard_map/unpack/pallas_call | solution.py:414
  (30 shorter events, 0.4 us)
Async XLA Ops:
  0.6 1.0 %copy-start = (bf16[4,8,64,64]{3,2,1,0:T(8,128)(2,1)S(1)}, bf16[4,8,64,64]{3,2,1,0:T(8,128)(2,1)}, u32[]{:S(2)}) copy-start(bf16[4,8,64,64]{3,2,1,0:T(8,128)(2,1)} %own.5) | copy-start | bytes 786436
  1.7 0.9 %copy-start.2 = (bf16[2,4,64,128]{3,2,1,0:T(8,128)(2,1)S(1)}, bf16[2,4,64,128]{3,2,1,0:T(8,128)(2,1)}, u32[]{:S(2)}) copy-start(bf16[2,4,64,128]{3,2,1,0:T(8,128)(2,1)} %cot.5) | copy-start | bytes 393220
  2.6 10.5 %copy-start.5 = (bf16[3,3,3,64,64]{4,3,2,1,0:T(8,128)(2,1)S(1)}, bf16[3,3,3,64,64]{4,3,2,1,0:T(8,128)(2,1)}, u32[]{:S(2)}) copy-start(bf16[3,3,3,64,64]{4,3,2,1,0:T(8,128)(2,1)} %w_up.5) | copy-start | bytes 663556
  2.7 4.7 %collective-permute-start = (bf16[8,64,128]{2,1,0:T(8,128)(2,1)S(1)}, bf16[8,64,128]{2,1,0:T(8,128)(2,1)S(1)}, u32[]{:S(2)}, u32[]{:S(2)}) collective-permute-start(bf16[8,64,128]{2,1,0:T(8,128)(2,1)S(1)} %get-tuple-element.32), channel_id=1, source_target_pairs={{0,16},{16,0},{32,48},{48,32},{64,80},{80,64},{96,112},{112,96},{1... | collective-permute-start | bytes 393224 | tf_op jit(solution)/shard_map/ppermute | solution.py:502
  4.2 6.3 %collective-permute-start.1 = (bf16[8,64,128]{2,1,0:T(8,128)(2,1)S(1)}, bf16[8,64,128]{2,1,0:T(8,128)(2,1)S(1)}, u32[]{:S(2)}, u32[]{:S(2)}) collective-permute-start(bf16[8,64,128]{2,1,0:T(8,128)(2,1)S(1)} %get-tuple-element.33), channel_id=1, source_target_pairs={{16,32},{32,16},{48,64},{64,48},{80,96},{96,80},{17,33},{33,17},{4... | collective-permute-start | bytes 393224 | tf_op jit(solution)/shard_map/ppermute | solution.py:503
  10.5 2.6 %copy-start.4 = (bf16[3,3,3,64,128]{4,3,2,1,0:T(8,128)(2,1)S(1)}, bf16[3,3,3,64,128]{4,3,2,1,0:T(8,128)(2,1)}, u32[]{:S(2)}) copy-start(bf16[3,3,3,64,128]{4,3,2,1,0:T(8,128)(2,1)} %w_deep.3) | copy-start | bytes 1327108
  10.5 2.6 %copy-start.1 = (bf16[4,8,64,64]{3,2,1,0:T(8,128)(2,1)S(1)}, bf16[4,8,64,64]{3,2,1,0:T(8,128)(2,1)}, u32[]{:S(2)}) copy-start(bf16[4,8,64,64]{3,2,1,0:T(8,128)(2,1)} %own.5) | copy-start | bytes 786436
  10.6 2.5 %copy-start.3 = (bf16[2,4,64,128]{3,2,1,0:T(8,128)(2,1)S(1)}, bf16[2,4,64,128]{3,2,1,0:T(8,128)(2,1)}, u32[]{:S(2)}) copy-start(bf16[2,4,64,128]{3,2,1,0:T(8,128)(2,1)} %cot.5) | copy-start | bytes 393220
  10.6 5.7 %collective-permute-start.2 = (bf16[7,64,128]{2,1,0:T(8,128)(2,1)S(1)}, bf16[7,64,128]{2,1,0:T(8,128)(2,1)S(1)}, u32[]{:S(2)}, u32[]{:S(2)}) collective-permute-start(bf16[7,64,128]{2,1,0:T(8,128)(2,1)S(1)} %get-tuple-element.73), channel_id=1, source_target_pairs={{0,1},{1,0},{2,3},{3,2},{4,5},{5,4},{6,7},{7,6},{8,9},{9,8},{10,11... | collective-permute-start | bytes 344072 | tf_op jit(solution)/shard_map/ppermute | solution.py:502
  12.4 3.9 %collective-permute-start.3 = (bf16[7,64,128]{2,1,0:T(8,128)(2,1)S(1)}, bf16[7,64,128]{2,1,0:T(8,128)(2,1)S(1)}, u32[]{:S(2)}, u32[]{:S(2)}) collective-permute-start(bf16[7,64,128]{2,1,0:T(8,128)(2,1)S(1)} %get-tuple-element.72), channel_id=1, source_target_pairs={{1,2},{2,1},{3,4},{4,3},{5,6},{6,5},{7,8},{8,7},{9,10},{10,9},{11,... | collective-permute-start | bytes 344072 | tf_op jit(solution)/shard_map/ppermute | solution.py:503
  19.7 1.7 %collective-permute-start.4 = (bf16[1344,128]{1,0:T(8,128)(2,1)S(1)}, bf16[1344,128]{1,0:T(8,128)(2,1)S(1)}, u32[]{:S(2)}, u32[]{:S(2)}) collective-permute-start(bf16[1344,128]{1,0:T(8,128)(2,1)S(1)} %get-tuple-element.40), channel_id=1, source_target_pairs={{0,16},{16,0},{32,48},{48,32},{64,80},{80,64},{96,112},{112,96},{1... | collective-permute-start | bytes 1032200 | tf_op jit(solution)/shard_map/ppermute | solution.py:441
  19.8 1.7 %collective-permute-start.5 = (bf16[4,64,128]{2,1,0:T(8,128)(2,1)S(1)}, bf16[4,64,128]{2,1,0:T(8,128)(2,1)S(1)}, u32[]{:S(2)}, u32[]{:S(2)}) collective-permute-start(bf16[4,64,128]{2,1,0:T(8,128)(2,1)S(1)} %get-tuple-element.41), channel_id=1, source_target_pairs={{0,16},{16,0},{32,48},{48,32},{64,80},{80,64},{96,112},{112,96},{1... | collective-permute-start | bytes 196616 | tf_op jit(solution)/shard_map/ppermute | solution.py:542
  21.6 7.1 %collective-permute-start.6 = (bf16[336,128]{1,0:T(8,128)(2,1)S(1)}, bf16[336,128]{1,0:T(8,128)(2,1)S(1)}, u32[]{:S(2)}, u32[]{:S(2)}) collective-permute-start(bf16[336,128]{1,0:T(8,128)(2,1)S(1)} %get-tuple-element.65), channel_id=1, source_target_pairs={{0,1},{1,0},{2,3},{3,2},{4,5},{5,4},{6,7},{7,6},{8,9},{9,8},{10,11... | collective-permute-start | bytes 258056 | tf_op jit(solution)/shard_map/ppermute | solution.py:441
  25.9 3.7 %collective-permute-start.7 = (bf16[336,128]{1,0:T(8,128)(2,1)S(1)}, bf16[336,128]{1,0:T(8,128)(2,1)S(1)}, u32[]{:S(2)}, u32[]{:S(2)}) collective-permute-start(bf16[336,128]{1,0:T(8,128)(2,1)S(1)} %get-tuple-element.67), channel_id=1, source_target_pairs={{0,4},{1,5},{2,6},{3,7},{4,0},{5,1},{6,2},{7,3},{8,12},{9,13},{10,... | collective-permute-start | bytes 258056 | tf_op jit(solution)/shard_map/ppermute | solution.py:441
  27.1 4.4 %collective-permute-start.8 = (bf16[336,128]{1,0:T(8,128)(2,1)S(1)}, bf16[336,128]{1,0:T(8,128)(2,1)S(1)}, u32[]{:S(2)}, u32[]{:S(2)}) collective-permute-start(bf16[336,128]{1,0:T(8,128)(2,1)S(1)} %get-tuple-element.66), channel_id=1, source_target_pairs={{0,5},{1,4},{2,7},{3,6},{4,1},{5,0},{6,3},{7,2},{8,13},{9,12},{10,... | collective-permute-start | bytes 258056 | tf_op jit(solution)/shard_map/ppermute | solution.py:441
  31.5 9.2 %collective-permute-start.9 = (bf16[336,128]{1,0:T(8,128)(2,1)S(1)}, bf16[336,128]{1,0:T(8,128)(2,1)S(1)}, u32[]{:S(2)}, u32[]{:S(2)}) collective-permute-start(bf16[336,128]{1,0:T(8,128)(2,1)S(1)} %add_convert_fusion.5), channel_id=1, source_target_pairs={{0,3},{1,2},{2,1},{3,0},{4,7},{5,6},{6,5},{7,4},{8,11},{9,10},{10,... | collective-permute-start | bytes 258056 | tf_op jit(solution)/shard_map/ppermute | solution.py:441
  34.5 8.2 %collective-permute-start.10 = (bf16[4,64,128]{2,1,0:T(8,128)(2,1)S(1)}, bf16[4,64,128]{2,1,0:T(8,128)(2,1)S(1)}, u32[]{:S(2)}, u32[]{:S(2)}) collective-permute-start(bf16[4,64,128]{2,1,0:T(8,128)(2,1)S(1)} %get-tuple-element.45), channel_id=1, source_target_pairs={{16,32},{32,16},{48,64},{64,48},{80,96},{96,80},{17,33},{33,17},{4... | collective-permute-start | bytes 196616 | tf_op jit(solution)/shard_map/ppermute | solution.py:547
  42.7 4.5 %collective-permute-start.11 = (bf16[336,128]{1,0:T(8,128)(2,1)S(1)}, bf16[336,128]{1,0:T(8,128)(2,1)S(1)}, u32[]{:S(2)}, u32[]{:S(2)}) collective-permute-start(bf16[336,128]{1,0:T(8,128)(2,1)S(1)} %add_convert_fusion.4), channel_id=1, source_target_pairs={{0,12},{1,13},{2,14},{3,15},{4,8},{5,9},{6,10},{7,11},{8,4},{9,5},... | collective-permute-start | bytes 258056 | tf_op jit(solution)/shard_map/ppermute | solution.py:441
  44.2 3.1 %collective-permute-start.12 = (bf16[3,64,128]{2,1,0:T(8,128)(2,1)S(1)}, bf16[3,64,128]{2,1,0:T(8,128)(2,1)S(1)}, u32[]{:S(2)}, u32[]{:S(2)}) collective-permute-start(bf16[3,64,128]{2,1,0:T(8,128)(2,1)S(1)} %get-tuple-element.83), channel_id=1, source_target_pairs={{0,1},{1,0},{2,3},{3,2},{4,5},{5,4},{6,7},{7,6},{8,9},{9,8},{10,11... | collective-permute-start | bytes 147464 | tf_op jit(solution)/shard_map/ppermute | solution.py:551
  47.2 3.8 %collective-permute-start.13 = (bf16[336,128]{1,0:T(8,128)(2,1)S(1)}, bf16[336,128]{1,0:T(8,128)(2,1)S(1)}, u32[]{:S(2)}, u32[]{:S(2)}) collective-permute-start(bf16[336,128]{1,0:T(8,128)(2,1)S(1)} %add_convert_fusion.3), channel_id=1, source_target_pairs={{0,32},{16,48},{32,0},{48,16},{64,96},{80,112},{96,64},{112,80},{1... | collective-permute-start | bytes 258056 | tf_op jit(solution)/shard_map/ppermute | solution.py:441
  49.2 1.9 %collective-permute-start.14 = (bf16[3,64,128]{2,1,0:T(8,128)(2,1)S(1)}, bf16[3,64,128]{2,1,0:T(8,128)(2,1)S(1)}, u32[]{:S(2)}, u32[]{:S(2)}) collective-permute-start(bf16[3,64,128]{2,1,0:T(8,128)(2,1)S(1)} %get-tuple-element.52), channel_id=1, source_target_pairs={{1,2},{2,1},{3,4},{4,3},{5,6},{6,5},{7,8},{8,7},{9,10},{10,9},{11,... | collective-permute-start | bytes 147464 | tf_op jit(solution)/shard_map/ppermute | solution.py:554
  51.1 4.6 %collective-permute-start.15 = (bf16[336,128]{1,0:T(8,128)(2,1)S(1)}, bf16[336,128]{1,0:T(8,128)(2,1)S(1)}, u32[]{:S(2)}, u32[]{:S(2)}) collective-permute-start(bf16[336,128]{1,0:T(8,128)(2,1)S(1)} %add_convert_fusion.2), channel_id=1, source_target_pairs={{0,96},{16,112},{32,64},{48,80},{64,32},{80,48},{96,0},{112,16},{1... | collective-permute-start | bytes 258056 | tf_op jit(solution)/shard_map/ppermute | solution.py:441
  55.7 6.8 %collective-permute-start.16 = (bf16[336,128]{1,0:T(8,128)(2,1)S(1)}, bf16[336,128]{1,0:T(8,128)(2,1)S(1)}, u32[]{:S(2)}, u32[]{:S(2)}) collective-permute-start(bf16[336,128]{1,0:T(8,128)(2,1)S(1)} %add_convert_fusion.1), channel_id=1, source_target_pairs={{0,1},{1,0},{2,3},{3,2},{4,5},{5,4},{6,7},{7,6},{8,9},{9,8},{10,11... | collective-permute-start | bytes 258056 | tf_op jit(solution)/shard_map/ppermute | solution.py:441
  59.1 4.2 %collective-permute-start.17 = (bf16[336,128]{1,0:T(8,128)(2,1)S(1)}, bf16[336,128]{1,0:T(8,128)(2,1)S(1)}, u32[]{:S(2)}, u32[]{:S(2)}) collective-permute-start(bf16[336,128]{1,0:T(8,128)(2,1)S(1)} %add_convert_fusion.1), channel_id=1, source_target_pairs={{0,4},{1,5},{2,6},{3,7},{4,0},{5,1},{6,2},{7,3},{8,12},{9,13},{10,... | collective-permute-start | bytes 258056 | tf_op jit(solution)/shard_map/ppermute | solution.py:441
  61.5 4.3 %collective-permute-start.18 = (bf16[336,128]{1,0:T(8,128)(2,1)S(1)}, bf16[336,128]{1,0:T(8,128)(2,1)S(1)}, u32[]{:S(2)}, u32[]{:S(2)}) collective-permute-start(bf16[336,128]{1,0:T(8,128)(2,1)S(1)} %add_convert_fusion.1), channel_id=1, source_target_pairs={{0,5},{1,4},{2,7},{3,6},{4,1},{5,0},{6,3},{7,2},{8,13},{9,12},{10,... | collective-permute-start | bytes 258056 | tf_op jit(solution)/shard_map/ppermute | solution.py:441
  65.9 6.8 %collective-permute-start.19 = (bf16[1344,128]{1,0:T(8,128)(2,1)S(1)}, bf16[1344,128]{1,0:T(8,128)(2,1)S(1)}, u32[]{:S(2)}, u32[]{:S(2)}) collective-permute-start(bf16[1344,128]{1,0:T(8,128)(2,1)S(1)} %pad_maximum_fusion.mine), channel_id=1, source_target_pairs={{0,16},{16,0},{32,48},{48,32},{64,80},{80,64},{96,112},{112,96},{1... | collective-permute-start | bytes 1032200 | tf_op jit(solution)/shard_map/ppermute | solution.py:441

commit v4 on v3

--- a/solution.py
+++ b/solution.py
@@ -14,12 +14,12 @@
 
 PAIR_ROW = 9 * 64
 DEEP_ROW = 14 * 64
-PAY_ROWS = 42 * 64
+PAY_ROWS = 41 * 64
 HALF_ROWS = PAY_ROWS // 2
 
-CORE = ("gx", 1, (0,))
-Y_NEAR = ("gx", 2, (1, 2))
-Y_FAR = ("gx", 6, (2,))
+CORE = ("gx", 1, (0, 1))
+Y_NEAR = ("gx", 3, (1, 2))
+Y_FAR = ("gx", 7, (2,))
 Z_NEAR = ("gy", 1, (0, 1))
 Z_FAR = ("gy", 3, (1,))
 X_NEAR = ("gy", 4, (2, 3))
@@ -51,30 +51,54 @@
     return jnp.concatenate([taps[x + at_x, y + at_y] for x in range(2) for y in ys], axis=0)
 
 
-def faces_kernel(odd, own, cot, to_core, to_chip, y_head, y_tail):
+def faces_kernel(
+    odd, own, cot, to_core, to_chip, y_head, y_tail, x_first, x_last, y_first, y_last, deep, sems
+):
+    copies = [
+        pltpu.make_async_copy(source, target, sems.at[k])
+        for k, (source, target) in enumerate(
+            [
+                (own.at[0], x_first),
+                (own.at[3], x_last),
+                (own.at[:, 0], y_first),
+                (own.at[:, 7], y_last),
+                (cot, deep),
+            ]
+        )
+    ]
+    for copy in copies:
+        copy.start()
+    for copy in copies:
+        copy.wait()
     swapped = odd[0] == 1
     for k in range(4):
-        head = jnp.concatenate([own[0, 2 * k + 1], own[0, 2 * k]], axis=1)
-        tail = jnp.concatenate([own[3, 2 * k], own[3, 2 * k + 1]], axis=1)
+        head = jnp.concatenate([x_first[2 * k + 1], x_first[2 * k]], axis=1)
+        tail = jnp.concatenate([x_last[2 * k], x_last[2 * k + 1]], axis=1)
         to_core[k] = jnp.where(swapped, head, tail)
         to_chip[k] = jnp.where(swapped, tail, head)
-        to_core[4 + k] = jnp.where(swapped, cot[0, k], cot[1, k])
-        to_chip[4 + k] = jnp.where(swapped, cot[1, k], cot[0, k])
+        to_core[4 + k] = jnp.where(swapped, deep[0, k], deep[1, k])
+        to_chip[4 + k] = jnp.where(swapped, deep[1, k], deep[0, k])
     for k in range(2):
-        y_head[k] = jnp.concatenate([own[2 * k, 0], own[2 * k + 1, 0]], axis=1)
-        y_tail[k] = jnp.concatenate([own[2 * k, 7], own[2 * k + 1, 7]], axis=1)
-        y_head[2 + k] = cot[k, 0]
-        y_tail[2 + k] = cot[k, 3]
+        y_head[k] = jnp.concatenate([y_first[2 * k], y_first[2 * k + 1]], axis=1)
+        y_tail[k] = jnp.concatenate([y_last[2 * k], y_last[2 * k + 1]], axis=1)
+        y_head[2 + k] = deep[k, 0]
+        y_tail[2 + k] = deep[k, 3]
 
 
 def faces(odd, own, cot):
-    vmem = pl.BlockSpec(memory_space=pltpu.VMEM)
+    hbm = pl.BlockSpec(memory_space=pltpu.HBM)
     return pl.pallas_call(
         faces_kernel,
-        in_specs=[pl.BlockSpec(memory_space=pltpu.SMEM), vmem, vmem],
-        out_shape=[jax.ShapeDtypeStruct((8, 64, 128), BF16)] * 2
-        + [jax.ShapeDtypeStruct((4, 64, 128), BF16)] * 2,
-        compiler_params=pltpu.CompilerParams(vmem_limit_bytes=6 * 1024 * 1024),
+        in_specs=[pl.BlockSpec(memory_space=pltpu.SMEM), hbm, hbm],
+        out_shape=[pltpu.VMEM((8, 64, 128), BF16)] * 2 + [pltpu.VMEM((4, 64, 128), BF16)] * 2,
+        scratch_shapes=[
+            pltpu.VMEM((8, 64, 64), BF16),
+            pltpu.VMEM((8, 64, 64), BF16),
+            pltpu.VMEM((4, 64, 64), BF16),
+            pltpu.VMEM((4, 64, 64), BF16),
+            pltpu.VMEM((2, 4, 64, 128), BF16),
+            pltpu.SemaphoreType.DMA((5,)),
+        ],
         name="faces",
     )(odd, own, cot)
 
@@ -217,7 +241,7 @@
 
 
 def outer_kernel(
-    odd_x, odd_y, own, cot, core, chip, near, far, w_up, w_deep, sums_in, deep_in, inner,
+    odd_x, odd_y, part, own, cot, core, chip, near, far, w_up, w_deep, sums_in, deep_in, inner,
     keep, send, outer, to_core, to_chip, gy_head, gy_tail,
     taps, cot_taps, blocks, sums, payload,
 ):
@@ -287,18 +311,17 @@
         right = sums[2 * k + 1, :, 128:192] if k < 4 else jnp.zeros((64, 64), F32)
         top = PAIR_ROW + k * 64
         payload[top : top + 64, :] = jnp.concatenate([left, right], axis=1).astype(BF16)
-    payload[PAY_ROWS - 64 :, :] = jnp.zeros((64, 128), BF16)
-    mine = pl.multiple_of(odd_x[0] * HALF_ROWS, HALF_ROWS)
+    mine = pl.multiple_of(part[0] * HALF_ROWS, HALF_ROWS)
     keep[...] = payload[pl.ds(mine, HALF_ROWS), :]
     send[...] = payload[pl.ds(HALF_ROWS - mine, HALF_ROWS), :]
 
 
-def outer_grads(odd_x, odd_y, own, cot, core, chip, near, far, w_up, w_deep, sums, deep, inner):
+def outer_grads(odd_x, odd_y, part, own, cot, core, chip, near, far, w_up, w_deep, sums, deep, inner):
     smem = pl.BlockSpec(memory_space=pltpu.SMEM)
     vmem = pl.BlockSpec(memory_space=pltpu.VMEM)
     return pl.pallas_call(
         outer_kernel,
-        in_specs=[smem, smem] + [vmem] * 11,
+        in_specs=[smem] * 3 + [vmem] * 11,
         out_shape=[
             jax.ShapeDtypeStruct((HALF_ROWS, 128), BF16),
             jax.ShapeDtypeStruct((HALF_ROWS, 128), BF16),
@@ -320,33 +343,10 @@
             flops=2_000_000_000, bytes_accessed=4_000_000, transcendentals=65536
         ),
         name="outer_grads",
-    )(odd_x, odd_y, own, cot, core, chip, near, far, w_up, w_deep, sums, deep, inner)
-
-
-def input_kernel(odd_x, odd_y, inner, outer, core, chip, near, far, w_up, out, taps):
-    swap_x = odd_x[0] == 1
-    swap_y = odd_y[0] == 1
-
-    def x_lo(k):
-        return jnp.where(swap_x, core[k], chip[k])
-
-    def x_hi(k):
-        return jnp.where(swap_x, chip[k], core[k])
-
-    def y_lo(k):
-        return jnp.where(swap_y, near[k], far[k])
-
-    def y_hi(k):
-        return jnp.where(swap_y, far[k], near[k])
-
-    def own(u, v):
-        at = (u % 2) * 128 + (v % 2) * 64
-        top = ((u // 2) * 2 + (v // 2 in (2, 3))) * 64
-        return (inner if v // 2 in INNER else outer)[top : top + 64, at : at + 64]
-
-    for x in range(6):
-        for y in range(10):
-            taps[x, y] = depth_taps(level_column(x, y, own, x_lo, x_hi, y_lo, y_hi), 64)
+    )(odd_x, odd_y, part, own, cot, core, chip, near, far, w_up, w_deep, sums, deep, inner)
+
+
+def input_columns(ys, taps, w_up):
     empty = jnp.zeros((64, 256), BF16)
     spare = jnp.zeros((64, 64), BF16)
     weights = {}
@@ -355,7 +355,7 @@
             weights[a, b] = jnp.concatenate(
                 [w_up[a, b, 2], w_up[a, b, 1], w_up[a, b, 0], spare], axis=1
             )
-    total = jnp.zeros((512, 256), F32)
+    total = jnp.zeros((2 * len(ys) * 64, 256), F32)
     for x in range(4):
         for y in range(4):
             block = jnp.concatenate(
@@ -363,30 +363,96 @@
                 axis=0,
             )
             total = total + lax.dot_general(
-                window(taps, x, y, range(4)), block, (((1,), (1,)), ((), ())), preferred_element_type=F32
+                window(taps, x, y, ys), block, (((1,), (1,)), ((), ())),
+                preferred_element_type=F32,
             )
-    total = total.astype(BF16)
-    for x in range(4):
-        for y in range(8):
-            at = (x % 2) * 128 + (y % 2) * 64
-            top = ((x // 2) * 4 + y // 2) * 64
-            out[x, y] = total[top : top + 64, at : at + 64]
-
-
-def local_input(odd_x, odd_y, inner, outer, core, chip, near, far, w_up):
+    return total.astype(BF16)
+
+
+def picked(inner, outer, x, y):
+    at = (x % 2) * 128 + (y % 2) * 64
+    top = ((x // 2) * 2 + (y // 2 in (2, 3))) * 64
+    return (inner if y // 2 in INNER else outer)[top : top + 64, at : at + 64]
+
+
+def inner_input_kernel(odd_x, inner, outer, core, chip, w_up, out, taps):
+    swap_x = odd_x[0] == 1
+
+    def x_lo(k):
+        return jnp.where(swap_x, core[k], chip[k])
+
+    def x_hi(k):
+        return jnp.where(swap_x, chip[k], core[k])
+
+    def own(u, v):
+        return picked(inner, outer, u, v)
+
+    for x in range(6):
+        for y in range(2, 8):
+            taps[x, y] = depth_taps(level_column(x, y, own, x_lo, x_hi, None, None), 64)
+    out[...] = input_columns(INNER, taps, w_up)
+
+
+def inner_input(odd_x, inner, outer, core, chip, w_up):
     smem = pl.BlockSpec(memory_space=pltpu.SMEM)
     vmem = pl.BlockSpec(memory_space=pltpu.VMEM)
     return pl.pallas_call(
-        input_kernel,
-        in_specs=[smem, smem] + [vmem] * 7,
+        inner_input_kernel,
+        in_specs=[smem] + [vmem] * 5,
+        out_shape=jax.ShapeDtypeStruct((256, 256), BF16),
+        scratch_shapes=[pltpu.VMEM((6, 10, 64, 256), BF16)],
+        compiler_params=pltpu.CompilerParams(vmem_limit_bytes=VMEM_BYTES),
+        cost_estimate=pl.CostEstimate(
+            flops=500_000_000, bytes_accessed=2_000_000, transcendentals=0
+        ),
+        name="inner_input",
+    )(odd_x, inner, outer, core, chip, w_up)
+
+
+def outer_input_kernel(
+    odd_x, odd_y, inner, outer, core, chip, near, far, w_up, inner_part, out, taps
+):
+    swap_x = odd_x[0] == 1
+    swap_y = odd_y[0] == 1
+
+    def x_lo(k):
+        return jnp.where(swap_x, core[k], chip[k])
+
+    def x_hi(k):
+        return jnp.where(swap_x, chip[k], core[k])
+
+    def y_lo(k):
+        return jnp.where(swap_y, near[k], far[k])
+
+    def y_hi(k):
+        return jnp.where(swap_y, far[k], near[k])
+
+    def own(u, v):
+        return picked(inner, outer, u, v)
+
+    for x in range(6):
+        for y in (0, 1, 2, 3, 6, 7, 8, 9):
+            taps[x, y] = depth_taps(level_column(x, y, own, x_lo, x_hi, y_lo, y_hi), 64)
+    outer_part = input_columns(OUTER, taps, w_up)
+    for x in range(4):
+        for y in range(8):
+            out[x, y] = picked(inner_part, outer_part, x, y)
+
+
+def outer_input(odd_x, odd_y, inner, outer, core, chip, near, far, w_up, inner_part):
+    smem = pl.BlockSpec(memory_space=pltpu.SMEM)
+    vmem = pl.BlockSpec(memory_space=pltpu.VMEM)
+    return pl.pallas_call(
+        outer_input_kernel,
+        in_specs=[smem, smem] + [vmem] * 8,
         out_shape=jax.ShapeDtypeStruct((4, 8, 64, 64), BF16),
         scratch_shapes=[pltpu.VMEM((6, 10, 64, 256), BF16)],
         compiler_params=pltpu.CompilerParams(vmem_limit_bytes=VMEM_BYTES),
         cost_estimate=pl.CostEstimate(
-            flops=1_000_000_000, bytes_accessed=4_000_000, transcendentals=0
+            flops=500_000_000, bytes_accessed=4_000_000, transcendentals=0
         ),
-        name="local_input",
-    )(odd_x, odd_y, inner, outer, core, chip, near, far, w_up)
+        name="outer_input",
+    )(odd_x, odd_y, inner, outer, core, chip, near, far, w_up, inner_part)
 
 
 def unpack_kernel(up_scale, deep_scale, odd, mine, other, up, deep, payload):
@@ -470,14 +536,27 @@
     return tree_sum(found)
 
 
-def swap_sum(value, steps):
-    return tree_sum([value] + [swap(value, steps, k) for k in range(1, 1 << len(steps))])
-
-
-def gather(value, steps):
+def swap_sum(value, step):
+    return tree_sum([value, swap(value, (step,), 1)])
+
+
+def swap_sum_with(value, step, rider):
+    rows = value.shape[0]
+    got = swap(jnp.concatenate([value, rider]), (step,), 1)
+    return tree_sum([value, got[:rows]]), got[rows:]
+
+
+def gather(value, steps, riders):
     parts = 1 << len(steps)
+    rows = value.shape[0]
     me = place_of(steps)
-    found = [value] + [swap(value, steps, k) for k in range(1, parts)]
+    found, came = [value], []
+    for k in range(1, parts):
+        rider = riders[k - 1]
+        sent = value if rider is None else jnp.concatenate([value, rider])
+        got = swap(sent, steps, k)
+        found.append(got[:rows])
+        came.append(got[rows:])
     for place in range(len(steps)):
         near = ((me >> place) & 1) == 0
         other = 1 << place
@@ -487,7 +566,7 @@
             else jnp.where(near, found[i | other], found[i & ~other])
             for i in range(parts)
         ]
-    return jnp.concatenate(found)
+    return jnp.concatenate(found), came
 
 
 def pairs_of(axis, first):
@@ -495,6 +574,10 @@
     for i in range(first, lax.axis_size(axis) - 1, 2):
         found += [(i, i + 1), (i + 1, i)]
     return found
+
+
+def chip_pairs(which):
+    return [pair for pair in pairs_of("gx", 1) if (pair[0] + 1) // 2 % 2 == which]
 
 
 def both_sides(first, second, axis):
@@ -525,8 +608,13 @@
     odd_x = (lax.axis_index("gx") & 1).astype(jnp.int32)
     odd_y = (lax.axis_index("gy") & 1).astype(jnp.int32)
     flag_x, flag_y = odd_x.reshape(1), odd_y.reshape(1)
-
-    to_core, to_chip, y_head, y_tail = faces(flag_x, level_input, deep_cotangent)
+    part = side_bit(CORE).astype(jnp.int32).reshape(1)
+
+    to_core, to_chip, y_head, y_tail = faces(
+        flag_x,
+        pltpu.with_memory_space_constraint(level_input, pltpu.HBM),
+        pltpu.with_memory_space_constraint(deep_cotangent, pltpu.HBM),
+    )
     core, chip = both_sides(to_core, to_chip, "gx")
     to_near, to_far = column_ends(odd_x, odd_y, core, chip, y_head, y_tail, True)
     near, far = both_sides(to_near, to_far, "gy")
@@ -535,32 +623,42 @@
         flag_x, level_input, deep_cotangent, core, chip, weight_upper, weight_deep
     )
     keep, send, outer, to_core, to_chip, y_head, y_tail = outer_grads(
-        flag_x, flag_y, level_input, deep_cotangent, core, chip, near, far,
+        flag_x, flag_y, part, level_input, deep_cotangent, core, chip, near, far,
         weight_upper, weight_deep, sums, deep, inner,
     )
+    at_x, at_y = lax.axis_index("gx"), lax.axis_index("gy")
     total = tree_sum([keep, swap(send, (CORE,), 1)])
     core = lax.ppermute(to_core, "gx", pairs_of("gx", 0))
     total, core = lax.optimization_barrier((total, core))
     total = scatter_sum(total, (Z_NEAR, X_NEAR))
     total, to_chip = lax.optimization_barrier((total, to_chip))
-    total = swap_sum(total, (Z_FAR,))
-    chip = lax.ppermute(to_chip, "gx", pairs_of("gx", 1))
-    total, chip = lax.optimization_barrier((total, chip))
+    first = lax.ppermute(to_chip, "gx", chip_pairs(1))
+    total = swap_sum(total, Y_NEAR)
+    total, to_chip, first = lax.optimization_barrier((total, to_chip, first))
+    second = lax.ppermute(to_chip, "gx", chip_pairs(0))
+    total = swap_sum(total, Y_FAR)
+    chip = jnp.where((((at_x + 1) >> 1) & 1) == 1, first, second)
+    inner_part = inner_input(flag_x, inner, outer, core, chip, weight_upper)
     to_near, to_far = column_ends(odd_x, odd_y, core, chip, y_head, y_tail, False)
-    total = swap_sum(total, (X_FAR,))
-    near = lax.ppermute(to_near, "gy", pairs_of("gy", 0))
-    total, near, to_far = lax.optimization_barrier((total, near, to_far))
-    total = swap_sum(total, (Y_NEAR,))
-    far = lax.ppermute(to_far, "gy", pairs_of("gy", 1))
-    total, far = lax.optimization_barrier((total, far))
-    input_grad = local_input(
-        flag_x, flag_y, inner, outer, core, chip, near, far, weight_upper
-    )
-    total = swap_sum(total, (Y_FAR,))
-    total, input_grad = lax.optimization_barrier((total, input_grad))
-    total = gather(total, (Z_NEAR, X_NEAR))
+    total, direct = swap_sum_with(total, Z_FAR, to_far.reshape(-1, 128))
+    total, handed_far = swap_sum_with(total, X_FAR, direct)
+    total, inner_part = lax.optimization_barrier((total, inner_part))
+    total, (near, handed_near, _) = gather(
+        total, (Z_NEAR, X_NEAR), (to_near.reshape(-1, 128), direct, None)
+    )
+    plane, depth = at_y >> 2, at_y & 3
+    none = jnp.zeros_like(direct)
+    handed = jnp.where(
+        ((depth == 0) & (plane == 2)) | ((depth == 3) & (plane == 1)), handed_far, handed_near
+    )
+    ends = (at_y == 0) | (at_y == lax.axis_size("gy") - 1)
+    far = jnp.where((depth == 1) | (depth == 2), direct, jnp.where(ends, none, handed))
+    input_grad = outer_input(
+        flag_x, flag_y, inner, outer, core, chip, near.reshape(to_near.shape),
+        far.reshape(to_far.shape), weight_upper, inner_part,
+    )
     other = swap(total, (CORE,), 1)
-    upper, deep = unpack(flag_x, total, other, up_scale, deep_scale)
+    upper, deep = unpack(part, total, other, up_scale, deep_scale)
     return (input_grad, upper, deep)
 
 

time: 74.4 us -> 70.5 us (0.948); the launches traced: 74.2 us -> 69.2 us
  starting transfers between devices: 41.2 us -> 30.9 us
  waiting for transfers between devices: 19.3 us -> 24.9 us
  local copies, waits for them, and re-layouts: 2.04 us -> 0.11 us
  Pallas kernels: 10.3 us -> 11.8 us
    ppermute x12, starting transfers between devices: 25.9 us -> 20.7 us  [swap(): lax.ppermute(value, axis, [(i, i ^ masks[axis]) for i in range(count)])]
    ppermute x3 -> x2, starting transfers between devices: 7.62 us -> 2.57 us  [the longest x1 1.92 us: local(): first = lax.ppermute(to_chip, 'gx', chip_pairs(1))]
    ppermute x12, waiting for transfers between devices: 14.3 us -> 18.5 us  [swap(): lax.ppermute(value, axis, [(i, i ^ masks[axis]) for i in range(count)])]
    unnamed x16 -> x12, local copies, waits for them, and re-layouts: 2 us -> 0.06 us
    ppermute x3 -> x2, waiting for transfers between devices: 1.89 us -> 3.4 us  [the longest x1 3.4 us: local(): first = lax.ppermute(to_chip, 'gx', chip_pairs(1))]
    pallas_call x1, Pallas kernels: 0.12 us -> 1.34 us  [faces(): pl.pallas_call(faces_kernel, in_specs=[pl.BlockSpec(memory_space=pltpu.SM...]
    pallas_call x2 -> x3, Pallas kernels: 5.51 us -> 5.8 us  [the longest x1 3.34 us: outer_grads(): pl.pallas_call(outer_kernel, in_specs=[smem] * 3 + [vmem] * 11, out_shape...]
  transfers between devices with their start and end apart: 20 -> 19, of which waited for: 12 -> 10; matrix products, arithmetic and copies ran while one was open for 0% -> 0% of each run, Pallas kernels for 7% -> 8%
where the time goes in v4:
time: 70.5 us; the launch traced here: 69.2 us
  starting transfers between devices  30.9 us (44%)
  waiting for transfers between devices  24.9 us (35%)
  Pallas kernels  11.8 us (17%)
  between operations  1 us (1%)
    ppermute x12, starting transfers between devices, swap(): lax.ppermute(value, axis, [(i, i ^ masks[axis]) for i in range(count)])  20.7 us
    ppermute x12, waiting for transfers between devices, swap(): lax.ppermute(value, axis, [(i, i ^ masks[axis]) for i in range(count)])  18.5 us
    ppermute x2, starting transfers between devices, both_sides(): lax.ppermute(second, axis, pairs_of(axis, 1))  3.84 us
    ppermute x1, waiting for transfers between devices, local(): first = lax.ppermute(to_chip, 'gx', chip_pairs(1))  3.4 us
    pallas_call x1, Pallas kernels, outer_grads(): pl.pallas_call(outer_kernel, in_specs=[smem] * 3 + [vmem] * 11, out_shape...  3.34 us
    ppermute x2, starting transfers between devices, both_sides(): lax.ppermute(first, axis, pairs_of(axis, 0))  3.3 us
    pallas_call x1, Pallas kernels, inner_grads(): pl.pallas_call(inner_kernel, in_specs=[smem] + [vmem] * 6, out_shape=[jax...  3.19 us
    ppermute x2, waiting for transfers between devices, both_sides(): lax.ppermute(second, axis, pairs_of(axis, 1))  3.03 us
  transfers between devices with their start and end apart: 19, of which 10 were waited for; matrix products, arithmetic and copies ran while one was open for 0% of the time, Pallas kernels for 8%

profile of v4, /device:TPU:1, one launch (start us, length us, event | category | flops | bytes accessed | tf_op | source)
XLA Modules:
  0.0 69.2 jit_solution(3329735521138392573)
XLA Ops:
  0.6 1.3 %faces.1 = (bf16[8,64,128]{2,1,0:T(8,128)(2,1)S(1)}, bf16[8,64,128]{2,1,0:T(8,128)(2,1)S(1)}, bf16[4,64,128]{2,1,0:T(8,128)(2,1)S(1)}, bf16[4,64,128]{2,1,0:T(8,128)(2,1)S(1)}) custom-call(s32[1]{0:T(128)} %bitcast.odd.odd_x, bf16[4,8,64,64]{3,2,1,0:T(8,128)(2,1)} %own.5, bf16[2,4,64,128]{3,2,1,0:T(8,128)(2,1)} %cot.5), custom_call_target="tpu_custom_call" | custom-call | tf_op jit(solution)/shard_map/faces/pallas_call | solution.py:90
  2.0 1.5 %collective-permute-start = (bf16[8,64,128]{2,1,0:T(8,128)(2,1)S(1)}, bf16[8,64,128]{2,1,0:T(8,128)(2,1)S(1)}, u32[]{:S(2)}, u32[]{:S(2)}) collective-permute-start(bf16[8,64,128]{2,1,0:T(8,128)(2,1)S(1)} %get-tuple-element.28), channel_id=1, source_target_pairs={{0,16},{16,0},{32,48},{48,32},{64,80},{80,64},{96,112},{112,96},{1... | collective-permute-start | bytes 393224 | tf_op jit(solution)/shard_map/ppermute | solution.py:585
  3.5 3.2 %collective-permute-start.1 = (bf16[8,64,128]{2,1,0:T(8,128)(2,1)S(1)}, bf16[8,64,128]{2,1,0:T(8,128)(2,1)S(1)}, u32[]{:S(2)}, u32[]{:S(2)}) collective-permute-start(bf16[8,64,128]{2,1,0:T(8,128)(2,1)S(1)} %get-tuple-element.29), channel_id=1, source_target_pairs={{16,32},{32,16},{48,64},{64,48},{80,96},{96,80},{17,33},{33,17},{4... | collective-permute-start | bytes 393224 | tf_op jit(solution)/shard_map/ppermute | solution.py:586
  6.7 0.0 collective-permute-done.core
  6.7 3.0 %collective-permute-done.1.chip = bf16[8,64,128]{2,1,0:T(8,128)(2,1)S(1)} collective-permute-done((bf16[8,64,128]{2,1,0:T(8,128)(2,1)S(1)}, bf16[8,64,128]{2,1,0:T(8,128)(2,1)S(1)}, u32[]{:S(2)}, u32[]{:S(2)}) %collective-permute-start.1) | collective-permute-done | bytes 131104 | tf_op jit(solution)/shard_map/ppermute | solution.py:586
  9.8 0.0 copy-start
  9.9 0.0 copy-start.1
  9.9 1.8 %collective-permute-start.2 = (bf16[7,64,128]{2,1,0:T(8,128)(2,1)S(1)}, bf16[7,64,128]{2,1,0:T(8,128)(2,1)S(1)}, u32[]{:S(2)}, u32[]{:S(2)}) collective-permute-start(bf16[7,64,128]{2,1,0:T(8,128)(2,1)S(1)} %get-tuple-element.67), channel_id=1, source_target_pairs={{0,1},{1,0},{2,3},{3,2},{4,5},{5,4},{6,7},{7,6},{8,9},{9,8},{10,11... | collective-permute-start | bytes 344072 | tf_op jit(solution)/shard_map/ppermute | solution.py:585
  11.7 0.7 collective-permute-start.3
  12.4 3.2 %inner_grads.1 = (f32[9,64,256]{2,1,0:T(8,128)S(1)}, f32[27,64,128]{2,1,0:T(8,128)S(1)}, bf16[256,256]{1,0:T(8,128)(2,1)S(1)}) custom-call(s32[1]{0:T(128)} %bitcast.odd.odd_x, bf16[4,8,64,64]{3,2,1,0:T(8,128)(2,1)S(1)} %copy-done, bf16[2,4,64,128]{3,2,1,0:T(8,128)(2,1)S(1)} %copy-done.1, bf16[8,64,128]{2,1,0:T(8,128)(2,1)S(1)} %collective-permute-done.core, ...), custom_call_target="tpu_custom_call" | custom-call | flops 2000000000 | bytes 4000000 | tf_op jit(solution)/shard_map/inner_grads/pallas_call | solution.py:222
  15.6 0.0 collective-permute-done.2.near
  15.6 0.0 collective-permute-done.3.far
  15.7 3.3 %outer_grads.1 = (bf16[1312,128]{1,0:T(8,128)(2,1)S(1)}, bf16[1312,128]{1,0:T(8,128)(2,1)S(1)}, bf16[256,256]{1,0:T(8,128)(2,1)S(1)}, bf16[4,64,128]{2,1,0:T(8,1...) custom-call(s32[1]{0:T(128)} %bitcast.odd.odd_x, ...), custom_call_target="tpu_custom_call" | custom-call | flops 2000000000 | bytes 4000000 | tf_op jit(solution)/shard_map/outer_grads/pallas_call | solution.py:322
  19.0 0.1 collective-permute-start.4
  19.1 0.5 collective-permute-start.5
  19.6 1.1 %collective-permute-done.4 = bf16[1312,128]{1,0:T(8,128)(2,1)S(1)} collective-permute-done((bf16[1312,128]{1,0:T(8,128)(2,1)S(1)}, bf16[1312,128]{1,0:T(8,128)(2,1)S(1)}, u32[]{:S(2)}, u32[]{:S(2)}) %collective-permute-start.4) | collective-permute-done | bytes 335904 | tf_op jit(solution)/shard_map/ppermute | solution.py:507
  20.7 0.1 add_convert_fusion
  20.8 0.0 collective-permute-done.5.core
  20.9 5.2 %collective-permute-start.8 = (bf16[328,128]{1,0:T(8,128)(2,1)S(1)}, bf16[328,128]{1,0:T(8,128)(2,1)S(1)}, u32[]{:S(2)}, u32[]{:S(2)}) collective-permute-start(bf16[328,128]{1,0:T(8,128)(2,1)S(1)} %get-tuple-element.60), channel_id=1, source_target_pairs={{0,5},{1,4},{2,7},{3,6},{4,1},{5,0},{6,3},{7,2},{8,13},{9,12},{10,... | collective-permute-start | bytes 251912 | tf_op jit(solution)/shard_map/ppermute | solution.py:507
  26.1 0.3 collective-permute-start.7
  26.3 0.7 %collective-permute-start.6 = (bf16[328,128]{1,0:T(8,128)(2,1)S(1)}, bf16[328,128]{1,0:T(8,128)(2,1)S(1)}, u32[]{:S(2)}, u32[]{:S(2)}) collective-permute-start(bf16[328,128]{1,0:T(8,128)(2,1)S(1)} %get-tuple-element.59), channel_id=1, source_target_pairs={{0,1},{1,0},{2,3},{3,2},{4,5},{5,4},{6,7},{7,6},{8,9},{9,8},{10,11... | collective-permute-start | bytes 251912 | tf_op jit(solution)/shard_map/ppermute | solution.py:507
  27.0 1.8 %collective-permute-done.8 = bf16[328,128]{1,0:T(8,128)(2,1)S(1)} collective-permute-done((bf16[328,128]{1,0:T(8,128)(2,1)S(1)}, bf16[328,128]{1,0:T(8,128)(2,1)S(1)}, u32[]{:S(2)}, u32[]{:S(2)}) %collective-permute-start.8) | collective-permute-done | bytes 84000 | tf_op jit(solution)/shard_map/ppermute | solution.py:507
  28.8 1.8 %collective-permute-done.7 = bf16[328,128]{1,0:T(8,128)(2,1)S(1)} collective-permute-done((bf16[328,128]{1,0:T(8,128)(2,1)S(1)}, bf16[328,128]{1,0:T(8,128)(2,1)S(1)}, u32[]{:S(2)}, u32[]{:S(2)}) %collective-permute-start.7) | collective-permute-done | bytes 84000 | tf_op jit(solution)/shard_map/ppermute | solution.py:507
  30.6 0.0 collective-permute-done.6
  30.7 3.3 %collective-permute-start.9 = (bf16[328,128]{1,0:T(8,128)(2,1)S(1)}, bf16[328,128]{1,0:T(8,128)(2,1)S(1)}, u32[]{:S(2)}, u32[]{:S(2)}) collective-permute-start(bf16[328,128]{1,0:T(8,128)(2,1)S(1)} %add_convert_fusion.5), channel_id=1, source_target_pairs={{0,48},{16,32},{32,16},{48,0},{64,112},{80,96},{96,80},{112,64},{1... | collective-permute-start | bytes 251912 | tf_op jit(solution)/shard_map/ppermute | solution.py:507
  34.0 1.9 %collective-permute-start.10 = (bf16[4,64,128]{2,1,0:T(8,128)(2,1)S(1)}, bf16[4,64,128]{2,1,0:T(8,128)(2,1)S(1)}, u32[]{:S(2)}, u32[]{:S(2)}) collective-permute-start(bf16[4,64,128]{2,1,0:T(8,128)(2,1)S(1)} %get-tuple-element.45), channel_id=1, source_target_pairs={{16,32},{32,16},{80,96},{96,80},{17,33},{33,17},{81,97},{97,81},{1... | collective-permute-start | bytes 196616 | tf_op jit(solution)/shard_map/ppermute | solution.py:635
  35.9 0.2 collective-permute-done.9
  36.1 3.4 %collective-permute-done.10 = bf16[4,64,128]{2,1,0:T(8,128)(2,1)S(1)} collective-permute-done((bf16[4,64,128]{2,1,0:T(8,128)(2,1)S(1)}, bf16[4,64,128]{2,1,0:T(8,128)(2,1)S(1)}, u32[]{:S(2)}, u32[]{:S(2)}) %collective-permute-start.10) | collective-permute-done | bytes 65568 | tf_op jit(solution)/shard_map/ppermute | solution.py:635
  39.5 0.7 collective-permute-start.11
  40.2 1.5 %collective-permute-start.12 = (bf16[328,128]{1,0:T(8,128)(2,1)S(1)}, bf16[328,128]{1,0:T(8,128)(2,1)S(1)}, u32[]{:S(2)}, u32[]{:S(2)}) collective-permute-start(bf16[328,128]{1,0:T(8,128)(2,1)S(1)} %add_convert_fusion.4), channel_id=1, source_target_pairs={{0,112},{16,96},{32,80},{48,64},{64,48},{80,32},{96,16},{112,0},{1... | collective-permute-start | bytes 251912 | tf_op jit(solution)/shard_map/ppermute | solution.py:507
  41.7 0.0 collective-permute-done.11
  41.8 3.6 %collective-permute-done.12 = bf16[328,128]{1,0:T(8,128)(2,1)S(1)} collective-permute-done((bf16[328,128]{1,0:T(8,128)(2,1)S(1)}, bf16[328,128]{1,0:T(8,128)(2,1)S(1)}, u32[]{:S(2)}, u32[]{:S(2)}) %collective-permute-start.12) | collective-permute-done | bytes 84000 | tf_op jit(solution)/shard_map/ppermute | solution.py:507
  45.4 3.5 %collective-permute-start.13 = (bf16[520,128]{1,0:T(8,128)(2,1)S(1)}, bf16[520,128]{1,0:T(8,128)(2,1)S(1)}, u32[]{:S(2)}, u32[]{:S(2)}) collective-permute-start(bf16[520,128]{1,0:T(8,128)(2,1)S(1)} %pad_maximum_fusion.4), channel_id=1, source_target_pairs={{0,3},{1,2},{2,1},{3,0},{4,7},{5,6},{6,5},{7,4},{8,11},{9,10},{10,... | collective-permute-start | bytes 399368 | tf_op jit(solution)/shard_map/ppermute | solution.py:507
  48.9 2.4 %collective-permute-done.13 = bf16[520,128]{1,0:T(8,128)(2,1)S(1)} collective-permute-done((bf16[520,128]{1,0:T(8,128)(2,1)S(1)}, bf16[520,128]{1,0:T(8,128)(2,1)S(1)}, u32[]{:S(2)}, u32[]{:S(2)}) %collective-permute-start.13) | collective-permute-done | bytes 133152 | tf_op jit(solution)/shard_map/ppermute | solution.py:507
  51.3 3.0 %collective-permute-start.14 = (bf16[520,128]{1,0:T(8,128)(2,1)S(1)}, bf16[520,128]{1,0:T(8,128)(2,1)S(1)}, u32[]{:S(2)}, u32[]{:S(2)}) collective-permute-start(bf16[520,128]{1,0:T(8,128)(2,1)S(1)} %pad_maximum_fusion.2), channel_id=1, source_target_pairs={{0,12},{1,13},{2,14},{3,15},{4,8},{5,9},{6,10},{7,11},{8,4},{9,5},... | collective-permute-start | bytes 399368 | tf_op jit(solution)/shard_map/ppermute | solution.py:507
  54.3 0.8 %inner_input.1.inner_part = bf16[256,256]{1,0:T(8,128)(2,1)S(1)} custom-call(s32[1]{0:T(128)} %bitcast.odd.odd_x, bf16[256,256]{1,0:T(8,128)(2,1)S(1)} %get-tuple-element.30.inner, bf16[256,256]{1,0:T(8,128)(2,1)S(1)} %get-tuple-element.35.outer, bf16[4,64,128]{2,1,0:T(8,128)(2,1)S(1)} %collective-permute-done.5.core, ...), custom_call_target="tpu_custom_call" | custom-call | flops 500000000 | bytes 2000000 | tf_op jit(solution)/shard_map/inner_input/pallas_call | solution.py:399
  55.1 1.7 %collective-permute-done.14 = bf16[520,128]{1,0:T(8,128)(2,1)S(1)} collective-permute-done((bf16[520,128]{1,0:T(8,128)(2,1)S(1)}, bf16[520,128]{1,0:T(8,128)(2,1)S(1)}, u32[]{:S(2)}, u32[]{:S(2)}) %collective-permute-start.14) | collective-permute-done | bytes 133152 | tf_op jit(solution)/shard_map/ppermute | solution.py:507
  56.8 0.1 collective-permute-start.15
  56.9 0.6 collective-permute-start.16
  57.5 2.1 %collective-permute-start.17 = (bf16[328,128]{1,0:T(8,128)(2,1)S(1)}, bf16[328,128]{1,0:T(8,128)(2,1)S(1)}, u32[]{:S(2)}, u32[]{:S(2)}) collective-permute-start(bf16[328,128]{1,0:T(8,128)(2,1)S(1)} %add_convert_fusion.1), channel_id=1, source_target_pairs={{0,5},{1,4},{2,7},{3,6},{4,1},{5,0},{6,3},{7,2},{8,13},{9,12},{10,... | collective-permute-start | bytes 251912 | tf_op jit(solution)/shard_map/ppermute | solution.py:507
  59.5 5.9 %collective-permute-done.17 = bf16[328,128]{1,0:T(8,128)(2,1)S(1)} collective-permute-done((bf16[328,128]{1,0:T(8,128)(2,1)S(1)}, bf16[328,128]{1,0:T(8,128)(2,1)S(1)}, u32[]{:S(2)}, u32[]{:S(2)}) %collective-permute-start.17) | collective-permute-done | bytes 84000 | tf_op jit(solution)/shard_map/ppermute | solution.py:507
  65.4 0.0 collective-permute-done.15
  65.4 0.0 collective-permute-done.16
  65.4 0.1 broadcast_select_fusion.11
  65.6 0.5 collective-permute-start.18
  66.1 1.7 %outer_input.1 = bf16[4,8,64,64]{3,2,1,0:T(8,128)(2,1)} custom-call(s32[1]{0:T(128)} %bitcast.odd.odd_x, s32[1]{0:T(128)} %bitcast.1.odd_y, bf16[256,256]{1,0:T(8,128)(2,1)S(1)} %get-tuple-element.30.inner, bf16[256,256]{1,0:T(8,128)(2,1)S(1)} %get-tuple-element.35.outer, bf16[4,64,128]{2,1,0:T(8,128)(2,1)S(1)} %collective-permute-done.5.core, ...), custom_call_target="tpu_custom_call" | custom-call | flops 500000000 | bytes 4000000 | tf_op jit(solution)/shard_map/outer_input/pallas_call | solution.py:445
  67.8 0.0 collective-permute-done.18.other
  67.8 1.5 %unpack.1 = (f32[3,3,3,64,64]{4,3,2,1,0:T(8,128)}, f32[3,3,3,64,128]{4,3,2,1,0:T(8,128)}) custom-call(s32[1]{0:T(128)} %bitcast.2.part.odd, bf16[1312,128]{1,0:T(8,128)(2,1)S(1)} %pad_maximum_fusion.mine, bf16[1312,128]{1,0:T(8,128)(2,1)S(1)} %collective-permute-done.18.other), custom_call_target="tpu_custom_call" | custom-call | tf_op jit(solution)/shard_map/unpack/pallas_call | solution.py:480
  (32 shorter events, 0.5 us)
Async XLA Ops:
  0.6 11.8 %copy-start.3 = (bf16[3,3,3,64,64]{4,3,2,1,0:T(8,128)(2,1)S(1)}, bf16[3,3,3,64,64]{4,3,2,1,0:T(8,128)(2,1)}, u32[]{:S(2)}) copy-start(bf16[3,3,3,64,64]{4,3,2,1,0:T(8,128)(2,1)} %w_up.7) | copy-start | bytes 663556
  2.0 4.7 %collective-permute-start = (bf16[8,64,128]{2,1,0:T(8,128)(2,1)S(1)}, bf16[8,64,128]{2,1,0:T(8,128)(2,1)S(1)}, u32[]{:S(2)}, u32[]{:S(2)}) collective-permute-start(bf16[8,64,128]{2,1,0:T(8,128)(2,1)S(1)} %get-tuple-element.28), channel_id=1, source_target_pairs={{0,16},{16,0},{32,48},{48,32},{64,80},{80,64},{96,112},{112,96},{1... | collective-permute-start | bytes 393224 | tf_op jit(solution)/shard_map/ppermute | solution.py:585
  3.5 6.3 %collective-permute-start.1 = (bf16[8,64,128]{2,1,0:T(8,128)(2,1)S(1)}, bf16[8,64,128]{2,1,0:T(8,128)(2,1)S(1)}, u32[]{:S(2)}, u32[]{:S(2)}) collective-permute-start(bf16[8,64,128]{2,1,0:T(8,128)(2,1)S(1)} %get-tuple-element.29), channel_id=1, source_target_pairs={{16,32},{32,16},{48,64},{64,48},{80,96},{96,80},{17,33},{33,17},{4... | collective-permute-start | bytes 393224 | tf_op jit(solution)/shard_map/ppermute | solution.py:586
  9.8 2.6 %copy-start.2 = (bf16[3,3,3,64,128]{4,3,2,1,0:T(8,128)(2,1)S(1)}, bf16[3,3,3,64,128]{4,3,2,1,0:T(8,128)(2,1)}, u32[]{:S(2)}) copy-start(bf16[3,3,3,64,128]{4,3,2,1,0:T(8,128)(2,1)} %w_deep.3) | copy-start | bytes 1327108
  9.8 2.6 %copy-start = (bf16[4,8,64,64]{3,2,1,0:T(8,128)(2,1)S(1)}, bf16[4,8,64,64]{3,2,1,0:T(8,128)(2,1)}, u32[]{:S(2)}) copy-start(bf16[4,8,64,64]{3,2,1,0:T(8,128)(2,1)} %own.5) | copy-start | bytes 786436
  9.9 2.5 %copy-start.1 = (bf16[2,4,64,128]{3,2,1,0:T(8,128)(2,1)S(1)}, bf16[2,4,64,128]{3,2,1,0:T(8,128)(2,1)}, u32[]{:S(2)}) copy-start(bf16[2,4,64,128]{3,2,1,0:T(8,128)(2,1)} %cot.5) | copy-start | bytes 393220
  9.9 5.7 %collective-permute-start.2 = (bf16[7,64,128]{2,1,0:T(8,128)(2,1)S(1)}, bf16[7,64,128]{2,1,0:T(8,128)(2,1)S(1)}, u32[]{:S(2)}, u32[]{:S(2)}) collective-permute-start(bf16[7,64,128]{2,1,0:T(8,128)(2,1)S(1)} %get-tuple-element.67), channel_id=1, source_target_pairs={{0,1},{1,0},{2,3},{3,2},{4,5},{5,4},{6,7},{7,6},{8,9},{9,8},{10,11... | collective-permute-start | bytes 344072 | tf_op jit(solution)/shard_map/ppermute | solution.py:585
  11.7 3.9 %collective-permute-start.3 = (bf16[7,64,128]{2,1,0:T(8,128)(2,1)S(1)}, bf16[7,64,128]{2,1,0:T(8,128)(2,1)S(1)}, u32[]{:S(2)}, u32[]{:S(2)}) collective-permute-start(bf16[7,64,128]{2,1,0:T(8,128)(2,1)S(1)} %get-tuple-element.66), channel_id=1, source_target_pairs={{1,2},{2,1},{3,4},{4,3},{5,6},{6,5},{7,8},{8,7},{9,10},{10,9},{11,... | collective-permute-start | bytes 344072 | tf_op jit(solution)/shard_map/ppermute | solution.py:586
  19.0 1.7 %collective-permute-start.4 = (bf16[1312,128]{1,0:T(8,128)(2,1)S(1)}, bf16[1312,128]{1,0:T(8,128)(2,1)S(1)}, u32[]{:S(2)}, u32[]{:S(2)}) collective-permute-start(bf16[1312,128]{1,0:T(8,128)(2,1)S(1)} %get-tuple-element.37), channel_id=1, source_target_pairs={{0,16},{16,0},{32,48},{48,32},{64,80},{80,64},{96,112},{112,96},{1... | collective-permute-start | bytes 1007624 | tf_op jit(solution)/shard_map/ppermute | solution.py:507
  19.1 1.7 %collective-permute-start.5 = (bf16[4,64,128]{2,1,0:T(8,128)(2,1)S(1)}, bf16[4,64,128]{2,1,0:T(8,128)(2,1)S(1)}, u32[]{:S(2)}, u32[]{:S(2)}) collective-permute-start(bf16[4,64,128]{2,1,0:T(8,128)(2,1)S(1)} %get-tuple-element.38), channel_id=1, source_target_pairs={{0,16},{16,0},{32,48},{48,32},{64,80},{80,64},{96,112},{112,96},{1... | collective-permute-start | bytes 196616 | tf_op jit(solution)/shard_map/ppermute | solution.py:631
  20.9 8.0 %collective-permute-start.8 = (bf16[328,128]{1,0:T(8,128)(2,1)S(1)}, bf16[328,128]{1,0:T(8,128)(2,1)S(1)}, u32[]{:S(2)}, u32[]{:S(2)}) collective-permute-start(bf16[328,128]{1,0:T(8,128)(2,1)S(1)} %get-tuple-element.60), channel_id=1, source_target_pairs={{0,5},{1,4},{2,7},{3,6},{4,1},{5,0},{6,3},{7,2},{8,13},{9,12},{10,... | collective-permute-start | bytes 251912 | tf_op jit(solution)/shard_map/ppermute | solution.py:507
  26.1 4.5 %collective-permute-start.7 = (bf16[328,128]{1,0:T(8,128)(2,1)S(1)}, bf16[328,128]{1,0:T(8,128)(2,1)S(1)}, u32[]{:S(2)}, u32[]{:S(2)}) collective-permute-start(bf16[328,128]{1,0:T(8,128)(2,1)S(1)} %get-tuple-element.61), channel_id=1, source_target_pairs={{0,4},{1,5},{2,6},{3,7},{4,0},{5,1},{6,2},{7,3},{8,12},{9,13},{10,... | collective-permute-start | bytes 251912 | tf_op jit(solution)/shard_map/ppermute | solution.py:507
  26.3 4.3 %collective-permute-start.6 = (bf16[328,128]{1,0:T(8,128)(2,1)S(1)}, bf16[328,128]{1,0:T(8,128)(2,1)S(1)}, u32[]{:S(2)}, u32[]{:S(2)}) collective-permute-start(bf16[328,128]{1,0:T(8,128)(2,1)S(1)} %get-tuple-element.59), channel_id=1, source_target_pairs={{0,1},{1,0},{2,3},{3,2},{4,5},{5,4},{6,7},{7,6},{8,9},{9,8},{10,11... | collective-permute-start | bytes 251912 | tf_op jit(solution)/shard_map/ppermute | solution.py:507
  30.7 5.4 %collective-permute-start.9 = (bf16[328,128]{1,0:T(8,128)(2,1)S(1)}, bf16[328,128]{1,0:T(8,128)(2,1)S(1)}, u32[]{:S(2)}, u32[]{:S(2)}) collective-permute-start(bf16[328,128]{1,0:T(8,128)(2,1)S(1)} %add_convert_fusion.5), channel_id=1, source_target_pairs={{0,48},{16,32},{32,16},{48,0},{64,112},{80,96},{96,80},{112,64},{1... | collective-permute-start | bytes 251912 | tf_op jit(solution)/shard_map/ppermute | solution.py:507
  34.0 5.6 %collective-permute-start.10 = (bf16[4,64,128]{2,1,0:T(8,128)(2,1)S(1)}, bf16[4,64,128]{2,1,0:T(8,128)(2,1)S(1)}, u32[]{:S(2)}, u32[]{:S(2)}) collective-permute-start(bf16[4,64,128]{2,1,0:T(8,128)(2,1)S(1)} %get-tuple-element.45), channel_id=1, source_target_pairs={{16,32},{32,16},{80,96},{96,80},{17,33},{33,17},{81,97},{97,81},{1... | collective-permute-start | bytes 196616 | tf_op jit(solution)/shard_map/ppermute | solution.py:635
  39.5 2.2 %collective-permute-start.11 = (bf16[4,64,128]{2,1,0:T(8,128)(2,1)S(1)}, bf16[4,64,128]{2,1,0:T(8,128)(2,1)S(1)}, u32[]{:S(2)}, u32[]{:S(2)}) collective-permute-start(bf16[4,64,128]{2,1,0:T(8,128)(2,1)S(1)} %get-tuple-element.45), channel_id=1, source_target_pairs={{48,64},{64,48},{49,65},{65,49},{50,66},{66,50},{51,67},{67,51},{5... | collective-permute-start | bytes 196616 | tf_op jit(solution)/shard_map/ppermute | solution.py:638
  40.2 5.2 %collective-permute-start.12 = (bf16[328,128]{1,0:T(8,128)(2,1)S(1)}, bf16[328,128]{1,0:T(8,128)(2,1)S(1)}, u32[]{:S(2)}, u32[]{:S(2)}) collective-permute-start(bf16[328,128]{1,0:T(8,128)(2,1)S(1)} %add_convert_fusion.4), channel_id=1, source_target_pairs={{0,112},{16,96},{32,80},{48,64},{64,48},{80,32},{96,16},{112,0},{1... | collective-permute-start | bytes 251912 | tf_op jit(solution)/shard_map/ppermute | solution.py:507
  45.4 5.8 %collective-permute-start.13 = (bf16[520,128]{1,0:T(8,128)(2,1)S(1)}, bf16[520,128]{1,0:T(8,128)(2,1)S(1)}, u32[]{:S(2)}, u32[]{:S(2)}) collective-permute-start(bf16[520,128]{1,0:T(8,128)(2,1)S(1)} %pad_maximum_fusion.4), channel_id=1, source_target_pairs={{0,3},{1,2},{2,1},{3,0},{4,7},{5,6},{6,5},{7,4},{8,11},{9,10},{10,... | collective-permute-start | bytes 399368 | tf_op jit(solution)/shard_map/ppermute | solution.py:507
  51.3 5.4 %collective-permute-start.14 = (bf16[520,128]{1,0:T(8,128)(2,1)S(1)}, bf16[520,128]{1,0:T(8,128)(2,1)S(1)}, u32[]{:S(2)}, u32[]{:S(2)}) collective-permute-start(bf16[520,128]{1,0:T(8,128)(2,1)S(1)} %pad_maximum_fusion.2), channel_id=1, source_target_pairs={{0,12},{1,13},{2,14},{3,15},{4,8},{5,9},{6,10},{7,11},{8,4},{9,5},... | collective-permute-start | bytes 399368 | tf_op jit(solution)/shard_map/ppermute | solution.py:507
  56.8 8.6 %collective-permute-start.15 = (bf16[520,128]{1,0:T(8,128)(2,1)S(1)}, bf16[520,128]{1,0:T(8,128)(2,1)S(1)}, u32[]{:S(2)}, u32[]{:S(2)}) collective-permute-start(bf16[520,128]{1,0:T(8,128)(2,1)S(1)} %get-tuple-element.77), channel_id=1, source_target_pairs={{0,1},{1,0},{2,3},{3,2},{4,5},{5,4},{6,7},{7,6},{8,9},{9,8},{10,11... | collective-permute-start | bytes 399368 | tf_op jit(solution)/shard_map/ppermute | solution.py:507
  56.9 8.5 %collective-permute-start.16 = (bf16[520,128]{1,0:T(8,128)(2,1)S(1)}, bf16[520,128]{1,0:T(8,128)(2,1)S(1)}, u32[]{:S(2)}, u32[]{:S(2)}) collective-permute-start(bf16[520,128]{1,0:T(8,128)(2,1)S(1)} %get-tuple-element.76), channel_id=1, source_target_pairs={{0,4},{1,5},{2,6},{3,7},{4,0},{5,1},{6,2},{7,3},{8,12},{9,13},{10,... | collective-permute-start | bytes 399368 | tf_op jit(solution)/shard_map/ppermute | solution.py:507
  57.5 8.0 %collective-permute-start.17 = (bf16[328,128]{1,0:T(8,128)(2,1)S(1)}, bf16[328,128]{1,0:T(8,128)(2,1)S(1)}, u32[]{:S(2)}, u32[]{:S(2)}) collective-permute-start(bf16[328,128]{1,0:T(8,128)(2,1)S(1)} %add_convert_fusion.1), channel_id=1, source_target_pairs={{0,5},{1,4},{2,7},{3,6},{4,1},{5,0},{6,3},{7,2},{8,13},{9,12},{10,... | collective-permute-start | bytes 251912 | tf_op jit(solution)/shard_map/ppermute | solution.py:507
  65.6 2.2 %collective-permute-start.18 = (bf16[1312,128]{1,0:T(8,128)(2,1)S(1)}, bf16[1312,128]{1,0:T(8,128)(2,1)S(1)}, u32[]{:S(2)}, u32[]{:S(2)}) collective-permute-start(bf16[1312,128]{1,0:T(8,128)(2,1)S(1)} %pad_maximum_fusion.mine), channel_id=1, source_target_pairs={{0,16},{16,0},{32,48},{48,32},{64,80},{80,64},{96,112},{112,96},{1... | collective-permute-start | bytes 1007624 | tf_op jit(solution)/shard_map/ppermute | solution.py:507

commit v5 on v4

--- a/solution.py
+++ b/solution.py
@@ -570,21 +570,23 @@
 
 
 def pairs_of(axis, first):
+    count = lax.axis_size(axis)
     found = []
-    for i in range(first, lax.axis_size(axis) - 1, 2):
-        found += [(i, i + 1), (i + 1, i)]
+    for i in range(first, count, 2):
+        found += [(i, (i + 1) % count), ((i + 1) % count, i)]
     return found
 
 
-def chip_pairs(which):
-    return [pair for pair in pairs_of("gx", 1) if (pair[0] + 1) // 2 % 2 == which]
-
-
 def both_sides(first, second, axis):
-    return (
-        lax.ppermute(first, axis, pairs_of(axis, 0)),
-        lax.ppermute(second, axis, pairs_of(axis, 1)),
-    )
+    even = lax.ppermute(first, axis, pairs_of(axis, 0))
+    odd = lax.ppermute(second, axis, pairs_of(axis, 1))
+    return even, inside(odd, axis)
+
+
+def inside(value, axis):
+    index = lax.axis_index(axis)
+    edge = (index == 0) | (index == lax.axis_size(axis) - 1)
+    return jnp.where(edge, jnp.zeros_like(value), value)
 
 
 def column_ends(odd_x, odd_y, core, chip, head, tail, level_rows):
@@ -632,20 +634,21 @@
     total, core = lax.optimization_barrier((total, core))
     total = scatter_sum(total, (Z_NEAR, X_NEAR))
     total, to_chip = lax.optimization_barrier((total, to_chip))
-    first = lax.ppermute(to_chip, "gx", chip_pairs(1))
+    first = swap(to_chip, (Y_NEAR,), 1)
     total = swap_sum(total, Y_NEAR)
-    total, to_chip, first = lax.optimization_barrier((total, to_chip, first))
-    second = lax.ppermute(to_chip, "gx", chip_pairs(0))
+    total, to_chip = lax.optimization_barrier((total, to_chip))
+    second = swap(to_chip, (Y_FAR,), 1)
     total = swap_sum(total, Y_FAR)
     chip = jnp.where((((at_x + 1) >> 1) & 1) == 1, first, second)
+    chip = inside(chip, "gx")
     inner_part = inner_input(flag_x, inner, outer, core, chip, weight_upper)
     to_near, to_far = column_ends(odd_x, odd_y, core, chip, y_head, y_tail, False)
     total, direct = swap_sum_with(total, Z_FAR, to_far.reshape(-1, 128))
+    near = swap(to_near, (Z_NEAR,), 1)
+    total, near = lax.optimization_barrier((total, near))
     total, handed_far = swap_sum_with(total, X_FAR, direct)
     total, inner_part = lax.optimization_barrier((total, inner_part))
-    total, (near, handed_near, _) = gather(
-        total, (Z_NEAR, X_NEAR), (to_near.reshape(-1, 128), direct, None)
-    )
+    total, (_, handed_near, _) = gather(total, (Z_NEAR, X_NEAR), (None, direct, None))
     plane, depth = at_y >> 2, at_y & 3
     none = jnp.zeros_like(direct)
     handed = jnp.where(
@@ -654,8 +657,7 @@
     ends = (at_y == 0) | (at_y == lax.axis_size("gy") - 1)
     far = jnp.where((depth == 1) | (depth == 2), direct, jnp.where(ends, none, handed))
     input_grad = outer_input(
-        flag_x, flag_y, inner, outer, core, chip, near.reshape(to_near.shape),
-        far.reshape(to_far.shape), weight_upper, inner_part,
+        flag_x, flag_y, inner, outer, core, chip, near, far.reshape(to_far.shape), weight_upper, inner_part,
     )
     other = swap(total, (CORE,), 1)
     upper, deep = unpack(part, total, other, up_scale, deep_scale)

time: 70.5 us -> 68.2 us (0.967); the launches traced: 69.2 us -> 68 us
  starting transfers between devices: 30.9 us -> 28.3 us
  waiting for transfers between devices: 24.9 us -> 26.4 us
    ppermute x12 -> x15, waiting for transfers between devices: 18.5 us -> 23.1 us  [swap(): lax.ppermute(value, axis, [(i, i ^ masks[axis]) for i in range(count)])]
    ppermute x6 -> x4, waiting for transfers between devices: 6.43 us -> 3.31 us  [the longest x2 3.31 us: both_sides(): odd = lax.ppermute(second, axis, pairs_of(axis, 1))]
    ppermute x12 -> x15, starting transfers between devices: 20.7 us -> 19.1 us  [swap(): lax.ppermute(value, axis, [(i, i ^ masks[axis]) for i in range(count)])]
    ppermute x6 -> x4, starting transfers between devices: 9.72 us -> 9.1 us  [the longest x2 5.8 us: both_sides(): odd = lax.ppermute(second, axis, pairs_of(axis, 1))]
  transfers between devices with their start and end apart: 19 -> 20, of which waited for: 10 -> 11; matrix products, arithmetic and copies ran while one was open for 0% -> 0% of each run, Pallas kernels for 8% -> 8%
where the time goes in v5:
time: 68.2 us; the launch traced here: 68 us
  starting transfers between devices  28.3 us (41%)
  waiting for transfers between devices  26.4 us (39%)
  Pallas kernels  11.7 us (17%)
  between operations  0.93 us (1%)
    ppermute x15, waiting for transfers between devices, swap(): lax.ppermute(value, axis, [(i, i ^ masks[axis]) for i in range(count)])  23.1 us
    ppermute x15, starting transfers between devices, swap(): lax.ppermute(value, axis, [(i, i ^ masks[axis]) for i in range(count)])  19.1 us
    ppermute x2, starting transfers between devices, both_sides(): odd = lax.ppermute(second, axis, pairs_of(axis, 1))  5.8 us
    pallas_call x1, Pallas kernels, outer_grads(): pl.pallas_call(outer_kernel, in_specs=[smem] * 3 + [vmem] * 11, out_shape...  3.32 us
    ppermute x2, waiting for transfers between devices, both_sides(): odd = lax.ppermute(second, axis, pairs_of(axis, 1))  3.31 us
    ppermute x2, starting transfers between devices, both_sides(): even = lax.ppermute(first, axis, pairs_of(axis, 0))  3.3 us
    pallas_call x1, Pallas kernels, inner_grads(): pl.pallas_call(inner_kernel, in_specs=[smem] + [vmem] * 6, out_shape=[jax...  3.19 us
    pallas_call x1, Pallas kernels, outer_input(): pl.pallas_call(outer_input_kernel, in_specs=[smem, smem] + [vmem] * 8, ou...  1.69 us
  transfers between devices with their start and end apart: 20, of which 11 were waited for; matrix products, arithmetic and copies ran while one was open for 0% of the time, Pallas kernels for 8%

profile of v5, /device:TPU:1, one launch (start us, length us, event | category | flops | bytes accessed | tf_op | source)
XLA Modules:
  0.0 68.0 jit_solution(10564387762797886581)
XLA Ops:
  0.6 1.3 %faces.1 = (bf16[8,64,128]{2,1,0:T(8,128)(2,1)S(1)}, bf16[8,64,128]{2,1,0:T(8,128)(2,1)S(1)}, bf16[4,64,128]{2,1,0:T(8,128)(2,1)S(1)}, bf16[4,64,128]{2,1,0:T(8,128)(2,1)S(1)}) custom-call(s32[1]{0:T(128)} %bitcast.odd.odd_x, bf16[4,8,64,64]{3,2,1,0:T(8,128)(2,1)} %own.5, bf16[2,4,64,128]{3,2,1,0:T(8,128)(2,1)} %cot.5), custom_call_target="tpu_custom_call" | custom-call | tf_op jit(solution)/shard_map/faces/pallas_call | solution.py:90
  1.9 1.5 %collective-permute-start = (bf16[8,64,128]{2,1,0:T(8,128)(2,1)S(1)}, bf16[8,64,128]{2,1,0:T(8,128)(2,1)S(1)}, u32[]{:S(2)}, u32[]{:S(2)}) collective-permute-start(bf16[8,64,128]{2,1,0:T(8,128)(2,1)S(1)} %get-tuple-element.29), channel_id=1, source_target_pairs={{0,16},{16,0},{32,48},{48,32},{64,80},{80,64},{96,112},{112,96},{1... | collective-permute-start | bytes 393224 | tf_op jit(solution)/shard_map/ppermute | solution.py:581
  3.4 1.4 %collective-permute-start.1 = (bf16[8,64,128]{2,1,0:T(8,128)(2,1)S(1)}, bf16[8,64,128]{2,1,0:T(8,128)(2,1)S(1)}, u32[]{:S(2)}, u32[]{:S(2)}) collective-permute-start(bf16[8,64,128]{2,1,0:T(8,128)(2,1)S(1)} %get-tuple-element.30), channel_id=1, source_target_pairs={{16,32},{32,16},{48,64},{64,48},{80,96},{96,80},{112,0},{0,112},{1... | collective-permute-start | bytes 393224 | tf_op jit(solution)/shard_map/ppermute | solution.py:582
  4.8 0.0 collective-permute-done.core
  4.8 3.3 %collective-permute-done.1 = bf16[8,64,128]{2,1,0:T(8,128)(2,1)S(1)} collective-permute-done((bf16[8,64,128]{2,1,0:T(8,128)(2,1)S(1)}, bf16[8,64,128]{2,1,0:T(8,128)(2,1)S(1)}, u32[]{:S(2)}, u32[]{:S(2)}) %collective-permute-start.1) | collective-permute-done | bytes 131104 | tf_op jit(solution)/shard_map/ppermute | solution.py:582
  8.1 0.0 copy-start
  8.2 0.0 copy-start.2
  8.3 0.0 copy-start.1
  8.3 1.8 %collective-permute-start.2 = (bf16[7,64,128]{2,1,0:T(8,128)(2,1)S(1)}, bf16[7,64,128]{2,1,0:T(8,128)(2,1)S(1)}, u32[]{:S(2)}, u32[]{:S(2)}) collective-permute-start(bf16[7,64,128]{2,1,0:T(8,128)(2,1)S(1)} %get-tuple-element.69), channel_id=1, source_target_pairs={{0,1},{1,0},{2,3},{3,2},{4,5},{5,4},{6,7},{7,6},{8,9},{9,8},{10,11... | collective-permute-start | bytes 344072 | tf_op jit(solution)/shard_map/ppermute | solution.py:581
  10.1 4.4 %collective-permute-start.3 = (bf16[7,64,128]{2,1,0:T(8,128)(2,1)S(1)}, bf16[7,64,128]{2,1,0:T(8,128)(2,1)S(1)}, u32[]{:S(2)}, u32[]{:S(2)}) collective-permute-start(bf16[7,64,128]{2,1,0:T(8,128)(2,1)S(1)} %get-tuple-element.68), channel_id=1, source_target_pairs={{1,2},{2,1},{3,4},{4,3},{5,6},{6,5},{7,8},{8,7},{9,10},{10,9},{11,... | collective-permute-start | bytes 344072 | tf_op jit(solution)/shard_map/ppermute | solution.py:582
  14.6 3.2 %inner_grads.1 = (f32[9,64,256]{2,1,0:T(8,128)S(1)}, f32[27,64,128]{2,1,0:T(8,128)S(1)}, bf16[256,256]{1,0:T(8,128)(2,1)S(1)}) custom-call(s32[1]{0:T(128)} %bitcast.odd.odd_x, bf16[4,8,64,64]{3,2,1,0:T(8,128)(2,1)S(1)} %copy-done, bf16[2,4,64,128]{3,2,1,0:T(8,128)(2,1)S(1)} %copy-done.1, bf16[8,64,128]{2,1,0:T(8,128)(2,1)S(1)} %collective-permute-done.core, ...), custom_call_target="tpu_custom_call" | custom-call | flops 2000000000 | bytes 4000000 | tf_op jit(solution)/shard_map/inner_grads/pallas_call | solution.py:222
  17.8 0.0 collective-permute-done.2.near
  17.8 3.3 %outer_grads.1 = (bf16[1312,128]{1,0:T(8,128)(2,1)S(1)}, bf16[1312,128]{1,0:T(8,128)(2,1)S(1)}, bf16[256,256]{1,0:T(8,128)(2,1)S(1)}, bf16[4,64,128]{2,1,0:T(8,1...) custom-call(s32[1]{0:T(128)} %bitcast.odd.odd_x, ...), custom_call_target="tpu_custom_call" | custom-call | flops 2000000000 | bytes 4000000 | tf_op jit(solution)/shard_map/outer_grads/pallas_call | solution.py:322
  21.1 1.9 %collective-permute-start.4 = (bf16[1312,128]{1,0:T(8,128)(2,1)S(1)}, bf16[1312,128]{1,0:T(8,128)(2,1)S(1)}, u32[]{:S(2)}, u32[]{:S(2)}) collective-permute-start(bf16[1312,128]{1,0:T(8,128)(2,1)S(1)} %get-tuple-element.38), channel_id=1, source_target_pairs={{0,16},{16,0},{32,48},{48,32},{64,80},{80,64},{96,112},{112,96},{1... | collective-permute-start | bytes 1007624 | tf_op jit(solution)/shard_map/ppermute | solution.py:507
  23.0 0.1 collective-permute-start.5
  23.2 1.1 %collective-permute-done.4 = bf16[1312,128]{1,0:T(8,128)(2,1)S(1)} collective-permute-done((bf16[1312,128]{1,0:T(8,128)(2,1)S(1)}, bf16[1312,128]{1,0:T(8,128)(2,1)S(1)}, u32[]{:S(2)}, u32[]{:S(2)}) %collective-permute-start.4) | collective-permute-done | bytes 335904 | tf_op jit(solution)/shard_map/ppermute | solution.py:507
  24.3 0.1 add_convert_fusion
  24.4 0.0 collective-permute-done.5.core
  24.4 0.1 collective-permute-start.8
  24.5 0.1 collective-permute-start.7
  24.6 2.5 %collective-permute-start.6 = (bf16[328,128]{1,0:T(8,128)(2,1)S(1)}, bf16[328,128]{1,0:T(8,128)(2,1)S(1)}, u32[]{:S(2)}, u32[]{:S(2)}) collective-permute-start(bf16[328,128]{1,0:T(8,128)(2,1)S(1)} %get-tuple-element.63), channel_id=1, source_target_pairs={{0,1},{1,0},{2,3},{3,2},{4,5},{5,4},{6,7},{7,6},{8,9},{9,8},{10,11... | collective-permute-start | bytes 251912 | tf_op jit(solution)/shard_map/ppermute | solution.py:507
  27.2 2.0 %collective-permute-done.8 = bf16[328,128]{1,0:T(8,128)(2,1)S(1)} collective-permute-done((bf16[328,128]{1,0:T(8,128)(2,1)S(1)}, bf16[328,128]{1,0:T(8,128)(2,1)S(1)}, u32[]{:S(2)}, u32[]{:S(2)}) %collective-permute-start.8) | collective-permute-done | bytes 84000 | tf_op jit(solution)/shard_map/ppermute | solution.py:507
  29.1 2.4 %collective-permute-done.6 = bf16[328,128]{1,0:T(8,128)(2,1)S(1)} collective-permute-done((bf16[328,128]{1,0:T(8,128)(2,1)S(1)}, bf16[328,128]{1,0:T(8,128)(2,1)S(1)}, u32[]{:S(2)}, u32[]{:S(2)}) %collective-permute-start.6) | collective-permute-done | bytes 84000 | tf_op jit(solution)/shard_map/ppermute | solution.py:507
  31.6 1.0 %collective-permute-start.10 = (bf16[328,128]{1,0:T(8,128)(2,1)S(1)}, bf16[328,128]{1,0:T(8,128)(2,1)S(1)}, u32[]{:S(2)}, u32[]{:S(2)}) collective-permute-start(bf16[328,128]{1,0:T(8,128)(2,1)S(1)} %add_convert_fusion.5), channel_id=1, source_target_pairs={{0,48},{16,32},{32,16},{48,0},{64,112},{80,96},{96,80},{112,64},{1... | collective-permute-start | bytes 251912 | tf_op jit(solution)/shard_map/ppermute | solution.py:507
  32.6 0.9 %collective-permute-start.9 = (bf16[4,64,128]{2,1,0:T(8,128)(2,1)S(1)}, bf16[4,64,128]{2,1,0:T(8,128)(2,1)S(1)}, u32[]{:S(2)}, u32[]{:S(2)}) collective-permute-start(bf16[4,64,128]{2,1,0:T(8,128)(2,1)S(1)} %get-tuple-element.45), channel_id=1, source_target_pairs={{0,48},{16,32},{32,16},{48,0},{64,112},{80,96},{96,80},{112,64},{1... | collective-permute-start | bytes 196616 | tf_op jit(solution)/shard_map/ppermute | solution.py:507
  33.4 3.3 %collective-permute-done.10 = bf16[328,128]{1,0:T(8,128)(2,1)S(1)} collective-permute-done((bf16[328,128]{1,0:T(8,128)(2,1)S(1)}, bf16[328,128]{1,0:T(8,128)(2,1)S(1)}, u32[]{:S(2)}, u32[]{:S(2)}) %collective-permute-start.10) | collective-permute-done | bytes 84000 | tf_op jit(solution)/shard_map/ppermute | solution.py:507
  36.8 2.6 %collective-permute-start.11 = (bf16[4,64,128]{2,1,0:T(8,128)(2,1)S(1)}, bf16[4,64,128]{2,1,0:T(8,128)(2,1)S(1)}, u32[]{:S(2)}, u32[]{:S(2)}) collective-permute-start(bf16[4,64,128]{2,1,0:T(8,128)(2,1)S(1)} %get-tuple-element.45), channel_id=1, source_target_pairs={{0,112},{16,96},{32,80},{48,64},{64,48},{80,32},{96,16},{112,0},{1... | collective-permute-start | bytes 196616 | tf_op jit(solution)/shard_map/ppermute | solution.py:507
  39.3 0.5 collective-permute-start.12
  39.8 0.0 collective-permute-done.9
  39.8 2.2 %collective-permute-done.11 = bf16[4,64,128]{2,1,0:T(8,128)(2,1)S(1)} collective-permute-done((bf16[4,64,128]{2,1,0:T(8,128)(2,1)S(1)}, bf16[4,64,128]{2,1,0:T(8,128)(2,1)S(1)}, u32[]{:S(2)}, u32[]{:S(2)}) %collective-permute-start.11) | collective-permute-done | bytes 65568 | tf_op jit(solution)/shard_map/ppermute | solution.py:507
  42.1 2.9 %collective-permute-done.12 = bf16[328,128]{1,0:T(8,128)(2,1)S(1)} collective-permute-done((bf16[328,128]{1,0:T(8,128)(2,1)S(1)}, bf16[328,128]{1,0:T(8,128)(2,1)S(1)}, u32[]{:S(2)}, u32[]{:S(2)}) %collective-permute-start.12) | collective-permute-done | bytes 84000 | tf_op jit(solution)/shard_map/ppermute | solution.py:507
  45.0 1.2 %collective-permute-start.13 = (bf16[520,128]{1,0:T(8,128)(2,1)S(1)}, bf16[520,128]{1,0:T(8,128)(2,1)S(1)}, u32[]{:S(2)}, u32[]{:S(2)}) collective-permute-start(bf16[520,128]{1,0:T(8,128)(2,1)S(1)} %pad_maximum_fusion.3), channel_id=1, source_target_pairs={{0,3},{1,2},{2,1},{3,0},{4,7},{5,6},{6,5},{7,4},{8,11},{9,10},{10,... | collective-permute-start | bytes 399368 | tf_op jit(solution)/shard_map/ppermute | solution.py:507
  46.1 0.0 collective-permute-start.14
  46.1 4.9 %collective-permute-done.13 = bf16[520,128]{1,0:T(8,128)(2,1)S(1)} collective-permute-done((bf16[520,128]{1,0:T(8,128)(2,1)S(1)}, bf16[520,128]{1,0:T(8,128)(2,1)S(1)}, u32[]{:S(2)}, u32[]{:S(2)}) %collective-permute-start.13) | collective-permute-done | bytes 133152 | tf_op jit(solution)/shard_map/ppermute | solution.py:507
  51.1 2.5 %collective-permute-start.15 = (bf16[520,128]{1,0:T(8,128)(2,1)S(1)}, bf16[520,128]{1,0:T(8,128)(2,1)S(1)}, u32[]{:S(2)}, u32[]{:S(2)}) collective-permute-start(bf16[520,128]{1,0:T(8,128)(2,1)S(1)} %pad_maximum_fusion.2), channel_id=1, source_target_pairs={{0,12},{1,13},{2,14},{3,15},{4,8},{5,9},{6,10},{7,11},{8,4},{9,5},... | collective-permute-start | bytes 399368 | tf_op jit(solution)/shard_map/ppermute | solution.py:507
  53.5 0.8 %inner_input.1.inner_part = bf16[256,256]{1,0:T(8,128)(2,1)S(1)} custom-call(s32[1]{0:T(128)} %bitcast.odd.odd_x, bf16[256,256]{1,0:T(8,128)(2,1)S(1)} %get-tuple-element.31.inner, bf16[256,256]{1,0:T(8,128)(2,1)S(1)} %get-tuple-element.36.outer, bf16[4,64,128]{2,1,0:T(8,128)(2,1)S(1)} %collective-permute-done.5.core, ...), custom_call_target="tpu_custom_call" | custom-call | flops 500000000 | bytes 2000000 | tf_op jit(solution)/shard_map/inner_input/pallas_call | solution.py:399
  54.3 1.9 %collective-permute-done.15 = bf16[520,128]{1,0:T(8,128)(2,1)S(1)} collective-permute-done((bf16[520,128]{1,0:T(8,128)(2,1)S(1)}, bf16[520,128]{1,0:T(8,128)(2,1)S(1)}, u32[]{:S(2)}, u32[]{:S(2)}) %collective-permute-start.15) | collective-permute-done | bytes 133152 | tf_op jit(solution)/shard_map/ppermute | solution.py:507
  56.3 0.1 collective-permute-start.16
  56.4 0.1 collective-permute-start.17
  56.5 2.5 %collective-permute-start.18 = (bf16[328,128]{1,0:T(8,128)(2,1)S(1)}, bf16[328,128]{1,0:T(8,128)(2,1)S(1)}, u32[]{:S(2)}, u32[]{:S(2)}) collective-permute-start(bf16[328,128]{1,0:T(8,128)(2,1)S(1)} %add_convert_fusion.1), channel_id=1, source_target_pairs={{0,5},{1,4},{2,7},{3,6},{4,1},{5,0},{6,3},{7,2},{8,13},{9,12},{10,... | collective-permute-start | bytes 251912 | tf_op jit(solution)/shard_map/ppermute | solution.py:507
  59.0 0.8 %collective-permute-done.17 = bf16[328,128]{1,0:T(8,128)(2,1)S(1)} collective-permute-done((bf16[328,128]{1,0:T(8,128)(2,1)S(1)}, bf16[328,128]{1,0:T(8,128)(2,1)S(1)}, u32[]{:S(2)}, u32[]{:S(2)}) %collective-permute-start.17) | collective-permute-done | bytes 84000 | tf_op jit(solution)/shard_map/ppermute | solution.py:507
  59.8 1.7 %collective-permute-done.18 = bf16[328,128]{1,0:T(8,128)(2,1)S(1)} collective-permute-done((bf16[328,128]{1,0:T(8,128)(2,1)S(1)}, bf16[328,128]{1,0:T(8,128)(2,1)S(1)}, u32[]{:S(2)}, u32[]{:S(2)}) %collective-permute-start.18) | collective-permute-done | bytes 84000 | tf_op jit(solution)/shard_map/ppermute | solution.py:507
  61.5 0.0 collective-permute-done.16
  61.5 0.1 broadcast_select_fusion.13
  61.6 3.3 %collective-permute-start.19 = (bf16[1312,128]{1,0:T(8,128)(2,1)S(1)}, bf16[1312,128]{1,0:T(8,128)(2,1)S(1)}, u32[]{:S(2)}, u32[]{:S(2)}) collective-permute-start(bf16[1312,128]{1,0:T(8,128)(2,1)S(1)} %pad_maximum_fusion.mine), channel_id=1, source_target_pairs={{0,16},{16,0},{32,48},{48,32},{64,80},{80,64},{96,112},{112,96},{1... | collective-permute-start | bytes 1007624 | tf_op jit(solution)/shard_map/ppermute | solution.py:507
  64.9 1.7 %outer_input.1 = bf16[4,8,64,64]{3,2,1,0:T(8,128)(2,1)} custom-call(s32[1]{0:T(128)} %bitcast.odd.odd_x, s32[1]{0:T(128)} %bitcast.1.odd_y, bf16[256,256]{1,0:T(8,128)(2,1)S(1)} %get-tuple-element.31.inner, bf16[256,256]{1,0:T(8,128)(2,1)S(1)} %get-tuple-element.36.outer, bf16[4,64,128]{2,1,0:T(8,128)(2,1)S(1)} %collective-permute-done.5.core, ...), custom_call_target="tpu_custom_call" | custom-call | flops 500000000 | bytes 4000000 | tf_op jit(solution)/shard_map/outer_input/pallas_call | solution.py:445
  66.6 0.0 collective-permute-done.19.other
  66.6 1.5 %unpack.1 = (f32[3,3,3,64,64]{4,3,2,1,0:T(8,128)}, f32[3,3,3,64,128]{4,3,2,1,0:T(8,128)}) custom-call(s32[1]{0:T(128)} %bitcast.2.part.odd, bf16[1312,128]{1,0:T(8,128)(2,1)S(1)} %pad_maximum_fusion.mine, bf16[1312,128]{1,0:T(8,128)(2,1)S(1)} %collective-permute-done.19.other), custom_call_target="tpu_custom_call" | custom-call | tf_op jit(solution)/shard_map/unpack/pallas_call | solution.py:480
  (35 shorter events, 0.5 us)
Async XLA Ops:
  1.9 2.9 %collective-permute-start = (bf16[8,64,128]{2,1,0:T(8,128)(2,1)S(1)}, bf16[8,64,128]{2,1,0:T(8,128)(2,1)S(1)}, u32[]{:S(2)}, u32[]{:S(2)}) collective-permute-start(bf16[8,64,128]{2,1,0:T(8,128)(2,1)S(1)} %get-tuple-element.29), channel_id=1, source_target_pairs={{0,16},{16,0},{32,48},{48,32},{64,80},{80,64},{96,112},{112,96},{1... | collective-permute-start | bytes 393224 | tf_op jit(solution)/shard_map/ppermute | solution.py:581
  3.4 4.7 %collective-permute-start.1 = (bf16[8,64,128]{2,1,0:T(8,128)(2,1)S(1)}, bf16[8,64,128]{2,1,0:T(8,128)(2,1)S(1)}, u32[]{:S(2)}, u32[]{:S(2)}) collective-permute-start(bf16[8,64,128]{2,1,0:T(8,128)(2,1)S(1)} %get-tuple-element.30), channel_id=1, source_target_pairs={{16,32},{32,16},{48,64},{64,48},{80,96},{96,80},{112,0},{0,112},{1... | collective-permute-start | bytes 393224 | tf_op jit(solution)/shard_map/ppermute | solution.py:582
  8.1 6.4 %copy-start.3 = (bf16[3,3,3,64,64]{4,3,2,1,0:T(8,128)(2,1)S(1)}, bf16[3,3,3,64,64]{4,3,2,1,0:T(8,128)(2,1)}, u32[]{:S(2)}) copy-start(bf16[3,3,3,64,64]{4,3,2,1,0:T(8,128)(2,1)} %w_up.7) | copy-start | bytes 663556
  8.1 6.4 %copy-start = (bf16[4,8,64,64]{3,2,1,0:T(8,128)(2,1)S(1)}, bf16[4,8,64,64]{3,2,1,0:T(8,128)(2,1)}, u32[]{:S(2)}) copy-start(bf16[4,8,64,64]{3,2,1,0:T(8,128)(2,1)} %own.5) | copy-start | bytes 786436
  8.2 6.4 %copy-start.2 = (bf16[3,3,3,64,128]{4,3,2,1,0:T(8,128)(2,1)S(1)}, bf16[3,3,3,64,128]{4,3,2,1,0:T(8,128)(2,1)}, u32[]{:S(2)}) copy-start(bf16[3,3,3,64,128]{4,3,2,1,0:T(8,128)(2,1)} %w_deep.3) | copy-start | bytes 1327108
  8.3 6.3 %copy-start.1 = (bf16[2,4,64,128]{3,2,1,0:T(8,128)(2,1)S(1)}, bf16[2,4,64,128]{3,2,1,0:T(8,128)(2,1)}, u32[]{:S(2)}) copy-start(bf16[2,4,64,128]{3,2,1,0:T(8,128)(2,1)} %cot.5) | copy-start | bytes 393220
  8.3 9.5 %collective-permute-start.2 = (bf16[7,64,128]{2,1,0:T(8,128)(2,1)S(1)}, bf16[7,64,128]{2,1,0:T(8,128)(2,1)S(1)}, u32[]{:S(2)}, u32[]{:S(2)}) collective-permute-start(bf16[7,64,128]{2,1,0:T(8,128)(2,1)S(1)} %get-tuple-element.69), channel_id=1, source_target_pairs={{0,1},{1,0},{2,3},{3,2},{4,5},{5,4},{6,7},{7,6},{8,9},{9,8},{10,11... | collective-permute-start | bytes 344072 | tf_op jit(solution)/shard_map/ppermute | solution.py:581
  10.1 7.7 %collective-permute-start.3 = (bf16[7,64,128]{2,1,0:T(8,128)(2,1)S(1)}, bf16[7,64,128]{2,1,0:T(8,128)(2,1)S(1)}, u32[]{:S(2)}, u32[]{:S(2)}) collective-permute-start(bf16[7,64,128]{2,1,0:T(8,128)(2,1)S(1)} %get-tuple-element.68), channel_id=1, source_target_pairs={{1,2},{2,1},{3,4},{4,3},{5,6},{6,5},{7,8},{8,7},{9,10},{10,9},{11,... | collective-permute-start | bytes 344072 | tf_op jit(solution)/shard_map/ppermute | solution.py:582
  21.1 3.2 %collective-permute-start.4 = (bf16[1312,128]{1,0:T(8,128)(2,1)S(1)}, bf16[1312,128]{1,0:T(8,128)(2,1)S(1)}, u32[]{:S(2)}, u32[]{:S(2)}) collective-permute-start(bf16[1312,128]{1,0:T(8,128)(2,1)S(1)} %get-tuple-element.38), channel_id=1, source_target_pairs={{0,16},{16,0},{32,48},{48,32},{64,80},{80,64},{96,112},{112,96},{1... | collective-permute-start | bytes 1007624 | tf_op jit(solution)/shard_map/ppermute | solution.py:507
  23.0 1.4 %collective-permute-start.5 = (bf16[4,64,128]{2,1,0:T(8,128)(2,1)S(1)}, bf16[4,64,128]{2,1,0:T(8,128)(2,1)S(1)}, u32[]{:S(2)}, u32[]{:S(2)}) collective-permute-start(bf16[4,64,128]{2,1,0:T(8,128)(2,1)S(1)} %get-tuple-element.39), channel_id=1, source_target_pairs={{0,16},{16,0},{32,48},{48,32},{64,80},{80,64},{96,112},{112,96},{1... | collective-permute-start | bytes 196616 | tf_op jit(solution)/shard_map/ppermute | solution.py:633
  24.4 4.7 %collective-permute-start.8 = (bf16[328,128]{1,0:T(8,128)(2,1)S(1)}, bf16[328,128]{1,0:T(8,128)(2,1)S(1)}, u32[]{:S(2)}, u32[]{:S(2)}) collective-permute-start(bf16[328,128]{1,0:T(8,128)(2,1)S(1)} %get-tuple-element.64), channel_id=1, source_target_pairs={{0,5},{1,4},{2,7},{3,6},{4,1},{5,0},{6,3},{7,2},{8,13},{9,12},{10,... | collective-permute-start | bytes 251912 | tf_op jit(solution)/shard_map/ppermute | solution.py:507
  24.5 4.6 %collective-permute-start.7 = (bf16[328,128]{1,0:T(8,128)(2,1)S(1)}, bf16[328,128]{1,0:T(8,128)(2,1)S(1)}, u32[]{:S(2)}, u32[]{:S(2)}) collective-permute-start(bf16[328,128]{1,0:T(8,128)(2,1)S(1)} %get-tuple-element.65), channel_id=1, source_target_pairs={{0,4},{1,5},{2,6},{3,7},{4,0},{5,1},{6,2},{7,3},{8,12},{9,13},{10,... | collective-permute-start | bytes 251912 | tf_op jit(solution)/shard_map/ppermute | solution.py:507
  24.6 6.9 %collective-permute-start.6 = (bf16[328,128]{1,0:T(8,128)(2,1)S(1)}, bf16[328,128]{1,0:T(8,128)(2,1)S(1)}, u32[]{:S(2)}, u32[]{:S(2)}) collective-permute-start(bf16[328,128]{1,0:T(8,128)(2,1)S(1)} %get-tuple-element.63), channel_id=1, source_target_pairs={{0,1},{1,0},{2,3},{3,2},{4,5},{5,4},{6,7},{7,6},{8,9},{9,8},{10,11... | collective-permute-start | bytes 251912 | tf_op jit(solution)/shard_map/ppermute | solution.py:507
  31.6 5.2 %collective-permute-start.10 = (bf16[328,128]{1,0:T(8,128)(2,1)S(1)}, bf16[328,128]{1,0:T(8,128)(2,1)S(1)}, u32[]{:S(2)}, u32[]{:S(2)}) collective-permute-start(bf16[328,128]{1,0:T(8,128)(2,1)S(1)} %add_convert_fusion.5), channel_id=1, source_target_pairs={{0,48},{16,32},{32,16},{48,0},{64,112},{80,96},{96,80},{112,64},{1... | collective-permute-start | bytes 251912 | tf_op jit(solution)/shard_map/ppermute | solution.py:507
  32.6 7.3 %collective-permute-start.9 = (bf16[4,64,128]{2,1,0:T(8,128)(2,1)S(1)}, bf16[4,64,128]{2,1,0:T(8,128)(2,1)S(1)}, u32[]{:S(2)}, u32[]{:S(2)}) collective-permute-start(bf16[4,64,128]{2,1,0:T(8,128)(2,1)S(1)} %get-tuple-element.45), channel_id=1, source_target_pairs={{0,48},{16,32},{32,16},{48,0},{64,112},{80,96},{96,80},{112,64},{1... | collective-permute-start | bytes 196616 | tf_op jit(solution)/shard_map/ppermute | solution.py:507
  36.8 5.2 %collective-permute-start.11 = (bf16[4,64,128]{2,1,0:T(8,128)(2,1)S(1)}, bf16[4,64,128]{2,1,0:T(8,128)(2,1)S(1)}, u32[]{:S(2)}, u32[]{:S(2)}) collective-permute-start(bf16[4,64,128]{2,1,0:T(8,128)(2,1)S(1)} %get-tuple-element.45), channel_id=1, source_target_pairs={{0,112},{16,96},{32,80},{48,64},{64,48},{80,32},{96,16},{112,0},{1... | collective-permute-start | bytes 196616 | tf_op jit(solution)/shard_map/ppermute | solution.py:507
  39.3 5.6 %collective-permute-start.12 = (bf16[328,128]{1,0:T(8,128)(2,1)S(1)}, bf16[328,128]{1,0:T(8,128)(2,1)S(1)}, u32[]{:S(2)}, u32[]{:S(2)}) collective-permute-start(bf16[328,128]{1,0:T(8,128)(2,1)S(1)} %add_convert_fusion.4), channel_id=1, source_target_pairs={{0,112},{16,96},{32,80},{48,64},{64,48},{80,32},{96,16},{112,0},{1... | collective-permute-start | bytes 251912 | tf_op jit(solution)/shard_map/ppermute | solution.py:507
  45.0 6.0 %collective-permute-start.13 = (bf16[520,128]{1,0:T(8,128)(2,1)S(1)}, bf16[520,128]{1,0:T(8,128)(2,1)S(1)}, u32[]{:S(2)}, u32[]{:S(2)}) collective-permute-start(bf16[520,128]{1,0:T(8,128)(2,1)S(1)} %pad_maximum_fusion.3), channel_id=1, source_target_pairs={{0,3},{1,2},{2,1},{3,0},{4,7},{5,6},{6,5},{7,4},{8,11},{9,10},{10,... | collective-permute-start | bytes 399368 | tf_op jit(solution)/shard_map/ppermute | solution.py:507
  46.1 4.9 %collective-permute-start.14 = (bf16[3,64,128]{2,1,0:T(8,128)(2,1)S(1)}, bf16[3,64,128]{2,1,0:T(8,128)(2,1)S(1)}, u32[]{:S(2)}, u32[]{:S(2)}) collective-permute-start(bf16[3,64,128]{2,1,0:T(8,128)(2,1)S(1)} %get-tuple-element.76), channel_id=1, source_target_pairs={{0,1},{1,0},{2,3},{3,2},{4,5},{5,4},{6,7},{7,6},{8,9},{9,8},{10,11... | collective-permute-start | bytes 147464 | tf_op jit(solution)/shard_map/ppermute | solution.py:507
  51.1 5.1 %collective-permute-start.15 = (bf16[520,128]{1,0:T(8,128)(2,1)S(1)}, bf16[520,128]{1,0:T(8,128)(2,1)S(1)}, u32[]{:S(2)}, u32[]{:S(2)}) collective-permute-start(bf16[520,128]{1,0:T(8,128)(2,1)S(1)} %pad_maximum_fusion.2), channel_id=1, source_target_pairs={{0,12},{1,13},{2,14},{3,15},{4,8},{5,9},{6,10},{7,11},{8,4},{9,5},... | collective-permute-start | bytes 399368 | tf_op jit(solution)/shard_map/ppermute | solution.py:507
  56.3 5.2 %collective-permute-start.16 = (bf16[520,128]{1,0:T(8,128)(2,1)S(1)}, bf16[520,128]{1,0:T(8,128)(2,1)S(1)}, u32[]{:S(2)}, u32[]{:S(2)}) collective-permute-start(bf16[520,128]{1,0:T(8,128)(2,1)S(1)} %pad_maximum_fusion.1), channel_id=1, source_target_pairs={{0,4},{1,5},{2,6},{3,7},{4,0},{5,1},{6,2},{7,3},{8,12},{9,13},{10,... | collective-permute-start | bytes 399368 | tf_op jit(solution)/shard_map/ppermute | solution.py:507
  56.4 3.4 %collective-permute-start.17 = (bf16[328,128]{1,0:T(8,128)(2,1)S(1)}, bf16[328,128]{1,0:T(8,128)(2,1)S(1)}, u32[]{:S(2)}, u32[]{:S(2)}) collective-permute-start(bf16[328,128]{1,0:T(8,128)(2,1)S(1)} %add_convert_fusion.1), channel_id=1, source_target_pairs={{0,1},{1,0},{2,3},{3,2},{4,5},{5,4},{6,7},{7,6},{8,9},{9,8},{10,11... | collective-permute-start | bytes 251912 | tf_op jit(solution)/shard_map/ppermute | solution.py:507
  56.5 5.0 %collective-permute-start.18 = (bf16[328,128]{1,0:T(8,128)(2,1)S(1)}, bf16[328,128]{1,0:T(8,128)(2,1)S(1)}, u32[]{:S(2)}, u32[]{:S(2)}) collective-permute-start(bf16[328,128]{1,0:T(8,128)(2,1)S(1)} %add_convert_fusion.1), channel_id=1, source_target_pairs={{0,5},{1,4},{2,7},{3,6},{4,1},{5,0},{6,3},{7,2},{8,13},{9,12},{10,... | collective-permute-start | bytes 251912 | tf_op jit(solution)/shard_map/ppermute | solution.py:507
  61.6 5.0 %collective-permute-start.19 = (bf16[1312,128]{1,0:T(8,128)(2,1)S(1)}, bf16[1312,128]{1,0:T(8,128)(2,1)S(1)}, u32[]{:S(2)}, u32[]{:S(2)}) collective-permute-start(bf16[1312,128]{1,0:T(8,128)(2,1)S(1)} %pad_maximum_fusion.mine), channel_id=1, source_target_pairs={{0,16},{16,0},{32,48},{48,32},{64,80},{80,64},{96,112},{112,96},{1... | collective-permute-start | bytes 1007624 | tf_op jit(solution)/shard_map/ppermute | solution.py:507

commit v6 on v5

--- a/solution.py
+++ b/solution.py
@@ -173,13 +173,18 @@
                 deep((a * 3 + b) * 3 + 2 - j, out[:, j * 128 : j * 128 + 128])
     for x in range(4):
         for y in range(4):
-            part = jnp.dot(grad_t, window(taps, x, y, ys), preferred_element_type=F32)
-            for s in range(2):
-                for t in range(2):
-                    a, b = x - s, y - t
-                    if 0 <= a < 3 and 0 <= b < 3:
-                        top = (s * 2 + t) * 64
-                        sums(a * 3 + b, part[top : top + 64], s == 0 and t == 0)
+            kept = [
+                (s, t)
+                for s in range(2)
+                for t in range(2)
+                if 0 <= x - s < 3 and 0 <= y - t < 3
+            ]
+            left = jnp.concatenate(
+                [grad_t[(s * 2 + t) * 64 : (s * 2 + t) * 64 + 64] for s, t in kept], axis=0
+            )
+            part = jnp.dot(left, window(taps, x, y, ys), preferred_element_type=F32)
+            for k, (s, t) in enumerate(kept):
+                sums((x - s) * 3 + y - t, part[k * 64 : k * 64 + 64], s == 0 and t == 0)
     return grad.astype(BF16)
 
 
@@ -346,7 +351,7 @@
     )(odd_x, odd_y, part, own, cot, core, chip, near, far, w_up, w_deep, sums, deep, inner)
 
 
-def input_columns(ys, taps, w_up):
+def input_columns(ys, at_ys, taps, w_up):
     empty = jnp.zeros((64, 256), BF16)
     spare = jnp.zeros((64, 64), BF16)
     weights = {}
@@ -357,7 +362,7 @@
             )
     total = jnp.zeros((2 * len(ys) * 64, 256), F32)
     for x in range(4):
-        for y in range(4):
+        for y in at_ys:
             block = jnp.concatenate(
                 [weights.get((s + 2 - x, t + 2 - y), empty) for s in range(2) for t in range(2)],
                 axis=0,
@@ -366,7 +371,7 @@
                 window(taps, x, y, ys), block, (((1,), (1,)), ((), ())),
                 preferred_element_type=F32,
             )
-    return total.astype(BF16)
+    return total
 
 
 def picked(inner, outer, x, y):
@@ -388,9 +393,11 @@
         return picked(inner, outer, u, v)
 
     for x in range(6):
-        for y in range(2, 8):
+        taps[x, 0] = jnp.zeros((64, 256), BF16)
+        taps[x, 9] = jnp.zeros((64, 256), BF16)
+        for y in range(1, 9):
             taps[x, y] = depth_taps(level_column(x, y, own, x_lo, x_hi, None, None), 64)
-    out[...] = input_columns(INNER, taps, w_up)
+    out[...] = input_columns(range(4), range(4), taps, w_up)
 
 
 def inner_input(odd_x, inner, outer, core, chip, w_up):
@@ -399,7 +406,7 @@
     return pl.pallas_call(
         inner_input_kernel,
         in_specs=[smem] + [vmem] * 5,
-        out_shape=jax.ShapeDtypeStruct((256, 256), BF16),
+        out_shape=jax.ShapeDtypeStruct((512, 256), F32),
         scratch_shapes=[pltpu.VMEM((6, 10, 64, 256), BF16)],
         compiler_params=pltpu.CompilerParams(vmem_limit_bytes=VMEM_BYTES),
         cost_estimate=pl.CostEstimate(
@@ -409,17 +416,8 @@
     )(odd_x, inner, outer, core, chip, w_up)
 
 
-def outer_input_kernel(
-    odd_x, odd_y, inner, outer, core, chip, near, far, w_up, inner_part, out, taps
-):
-    swap_x = odd_x[0] == 1
+def outer_input_kernel(odd_y, near, far, w_up, part, out, taps):
     swap_y = odd_y[0] == 1
-
-    def x_lo(k):
-        return jnp.where(swap_x, core[k], chip[k])
-
-    def x_hi(k):
-        return jnp.where(swap_x, chip[k], core[k])
 
     def y_lo(k):
         return jnp.where(swap_y, near[k], far[k])
@@ -427,64 +425,88 @@
     def y_hi(k):
         return jnp.where(swap_y, far[k], near[k])
 
-    def own(u, v):
-        return picked(inner, outer, u, v)
-
     for x in range(6):
-        for y in (0, 1, 2, 3, 6, 7, 8, 9):
-            taps[x, y] = depth_taps(level_column(x, y, own, x_lo, x_hi, y_lo, y_hi), 64)
-    outer_part = input_columns(OUTER, taps, w_up)
-    for x in range(4):
-        for y in range(8):
-            out[x, y] = picked(inner_part, outer_part, x, y)
-
-
-def outer_input(odd_x, odd_y, inner, outer, core, chip, near, far, w_up, inner_part):
-    smem = pl.BlockSpec(memory_space=pltpu.SMEM)
+        for y in (0, 9):
+            taps[x, y] = depth_taps(level_column(x, y, None, None, None, y_lo, y_hi), 64)
+    ends = {
+        0: input_columns((0,), (0,), taps, w_up),
+        3: input_columns((3,), (3,), taps, w_up),
+    }
+    for x in range(2):
+        for y in range(4):
+            top = (x * 4 + y) * 64
+            rows = part[top : top + 64]
+            if y in OUTER:
+                rows = rows + ends[y][x * 64 : x * 64 + 64]
+            rows = rows.astype(BF16)
+            for s in range(2):
+                for t in range(2):
+                    at = s * 128 + t * 64
+                    out[2 * x + s, 2 * y + t] = rows[:, at : at + 64]
+
+
+def outer_input(odd_y, near, far, w_up, part):
     vmem = pl.BlockSpec(memory_space=pltpu.VMEM)
     return pl.pallas_call(
         outer_input_kernel,
-        in_specs=[smem, smem] + [vmem] * 8,
+        in_specs=[pl.BlockSpec(memory_space=pltpu.SMEM)] + [vmem] * 4,
         out_shape=jax.ShapeDtypeStruct((4, 8, 64, 64), BF16),
         scratch_shapes=[pltpu.VMEM((6, 10, 64, 256), BF16)],
         compiler_params=pltpu.CompilerParams(vmem_limit_bytes=VMEM_BYTES),
         cost_estimate=pl.CostEstimate(
-            flops=500_000_000, bytes_accessed=4_000_000, transcendentals=0
+            flops=300_000_000, bytes_accessed=4_000_000, transcendentals=0
         ),
         name="outer_input",
-    )(odd_x, odd_y, inner, outer, core, chip, near, far, w_up, inner_part)
-
-
-def unpack_kernel(up_scale, deep_scale, odd, mine, other, up, deep, payload):
+    )(odd_y, near, far, w_up, part)
+
+
+def unpack_kernel(
+    up_scale, deep_scale, odd, mine, other, up_out, deep_out, payload, up, deep, sems
+):
     first = pl.multiple_of(odd[0] * HALF_ROWS, HALF_ROWS)
     payload[pl.ds(first, HALF_ROWS), :] = mine[...]
     payload[pl.ds(HALF_ROWS - first, HALF_ROWS), :] = other[...]
-    for k in range(9):
-        a, b = k // 3, k % 3
-        pair = payload[k * 64 : k * 64 + 64, :].astype(F32).T * up_scale
-        up[a, b, 0] = pair[:64]
-        up[a, b, 1] = pair[64:]
-    for k in range(5):
-        top = PAIR_ROW + k * 64
-        pair = payload[top : top + 64, :].astype(F32).T * up_scale
-        up[2 * k // 3, 2 * k % 3, 2] = pair[:64]
-        if k < 4:
-            up[(2 * k + 1) // 3, (2 * k + 1) % 3, 2] = pair[64:]
-    for k in range(27):
-        top = DEEP_ROW + k * 64
-        deep[k // 9, k // 3 % 3, k % 3] = payload[top : top + 64, :].astype(F32) * deep_scale
+    copies = []
+    pairs = {}
+    for a in range(3):
+        for k in range(a * 9, a * 9 + 9):
+            top = DEEP_ROW + k * 64
+            deep[a, k // 3 % 3, k % 3] = payload[top : top + 64, :].astype(F32) * deep_scale
+        copies.append(pltpu.make_async_copy(deep.at[a], deep_out.at[a], sems.at[a]))
+        copies[-1].start()
+    for a in range(3):
+        for b in range(3):
+            k = a * 3 + b
+            pair = payload[k * 64 : k * 64 + 64, :].astype(F32).T * up_scale
+            up[a, b, 0] = pair[:64]
+            up[a, b, 1] = pair[64:]
+            if k % 2 == 0:
+                top = PAIR_ROW + k // 2 * 64
+                pairs[k // 2] = payload[top : top + 64, :].astype(F32).T * up_scale
+            up[a, b, 2] = pairs[k // 2][k % 2 * 64 : k % 2 * 64 + 64]
+        copies.append(pltpu.make_async_copy(up.at[a], up_out.at[a], sems.at[3 + a]))
+        copies[-1].start()
+    for copy in copies:
+        copy.wait()
 
 
 def unpack(odd, mine, other, up_scale, deep_scale):
     vmem = pl.BlockSpec(memory_space=pltpu.VMEM)
+    hbm = pl.BlockSpec(memory_space=pltpu.HBM)
     return pl.pallas_call(
         functools.partial(unpack_kernel, up_scale, deep_scale),
         in_specs=[pl.BlockSpec(memory_space=pltpu.SMEM), vmem, vmem],
+        out_specs=[hbm, hbm],
         out_shape=[
             jax.ShapeDtypeStruct((3, 3, 3, 64, 64), F32),
             jax.ShapeDtypeStruct((3, 3, 3, 64, 128), F32),
         ],
-        scratch_shapes=[pltpu.VMEM((PAY_ROWS, 128), BF16)],
+        scratch_shapes=[
+            pltpu.VMEM((PAY_ROWS, 128), BF16),
+            pltpu.VMEM((3, 3, 3, 64, 64), F32),
+            pltpu.VMEM((3, 3, 3, 64, 128), F32),
+            pltpu.SemaphoreType.DMA((6,)),
+        ],
         compiler_params=pltpu.CompilerParams(vmem_limit_bytes=VMEM_BYTES),
         name="unpack",
     )(odd, mine, other)
@@ -657,7 +679,7 @@
     ends = (at_y == 0) | (at_y == lax.axis_size("gy") - 1)
     far = jnp.where((depth == 1) | (depth == 2), direct, jnp.where(ends, none, handed))
     input_grad = outer_input(
-        flag_x, flag_y, inner, outer, core, chip, near, far.reshape(to_far.shape), weight_upper, inner_part,
+        flag_y, near, far.reshape(to_far.shape), weight_upper, inner_part
     )
     other = swap(total, (CORE,), 1)
     upper, deep = unpack(part, total, other, up_scale, deep_scale)

time: 68.2 us -> 67.2 us (0.985)
  Pallas kernels: 11.7 us -> 10.7 us
  starting transfers between devices: 28.3 us -> 29 us
    ppermute x15, starting transfers between devices: 19.1 us -> 19.8 us  [swap(): lax.ppermute(value, axis, [(i, i ^ masks[axis]) for i in range(count)])]
where the time goes in v6:
time: 67.2 us; the launch traced here: 67.1 us
  starting transfers between devices  29 us (43%)
  waiting for transfers between devices  25.8 us (38%)
  Pallas kernels  10.7 us (16%)
  between operations  0.93 us (1%)
    ppermute x15, waiting for transfers between devices, swap(): lax.ppermute(value, axis, [(i, i ^ masks[axis]) for i in range(count)])  22.5 us
    ppermute x15, starting transfers between devices, swap(): lax.ppermute(value, axis, [(i, i ^ masks[axis]) for i in range(count)])  19.8 us
    ppermute x2, starting transfers between devices, both_sides(): odd = lax.ppermute(second, axis, pairs_of(axis, 1))  5.8 us
    ppermute x2, waiting for transfers between devices, both_sides(): odd = lax.ppermute(second, axis, pairs_of(axis, 1))  3.31 us
    ppermute x2, starting transfers between devices, both_sides(): even = lax.ppermute(first, axis, pairs_of(axis, 0))  3.3 us
    pallas_call x1, Pallas kernels, outer_grads(): pl.pallas_call(outer_kernel, in_specs=[smem] * 3 + [vmem] * 11, out_shape...  2.8 us
    pallas_call x1, Pallas kernels, inner_grads(): pl.pallas_call(inner_kernel, in_specs=[smem] + [vmem] * 6, out_shape=[jax...  2.56 us
    pallas_call x1, Pallas kernels, unpack(): pl.pallas_call(functools.partial(unpack_kernel, up_scale, deep_scale), in...  1.37 us
  transfers between devices with their start and end apart: 20, of which 11 were waited for; matrix products, arithmetic and copies ran while one was open for 0% of the time, Pallas kernels for 8%

profile of v6, /device:TPU:1, one launch (start us, length us, event | category | flops | bytes accessed | tf_op | source)
XLA Modules:
  0.0 67.1 jit_solution(8465495010780126430)
XLA Ops:
  0.6 1.3 %faces.1 = (bf16[8,64,128]{2,1,0:T(8,128)(2,1)S(1)}, bf16[8,64,128]{2,1,0:T(8,128)(2,1)S(1)}, bf16[4,64,128]{2,1,0:T(8,128)(2,1)S(1)}, bf16[4,64,128]{2,1,0:T(8,128)(2,1)S(1)}) custom-call(s32[1]{0:T(128)} %bitcast.1.odd.odd_x, bf16[4,8,64,64]{3,2,1,0:T(8,128)(2,1)} %own.5, bf16[2,4,64,128]{3,2,1,0:T(8,128)(2,1)} %cot.5), custom_call_target="tpu_custom_call" | custom-call | tf_op jit(solution)/shard_map/faces/pallas_call | solution.py:90
  1.9 1.5 %collective-permute-start = (bf16[8,64,128]{2,1,0:T(8,128)(2,1)S(1)}, bf16[8,64,128]{2,1,0:T(8,128)(2,1)S(1)}, u32[]{:S(2)}, u32[]{:S(2)}) collective-permute-start(bf16[8,64,128]{2,1,0:T(8,128)(2,1)S(1)} %get-tuple-element.29), channel_id=1, source_target_pairs={{0,16},{16,0},{32,48},{48,32},{64,80},{80,64},{96,112},{112,96},{1... | collective-permute-start | bytes 393224 | tf_op jit(solution)/shard_map/ppermute | solution.py:603
  3.4 1.4 %collective-permute-start.1 = (bf16[8,64,128]{2,1,0:T(8,128)(2,1)S(1)}, bf16[8,64,128]{2,1,0:T(8,128)(2,1)S(1)}, u32[]{:S(2)}, u32[]{:S(2)}) collective-permute-start(bf16[8,64,128]{2,1,0:T(8,128)(2,1)S(1)} %get-tuple-element.30), channel_id=1, source_target_pairs={{16,32},{32,16},{48,64},{64,48},{80,96},{96,80},{112,0},{0,112},{1... | collective-permute-start | bytes 393224 | tf_op jit(solution)/shard_map/ppermute | solution.py:604
  4.8 0.0 collective-permute-done.core
  4.8 3.3 %collective-permute-done.1 = bf16[8,64,128]{2,1,0:T(8,128)(2,1)S(1)} collective-permute-done((bf16[8,64,128]{2,1,0:T(8,128)(2,1)S(1)}, bf16[8,64,128]{2,1,0:T(8,128)(2,1)S(1)}, u32[]{:S(2)}, u32[]{:S(2)}) %collective-permute-start.1) | collective-permute-done | bytes 131104 | tf_op jit(solution)/shard_map/ppermute | solution.py:604
  8.1 0.0 copy-start
  8.2 0.0 copy-start.1
  8.3 0.0 copy-start.2
  8.3 1.8 %collective-permute-start.2 = (bf16[7,64,128]{2,1,0:T(8,128)(2,1)S(1)}, bf16[7,64,128]{2,1,0:T(8,128)(2,1)S(1)}, u32[]{:S(2)}, u32[]{:S(2)}) collective-permute-start(bf16[7,64,128]{2,1,0:T(8,128)(2,1)S(1)} %get-tuple-element.69), channel_id=1, source_target_pairs={{0,1},{1,0},{2,3},{3,2},{4,5},{5,4},{6,7},{7,6},{8,9},{9,8},{10,11... | collective-permute-start | bytes 344072 | tf_op jit(solution)/shard_map/ppermute | solution.py:603
  10.1 4.4 %collective-permute-start.3 = (bf16[7,64,128]{2,1,0:T(8,128)(2,1)S(1)}, bf16[7,64,128]{2,1,0:T(8,128)(2,1)S(1)}, u32[]{:S(2)}, u32[]{:S(2)}) collective-permute-start(bf16[7,64,128]{2,1,0:T(8,128)(2,1)S(1)} %get-tuple-element.68), channel_id=1, source_target_pairs={{1,2},{2,1},{3,4},{4,3},{5,6},{6,5},{7,8},{8,7},{9,10},{10,9},{11,... | collective-permute-start | bytes 344072 | tf_op jit(solution)/shard_map/ppermute | solution.py:604
  14.6 2.6 %inner_grads.1 = (f32[9,64,256]{2,1,0:T(8,128)S(1)}, f32[27,64,128]{2,1,0:T(8,128)S(1)}, bf16[256,256]{1,0:T(8,128)(2,1)S(1)}) custom-call(s32[1]{0:T(128)} %bitcast.1.odd.odd_x, bf16[4,8,64,64]{3,2,1,0:T(8,128)(2,1)S(1)} %copy-done, bf16[2,4,64,128]{3,2,1,0:T(8,128)(2,1)S(1)} %copy-done.2, bf16[8,64,128]{2,1,0:T(8,128)(2,1)S(1)} %collective-permute-done.core, ...), custom_call_target="tpu_custom_call" | custom-call | flops 2000000000 | bytes 4000000 | tf_op jit(solution)/shard_map/inner_grads/pallas_call | solution.py:227
  17.1 0.0 collective-permute-done.3
  17.2 0.0 collective-permute-done.2.near
  17.2 2.8 %outer_grads.1 = (bf16[1312,128]{1,0:T(8,128)(2,1)S(1)}, bf16[1312,128]{1,0:T(8,128)(2,1)S(1)}, bf16[256,256]{1,0:T(8,128)(2,1)S(1)}, bf16[4,64,128]{2,1,0:T(8,1...) custom-call(s32[1]{0:T(128)} %bitcast.1.odd.odd_x, ...), custom_call_target="tpu_custom_call" | custom-call | flops 2000000000 | bytes 4000000 | tf_op jit(solution)/shard_map/outer_grads/pallas_call | solution.py:327
  20.0 2.5 %collective-permute-start.4 = (bf16[1312,128]{1,0:T(8,128)(2,1)S(1)}, bf16[1312,128]{1,0:T(8,128)(2,1)S(1)}, u32[]{:S(2)}, u32[]{:S(2)}) collective-permute-start(bf16[1312,128]{1,0:T(8,128)(2,1)S(1)} %get-tuple-element.37), channel_id=1, source_target_pairs={{0,16},{16,0},{32,48},{48,32},{64,80},{80,64},{96,112},{112,96},{1... | collective-permute-start | bytes 1007624 | tf_op jit(solution)/shard_map/ppermute | solution.py:529
  22.5 0.1 collective-permute-start.5
  22.6 1.1 %collective-permute-done.4 = bf16[1312,128]{1,0:T(8,128)(2,1)S(1)} collective-permute-done((bf16[1312,128]{1,0:T(8,128)(2,1)S(1)}, bf16[1312,128]{1,0:T(8,128)(2,1)S(1)}, u32[]{:S(2)}, u32[]{:S(2)}) %collective-permute-start.4) | collective-permute-done | bytes 335904 | tf_op jit(solution)/shard_map/ppermute | solution.py:529
  23.8 0.1 add_convert_fusion
  23.9 0.0 collective-permute-done.5.core
  23.9 0.1 collective-permute-start.8
  24.0 0.1 collective-permute-start.7
  24.1 2.5 %collective-permute-start.6 = (bf16[328,128]{1,0:T(8,128)(2,1)S(1)}, bf16[328,128]{1,0:T(8,128)(2,1)S(1)}, u32[]{:S(2)}, u32[]{:S(2)}) collective-permute-start(bf16[328,128]{1,0:T(8,128)(2,1)S(1)} %get-tuple-element.63), channel_id=1, source_target_pairs={{0,1},{1,0},{2,3},{3,2},{4,5},{5,4},{6,7},{7,6},{8,9},{9,8},{10,11... | collective-permute-start | bytes 251912 | tf_op jit(solution)/shard_map/ppermute | solution.py:529
  26.7 2.0 %collective-permute-done.8 = bf16[328,128]{1,0:T(8,128)(2,1)S(1)} collective-permute-done((bf16[328,128]{1,0:T(8,128)(2,1)S(1)}, bf16[328,128]{1,0:T(8,128)(2,1)S(1)}, u32[]{:S(2)}, u32[]{:S(2)}) %collective-permute-start.8) | collective-permute-done | bytes 84000 | tf_op jit(solution)/shard_map/ppermute | solution.py:529
  28.6 2.4 %collective-permute-done.6 = bf16[328,128]{1,0:T(8,128)(2,1)S(1)} collective-permute-done((bf16[328,128]{1,0:T(8,128)(2,1)S(1)}, bf16[328,128]{1,0:T(8,128)(2,1)S(1)}, u32[]{:S(2)}, u32[]{:S(2)}) %collective-permute-start.6) | collective-permute-done | bytes 84000 | tf_op jit(solution)/shard_map/ppermute | solution.py:529
  31.1 1.0 %collective-permute-start.9 = (bf16[328,128]{1,0:T(8,128)(2,1)S(1)}, bf16[328,128]{1,0:T(8,128)(2,1)S(1)}, u32[]{:S(2)}, u32[]{:S(2)}) collective-permute-start(bf16[328,128]{1,0:T(8,128)(2,1)S(1)} %add_convert_fusion.5), channel_id=1, source_target_pairs={{0,48},{16,32},{32,16},{48,0},{64,112},{80,96},{96,80},{112,64},{1... | collective-permute-start | bytes 251912 | tf_op jit(solution)/shard_map/ppermute | solution.py:529
  32.0 0.8 %collective-permute-start.11 = (bf16[4,64,128]{2,1,0:T(8,128)(2,1)S(1)}, bf16[4,64,128]{2,1,0:T(8,128)(2,1)S(1)}, u32[]{:S(2)}, u32[]{:S(2)}) collective-permute-start(bf16[4,64,128]{2,1,0:T(8,128)(2,1)S(1)} %get-tuple-element.45), channel_id=1, source_target_pairs={{0,48},{16,32},{32,16},{48,0},{64,112},{80,96},{96,80},{112,64},{1... | collective-permute-start | bytes 196616 | tf_op jit(solution)/shard_map/ppermute | solution.py:529
  32.9 3.3 %collective-permute-done.9 = bf16[328,128]{1,0:T(8,128)(2,1)S(1)} collective-permute-done((bf16[328,128]{1,0:T(8,128)(2,1)S(1)}, bf16[328,128]{1,0:T(8,128)(2,1)S(1)}, u32[]{:S(2)}, u32[]{:S(2)}) %collective-permute-start.9) | collective-permute-done | bytes 84000 | tf_op jit(solution)/shard_map/ppermute | solution.py:529
  36.2 2.6 %collective-permute-start.12 = (bf16[4,64,128]{2,1,0:T(8,128)(2,1)S(1)}, bf16[4,64,128]{2,1,0:T(8,128)(2,1)S(1)}, u32[]{:S(2)}, u32[]{:S(2)}) collective-permute-start(bf16[4,64,128]{2,1,0:T(8,128)(2,1)S(1)} %get-tuple-element.45), channel_id=1, source_target_pairs={{0,112},{16,96},{32,80},{48,64},{64,48},{80,32},{96,16},{112,0},{1... | collective-permute-start | bytes 196616 | tf_op jit(solution)/shard_map/ppermute | solution.py:529
  38.8 0.5 collective-permute-start.10
  39.3 0.0 collective-permute-done.11
  39.3 2.2 %collective-permute-done.12 = bf16[4,64,128]{2,1,0:T(8,128)(2,1)S(1)} collective-permute-done((bf16[4,64,128]{2,1,0:T(8,128)(2,1)S(1)}, bf16[4,64,128]{2,1,0:T(8,128)(2,1)S(1)}, u32[]{:S(2)}, u32[]{:S(2)}) %collective-permute-start.12) | collective-permute-done | bytes 65568 | tf_op jit(solution)/shard_map/ppermute | solution.py:529
  41.5 2.9 %collective-permute-done.10 = bf16[328,128]{1,0:T(8,128)(2,1)S(1)} collective-permute-done((bf16[328,128]{1,0:T(8,128)(2,1)S(1)}, bf16[328,128]{1,0:T(8,128)(2,1)S(1)}, u32[]{:S(2)}, u32[]{:S(2)}) %collective-permute-start.10) | collective-permute-done | bytes 84000 | tf_op jit(solution)/shard_map/ppermute | solution.py:529
  44.5 1.2 %collective-permute-start.13 = (bf16[520,128]{1,0:T(8,128)(2,1)S(1)}, bf16[520,128]{1,0:T(8,128)(2,1)S(1)}, u32[]{:S(2)}, u32[]{:S(2)}) collective-permute-start(bf16[520,128]{1,0:T(8,128)(2,1)S(1)} %pad_maximum_fusion.3), channel_id=1, source_target_pairs={{0,3},{1,2},{2,1},{3,0},{4,7},{5,6},{6,5},{7,4},{8,11},{9,10},{10,... | collective-permute-start | bytes 399368 | tf_op jit(solution)/shard_map/ppermute | solution.py:529
  45.7 4.8 %collective-permute-done.13 = bf16[520,128]{1,0:T(8,128)(2,1)S(1)} collective-permute-done((bf16[520,128]{1,0:T(8,128)(2,1)S(1)}, bf16[520,128]{1,0:T(8,128)(2,1)S(1)}, u32[]{:S(2)}, u32[]{:S(2)}) %collective-permute-start.13) | collective-permute-done | bytes 133152 | tf_op jit(solution)/shard_map/ppermute | solution.py:529
  50.6 2.5 %collective-permute-start.15 = (bf16[520,128]{1,0:T(8,128)(2,1)S(1)}, bf16[520,128]{1,0:T(8,128)(2,1)S(1)}, u32[]{:S(2)}, u32[]{:S(2)}) collective-permute-start(bf16[520,128]{1,0:T(8,128)(2,1)S(1)} %pad_maximum_fusion.2), channel_id=1, source_target_pairs={{0,12},{1,13},{2,14},{3,15},{4,8},{5,9},{6,10},{7,11},{8,4},{9,5},... | collective-permute-start | bytes 399368 | tf_op jit(solution)/shard_map/ppermute | solution.py:529
  53.0 1.3 %inner_input.1.part = f32[512,256]{1,0:T(8,128)S(1)} custom-call(s32[1]{0:T(128)} %bitcast.1.odd.odd_x, bf16[256,256]{1,0:T(8,128)(2,1)S(1)} %get-tuple-element.35.inner, bf16[256,256]{1,0:T(8,128)(2,1)S(1)} %get-tuple-element.50.outer, bf16[4,64,128]{2,1,0:T(8,128)(2,1)S(1)} %collective-permute-done.5.core, bf16[4,64,128]{2,1,0:T(8,128)(2,1)S(1)} %get-tuple-element.56.chip, ...), custom_call_target="tpu_custom_call" | custom-call | flops 500000000 | bytes 2000000 | tf_op jit(solution)/shard_map/inner_input/pallas_call | solution.py:406
  54.3 1.4 %collective-permute-done.15 = bf16[520,128]{1,0:T(8,128)(2,1)S(1)} collective-permute-done((bf16[520,128]{1,0:T(8,128)(2,1)S(1)}, bf16[520,128]{1,0:T(8,128)(2,1)S(1)}, u32[]{:S(2)}, u32[]{:S(2)}) %collective-permute-start.15) | collective-permute-done | bytes 133152 | tf_op jit(solution)/shard_map/ppermute | solution.py:529
  55.7 0.1 collective-permute-start.16
  55.8 0.1 collective-permute-start.17
  55.9 2.5 %collective-permute-start.18 = (bf16[328,128]{1,0:T(8,128)(2,1)S(1)}, bf16[328,128]{1,0:T(8,128)(2,1)S(1)}, u32[]{:S(2)}, u32[]{:S(2)}) collective-permute-start(bf16[328,128]{1,0:T(8,128)(2,1)S(1)} %add_convert_fusion.1), channel_id=1, source_target_pairs={{0,5},{1,4},{2,7},{3,6},{4,1},{5,0},{6,3},{7,2},{8,13},{9,12},{10,... | collective-permute-start | bytes 251912 | tf_op jit(solution)/shard_map/ppermute | solution.py:529
  58.5 0.8 %collective-permute-done.17 = bf16[328,128]{1,0:T(8,128)(2,1)S(1)} collective-permute-done((bf16[328,128]{1,0:T(8,128)(2,1)S(1)}, bf16[328,128]{1,0:T(8,128)(2,1)S(1)}, u32[]{:S(2)}, u32[]{:S(2)}) %collective-permute-start.17) | collective-permute-done | bytes 84000 | tf_op jit(solution)/shard_map/ppermute | solution.py:529
  59.2 1.7 %collective-permute-done.18 = bf16[328,128]{1,0:T(8,128)(2,1)S(1)} collective-permute-done((bf16[328,128]{1,0:T(8,128)(2,1)S(1)}, bf16[328,128]{1,0:T(8,128)(2,1)S(1)}, u32[]{:S(2)}, u32[]{:S(2)}) %collective-permute-start.18) | collective-permute-done | bytes 84000 | tf_op jit(solution)/shard_map/ppermute | solution.py:529
  60.9 0.0 collective-permute-done.16
  60.9 0.1 broadcast_select_fusion.13
  61.1 3.3 %collective-permute-start.19 = (bf16[1312,128]{1,0:T(8,128)(2,1)S(1)}, bf16[1312,128]{1,0:T(8,128)(2,1)S(1)}, u32[]{:S(2)}, u32[]{:S(2)}) collective-permute-start(bf16[1312,128]{1,0:T(8,128)(2,1)S(1)} %pad_maximum_fusion.mine), channel_id=1, source_target_pairs={{0,16},{16,0},{32,48},{48,32},{64,80},{80,64},{96,112},{112,96},{1... | collective-permute-start | bytes 1007624 | tf_op jit(solution)/shard_map/ppermute | solution.py:529
  64.3 1.4 %outer_input.1 = bf16[4,8,64,64]{3,2,1,0:T(8,128)(2,1)} custom-call(s32[1]{0:T(128)} %bitcast.odd_y, bf16[3,64,128]{2,1,0:T(8,128)(2,1)S(1)} %collective-permute-done.14.near, bf16[3,64,128]{2,1,0:T(8,128)(2,1)S(1)} %bitcast.5, bf16[3,3,3,64,64]{4,3,2,1,0:T(8,128)(2,1)S(1)} %copy-done.1, f32[512,256]{1,0:T(8,128)S(1)} %inner_input.1.part), custom_call_target="tpu_custom_call" | custom-call | flops 300000000 | bytes 4000000 | tf_op jit(solution)/shard_map/outer_input/pallas_call | solution.py:450
  65.7 0.0 collective-permute-done.19.other
  65.7 1.4 %unpack.1 = (f32[3,3,3,64,64]{4,3,2,1,0:T(8,128)}, f32[3,3,3,64,128]{4,3,2,1,0:T(8,128)}) custom-call(s32[1]{0:T(128)} %bitcast.2.part.odd, bf16[1312,128]{1,0:T(8,128)(2,1)S(1)} %pad_maximum_fusion.mine, bf16[1312,128]{1,0:T(8,128)(2,1)S(1)} %collective-permute-done.19.other), custom_call_target="tpu_custom_call" | custom-call | tf_op jit(solution)/shard_map/unpack/pallas_call | solution.py:496
  (35 shorter events, 0.5 us)
Async XLA Ops:
  1.9 2.9 %collective-permute-start = (bf16[8,64,128]{2,1,0:T(8,128)(2,1)S(1)}, bf16[8,64,128]{2,1,0:T(8,128)(2,1)S(1)}, u32[]{:S(2)}, u32[]{:S(2)}) collective-permute-start(bf16[8,64,128]{2,1,0:T(8,128)(2,1)S(1)} %get-tuple-element.29), channel_id=1, source_target_pairs={{0,16},{16,0},{32,48},{48,32},{64,80},{80,64},{96,112},{112,96},{1... | collective-permute-start | bytes 393224 | tf_op jit(solution)/shard_map/ppermute | solution.py:603
  3.4 4.7 %collective-permute-start.1 = (bf16[8,64,128]{2,1,0:T(8,128)(2,1)S(1)}, bf16[8,64,128]{2,1,0:T(8,128)(2,1)S(1)}, u32[]{:S(2)}, u32[]{:S(2)}) collective-permute-start(bf16[8,64,128]{2,1,0:T(8,128)(2,1)S(1)} %get-tuple-element.30), channel_id=1, source_target_pairs={{16,32},{32,16},{48,64},{64,48},{80,96},{96,80},{112,0},{0,112},{1... | collective-permute-start | bytes 393224 | tf_op jit(solution)/shard_map/ppermute | solution.py:604
  8.1 6.4 %copy-start.3 = (bf16[3,3,3,64,128]{4,3,2,1,0:T(8,128)(2,1)S(1)}, bf16[3,3,3,64,128]{4,3,2,1,0:T(8,128)(2,1)}, u32[]{:S(2)}) copy-start(bf16[3,3,3,64,128]{4,3,2,1,0:T(8,128)(2,1)} %w_deep.3) | copy-start | bytes 1327108
  8.1 6.4 %copy-start = (bf16[4,8,64,64]{3,2,1,0:T(8,128)(2,1)S(1)}, bf16[4,8,64,64]{3,2,1,0:T(8,128)(2,1)}, u32[]{:S(2)}) copy-start(bf16[4,8,64,64]{3,2,1,0:T(8,128)(2,1)} %own.5) | copy-start | bytes 786436
  8.2 6.4 %copy-start.1 = (bf16[3,3,3,64,64]{4,3,2,1,0:T(8,128)(2,1)S(1)}, bf16[3,3,3,64,64]{4,3,2,1,0:T(8,128)(2,1)}, u32[]{:S(2)}) copy-start(bf16[3,3,3,64,64]{4,3,2,1,0:T(8,128)(2,1)} %w_up.7) | copy-start | bytes 663556
  8.3 6.3 %copy-start.2 = (bf16[2,4,64,128]{3,2,1,0:T(8,128)(2,1)S(1)}, bf16[2,4,64,128]{3,2,1,0:T(8,128)(2,1)}, u32[]{:S(2)}) copy-start(bf16[2,4,64,128]{3,2,1,0:T(8,128)(2,1)} %cot.5) | copy-start | bytes 393220
  8.3 8.9 %collective-permute-start.2 = (bf16[7,64,128]{2,1,0:T(8,128)(2,1)S(1)}, bf16[7,64,128]{2,1,0:T(8,128)(2,1)S(1)}, u32[]{:S(2)}, u32[]{:S(2)}) collective-permute-start(bf16[7,64,128]{2,1,0:T(8,128)(2,1)S(1)} %get-tuple-element.69), channel_id=1, source_target_pairs={{0,1},{1,0},{2,3},{3,2},{4,5},{5,4},{6,7},{7,6},{8,9},{9,8},{10,11... | collective-permute-start | bytes 344072 | tf_op jit(solution)/shard_map/ppermute | solution.py:603
  10.1 7.0 %collective-permute-start.3 = (bf16[7,64,128]{2,1,0:T(8,128)(2,1)S(1)}, bf16[7,64,128]{2,1,0:T(8,128)(2,1)S(1)}, u32[]{:S(2)}, u32[]{:S(2)}) collective-permute-start(bf16[7,64,128]{2,1,0:T(8,128)(2,1)S(1)} %get-tuple-element.68), channel_id=1, source_target_pairs={{1,2},{2,1},{3,4},{4,3},{5,6},{6,5},{7,8},{8,7},{9,10},{10,9},{11,... | collective-permute-start | bytes 344072 | tf_op jit(solution)/shard_map/ppermute | solution.py:604
  20.0 3.8 %collective-permute-start.4 = (bf16[1312,128]{1,0:T(8,128)(2,1)S(1)}, bf16[1312,128]{1,0:T(8,128)(2,1)S(1)}, u32[]{:S(2)}, u32[]{:S(2)}) collective-permute-start(bf16[1312,128]{1,0:T(8,128)(2,1)S(1)} %get-tuple-element.37), channel_id=1, source_target_pairs={{0,16},{16,0},{32,48},{48,32},{64,80},{80,64},{96,112},{112,96},{1... | collective-permute-start | bytes 1007624 | tf_op jit(solution)/shard_map/ppermute | solution.py:529
  22.5 1.4 %collective-permute-start.5 = (bf16[4,64,128]{2,1,0:T(8,128)(2,1)S(1)}, bf16[4,64,128]{2,1,0:T(8,128)(2,1)S(1)}, u32[]{:S(2)}, u32[]{:S(2)}) collective-permute-start(bf16[4,64,128]{2,1,0:T(8,128)(2,1)S(1)} %get-tuple-element.38), channel_id=1, source_target_pairs={{0,16},{16,0},{32,48},{48,32},{64,80},{80,64},{96,112},{112,96},{1... | collective-permute-start | bytes 196616 | tf_op jit(solution)/shard_map/ppermute | solution.py:655
  23.9 4.7 %collective-permute-start.8 = (bf16[328,128]{1,0:T(8,128)(2,1)S(1)}, bf16[328,128]{1,0:T(8,128)(2,1)S(1)}, u32[]{:S(2)}, u32[]{:S(2)}) collective-permute-start(bf16[328,128]{1,0:T(8,128)(2,1)S(1)} %get-tuple-element.64), channel_id=1, source_target_pairs={{0,5},{1,4},{2,7},{3,6},{4,1},{5,0},{6,3},{7,2},{8,13},{9,12},{10,... | collective-permute-start | bytes 251912 | tf_op jit(solution)/shard_map/ppermute | solution.py:529
  24.0 4.6 %collective-permute-start.7 = (bf16[328,128]{1,0:T(8,128)(2,1)S(1)}, bf16[328,128]{1,0:T(8,128)(2,1)S(1)}, u32[]{:S(2)}, u32[]{:S(2)}) collective-permute-start(bf16[328,128]{1,0:T(8,128)(2,1)S(1)} %get-tuple-element.65), channel_id=1, source_target_pairs={{0,4},{1,5},{2,6},{3,7},{4,0},{5,1},{6,2},{7,3},{8,12},{9,13},{10,... | collective-permute-start | bytes 251912 | tf_op jit(solution)/shard_map/ppermute | solution.py:529
  24.1 6.9 %collective-permute-start.6 = (bf16[328,128]{1,0:T(8,128)(2,1)S(1)}, bf16[328,128]{1,0:T(8,128)(2,1)S(1)}, u32[]{:S(2)}, u32[]{:S(2)}) collective-permute-start(bf16[328,128]{1,0:T(8,128)(2,1)S(1)} %get-tuple-element.63), channel_id=1, source_target_pairs={{0,1},{1,0},{2,3},{3,2},{4,5},{5,4},{6,7},{7,6},{8,9},{9,8},{10,11... | collective-permute-start | bytes 251912 | tf_op jit(solution)/shard_map/ppermute | solution.py:529
  31.1 5.2 %collective-permute-start.9 = (bf16[328,128]{1,0:T(8,128)(2,1)S(1)}, bf16[328,128]{1,0:T(8,128)(2,1)S(1)}, u32[]{:S(2)}, u32[]{:S(2)}) collective-permute-start(bf16[328,128]{1,0:T(8,128)(2,1)S(1)} %add_convert_fusion.5), channel_id=1, source_target_pairs={{0,48},{16,32},{32,16},{48,0},{64,112},{80,96},{96,80},{112,64},{1... | collective-permute-start | bytes 251912 | tf_op jit(solution)/shard_map/ppermute | solution.py:529
  32.0 7.3 %collective-permute-start.11 = (bf16[4,64,128]{2,1,0:T(8,128)(2,1)S(1)}, bf16[4,64,128]{2,1,0:T(8,128)(2,1)S(1)}, u32[]{:S(2)}, u32[]{:S(2)}) collective-permute-start(bf16[4,64,128]{2,1,0:T(8,128)(2,1)S(1)} %get-tuple-element.45), channel_id=1, source_target_pairs={{0,48},{16,32},{32,16},{48,0},{64,112},{80,96},{96,80},{112,64},{1... | collective-permute-start | bytes 196616 | tf_op jit(solution)/shard_map/ppermute | solution.py:529
  36.2 5.2 %collective-permute-start.12 = (bf16[4,64,128]{2,1,0:T(8,128)(2,1)S(1)}, bf16[4,64,128]{2,1,0:T(8,128)(2,1)S(1)}, u32[]{:S(2)}, u32[]{:S(2)}) collective-permute-start(bf16[4,64,128]{2,1,0:T(8,128)(2,1)S(1)} %get-tuple-element.45), channel_id=1, source_target_pairs={{0,112},{16,96},{32,80},{48,64},{64,48},{80,32},{96,16},{112,0},{1... | collective-permute-start | bytes 196616 | tf_op jit(solution)/shard_map/ppermute | solution.py:529
  38.8 5.6 %collective-permute-start.10 = (bf16[328,128]{1,0:T(8,128)(2,1)S(1)}, bf16[328,128]{1,0:T(8,128)(2,1)S(1)}, u32[]{:S(2)}, u32[]{:S(2)}) collective-permute-start(bf16[328,128]{1,0:T(8,128)(2,1)S(1)} %add_convert_fusion.4), channel_id=1, source_target_pairs={{0,112},{16,96},{32,80},{48,64},{64,48},{80,32},{96,16},{112,0},{1... | collective-permute-start | bytes 251912 | tf_op jit(solution)/shard_map/ppermute | solution.py:529
  44.5 6.0 %collective-permute-start.13 = (bf16[520,128]{1,0:T(8,128)(2,1)S(1)}, bf16[520,128]{1,0:T(8,128)(2,1)S(1)}, u32[]{:S(2)}, u32[]{:S(2)}) collective-permute-start(bf16[520,128]{1,0:T(8,128)(2,1)S(1)} %pad_maximum_fusion.3), channel_id=1, source_target_pairs={{0,3},{1,2},{2,1},{3,0},{4,7},{5,6},{6,5},{7,4},{8,11},{9,10},{10,... | collective-permute-start | bytes 399368 | tf_op jit(solution)/shard_map/ppermute | solution.py:529
  45.7 4.8 %collective-permute-start.14 = (bf16[3,64,128]{2,1,0:T(8,128)(2,1)S(1)}, bf16[3,64,128]{2,1,0:T(8,128)(2,1)S(1)}, u32[]{:S(2)}, u32[]{:S(2)}) collective-permute-start(bf16[3,64,128]{2,1,0:T(8,128)(2,1)S(1)} %get-tuple-element.76), channel_id=1, source_target_pairs={{0,1},{1,0},{2,3},{3,2},{4,5},{5,4},{6,7},{7,6},{8,9},{9,8},{10,11... | collective-permute-start | bytes 147464 | tf_op jit(solution)/shard_map/ppermute | solution.py:529
  50.6 5.1 %collective-permute-start.15 = (bf16[520,128]{1,0:T(8,128)(2,1)S(1)}, bf16[520,128]{1,0:T(8,128)(2,1)S(1)}, u32[]{:S(2)}, u32[]{:S(2)}) collective-permute-start(bf16[520,128]{1,0:T(8,128)(2,1)S(1)} %pad_maximum_fusion.2), channel_id=1, source_target_pairs={{0,12},{1,13},{2,14},{3,15},{4,8},{5,9},{6,10},{7,11},{8,4},{9,5},... | collective-permute-start | bytes 399368 | tf_op jit(solution)/shard_map/ppermute | solution.py:529
  55.7 5.2 %collective-permute-start.16 = (bf16[520,128]{1,0:T(8,128)(2,1)S(1)}, bf16[520,128]{1,0:T(8,128)(2,1)S(1)}, u32[]{:S(2)}, u32[]{:S(2)}) collective-permute-start(bf16[520,128]{1,0:T(8,128)(2,1)S(1)} %pad_maximum_fusion.1), channel_id=1, source_target_pairs={{0,4},{1,5},{2,6},{3,7},{4,0},{5,1},{6,2},{7,3},{8,12},{9,13},{10,... | collective-permute-start | bytes 399368 | tf_op jit(solution)/shard_map/ppermute | solution.py:529
  55.8 3.4 %collective-permute-start.17 = (bf16[328,128]{1,0:T(8,128)(2,1)S(1)}, bf16[328,128]{1,0:T(8,128)(2,1)S(1)}, u32[]{:S(2)}, u32[]{:S(2)}) collective-permute-start(bf16[328,128]{1,0:T(8,128)(2,1)S(1)} %add_convert_fusion.1), channel_id=1, source_target_pairs={{0,1},{1,0},{2,3},{3,2},{4,5},{5,4},{6,7},{7,6},{8,9},{9,8},{10,11... | collective-permute-start | bytes 251912 | tf_op jit(solution)/shard_map/ppermute | solution.py:529
  55.9 5.0 %collective-permute-start.18 = (bf16[328,128]{1,0:T(8,128)(2,1)S(1)}, bf16[328,128]{1,0:T(8,128)(2,1)S(1)}, u32[]{:S(2)}, u32[]{:S(2)}) collective-permute-start(bf16[328,128]{1,0:T(8,128)(2,1)S(1)} %add_convert_fusion.1), channel_id=1, source_target_pairs={{0,5},{1,4},{2,7},{3,6},{4,1},{5,0},{6,3},{7,2},{8,13},{9,12},{10,... | collective-permute-start | bytes 251912 | tf_op jit(solution)/shard_map/ppermute | solution.py:529
  61.1 4.6 %collective-permute-start.19 = (bf16[1312,128]{1,0:T(8,128)(2,1)S(1)}, bf16[1312,128]{1,0:T(8,128)(2,1)S(1)}, u32[]{:S(2)}, u32[]{:S(2)}) collective-permute-start(bf16[1312,128]{1,0:T(8,128)(2,1)S(1)} %pad_maximum_fusion.mine), channel_id=1, source_target_pairs={{0,16},{16,0},{32,48},{48,32},{64,80},{80,64},{96,112},{112,96},{1... | collective-permute-start | bytes 1007624 | tf_op jit(solution)/shard_map/ppermute | solution.py:529

commit v7 on v6

--- a/solution.py
+++ b/solution.py
@@ -656,11 +656,11 @@
     total, core = lax.optimization_barrier((total, core))
     total = scatter_sum(total, (Z_NEAR, X_NEAR))
     total, to_chip = lax.optimization_barrier((total, to_chip))
+    second = swap(to_chip, (Y_FAR,), 1)
+    total = swap_sum(total, Y_FAR)
+    total, to_chip = lax.optimization_barrier((total, to_chip))
     first = swap(to_chip, (Y_NEAR,), 1)
     total = swap_sum(total, Y_NEAR)
-    total, to_chip = lax.optimization_barrier((total, to_chip))
-    second = swap(to_chip, (Y_FAR,), 1)
-    total = swap_sum(total, Y_FAR)
     chip = jnp.where((((at_x + 1) >> 1) & 1) == 1, first, second)
     chip = inside(chip, "gx")
     inner_part = inner_input(flag_x, inner, outer, core, chip, weight_upper)

time: 67.2 us -> 66 us (0.982)
  waiting for transfers between devices: 25.8 us -> 24.7 us
    ppermute x15, waiting for transfers between devices: 22.5 us -> 21.3 us  [swap(): lax.ppermute(value, axis, [(i, i ^ masks[axis]) for i in range(count)])]
where the time goes in v7:
time: 66 us; the launch traced here: 65.9 us
  starting transfers between devices  29 us (44%)
  waiting for transfers between devices  24.7 us (37%)
  Pallas kernels  10.7 us (16%)
  between operations  0.94 us (1%)
    ppermute x15, waiting for transfers between devices, swap(): lax.ppermute(value, axis, [(i, i ^ masks[axis]) for i in range(count)])  21.3 us
    ppermute x15, starting transfers between devices, swap(): lax.ppermute(value, axis, [(i, i ^ masks[axis]) for i in range(count)])  19.8 us
    ppermute x2, starting transfers between devices, both_sides(): odd = lax.ppermute(second, axis, pairs_of(axis, 1))  5.8 us
    ppermute x2, waiting for transfers between devices, both_sides(): odd = lax.ppermute(second, axis, pairs_of(axis, 1))  3.31 us
    ppermute x2, starting transfers between devices, both_sides(): even = lax.ppermute(first, axis, pairs_of(axis, 0))  3.3 us
    pallas_call x1, Pallas kernels, outer_grads(): pl.pallas_call(outer_kernel, in_specs=[smem] * 3 + [vmem] * 11, out_shape...  2.8 us
    pallas_call x1, Pallas kernels, inner_grads(): pl.pallas_call(inner_kernel, in_specs=[smem] + [vmem] * 6, out_shape=[jax...  2.56 us
    pallas_call x1, Pallas kernels, unpack(): pl.pallas_call(functools.partial(unpack_kernel, up_scale, deep_scale), in...  1.37 us
  transfers between devices with their start and end apart: 20, of which 11 were waited for; matrix products, arithmetic and copies ran while one was open for 0% of the time, Pallas kernels for 8%

profile of v7, /device:TPU:1, one launch (start us, length us, event | category | flops | bytes accessed | tf_op | source)
XLA Modules:
  0.0 65.9 jit_solution(17773170270815743837)
XLA Ops:
  0.6 1.3 %faces.1 = (bf16[8,64,128]{2,1,0:T(8,128)(2,1)S(1)}, bf16[8,64,128]{2,1,0:T(8,128)(2,1)S(1)}, bf16[4,64,128]{2,1,0:T(8,128)(2,1)S(1)}, bf16[4,64,128]{2,1,0:T(8,128)(2,1)S(1)}) custom-call(s32[1]{0:T(128)} %bitcast.1.odd.odd_x, bf16[4,8,64,64]{3,2,1,0:T(8,128)(2,1)} %own.5, bf16[2,4,64,128]{3,2,1,0:T(8,128)(2,1)} %cot.5), custom_call_target="tpu_custom_call" | custom-call | tf_op jit(solution)/shard_map/faces/pallas_call | solution.py:90
  1.9 1.5 %collective-permute-start = (bf16[8,64,128]{2,1,0:T(8,128)(2,1)S(1)}, bf16[8,64,128]{2,1,0:T(8,128)(2,1)S(1)}, u32[]{:S(2)}, u32[]{:S(2)}) collective-permute-start(bf16[8,64,128]{2,1,0:T(8,128)(2,1)S(1)} %get-tuple-element.29), channel_id=1, source_target_pairs={{0,16},{16,0},{32,48},{48,32},{64,80},{80,64},{96,112},{112,96},{1... | collective-permute-start | bytes 393224 | tf_op jit(solution)/shard_map/ppermute | solution.py:603
  3.4 1.4 %collective-permute-start.1 = (bf16[8,64,128]{2,1,0:T(8,128)(2,1)S(1)}, bf16[8,64,128]{2,1,0:T(8,128)(2,1)S(1)}, u32[]{:S(2)}, u32[]{:S(2)}) collective-permute-start(bf16[8,64,128]{2,1,0:T(8,128)(2,1)S(1)} %get-tuple-element.30), channel_id=1, source_target_pairs={{16,32},{32,16},{48,64},{64,48},{80,96},{96,80},{112,0},{0,112},{1... | collective-permute-start | bytes 393224 | tf_op jit(solution)/shard_map/ppermute | solution.py:604
  4.8 0.0 collective-permute-done.core
  4.8 3.3 %collective-permute-done.1 = bf16[8,64,128]{2,1,0:T(8,128)(2,1)S(1)} collective-permute-done((bf16[8,64,128]{2,1,0:T(8,128)(2,1)S(1)}, bf16[8,64,128]{2,1,0:T(8,128)(2,1)S(1)}, u32[]{:S(2)}, u32[]{:S(2)}) %collective-permute-start.1) | collective-permute-done | bytes 131104 | tf_op jit(solution)/shard_map/ppermute | solution.py:604
  8.1 0.0 copy-start
  8.2 0.0 copy-start.1
  8.3 0.0 copy-start.2
  8.3 1.8 %collective-permute-start.2 = (bf16[7,64,128]{2,1,0:T(8,128)(2,1)S(1)}, bf16[7,64,128]{2,1,0:T(8,128)(2,1)S(1)}, u32[]{:S(2)}, u32[]{:S(2)}) collective-permute-start(bf16[7,64,128]{2,1,0:T(8,128)(2,1)S(1)} %get-tuple-element.69), channel_id=1, source_target_pairs={{0,1},{1,0},{2,3},{3,2},{4,5},{5,4},{6,7},{7,6},{8,9},{9,8},{10,11... | collective-permute-start | bytes 344072 | tf_op jit(solution)/shard_map/ppermute | solution.py:603
  10.1 4.4 %collective-permute-start.3 = (bf16[7,64,128]{2,1,0:T(8,128)(2,1)S(1)}, bf16[7,64,128]{2,1,0:T(8,128)(2,1)S(1)}, u32[]{:S(2)}, u32[]{:S(2)}) collective-permute-start(bf16[7,64,128]{2,1,0:T(8,128)(2,1)S(1)} %get-tuple-element.68), channel_id=1, source_target_pairs={{1,2},{2,1},{3,4},{4,3},{5,6},{6,5},{7,8},{8,7},{9,10},{10,9},{11,... | collective-permute-start | bytes 344072 | tf_op jit(solution)/shard_map/ppermute | solution.py:604
  14.6 2.6 %inner_grads.1 = (f32[9,64,256]{2,1,0:T(8,128)S(1)}, f32[27,64,128]{2,1,0:T(8,128)S(1)}, bf16[256,256]{1,0:T(8,128)(2,1)S(1)}) custom-call(s32[1]{0:T(128)} %bitcast.1.odd.odd_x, bf16[4,8,64,64]{3,2,1,0:T(8,128)(2,1)S(1)} %copy-done, bf16[2,4,64,128]{3,2,1,0:T(8,128)(2,1)S(1)} %copy-done.2, bf16[8,64,128]{2,1,0:T(8,128)(2,1)S(1)} %collective-permute-done.core, ...), custom_call_target="tpu_custom_call" | custom-call | flops 2000000000 | bytes 4000000 | tf_op jit(solution)/shard_map/inner_grads/pallas_call | solution.py:227
  17.1 0.0 collective-permute-done.3
  17.2 2.8 %outer_grads.1 = (bf16[1312,128]{1,0:T(8,128)(2,1)S(1)}, bf16[1312,128]{1,0:T(8,128)(2,1)S(1)}, bf16[256,256]{1,0:T(8,128)(2,1)S(1)}, bf16[4,64,128]{2,1,0:T(8,1...) custom-call(s32[1]{0:T(128)} %bitcast.1.odd.odd_x, ...), custom_call_target="tpu_custom_call" | custom-call | flops 2000000000 | bytes 4000000 | tf_op jit(solution)/shard_map/outer_grads/pallas_call | solution.py:327
  20.0 2.5 %collective-permute-start.4 = (bf16[1312,128]{1,0:T(8,128)(2,1)S(1)}, bf16[1312,128]{1,0:T(8,128)(2,1)S(1)}, u32[]{:S(2)}, u32[]{:S(2)}) collective-permute-start(bf16[1312,128]{1,0:T(8,128)(2,1)S(1)} %get-tuple-element.37), channel_id=1, source_target_pairs={{0,16},{16,0},{32,48},{48,32},{64,80},{80,64},{96,112},{112,96},{1... | collective-permute-start | bytes 1007624 | tf_op jit(solution)/shard_map/ppermute | solution.py:529
  22.5 0.1 collective-permute-start.5
  22.6 1.1 %collective-permute-done.4 = bf16[1312,128]{1,0:T(8,128)(2,1)S(1)} collective-permute-done((bf16[1312,128]{1,0:T(8,128)(2,1)S(1)}, bf16[1312,128]{1,0:T(8,128)(2,1)S(1)}, u32[]{:S(2)}, u32[]{:S(2)}) %collective-permute-start.4) | collective-permute-done | bytes 335904 | tf_op jit(solution)/shard_map/ppermute | solution.py:529
  23.8 0.1 add_convert_fusion
  23.9 0.0 collective-permute-done.5.core
  23.9 0.1 collective-permute-start.8
  24.0 0.1 collective-permute-start.7
  24.1 2.5 %collective-permute-start.6 = (bf16[328,128]{1,0:T(8,128)(2,1)S(1)}, bf16[328,128]{1,0:T(8,128)(2,1)S(1)}, u32[]{:S(2)}, u32[]{:S(2)}) collective-permute-start(bf16[328,128]{1,0:T(8,128)(2,1)S(1)} %get-tuple-element.63), channel_id=1, source_target_pairs={{0,1},{1,0},{2,3},{3,2},{4,5},{5,4},{6,7},{7,6},{8,9},{9,8},{10,11... | collective-permute-start | bytes 251912 | tf_op jit(solution)/shard_map/ppermute | solution.py:529
  26.7 2.0 %collective-permute-done.8 = bf16[328,128]{1,0:T(8,128)(2,1)S(1)} collective-permute-done((bf16[328,128]{1,0:T(8,128)(2,1)S(1)}, bf16[328,128]{1,0:T(8,128)(2,1)S(1)}, u32[]{:S(2)}, u32[]{:S(2)}) %collective-permute-start.8) | collective-permute-done | bytes 84000 | tf_op jit(solution)/shard_map/ppermute | solution.py:529
  28.6 0.0 collective-permute-done.7
  28.6 2.4 %collective-permute-done.6 = bf16[328,128]{1,0:T(8,128)(2,1)S(1)} collective-permute-done((bf16[328,128]{1,0:T(8,128)(2,1)S(1)}, bf16[328,128]{1,0:T(8,128)(2,1)S(1)}, u32[]{:S(2)}, u32[]{:S(2)}) %collective-permute-start.6) | collective-permute-done | bytes 84000 | tf_op jit(solution)/shard_map/ppermute | solution.py:529
  31.1 2.9 %collective-permute-start.9 = (bf16[328,128]{1,0:T(8,128)(2,1)S(1)}, bf16[328,128]{1,0:T(8,128)(2,1)S(1)}, u32[]{:S(2)}, u32[]{:S(2)}) collective-permute-start(bf16[328,128]{1,0:T(8,128)(2,1)S(1)} %add_convert_fusion.5), channel_id=1, source_target_pairs={{0,112},{16,96},{32,80},{48,64},{64,48},{80,32},{96,16},{112,0},{1... | collective-permute-start | bytes 251912 | tf_op jit(solution)/shard_map/ppermute | solution.py:529
  34.0 0.1 collective-permute-start.12
  34.1 3.1 %collective-permute-done.9 = bf16[328,128]{1,0:T(8,128)(2,1)S(1)} collective-permute-done((bf16[328,128]{1,0:T(8,128)(2,1)S(1)}, bf16[328,128]{1,0:T(8,128)(2,1)S(1)}, u32[]{:S(2)}, u32[]{:S(2)}) %collective-permute-start.9) | collective-permute-done | bytes 84000 | tf_op jit(solution)/shard_map/ppermute | solution.py:529
  37.3 0.1 collective-permute-start.11
  37.4 1.7 %collective-permute-start.10 = (bf16[328,128]{1,0:T(8,128)(2,1)S(1)}, bf16[328,128]{1,0:T(8,128)(2,1)S(1)}, u32[]{:S(2)}, u32[]{:S(2)}) collective-permute-start(bf16[328,128]{1,0:T(8,128)(2,1)S(1)} %add_convert_fusion.4), channel_id=1, source_target_pairs={{0,48},{16,32},{32,16},{48,0},{64,112},{80,96},{96,80},{112,64},{1... | collective-permute-start | bytes 251912 | tf_op jit(solution)/shard_map/ppermute | solution.py:529
  39.1 2.9 %collective-permute-done.11 = bf16[4,64,128]{2,1,0:T(8,128)(2,1)S(1)} collective-permute-done((bf16[4,64,128]{2,1,0:T(8,128)(2,1)S(1)}, bf16[4,64,128]{2,1,0:T(8,128)(2,1)S(1)}, u32[]{:S(2)}, u32[]{:S(2)}) %collective-permute-start.11) | collective-permute-done | bytes 65568 | tf_op jit(solution)/shard_map/ppermute | solution.py:529
  42.1 1.1 %collective-permute-done.10 = bf16[328,128]{1,0:T(8,128)(2,1)S(1)} collective-permute-done((bf16[328,128]{1,0:T(8,128)(2,1)S(1)}, bf16[328,128]{1,0:T(8,128)(2,1)S(1)}, u32[]{:S(2)}, u32[]{:S(2)}) %collective-permute-start.10) | collective-permute-done | bytes 84000 | tf_op jit(solution)/shard_map/ppermute | solution.py:529
  43.3 1.1 %collective-permute-start.13 = (bf16[520,128]{1,0:T(8,128)(2,1)S(1)}, bf16[520,128]{1,0:T(8,128)(2,1)S(1)}, u32[]{:S(2)}, u32[]{:S(2)}) collective-permute-start(bf16[520,128]{1,0:T(8,128)(2,1)S(1)} %pad_maximum_fusion.3), channel_id=1, source_target_pairs={{0,3},{1,2},{2,1},{3,0},{4,7},{5,6},{6,5},{7,4},{8,11},{9,10},{10,... | collective-permute-start | bytes 399368 | tf_op jit(solution)/shard_map/ppermute | solution.py:529
  44.4 0.0 collective-permute-start.14
  44.4 5.0 %collective-permute-done.13 = bf16[520,128]{1,0:T(8,128)(2,1)S(1)} collective-permute-done((bf16[520,128]{1,0:T(8,128)(2,1)S(1)}, bf16[520,128]{1,0:T(8,128)(2,1)S(1)}, u32[]{:S(2)}, u32[]{:S(2)}) %collective-permute-start.13) | collective-permute-done | bytes 133152 | tf_op jit(solution)/shard_map/ppermute | solution.py:529
  49.3 0.0 collective-permute-done.14.near
  49.4 2.5 %collective-permute-start.15 = (bf16[520,128]{1,0:T(8,128)(2,1)S(1)}, bf16[520,128]{1,0:T(8,128)(2,1)S(1)}, u32[]{:S(2)}, u32[]{:S(2)}) collective-permute-start(bf16[520,128]{1,0:T(8,128)(2,1)S(1)} %pad_maximum_fusion.2), channel_id=1, source_target_pairs={{0,12},{1,13},{2,14},{3,15},{4,8},{5,9},{6,10},{7,11},{8,4},{9,5},... | collective-permute-start | bytes 399368 | tf_op jit(solution)/shard_map/ppermute | solution.py:529
  51.8 1.3 %inner_input.1.part = f32[512,256]{1,0:T(8,128)S(1)} custom-call(s32[1]{0:T(128)} %bitcast.1.odd.odd_x, bf16[256,256]{1,0:T(8,128)(2,1)S(1)} %get-tuple-element.35.inner, bf16[256,256]{1,0:T(8,128)(2,1)S(1)} %get-tuple-element.50.outer, bf16[4,64,128]{2,1,0:T(8,128)(2,1)S(1)} %collective-permute-done.5.core, bf16[4,64,128]{2,1,0:T(8,128)(2,1)S(1)} %get-tuple-element.56.chip, ...), custom_call_target="tpu_custom_call" | custom-call | flops 500000000 | bytes 2000000 | tf_op jit(solution)/shard_map/inner_input/pallas_call | solution.py:406
  53.2 1.4 %collective-permute-done.15 = bf16[520,128]{1,0:T(8,128)(2,1)S(1)} collective-permute-done((bf16[520,128]{1,0:T(8,128)(2,1)S(1)}, bf16[520,128]{1,0:T(8,128)(2,1)S(1)}, u32[]{:S(2)}, u32[]{:S(2)}) %collective-permute-start.15) | collective-permute-done | bytes 133152 | tf_op jit(solution)/shard_map/ppermute | solution.py:529
  54.6 0.1 collective-permute-start.16
  54.7 0.1 collective-permute-start.17
  54.8 2.5 %collective-permute-start.18 = (bf16[328,128]{1,0:T(8,128)(2,1)S(1)}, bf16[328,128]{1,0:T(8,128)(2,1)S(1)}, u32[]{:S(2)}, u32[]{:S(2)}) collective-permute-start(bf16[328,128]{1,0:T(8,128)(2,1)S(1)} %add_convert_fusion.1), channel_id=1, source_target_pairs={{0,5},{1,4},{2,7},{3,6},{4,1},{5,0},{6,3},{7,2},{8,13},{9,12},{10,... | collective-permute-start | bytes 251912 | tf_op jit(solution)/shard_map/ppermute | solution.py:529
  57.3 0.8 %collective-permute-done.17 = bf16[328,128]{1,0:T(8,128)(2,1)S(1)} collective-permute-done((bf16[328,128]{1,0:T(8,128)(2,1)S(1)}, bf16[328,128]{1,0:T(8,128)(2,1)S(1)}, u32[]{:S(2)}, u32[]{:S(2)}) %collective-permute-start.17) | collective-permute-done | bytes 84000 | tf_op jit(solution)/shard_map/ppermute | solution.py:529
  58.1 1.5 %collective-permute-done.18 = bf16[328,128]{1,0:T(8,128)(2,1)S(1)} collective-permute-done((bf16[328,128]{1,0:T(8,128)(2,1)S(1)}, bf16[328,128]{1,0:T(8,128)(2,1)S(1)}, u32[]{:S(2)}, u32[]{:S(2)}) %collective-permute-start.18) | collective-permute-done | bytes 84000 | tf_op jit(solution)/shard_map/ppermute | solution.py:529
  59.6 0.1 broadcast_select_fusion.13
  59.7 3.4 %collective-permute-start.19 = (bf16[1312,128]{1,0:T(8,128)(2,1)S(1)}, bf16[1312,128]{1,0:T(8,128)(2,1)S(1)}, u32[]{:S(2)}, u32[]{:S(2)}) collective-permute-start(bf16[1312,128]{1,0:T(8,128)(2,1)S(1)} %pad_maximum_fusion.mine), channel_id=1, source_target_pairs={{0,16},{16,0},{32,48},{48,32},{64,80},{80,64},{96,112},{112,96},{1... | collective-permute-start | bytes 1007624 | tf_op jit(solution)/shard_map/ppermute | solution.py:529
  63.2 1.4 %outer_input.1 = bf16[4,8,64,64]{3,2,1,0:T(8,128)(2,1)} custom-call(s32[1]{0:T(128)} %bitcast.odd_y, bf16[3,64,128]{2,1,0:T(8,128)(2,1)S(1)} %collective-permute-done.14.near, bf16[3,64,128]{2,1,0:T(8,128)(2,1)S(1)} %bitcast.5, bf16[3,3,3,64,64]{4,3,2,1,0:T(8,128)(2,1)S(1)} %copy-done.1, f32[512,256]{1,0:T(8,128)S(1)} %inner_input.1.part), custom_call_target="tpu_custom_call" | custom-call | flops 300000000 | bytes 4000000 | tf_op jit(solution)/shard_map/outer_input/pallas_call | solution.py:450
  64.5 0.0 collective-permute-done.19.other
  64.5 1.4 %unpack.1 = (f32[3,3,3,64,64]{4,3,2,1,0:T(8,128)}, f32[3,3,3,64,128]{4,3,2,1,0:T(8,128)}) custom-call(s32[1]{0:T(128)} %bitcast.2.part.odd, bf16[1312,128]{1,0:T(8,128)(2,1)S(1)} %pad_maximum_fusion.mine, bf16[1312,128]{1,0:T(8,128)(2,1)S(1)} %collective-permute-done.19.other), custom_call_target="tpu_custom_call" | custom-call | tf_op jit(solution)/shard_map/unpack/pallas_call | solution.py:496
  (35 shorter events, 0.5 us)
Async XLA Ops:
  1.9 2.9 %collective-permute-start = (bf16[8,64,128]{2,1,0:T(8,128)(2,1)S(1)}, bf16[8,64,128]{2,1,0:T(8,128)(2,1)S(1)}, u32[]{:S(2)}, u32[]{:S(2)}) collective-permute-start(bf16[8,64,128]{2,1,0:T(8,128)(2,1)S(1)} %get-tuple-element.29), channel_id=1, source_target_pairs={{0,16},{16,0},{32,48},{48,32},{64,80},{80,64},{96,112},{112,96},{1... | collective-permute-start | bytes 393224 | tf_op jit(solution)/shard_map/ppermute | solution.py:603
  3.4 4.7 %collective-permute-start.1 = (bf16[8,64,128]{2,1,0:T(8,128)(2,1)S(1)}, bf16[8,64,128]{2,1,0:T(8,128)(2,1)S(1)}, u32[]{:S(2)}, u32[]{:S(2)}) collective-permute-start(bf16[8,64,128]{2,1,0:T(8,128)(2,1)S(1)} %get-tuple-element.30), channel_id=1, source_target_pairs={{16,32},{32,16},{48,64},{64,48},{80,96},{96,80},{112,0},{0,112},{1... | collective-permute-start | bytes 393224 | tf_op jit(solution)/shard_map/ppermute | solution.py:604
  8.1 6.4 %copy-start.3 = (bf16[3,3,3,64,128]{4,3,2,1,0:T(8,128)(2,1)S(1)}, bf16[3,3,3,64,128]{4,3,2,1,0:T(8,128)(2,1)}, u32[]{:S(2)}) copy-start(bf16[3,3,3,64,128]{4,3,2,1,0:T(8,128)(2,1)} %w_deep.3) | copy-start | bytes 1327108
  8.1 6.4 %copy-start = (bf16[4,8,64,64]{3,2,1,0:T(8,128)(2,1)S(1)}, bf16[4,8,64,64]{3,2,1,0:T(8,128)(2,1)}, u32[]{:S(2)}) copy-start(bf16[4,8,64,64]{3,2,1,0:T(8,128)(2,1)} %own.5) | copy-start | bytes 786436
  8.2 6.4 %copy-start.1 = (bf16[3,3,3,64,64]{4,3,2,1,0:T(8,128)(2,1)S(1)}, bf16[3,3,3,64,64]{4,3,2,1,0:T(8,128)(2,1)}, u32[]{:S(2)}) copy-start(bf16[3,3,3,64,64]{4,3,2,1,0:T(8,128)(2,1)} %w_up.7) | copy-start | bytes 663556
  8.3 6.3 %copy-start.2 = (bf16[2,4,64,128]{3,2,1,0:T(8,128)(2,1)S(1)}, bf16[2,4,64,128]{3,2,1,0:T(8,128)(2,1)}, u32[]{:S(2)}) copy-start(bf16[2,4,64,128]{3,2,1,0:T(8,128)(2,1)} %cot.5) | copy-start | bytes 393220
  8.3 8.9 %collective-permute-start.2 = (bf16[7,64,128]{2,1,0:T(8,128)(2,1)S(1)}, bf16[7,64,128]{2,1,0:T(8,128)(2,1)S(1)}, u32[]{:S(2)}, u32[]{:S(2)}) collective-permute-start(bf16[7,64,128]{2,1,0:T(8,128)(2,1)S(1)} %get-tuple-element.69), channel_id=1, source_target_pairs={{0,1},{1,0},{2,3},{3,2},{4,5},{5,4},{6,7},{7,6},{8,9},{9,8},{10,11... | collective-permute-start | bytes 344072 | tf_op jit(solution)/shard_map/ppermute | solution.py:603
  10.1 7.0 %collective-permute-start.3 = (bf16[7,64,128]{2,1,0:T(8,128)(2,1)S(1)}, bf16[7,64,128]{2,1,0:T(8,128)(2,1)S(1)}, u32[]{:S(2)}, u32[]{:S(2)}) collective-permute-start(bf16[7,64,128]{2,1,0:T(8,128)(2,1)S(1)} %get-tuple-element.68), channel_id=1, source_target_pairs={{1,2},{2,1},{3,4},{4,3},{5,6},{6,5},{7,8},{8,7},{9,10},{10,9},{11,... | collective-permute-start | bytes 344072 | tf_op jit(solution)/shard_map/ppermute | solution.py:604
  20.0 3.8 %collective-permute-start.4 = (bf16[1312,128]{1,0:T(8,128)(2,1)S(1)}, bf16[1312,128]{1,0:T(8,128)(2,1)S(1)}, u32[]{:S(2)}, u32[]{:S(2)}) collective-permute-start(bf16[1312,128]{1,0:T(8,128)(2,1)S(1)} %get-tuple-element.37), channel_id=1, source_target_pairs={{0,16},{16,0},{32,48},{48,32},{64,80},{80,64},{96,112},{112,96},{1... | collective-permute-start | bytes 1007624 | tf_op jit(solution)/shard_map/ppermute | solution.py:529
  22.5 1.4 %collective-permute-start.5 = (bf16[4,64,128]{2,1,0:T(8,128)(2,1)S(1)}, bf16[4,64,128]{2,1,0:T(8,128)(2,1)S(1)}, u32[]{:S(2)}, u32[]{:S(2)}) collective-permute-start(bf16[4,64,128]{2,1,0:T(8,128)(2,1)S(1)} %get-tuple-element.38), channel_id=1, source_target_pairs={{0,16},{16,0},{32,48},{48,32},{64,80},{80,64},{96,112},{112,96},{1... | collective-permute-start | bytes 196616 | tf_op jit(solution)/shard_map/ppermute | solution.py:655
  23.9 4.7 %collective-permute-start.8 = (bf16[328,128]{1,0:T(8,128)(2,1)S(1)}, bf16[328,128]{1,0:T(8,128)(2,1)S(1)}, u32[]{:S(2)}, u32[]{:S(2)}) collective-permute-start(bf16[328,128]{1,0:T(8,128)(2,1)S(1)} %get-tuple-element.64), channel_id=1, source_target_pairs={{0,5},{1,4},{2,7},{3,6},{4,1},{5,0},{6,3},{7,2},{8,13},{9,12},{10,... | collective-permute-start | bytes 251912 | tf_op jit(solution)/shard_map/ppermute | solution.py:529
  24.0 4.6 %collective-permute-start.7 = (bf16[328,128]{1,0:T(8,128)(2,1)S(1)}, bf16[328,128]{1,0:T(8,128)(2,1)S(1)}, u32[]{:S(2)}, u32[]{:S(2)}) collective-permute-start(bf16[328,128]{1,0:T(8,128)(2,1)S(1)} %get-tuple-element.65), channel_id=1, source_target_pairs={{0,4},{1,5},{2,6},{3,7},{4,0},{5,1},{6,2},{7,3},{8,12},{9,13},{10,... | collective-permute-start | bytes 251912 | tf_op jit(solution)/shard_map/ppermute | solution.py:529
  24.1 6.9 %collective-permute-start.6 = (bf16[328,128]{1,0:T(8,128)(2,1)S(1)}, bf16[328,128]{1,0:T(8,128)(2,1)S(1)}, u32[]{:S(2)}, u32[]{:S(2)}) collective-permute-start(bf16[328,128]{1,0:T(8,128)(2,1)S(1)} %get-tuple-element.63), channel_id=1, source_target_pairs={{0,1},{1,0},{2,3},{3,2},{4,5},{5,4},{6,7},{7,6},{8,9},{9,8},{10,11... | collective-permute-start | bytes 251912 | tf_op jit(solution)/shard_map/ppermute | solution.py:529
  31.1 6.2 %collective-permute-start.9 = (bf16[328,128]{1,0:T(8,128)(2,1)S(1)}, bf16[328,128]{1,0:T(8,128)(2,1)S(1)}, u32[]{:S(2)}, u32[]{:S(2)}) collective-permute-start(bf16[328,128]{1,0:T(8,128)(2,1)S(1)} %add_convert_fusion.5), channel_id=1, source_target_pairs={{0,112},{16,96},{32,80},{48,64},{64,48},{80,32},{96,16},{112,0},{1... | collective-permute-start | bytes 251912 | tf_op jit(solution)/shard_map/ppermute | solution.py:529
  34.0 5.1 %collective-permute-start.12 = (bf16[4,64,128]{2,1,0:T(8,128)(2,1)S(1)}, bf16[4,64,128]{2,1,0:T(8,128)(2,1)S(1)}, u32[]{:S(2)}, u32[]{:S(2)}) collective-permute-start(bf16[4,64,128]{2,1,0:T(8,128)(2,1)S(1)} %get-tuple-element.45), channel_id=1, source_target_pairs={{0,112},{16,96},{32,80},{48,64},{64,48},{80,32},{96,16},{112,0},{1... | collective-permute-start | bytes 196616 | tf_op jit(solution)/shard_map/ppermute | solution.py:529
  37.3 4.8 %collective-permute-start.11 = (bf16[4,64,128]{2,1,0:T(8,128)(2,1)S(1)}, bf16[4,64,128]{2,1,0:T(8,128)(2,1)S(1)}, u32[]{:S(2)}, u32[]{:S(2)}) collective-permute-start(bf16[4,64,128]{2,1,0:T(8,128)(2,1)S(1)} %get-tuple-element.45), channel_id=1, source_target_pairs={{0,48},{16,32},{32,16},{48,0},{64,112},{80,96},{96,80},{112,64},{1... | collective-permute-start | bytes 196616 | tf_op jit(solution)/shard_map/ppermute | solution.py:529
  37.4 5.9 %collective-permute-start.10 = (bf16[328,128]{1,0:T(8,128)(2,1)S(1)}, bf16[328,128]{1,0:T(8,128)(2,1)S(1)}, u32[]{:S(2)}, u32[]{:S(2)}) collective-permute-start(bf16[328,128]{1,0:T(8,128)(2,1)S(1)} %add_convert_fusion.4), channel_id=1, source_target_pairs={{0,48},{16,32},{32,16},{48,0},{64,112},{80,96},{96,80},{112,64},{1... | collective-permute-start | bytes 251912 | tf_op jit(solution)/shard_map/ppermute | solution.py:529
  43.3 6.0 %collective-permute-start.13 = (bf16[520,128]{1,0:T(8,128)(2,1)S(1)}, bf16[520,128]{1,0:T(8,128)(2,1)S(1)}, u32[]{:S(2)}, u32[]{:S(2)}) collective-permute-start(bf16[520,128]{1,0:T(8,128)(2,1)S(1)} %pad_maximum_fusion.3), channel_id=1, source_target_pairs={{0,3},{1,2},{2,1},{3,0},{4,7},{5,6},{6,5},{7,4},{8,11},{9,10},{10,... | collective-permute-start | bytes 399368 | tf_op jit(solution)/shard_map/ppermute | solution.py:529
  44.4 5.0 %collective-permute-start.14 = (bf16[3,64,128]{2,1,0:T(8,128)(2,1)S(1)}, bf16[3,64,128]{2,1,0:T(8,128)(2,1)S(1)}, u32[]{:S(2)}, u32[]{:S(2)}) collective-permute-start(bf16[3,64,128]{2,1,0:T(8,128)(2,1)S(1)} %get-tuple-element.76), channel_id=1, source_target_pairs={{0,1},{1,0},{2,3},{3,2},{4,5},{5,4},{6,7},{7,6},{8,9},{9,8},{10,11... | collective-permute-start | bytes 147464 | tf_op jit(solution)/shard_map/ppermute | solution.py:529
  49.4 5.1 %collective-permute-start.15 = (bf16[520,128]{1,0:T(8,128)(2,1)S(1)}, bf16[520,128]{1,0:T(8,128)(2,1)S(1)}, u32[]{:S(2)}, u32[]{:S(2)}) collective-permute-start(bf16[520,128]{1,0:T(8,128)(2,1)S(1)} %pad_maximum_fusion.2), channel_id=1, source_target_pairs={{0,12},{1,13},{2,14},{3,15},{4,8},{5,9},{6,10},{7,11},{8,4},{9,5},... | collective-permute-start | bytes 399368 | tf_op jit(solution)/shard_map/ppermute | solution.py:529
  54.6 5.0 %collective-permute-start.16 = (bf16[520,128]{1,0:T(8,128)(2,1)S(1)}, bf16[520,128]{1,0:T(8,128)(2,1)S(1)}, u32[]{:S(2)}, u32[]{:S(2)}) collective-permute-start(bf16[520,128]{1,0:T(8,128)(2,1)S(1)} %pad_maximum_fusion.1), channel_id=1, source_target_pairs={{0,4},{1,5},{2,6},{3,7},{4,0},{5,1},{6,2},{7,3},{8,12},{9,13},{10,... | collective-permute-start | bytes 399368 | tf_op jit(solution)/shard_map/ppermute | solution.py:529
  54.7 3.4 %collective-permute-start.17 = (bf16[328,128]{1,0:T(8,128)(2,1)S(1)}, bf16[328,128]{1,0:T(8,128)(2,1)S(1)}, u32[]{:S(2)}, u32[]{:S(2)}) collective-permute-start(bf16[328,128]{1,0:T(8,128)(2,1)S(1)} %add_convert_fusion.1), channel_id=1, source_target_pairs={{0,1},{1,0},{2,3},{3,2},{4,5},{5,4},{6,7},{7,6},{8,9},{9,8},{10,11... | collective-permute-start | bytes 251912 | tf_op jit(solution)/shard_map/ppermute | solution.py:529
  54.8 4.8 %collective-permute-start.18 = (bf16[328,128]{1,0:T(8,128)(2,1)S(1)}, bf16[328,128]{1,0:T(8,128)(2,1)S(1)}, u32[]{:S(2)}, u32[]{:S(2)}) collective-permute-start(bf16[328,128]{1,0:T(8,128)(2,1)S(1)} %add_convert_fusion.1), channel_id=1, source_target_pairs={{0,5},{1,4},{2,7},{3,6},{4,1},{5,0},{6,3},{7,2},{8,13},{9,12},{10,... | collective-permute-start | bytes 251912 | tf_op jit(solution)/shard_map/ppermute | solution.py:529
  59.7 4.8 %collective-permute-start.19 = (bf16[1312,128]{1,0:T(8,128)(2,1)S(1)}, bf16[1312,128]{1,0:T(8,128)(2,1)S(1)}, u32[]{:S(2)}, u32[]{:S(2)}) collective-permute-start(bf16[1312,128]{1,0:T(8,128)(2,1)S(1)} %pad_maximum_fusion.mine), channel_id=1, source_target_pairs={{0,16},{16,0},{32,48},{48,32},{64,80},{80,64},{96,112},{112,96},{1... | collective-permute-start | bytes 1007624 | tf_op jit(solution)/shard_map/ppermute | solution.py:529

commit v8 on v7

--- a/solution.py
+++ b/solution.py
@@ -39,6 +39,29 @@
 
 INNER = (1, 2)
 OUTER = (0, 3)
+
+
+def shifted(row):
+    row = row.astype(F32)
+    edge = jnp.zeros((1, row.shape[1]), F32)
+    return (
+        jnp.concatenate([edge, row[:-1]], axis=0),
+        row,
+        jnp.concatenate([row[1:], edge], axis=0),
+    )
+
+
+def build_taps(taps, ys, column):
+    for y in ys:
+        parts = [shifted(column(x, y)) for x in range(6)]
+        for block in range(2):
+            for x in range(3):
+                pieces = parts[2 * block + x] + (parts[2 * block + 3][x],)
+                taps[block, x, y] = jnp.concatenate(pieces, axis=1).astype(BF16)
+
+
+def level_window(taps, at_x, at_y, ys):
+    return jnp.concatenate([taps[x, at_x, 2 * y + at_y] for x in range(2) for y in ys], axis=0)
 
 
 def window(taps, at_x, at_y, ys):
@@ -122,27 +145,28 @@
 
 def build_blocks(w_up, blocks):
     empty = jnp.zeros((192, 64), BF16)
-    for x in range(3):
-        for y in range(4):
+    for y in range(4):
+        for x in range(3):
             left = w_up[x, y].reshape(192, 64) if y < 3 else empty
             right = w_up[x, y - 1].reshape(192, 64) if y > 0 else empty
             pair = jnp.concatenate([left, right], axis=1)
             blocks[x, y, 0:192, 0:128] = pair
-            blocks[x + 1, y, 0:192, 128:256] = pair
-    for y in range(4):
-        blocks[3, y, 0:192, 0:128] = jnp.zeros((192, 128), BF16)
+            if x < 2:
+                blocks[x + 1, y, 0:192, 128:256] = pair
+            else:
+                for c in range(3):
+                    blocks[c, y, 192:256, 128:256] = pair[c * 64 : c * 64 + 64]
+            blocks[x, y, 192:256, 0:128] = jnp.zeros((64, 128), BF16)
         blocks[0, y, 0:192, 128:256] = jnp.zeros((192, 128), BF16)
-        for x in range(4):
-            blocks[x, y, 192:256, :] = jnp.zeros((64, 256), BF16)
-
-
-def column_grads(ys, taps, cot_taps, blocks, w_deep, sums, deep):
+
+
+def column_grads(ys, taps, cot_taps, blocks, w_deep, sums, deep, last):
     rows = 2 * len(ys) * 64
     pre = jnp.zeros((rows, 256), F32)
-    for x in range(4):
+    for x in range(3):
         for y in range(4):
             pre = pre + jnp.dot(
-                window(taps, x, y, ys), blocks[x, y], preferred_element_type=F32
+                level_window(taps, x, y, ys), blocks[x, y], preferred_element_type=F32
             )
     sig = 1.0 / (1.0 + jnp.exp(-pre))
     act = pre * sig
@@ -171,24 +195,32 @@
             )
             for j in range(3):
                 deep((a * 3 + b) * 3 + 2 - j, out[:, j * 128 : j * 128 + 128])
-    for x in range(4):
+    for x in range(3):
         for y in range(4):
-            kept = [
-                (s, t)
-                for s in range(2)
-                for t in range(2)
-                if 0 <= x - s < 3 and 0 <= y - t < 3
-            ]
+            kept = [(s, t) for s in range(2) for t in range(2) if 0 <= y - t < 3]
             left = jnp.concatenate(
                 [grad_t[(s * 2 + t) * 64 : (s * 2 + t) * 64 + 64] for s, t in kept], axis=0
             )
-            part = jnp.dot(left, window(taps, x, y, ys), preferred_element_type=F32)
+            part = jnp.dot(left, level_window(taps, x, y, ys), preferred_element_type=F32)
             for k, (s, t) in enumerate(kept):
-                sums((x - s) * 3 + y - t, part[k * 64 : k * 64 + 64], s == 0 and t == 0)
+                piece = part[k * 64 : k * 64 + 64]
+                if x >= s:
+                    sums((x - s) * 3 + y - t, piece, s == 0 and t == 0)
+                if s == 1:
+                    place = (y - t) * 3 + x
+                    tail = piece[:, 192:256]
+                    last[place] = tail if t == 0 else last[place] + tail
     return grad.astype(BF16)
 
 
-def inner_kernel(odd_x, own, cot, core, chip, w_up, w_deep, sums, deep, inner, taps, cot_taps, blocks):
+def add_last(sums, last):
+    for b in range(3):
+        for c in range(3):
+            at = c * 64
+            sums[6 + b, :, at : at + 64] = sums[6 + b, :, at : at + 64] + last[b * 3 + c]
+
+
+def inner_kernel(odd_x, own, cot, core, chip, w_up, w_deep, sums, deep, inner, taps, cot_taps, blocks, last):
     swap_x = odd_x[0] == 1
 
     def x_lo(k):
@@ -197,10 +229,10 @@
     def x_hi(k):
         return jnp.where(swap_x, chip[k], core[k])
 
-    for x in range(6):
-        for y in range(2, 8):
-            row = level_column(x, y, lambda u, v: own[u, v], x_lo, x_hi, None, None)
-            taps[x, y] = depth_taps(row, 64)
+    def column(x, y):
+        return level_column(x, y, lambda u, v: own[u, v], x_lo, x_hi, None, None)
+
+    build_taps(taps, range(2, 8), column)
     for x in range(4):
         for y in range(1, 5):
             if x == 0:
@@ -218,7 +250,8 @@
     def add_deep(k, piece):
         deep[k] = piece
 
-    inner[...] = column_grads(INNER, taps, cot_taps, blocks, w_deep, add_sum, add_deep)
+    inner[...] = column_grads(INNER, taps, cot_taps, blocks, w_deep, add_sum, add_deep, last)
+    add_last(sums, last)
 
 
 def inner_grads(odd_x, own, cot, core, chip, w_up, w_deep):
@@ -233,9 +266,10 @@
             jax.ShapeDtypeStruct((256, 256), BF16),
         ],
         scratch_shapes=[
-            pltpu.VMEM((6, 10, 64, 256), BF16),
+            pltpu.VMEM((2, 3, 10, 64, 256), BF16),
             pltpu.VMEM((4, 6, 64, 384), BF16),
-            pltpu.VMEM((4, 4, 256, 256), BF16),
+            pltpu.VMEM((3, 4, 256, 256), BF16),
+            pltpu.VMEM((9, 64, 64), F32),
         ],
         compiler_params=pltpu.CompilerParams(vmem_limit_bytes=VMEM_BYTES),
         cost_estimate=pl.CostEstimate(
@@ -248,7 +282,7 @@
 def outer_kernel(
     odd_x, odd_y, part, own, cot, core, chip, near, far, w_up, w_deep, sums_in, deep_in, inner,
     keep, send, outer, to_core, to_chip, gy_head, gy_tail,
-    taps, cot_taps, blocks, sums, payload,
+    taps, cot_taps, blocks, last, sums, payload,
 ):
     swap_x = odd_x[0] == 1
     swap_y = odd_y[0] == 1
@@ -265,10 +299,10 @@
     def y_hi(k):
         return jnp.where(swap_y, far[k], near[k])
 
-    for x in range(6):
-        for y in (0, 1, 2, 3, 6, 7, 8, 9):
-            row = level_column(x, y, lambda u, v: own[u, v], x_lo, x_hi, y_lo, y_hi)
-            taps[x, y] = depth_taps(row, 64)
+    def column(x, y):
+        return level_column(x, y, lambda u, v: own[u, v], x_lo, x_hi, y_lo, y_hi)
+
+    build_taps(taps, (0, 1, 2, 3, 6, 7, 8, 9), column)
     for x in range(4):
         for y in range(6):
             if y == 0:
@@ -291,7 +325,8 @@
         top = DEEP_ROW + k * 64
         payload[top : top + 64, :] = (deep_in[k] + piece).astype(BF16)
 
-    rounded = column_grads(OUTER, taps, cot_taps, blocks, w_deep, add_sum, add_deep)
+    rounded = column_grads(OUTER, taps, cot_taps, blocks, w_deep, add_sum, add_deep, last)
+    add_last(sums, last)
     outer[...] = rounded
 
     def block(x, y):
@@ -337,9 +372,10 @@
             jax.ShapeDtypeStruct((2, 64, 128), BF16),
         ],
         scratch_shapes=[
-            pltpu.VMEM((6, 10, 64, 256), BF16),
+            pltpu.VMEM((2, 3, 10, 64, 256), BF16),
             pltpu.VMEM((4, 6, 64, 384), BF16),
-            pltpu.VMEM((4, 4, 256, 256), BF16),
+            pltpu.VMEM((3, 4, 256, 256), BF16),
+            pltpu.VMEM((9, 64, 64), F32),
             pltpu.VMEM((9, 64, 256), F32),
             pltpu.VMEM((PAY_ROWS, 128), BF16),
         ],

time: 66 us -> 65.9 us (level)
  transfers between devices with their start and end apart: 20 -> 20, of which waited for: 11 -> 12; matrix products, arithmetic and copies ran while one was open for 0% -> 0% of each run, Pallas kernels for 8% -> 8%
where the time goes in v8:
time: 65.9 us; the launch traced here: 65.7 us
  starting transfers between devices  29 us (44%)
  waiting for transfers between devices  24.8 us (38%)
  Pallas kernels  10.3 us (16%)
  between operations  0.93 us (1%)
    ppermute x15, waiting for transfers between devices, swap(): lax.ppermute(value, axis, [(i, i ^ masks[axis]) for i in range(count)])  21.3 us
    ppermute x15, starting transfers between devices, swap(): lax.ppermute(value, axis, [(i, i ^ masks[axis]) for i in range(count)])  19.8 us
    ppermute x2, starting transfers between devices, both_sides(): odd = lax.ppermute(second, axis, pairs_of(axis, 1))  5.8 us
    ppermute x2, waiting for transfers between devices, both_sides(): odd = lax.ppermute(second, axis, pairs_of(axis, 1))  3.46 us
    ppermute x2, starting transfers between devices, both_sides(): even = lax.ppermute(first, axis, pairs_of(axis, 0))  3.3 us
    pallas_call x1, Pallas kernels, outer_grads(): pl.pallas_call(outer_kernel, in_specs=[smem] * 3 + [vmem] * 11, out_shape...  2.63 us
    pallas_call x1, Pallas kernels, inner_grads(): pl.pallas_call(inner_kernel, in_specs=[smem] + [vmem] * 6, out_shape=[jax...  2.35 us
    pallas_call x1, Pallas kernels, unpack(): pl.pallas_call(functools.partial(unpack_kernel, up_scale, deep_scale), in...  1.37 us
  transfers between devices with their start and end apart: 20, of which 12 were waited for; matrix products, arithmetic and copies ran while one was open for 0% of the time, Pallas kernels for 8%

profile of v8, /device:TPU:1, one launch (start us, length us, event | category | flops | bytes accessed | tf_op | source)
XLA Modules:
  0.0 65.7 jit_solution(13023005583625322976)
XLA Ops:
  0.6 1.3 %faces.1 = (bf16[8,64,128]{2,1,0:T(8,128)(2,1)S(1)}, bf16[8,64,128]{2,1,0:T(8,128)(2,1)S(1)}, bf16[4,64,128]{2,1,0:T(8,128)(2,1)S(1)}, bf16[4,64,128]{2,1,0:T(8,128)(2,1)S(1)}) custom-call(s32[1]{0:T(128)} %bitcast.1.odd.odd_x, bf16[4,8,64,64]{3,2,1,0:T(8,128)(2,1)} %own.5, bf16[2,4,64,128]{3,2,1,0:T(8,128)(2,1)} %cot.5), custom_call_target="tpu_custom_call" | custom-call | tf_op jit(solution)/shard_map/faces/pallas_call | solution.py:113
  1.9 1.5 %collective-permute-start = (bf16[8,64,128]{2,1,0:T(8,128)(2,1)S(1)}, bf16[8,64,128]{2,1,0:T(8,128)(2,1)S(1)}, u32[]{:S(2)}, u32[]{:S(2)}) collective-permute-start(bf16[8,64,128]{2,1,0:T(8,128)(2,1)S(1)} %get-tuple-element.29), channel_id=1, source_target_pairs={{0,16},{16,0},{32,48},{48,32},{64,80},{80,64},{96,112},{112,96},{1... | collective-permute-start | bytes 393224 | tf_op jit(solution)/shard_map/ppermute | solution.py:639
  3.4 1.4 %collective-permute-start.1 = (bf16[8,64,128]{2,1,0:T(8,128)(2,1)S(1)}, bf16[8,64,128]{2,1,0:T(8,128)(2,1)S(1)}, u32[]{:S(2)}, u32[]{:S(2)}) collective-permute-start(bf16[8,64,128]{2,1,0:T(8,128)(2,1)S(1)} %get-tuple-element.30), channel_id=1, source_target_pairs={{16,32},{32,16},{48,64},{64,48},{80,96},{96,80},{112,0},{0,112},{1... | collective-permute-start | bytes 393224 | tf_op jit(solution)/shard_map/ppermute | solution.py:640
  4.8 0.0 collective-permute-done.core
  4.8 3.3 %collective-permute-done.1 = bf16[8,64,128]{2,1,0:T(8,128)(2,1)S(1)} collective-permute-done((bf16[8,64,128]{2,1,0:T(8,128)(2,1)S(1)}, bf16[8,64,128]{2,1,0:T(8,128)(2,1)S(1)}, u32[]{:S(2)}, u32[]{:S(2)}) %collective-permute-start.1) | collective-permute-done | bytes 131104 | tf_op jit(solution)/shard_map/ppermute | solution.py:640
  8.1 0.0 copy-start
  8.2 0.0 copy-start.1
  8.3 0.0 copy-start.2
  8.3 1.8 %collective-permute-start.2 = (bf16[7,64,128]{2,1,0:T(8,128)(2,1)S(1)}, bf16[7,64,128]{2,1,0:T(8,128)(2,1)S(1)}, u32[]{:S(2)}, u32[]{:S(2)}) collective-permute-start(bf16[7,64,128]{2,1,0:T(8,128)(2,1)S(1)} %get-tuple-element.69), channel_id=1, source_target_pairs={{0,1},{1,0},{2,3},{3,2},{4,5},{5,4},{6,7},{7,6},{8,9},{9,8},{10,11... | collective-permute-start | bytes 344072 | tf_op jit(solution)/shard_map/ppermute | solution.py:639
  10.1 4.4 %collective-permute-start.3 = (bf16[7,64,128]{2,1,0:T(8,128)(2,1)S(1)}, bf16[7,64,128]{2,1,0:T(8,128)(2,1)S(1)}, u32[]{:S(2)}, u32[]{:S(2)}) collective-permute-start(bf16[7,64,128]{2,1,0:T(8,128)(2,1)S(1)} %get-tuple-element.68), channel_id=1, source_target_pairs={{1,2},{2,1},{3,4},{4,3},{5,6},{6,5},{7,8},{8,7},{9,10},{10,9},{11,... | collective-permute-start | bytes 344072 | tf_op jit(solution)/shard_map/ppermute | solution.py:640
  14.6 2.4 %inner_grads.1 = (f32[9,64,256]{2,1,0:T(8,128)S(1)}, f32[27,64,128]{2,1,0:T(8,128)S(1)}, bf16[256,256]{1,0:T(8,128)(2,1)S(1)}) custom-call(s32[1]{0:T(128)} %bitcast.1.odd.odd_x, bf16[4,8,64,64]{3,2,1,0:T(8,128)(2,1)S(1)} %copy-done, bf16[2,4,64,128]{3,2,1,0:T(8,128)(2,1)S(1)} %copy-done.2, bf16[8,64,128]{2,1,0:T(8,128)(2,1)S(1)} %collective-permute-done.core, ...), custom_call_target="tpu_custom_call" | custom-call | flops 2000000000 | bytes 4000000 | tf_op jit(solution)/shard_map/inner_grads/pallas_call | solution.py:260
  16.9 0.2 collective-permute-done.3
  17.1 0.0 collective-permute-done.2.near
  17.1 2.6 %outer_grads.1 = (bf16[1312,128]{1,0:T(8,128)(2,1)S(1)}, bf16[1312,128]{1,0:T(8,128)(2,1)S(1)}, bf16[256,256]{1,0:T(8,128)(2,1)S(1)}, bf16[4,64,128]{2,1,0:T(8,1...) custom-call(s32[1]{0:T(128)} %bitcast.1.odd.odd_x, ...), custom_call_target="tpu_custom_call" | custom-call | flops 2000000000 | bytes 4000000 | tf_op jit(solution)/shard_map/outer_grads/pallas_call | solution.py:362
  19.7 2.6 %collective-permute-start.4 = (bf16[1312,128]{1,0:T(8,128)(2,1)S(1)}, bf16[1312,128]{1,0:T(8,128)(2,1)S(1)}, u32[]{:S(2)}, u32[]{:S(2)}) collective-permute-start(bf16[1312,128]{1,0:T(8,128)(2,1)S(1)} %get-tuple-element.37), channel_id=1, source_target_pairs={{0,16},{16,0},{32,48},{48,32},{64,80},{80,64},{96,112},{112,96},{1... | collective-permute-start | bytes 1007624 | tf_op jit(solution)/shard_map/ppermute | solution.py:565
  22.3 0.1 collective-permute-start.5
  22.5 1.1 %collective-permute-done.4 = bf16[1312,128]{1,0:T(8,128)(2,1)S(1)} collective-permute-done((bf16[1312,128]{1,0:T(8,128)(2,1)S(1)}, bf16[1312,128]{1,0:T(8,128)(2,1)S(1)}, u32[]{:S(2)}, u32[]{:S(2)}) %collective-permute-start.4) | collective-permute-done | bytes 335904 | tf_op jit(solution)/shard_map/ppermute | solution.py:565
  23.6 0.1 add_convert_fusion
  23.7 0.1 collective-permute-start.8
  23.8 0.1 collective-permute-start.7
  23.9 2.5 %collective-permute-start.6 = (bf16[328,128]{1,0:T(8,128)(2,1)S(1)}, bf16[328,128]{1,0:T(8,128)(2,1)S(1)}, u32[]{:S(2)}, u32[]{:S(2)}) collective-permute-start(bf16[328,128]{1,0:T(8,128)(2,1)S(1)} %get-tuple-element.63), channel_id=1, source_target_pairs={{0,1},{1,0},{2,3},{3,2},{4,5},{5,4},{6,7},{7,6},{8,9},{9,8},{10,11... | collective-permute-start | bytes 251912 | tf_op jit(solution)/shard_map/ppermute | solution.py:565
  26.5 2.0 %collective-permute-done.8 = bf16[328,128]{1,0:T(8,128)(2,1)S(1)} collective-permute-done((bf16[328,128]{1,0:T(8,128)(2,1)S(1)}, bf16[328,128]{1,0:T(8,128)(2,1)S(1)}, u32[]{:S(2)}, u32[]{:S(2)}) %collective-permute-start.8) | collective-permute-done | bytes 84000 | tf_op jit(solution)/shard_map/ppermute | solution.py:565
  28.4 0.0 collective-permute-done.7
  28.4 2.4 %collective-permute-done.6 = bf16[328,128]{1,0:T(8,128)(2,1)S(1)} collective-permute-done((bf16[328,128]{1,0:T(8,128)(2,1)S(1)}, bf16[328,128]{1,0:T(8,128)(2,1)S(1)}, u32[]{:S(2)}, u32[]{:S(2)}) %collective-permute-start.6) | collective-permute-done | bytes 84000 | tf_op jit(solution)/shard_map/ppermute | solution.py:565
  30.9 2.9 %collective-permute-start.9 = (bf16[328,128]{1,0:T(8,128)(2,1)S(1)}, bf16[328,128]{1,0:T(8,128)(2,1)S(1)}, u32[]{:S(2)}, u32[]{:S(2)}) collective-permute-start(bf16[328,128]{1,0:T(8,128)(2,1)S(1)} %add_convert_fusion.5), channel_id=1, source_target_pairs={{0,112},{16,96},{32,80},{48,64},{64,48},{80,32},{96,16},{112,0},{1... | collective-permute-start | bytes 251912 | tf_op jit(solution)/shard_map/ppermute | solution.py:565
  33.8 0.1 collective-permute-start.12
  33.9 3.2 %collective-permute-done.9 = bf16[328,128]{1,0:T(8,128)(2,1)S(1)} collective-permute-done((bf16[328,128]{1,0:T(8,128)(2,1)S(1)}, bf16[328,128]{1,0:T(8,128)(2,1)S(1)}, u32[]{:S(2)}, u32[]{:S(2)}) %collective-permute-start.9) | collective-permute-done | bytes 84000 | tf_op jit(solution)/shard_map/ppermute | solution.py:565
  37.1 0.1 collective-permute-start.11
  37.2 1.7 %collective-permute-start.10 = (bf16[328,128]{1,0:T(8,128)(2,1)S(1)}, bf16[328,128]{1,0:T(8,128)(2,1)S(1)}, u32[]{:S(2)}, u32[]{:S(2)}) collective-permute-start(bf16[328,128]{1,0:T(8,128)(2,1)S(1)} %add_convert_fusion.4), channel_id=1, source_target_pairs={{0,48},{16,32},{32,16},{48,0},{64,112},{80,96},{96,80},{112,64},{1... | collective-permute-start | bytes 251912 | tf_op jit(solution)/shard_map/ppermute | solution.py:565
  38.9 0.0 collective-permute-done.12
  38.9 2.9 %collective-permute-done.11 = bf16[4,64,128]{2,1,0:T(8,128)(2,1)S(1)} collective-permute-done((bf16[4,64,128]{2,1,0:T(8,128)(2,1)S(1)}, bf16[4,64,128]{2,1,0:T(8,128)(2,1)S(1)}, u32[]{:S(2)}, u32[]{:S(2)}) %collective-permute-start.11) | collective-permute-done | bytes 65568 | tf_op jit(solution)/shard_map/ppermute | solution.py:565
  41.9 1.1 %collective-permute-done.10 = bf16[328,128]{1,0:T(8,128)(2,1)S(1)} collective-permute-done((bf16[328,128]{1,0:T(8,128)(2,1)S(1)}, bf16[328,128]{1,0:T(8,128)(2,1)S(1)}, u32[]{:S(2)}, u32[]{:S(2)}) %collective-permute-start.10) | collective-permute-done | bytes 84000 | tf_op jit(solution)/shard_map/ppermute | solution.py:565
  43.1 1.1 %collective-permute-start.13 = (bf16[520,128]{1,0:T(8,128)(2,1)S(1)}, bf16[520,128]{1,0:T(8,128)(2,1)S(1)}, u32[]{:S(2)}, u32[]{:S(2)}) collective-permute-start(bf16[520,128]{1,0:T(8,128)(2,1)S(1)} %pad_maximum_fusion.3), channel_id=1, source_target_pairs={{0,3},{1,2},{2,1},{3,0},{4,7},{5,6},{6,5},{7,4},{8,11},{9,10},{10,... | collective-permute-start | bytes 399368 | tf_op jit(solution)/shard_map/ppermute | solution.py:565
  44.2 0.0 collective-permute-start.14
  44.2 4.9 %collective-permute-done.13 = bf16[520,128]{1,0:T(8,128)(2,1)S(1)} collective-permute-done((bf16[520,128]{1,0:T(8,128)(2,1)S(1)}, bf16[520,128]{1,0:T(8,128)(2,1)S(1)}, u32[]{:S(2)}, u32[]{:S(2)}) %collective-permute-start.13) | collective-permute-done | bytes 133152 | tf_op jit(solution)/shard_map/ppermute | solution.py:565
  49.2 0.0 collective-permute-done.14.near
  49.2 2.5 %collective-permute-start.15 = (bf16[520,128]{1,0:T(8,128)(2,1)S(1)}, bf16[520,128]{1,0:T(8,128)(2,1)S(1)}, u32[]{:S(2)}, u32[]{:S(2)}) collective-permute-start(bf16[520,128]{1,0:T(8,128)(2,1)S(1)} %pad_maximum_fusion.2), channel_id=1, source_target_pairs={{0,12},{1,13},{2,14},{3,15},{4,8},{5,9},{6,10},{7,11},{8,4},{9,5},... | collective-permute-start | bytes 399368 | tf_op jit(solution)/shard_map/ppermute | solution.py:565
  51.7 1.3 %inner_input.1.part = f32[512,256]{1,0:T(8,128)S(1)} custom-call(s32[1]{0:T(128)} %bitcast.1.odd.odd_x, bf16[256,256]{1,0:T(8,128)(2,1)S(1)} %get-tuple-element.35.inner, bf16[256,256]{1,0:T(8,128)(2,1)S(1)} %get-tuple-element.50.outer, bf16[4,64,128]{2,1,0:T(8,128)(2,1)S(1)} %collective-permute-done.5.core, bf16[4,64,128]{2,1,0:T(8,128)(2,1)S(1)} %get-tuple-element.56.chip, ...), custom_call_target="tpu_custom_call" | custom-call | flops 500000000 | bytes 2000000 | tf_op jit(solution)/shard_map/inner_input/pallas_call | solution.py:442
  53.0 1.4 %collective-permute-done.15 = bf16[520,128]{1,0:T(8,128)(2,1)S(1)} collective-permute-done((bf16[520,128]{1,0:T(8,128)(2,1)S(1)}, bf16[520,128]{1,0:T(8,128)(2,1)S(1)}, u32[]{:S(2)}, u32[]{:S(2)}) %collective-permute-start.15) | collective-permute-done | bytes 133152 | tf_op jit(solution)/shard_map/ppermute | solution.py:565
  54.4 0.1 collective-permute-start.16
  54.5 0.1 collective-permute-start.17
  54.6 2.5 %collective-permute-start.18 = (bf16[328,128]{1,0:T(8,128)(2,1)S(1)}, bf16[328,128]{1,0:T(8,128)(2,1)S(1)}, u32[]{:S(2)}, u32[]{:S(2)}) collective-permute-start(bf16[328,128]{1,0:T(8,128)(2,1)S(1)} %add_convert_fusion.1), channel_id=1, source_target_pairs={{0,5},{1,4},{2,7},{3,6},{4,1},{5,0},{6,3},{7,2},{8,13},{9,12},{10,... | collective-permute-start | bytes 251912 | tf_op jit(solution)/shard_map/ppermute | solution.py:565
  57.1 0.8 %collective-permute-done.17 = bf16[328,128]{1,0:T(8,128)(2,1)S(1)} collective-permute-done((bf16[328,128]{1,0:T(8,128)(2,1)S(1)}, bf16[328,128]{1,0:T(8,128)(2,1)S(1)}, u32[]{:S(2)}, u32[]{:S(2)}) %collective-permute-start.17) | collective-permute-done | bytes 84000 | tf_op jit(solution)/shard_map/ppermute | solution.py:565
  57.9 1.5 %collective-permute-done.18 = bf16[328,128]{1,0:T(8,128)(2,1)S(1)} collective-permute-done((bf16[328,128]{1,0:T(8,128)(2,1)S(1)}, bf16[328,128]{1,0:T(8,128)(2,1)S(1)}, u32[]{:S(2)}, u32[]{:S(2)}) %collective-permute-start.18) | collective-permute-done | bytes 84000 | tf_op jit(solution)/shard_map/ppermute | solution.py:565
  59.4 0.1 broadcast_select_fusion.13
  59.6 3.4 %collective-permute-start.19 = (bf16[1312,128]{1,0:T(8,128)(2,1)S(1)}, bf16[1312,128]{1,0:T(8,128)(2,1)S(1)}, u32[]{:S(2)}, u32[]{:S(2)}) collective-permute-start(bf16[1312,128]{1,0:T(8,128)(2,1)S(1)} %pad_maximum_fusion.mine), channel_id=1, source_target_pairs={{0,16},{16,0},{32,48},{48,32},{64,80},{80,64},{96,112},{112,96},{1... | collective-permute-start | bytes 1007624 | tf_op jit(solution)/shard_map/ppermute | solution.py:565
  63.0 1.4 %outer_input.1 = bf16[4,8,64,64]{3,2,1,0:T(8,128)(2,1)} custom-call(s32[1]{0:T(128)} %bitcast.odd_y, bf16[3,64,128]{2,1,0:T(8,128)(2,1)S(1)} %collective-permute-done.14.near, bf16[3,64,128]{2,1,0:T(8,128)(2,1)S(1)} %bitcast.5, bf16[3,3,3,64,64]{4,3,2,1,0:T(8,128)(2,1)S(1)} %copy-done.1, f32[512,256]{1,0:T(8,128)S(1)} %inner_input.1.part), custom_call_target="tpu_custom_call" | custom-call | flops 300000000 | bytes 4000000 | tf_op jit(solution)/shard_map/outer_input/pallas_call | solution.py:486
  64.4 1.4 %unpack.1 = (f32[3,3,3,64,64]{4,3,2,1,0:T(8,128)}, f32[3,3,3,64,128]{4,3,2,1,0:T(8,128)}) custom-call(s32[1]{0:T(128)} %bitcast.2.part.odd, bf16[1312,128]{1,0:T(8,128)(2,1)S(1)} %pad_maximum_fusion.mine, bf16[1312,128]{1,0:T(8,128)(2,1)S(1)} %collective-permute-done.19.other), custom_call_target="tpu_custom_call" | custom-call | tf_op jit(solution)/shard_map/unpack/pallas_call | solution.py:532
  (35 shorter events, 0.5 us)
Async XLA Ops:
  1.9 2.9 %collective-permute-start = (bf16[8,64,128]{2,1,0:T(8,128)(2,1)S(1)}, bf16[8,64,128]{2,1,0:T(8,128)(2,1)S(1)}, u32[]{:S(2)}, u32[]{:S(2)}) collective-permute-start(bf16[8,64,128]{2,1,0:T(8,128)(2,1)S(1)} %get-tuple-element.29), channel_id=1, source_target_pairs={{0,16},{16,0},{32,48},{48,32},{64,80},{80,64},{96,112},{112,96},{1... | collective-permute-start | bytes 393224 | tf_op jit(solution)/shard_map/ppermute | solution.py:639
  3.4 4.7 %collective-permute-start.1 = (bf16[8,64,128]{2,1,0:T(8,128)(2,1)S(1)}, bf16[8,64,128]{2,1,0:T(8,128)(2,1)S(1)}, u32[]{:S(2)}, u32[]{:S(2)}) collective-permute-start(bf16[8,64,128]{2,1,0:T(8,128)(2,1)S(1)} %get-tuple-element.30), channel_id=1, source_target_pairs={{16,32},{32,16},{48,64},{64,48},{80,96},{96,80},{112,0},{0,112},{1... | collective-permute-start | bytes 393224 | tf_op jit(solution)/shard_map/ppermute | solution.py:640
  8.1 6.4 %copy-start.3 = (bf16[3,3,3,64,128]{4,3,2,1,0:T(8,128)(2,1)S(1)}, bf16[3,3,3,64,128]{4,3,2,1,0:T(8,128)(2,1)}, u32[]{:S(2)}) copy-start(bf16[3,3,3,64,128]{4,3,2,1,0:T(8,128)(2,1)} %w_deep.3) | copy-start | bytes 1327108
  8.1 6.4 %copy-start = (bf16[4,8,64,64]{3,2,1,0:T(8,128)(2,1)S(1)}, bf16[4,8,64,64]{3,2,1,0:T(8,128)(2,1)}, u32[]{:S(2)}) copy-start(bf16[4,8,64,64]{3,2,1,0:T(8,128)(2,1)} %own.5) | copy-start | bytes 786436
  8.2 6.4 %copy-start.1 = (bf16[3,3,3,64,64]{4,3,2,1,0:T(8,128)(2,1)S(1)}, bf16[3,3,3,64,64]{4,3,2,1,0:T(8,128)(2,1)}, u32[]{:S(2)}) copy-start(bf16[3,3,3,64,64]{4,3,2,1,0:T(8,128)(2,1)} %w_up.7) | copy-start | bytes 663556
  8.3 6.3 %copy-start.2 = (bf16[2,4,64,128]{3,2,1,0:T(8,128)(2,1)S(1)}, bf16[2,4,64,128]{3,2,1,0:T(8,128)(2,1)}, u32[]{:S(2)}) copy-start(bf16[2,4,64,128]{3,2,1,0:T(8,128)(2,1)} %cot.5) | copy-start | bytes 393220
  8.3 8.8 %collective-permute-start.2 = (bf16[7,64,128]{2,1,0:T(8,128)(2,1)S(1)}, bf16[7,64,128]{2,1,0:T(8,128)(2,1)S(1)}, u32[]{:S(2)}, u32[]{:S(2)}) collective-permute-start(bf16[7,64,128]{2,1,0:T(8,128)(2,1)S(1)} %get-tuple-element.69), channel_id=1, source_target_pairs={{0,1},{1,0},{2,3},{3,2},{4,5},{5,4},{6,7},{7,6},{8,9},{9,8},{10,11... | collective-permute-start | bytes 344072 | tf_op jit(solution)/shard_map/ppermute | solution.py:639
  10.1 7.0 %collective-permute-start.3 = (bf16[7,64,128]{2,1,0:T(8,128)(2,1)S(1)}, bf16[7,64,128]{2,1,0:T(8,128)(2,1)S(1)}, u32[]{:S(2)}, u32[]{:S(2)}) collective-permute-start(bf16[7,64,128]{2,1,0:T(8,128)(2,1)S(1)} %get-tuple-element.68), channel_id=1, source_target_pairs={{1,2},{2,1},{3,4},{4,3},{5,6},{6,5},{7,8},{8,7},{9,10},{10,9},{11,... | collective-permute-start | bytes 344072 | tf_op jit(solution)/shard_map/ppermute | solution.py:640
  19.7 3.9 %collective-permute-start.4 = (bf16[1312,128]{1,0:T(8,128)(2,1)S(1)}, bf16[1312,128]{1,0:T(8,128)(2,1)S(1)}, u32[]{:S(2)}, u32[]{:S(2)}) collective-permute-start(bf16[1312,128]{1,0:T(8,128)(2,1)S(1)} %get-tuple-element.37), channel_id=1, source_target_pairs={{0,16},{16,0},{32,48},{48,32},{64,80},{80,64},{96,112},{112,96},{1... | collective-permute-start | bytes 1007624 | tf_op jit(solution)/shard_map/ppermute | solution.py:565
  22.3 1.4 %collective-permute-start.5 = (bf16[4,64,128]{2,1,0:T(8,128)(2,1)S(1)}, bf16[4,64,128]{2,1,0:T(8,128)(2,1)S(1)}, u32[]{:S(2)}, u32[]{:S(2)}) collective-permute-start(bf16[4,64,128]{2,1,0:T(8,128)(2,1)S(1)} %get-tuple-element.38), channel_id=1, source_target_pairs={{0,16},{16,0},{32,48},{48,32},{64,80},{80,64},{96,112},{112,96},{1... | collective-permute-start | bytes 196616 | tf_op jit(solution)/shard_map/ppermute | solution.py:691
  23.7 4.7 %collective-permute-start.8 = (bf16[328,128]{1,0:T(8,128)(2,1)S(1)}, bf16[328,128]{1,0:T(8,128)(2,1)S(1)}, u32[]{:S(2)}, u32[]{:S(2)}) collective-permute-start(bf16[328,128]{1,0:T(8,128)(2,1)S(1)} %get-tuple-element.64), channel_id=1, source_target_pairs={{0,5},{1,4},{2,7},{3,6},{4,1},{5,0},{6,3},{7,2},{8,13},{9,12},{10,... | collective-permute-start | bytes 251912 | tf_op jit(solution)/shard_map/ppermute | solution.py:565
  23.8 4.6 %collective-permute-start.7 = (bf16[328,128]{1,0:T(8,128)(2,1)S(1)}, bf16[328,128]{1,0:T(8,128)(2,1)S(1)}, u32[]{:S(2)}, u32[]{:S(2)}) collective-permute-start(bf16[328,128]{1,0:T(8,128)(2,1)S(1)} %get-tuple-element.65), channel_id=1, source_target_pairs={{0,4},{1,5},{2,6},{3,7},{4,0},{5,1},{6,2},{7,3},{8,12},{9,13},{10,... | collective-permute-start | bytes 251912 | tf_op jit(solution)/shard_map/ppermute | solution.py:565
  23.9 6.9 %collective-permute-start.6 = (bf16[328,128]{1,0:T(8,128)(2,1)S(1)}, bf16[328,128]{1,0:T(8,128)(2,1)S(1)}, u32[]{:S(2)}, u32[]{:S(2)}) collective-permute-start(bf16[328,128]{1,0:T(8,128)(2,1)S(1)} %get-tuple-element.63), channel_id=1, source_target_pairs={{0,1},{1,0},{2,3},{3,2},{4,5},{5,4},{6,7},{7,6},{8,9},{9,8},{10,11... | collective-permute-start | bytes 251912 | tf_op jit(solution)/shard_map/ppermute | solution.py:565
  30.9 6.2 %collective-permute-start.9 = (bf16[328,128]{1,0:T(8,128)(2,1)S(1)}, bf16[328,128]{1,0:T(8,128)(2,1)S(1)}, u32[]{:S(2)}, u32[]{:S(2)}) collective-permute-start(bf16[328,128]{1,0:T(8,128)(2,1)S(1)} %add_convert_fusion.5), channel_id=1, source_target_pairs={{0,112},{16,96},{32,80},{48,64},{64,48},{80,32},{96,16},{112,0},{1... | collective-permute-start | bytes 251912 | tf_op jit(solution)/shard_map/ppermute | solution.py:565
  33.8 5.1 %collective-permute-start.12 = (bf16[4,64,128]{2,1,0:T(8,128)(2,1)S(1)}, bf16[4,64,128]{2,1,0:T(8,128)(2,1)S(1)}, u32[]{:S(2)}, u32[]{:S(2)}) collective-permute-start(bf16[4,64,128]{2,1,0:T(8,128)(2,1)S(1)} %get-tuple-element.45), channel_id=1, source_target_pairs={{0,112},{16,96},{32,80},{48,64},{64,48},{80,32},{96,16},{112,0},{1... | collective-permute-start | bytes 196616 | tf_op jit(solution)/shard_map/ppermute | solution.py:565
  37.1 4.8 %collective-permute-start.11 = (bf16[4,64,128]{2,1,0:T(8,128)(2,1)S(1)}, bf16[4,64,128]{2,1,0:T(8,128)(2,1)S(1)}, u32[]{:S(2)}, u32[]{:S(2)}) collective-permute-start(bf16[4,64,128]{2,1,0:T(8,128)(2,1)S(1)} %get-tuple-element.45), channel_id=1, source_target_pairs={{0,48},{16,32},{32,16},{48,0},{64,112},{80,96},{96,80},{112,64},{1... | collective-permute-start | bytes 196616 | tf_op jit(solution)/shard_map/ppermute | solution.py:565
  37.2 5.9 %collective-permute-start.10 = (bf16[328,128]{1,0:T(8,128)(2,1)S(1)}, bf16[328,128]{1,0:T(8,128)(2,1)S(1)}, u32[]{:S(2)}, u32[]{:S(2)}) collective-permute-start(bf16[328,128]{1,0:T(8,128)(2,1)S(1)} %add_convert_fusion.4), channel_id=1, source_target_pairs={{0,48},{16,32},{32,16},{48,0},{64,112},{80,96},{96,80},{112,64},{1... | collective-permute-start | bytes 251912 | tf_op jit(solution)/shard_map/ppermute | solution.py:565
  43.1 6.0 %collective-permute-start.13 = (bf16[520,128]{1,0:T(8,128)(2,1)S(1)}, bf16[520,128]{1,0:T(8,128)(2,1)S(1)}, u32[]{:S(2)}, u32[]{:S(2)}) collective-permute-start(bf16[520,128]{1,0:T(8,128)(2,1)S(1)} %pad_maximum_fusion.3), channel_id=1, source_target_pairs={{0,3},{1,2},{2,1},{3,0},{4,7},{5,6},{6,5},{7,4},{8,11},{9,10},{10,... | collective-permute-start | bytes 399368 | tf_op jit(solution)/shard_map/ppermute | solution.py:565
  44.2 5.0 %collective-permute-start.14 = (bf16[3,64,128]{2,1,0:T(8,128)(2,1)S(1)}, bf16[3,64,128]{2,1,0:T(8,128)(2,1)S(1)}, u32[]{:S(2)}, u32[]{:S(2)}) collective-permute-start(bf16[3,64,128]{2,1,0:T(8,128)(2,1)S(1)} %get-tuple-element.76), channel_id=1, source_target_pairs={{0,1},{1,0},{2,3},{3,2},{4,5},{5,4},{6,7},{7,6},{8,9},{9,8},{10,11... | collective-permute-start | bytes 147464 | tf_op jit(solution)/shard_map/ppermute | solution.py:565
  49.2 5.1 %collective-permute-start.15 = (bf16[520,128]{1,0:T(8,128)(2,1)S(1)}, bf16[520,128]{1,0:T(8,128)(2,1)S(1)}, u32[]{:S(2)}, u32[]{:S(2)}) collective-permute-start(bf16[520,128]{1,0:T(8,128)(2,1)S(1)} %pad_maximum_fusion.2), channel_id=1, source_target_pairs={{0,12},{1,13},{2,14},{3,15},{4,8},{5,9},{6,10},{7,11},{8,4},{9,5},... | collective-permute-start | bytes 399368 | tf_op jit(solution)/shard_map/ppermute | solution.py:565
  54.4 5.0 %collective-permute-start.16 = (bf16[520,128]{1,0:T(8,128)(2,1)S(1)}, bf16[520,128]{1,0:T(8,128)(2,1)S(1)}, u32[]{:S(2)}, u32[]{:S(2)}) collective-permute-start(bf16[520,128]{1,0:T(8,128)(2,1)S(1)} %pad_maximum_fusion.1), channel_id=1, source_target_pairs={{0,4},{1,5},{2,6},{3,7},{4,0},{5,1},{6,2},{7,3},{8,12},{9,13},{10,... | collective-permute-start | bytes 399368 | tf_op jit(solution)/shard_map/ppermute | solution.py:565
  54.5 3.4 %collective-permute-start.17 = (bf16[328,128]{1,0:T(8,128)(2,1)S(1)}, bf16[328,128]{1,0:T(8,128)(2,1)S(1)}, u32[]{:S(2)}, u32[]{:S(2)}) collective-permute-start(bf16[328,128]{1,0:T(8,128)(2,1)S(1)} %add_convert_fusion.1), channel_id=1, source_target_pairs={{0,1},{1,0},{2,3},{3,2},{4,5},{5,4},{6,7},{7,6},{8,9},{9,8},{10,11... | collective-permute-start | bytes 251912 | tf_op jit(solution)/shard_map/ppermute | solution.py:565
  54.6 4.8 %collective-permute-start.18 = (bf16[328,128]{1,0:T(8,128)(2,1)S(1)}, bf16[328,128]{1,0:T(8,128)(2,1)S(1)}, u32[]{:S(2)}, u32[]{:S(2)}) collective-permute-start(bf16[328,128]{1,0:T(8,128)(2,1)S(1)} %add_convert_fusion.1), channel_id=1, source_target_pairs={{0,5},{1,4},{2,7},{3,6},{4,1},{5,0},{6,3},{7,2},{8,13},{9,12},{10,... | collective-permute-start | bytes 251912 | tf_op jit(solution)/shard_map/ppermute | solution.py:565
  59.6 4.8 %collective-permute-start.19 = (bf16[1312,128]{1,0:T(8,128)(2,1)S(1)}, bf16[1312,128]{1,0:T(8,128)(2,1)S(1)}, u32[]{:S(2)}, u32[]{:S(2)}) collective-permute-start(bf16[1312,128]{1,0:T(8,128)(2,1)S(1)} %pad_maximum_fusion.mine), channel_id=1, source_target_pairs={{0,16},{16,0},{32,48},{48,32},{64,80},{80,64},{96,112},{112,96},{1... | collective-permute-start | bytes 1007624 | tf_op jit(solution)/shard_map/ppermute | solution.py:565

commit v9 on v8

--- a/solution.py
+++ b/solution.py
@@ -497,28 +497,34 @@
 
 
 def unpack_kernel(
-    up_scale, deep_scale, odd, mine, other, up_out, deep_out, payload, up, deep, sems
+    up_scale, deep_scale, odd, mine, other, up_out, deep_out, up, deep, sems
 ):
-    first = pl.multiple_of(odd[0] * HALF_ROWS, HALF_ROWS)
-    payload[pl.ds(first, HALF_ROWS), :] = mine[...]
-    payload[pl.ds(HALF_ROWS - first, HALF_ROWS), :] = other[...]
+    def rows(top):
+        found = []
+        for part in range(2):
+            start = max(top - part * HALF_ROWS, 0)
+            stop = min(top + 64 - part * HALF_ROWS, HALF_ROWS)
+            if start < stop:
+                found.append(jnp.where(odd[0] == part, mine[start:stop], other[start:stop]))
+        return jnp.concatenate(found, axis=0).astype(F32)
+
     copies = []
     pairs = {}
     for a in range(3):
         for k in range(a * 9, a * 9 + 9):
             top = DEEP_ROW + k * 64
-            deep[a, k // 3 % 3, k % 3] = payload[top : top + 64, :].astype(F32) * deep_scale
+            deep[a, k // 3 % 3, k % 3] = rows(top) * deep_scale
         copies.append(pltpu.make_async_copy(deep.at[a], deep_out.at[a], sems.at[a]))
         copies[-1].start()
     for a in range(3):
         for b in range(3):
             k = a * 3 + b
-            pair = payload[k * 64 : k * 64 + 64, :].astype(F32).T * up_scale
+            pair = rows(k * 64).T * up_scale
             up[a, b, 0] = pair[:64]
             up[a, b, 1] = pair[64:]
             if k % 2 == 0:
                 top = PAIR_ROW + k // 2 * 64
-                pairs[k // 2] = payload[top : top + 64, :].astype(F32).T * up_scale
+                pairs[k // 2] = rows(top).T * up_scale
             up[a, b, 2] = pairs[k // 2][k % 2 * 64 : k % 2 * 64 + 64]
         copies.append(pltpu.make_async_copy(up.at[a], up_out.at[a], sems.at[3 + a]))
         copies[-1].start()
@@ -538,7 +544,6 @@
             jax.ShapeDtypeStruct((3, 3, 3, 64, 128), F32),
         ],
         scratch_shapes=[
-            pltpu.VMEM((PAY_ROWS, 128), BF16),
             pltpu.VMEM((3, 3, 3, 64, 64), F32),
             pltpu.VMEM((3, 3, 3, 64, 128), F32),
             pltpu.SemaphoreType.DMA((6,)),

time: 65.9 us -> 65.9 us (level)
  no operation moved by 1% of the time
where the time goes in v9:
time: 65.9 us; the launch traced here: 65.7 us
  starting transfers between devices  29 us (44%)
  waiting for transfers between devices  24.8 us (38%)
  Pallas kernels  10.3 us (16%)
  between operations  0.93 us (1%)
    ppermute x15, waiting for transfers between devices, swap(): lax.ppermute(value, axis, [(i, i ^ masks[axis]) for i in range(count)])  21.3 us
    ppermute x15, starting transfers between devices, swap(): lax.ppermute(value, axis, [(i, i ^ masks[axis]) for i in range(count)])  19.8 us
    ppermute x2, starting transfers between devices, both_sides(): odd = lax.ppermute(second, axis, pairs_of(axis, 1))  5.8 us
    ppermute x2, waiting for transfers between devices, both_sides(): odd = lax.ppermute(second, axis, pairs_of(axis, 1))  3.46 us
    ppermute x2, starting transfers between devices, both_sides(): even = lax.ppermute(first, axis, pairs_of(axis, 0))  3.3 us
    pallas_call x1, Pallas kernels, outer_grads(): pl.pallas_call(outer_kernel, in_specs=[smem] * 3 + [vmem] * 11, out_shape...  2.63 us
    pallas_call x1, Pallas kernels, inner_grads(): pl.pallas_call(inner_kernel, in_specs=[smem] + [vmem] * 6, out_shape=[jax...  2.35 us
    pallas_call x1, Pallas kernels, unpack(): pl.pallas_call(functools.partial(unpack_kernel, up_scale, deep_scale), in...  1.37 us
  transfers between devices with their start and end apart: 20, of which 12 were waited for; matrix products, arithmetic and copies ran while one was open for 0% of the time, Pallas kernels for 8%

profile of v9, /device:TPU:1, one launch (start us, length us, event | category | flops | bytes accessed | tf_op | source)
XLA Modules:
  0.0 65.7 jit_solution(77829313658356126)
XLA Ops:
  0.6 1.3 %faces.1 = (bf16[8,64,128]{2,1,0:T(8,128)(2,1)S(1)}, bf16[8,64,128]{2,1,0:T(8,128)(2,1)S(1)}, bf16[4,64,128]{2,1,0:T(8,128)(2,1)S(1)}, bf16[4,64,128]{2,1,0:T(8,128)(2,1)S(1)}) custom-call(s32[1]{0:T(128)} %bitcast.1.odd.odd_x, bf16[4,8,64,64]{3,2,1,0:T(8,128)(2,1)} %own.5, bf16[2,4,64,128]{3,2,1,0:T(8,128)(2,1)} %cot.5), custom_call_target="tpu_custom_call" | custom-call | tf_op jit(solution)/shard_map/faces/pallas_call | solution.py:113
  1.9 1.5 %collective-permute-start = (bf16[8,64,128]{2,1,0:T(8,128)(2,1)S(1)}, bf16[8,64,128]{2,1,0:T(8,128)(2,1)S(1)}, u32[]{:S(2)}, u32[]{:S(2)}) collective-permute-start(bf16[8,64,128]{2,1,0:T(8,128)(2,1)S(1)} %get-tuple-element.29), channel_id=1, source_target_pairs={{0,16},{16,0},{32,48},{48,32},{64,80},{80,64},{96,112},{112,96},{1... | collective-permute-start | bytes 393224 | tf_op jit(solution)/shard_map/ppermute | solution.py:644
  3.4 1.4 %collective-permute-start.1 = (bf16[8,64,128]{2,1,0:T(8,128)(2,1)S(1)}, bf16[8,64,128]{2,1,0:T(8,128)(2,1)S(1)}, u32[]{:S(2)}, u32[]{:S(2)}) collective-permute-start(bf16[8,64,128]{2,1,0:T(8,128)(2,1)S(1)} %get-tuple-element.30), channel_id=1, source_target_pairs={{16,32},{32,16},{48,64},{64,48},{80,96},{96,80},{112,0},{0,112},{1... | collective-permute-start | bytes 393224 | tf_op jit(solution)/shard_map/ppermute | solution.py:645
  4.8 0.0 collective-permute-done.core
  4.8 3.3 %collective-permute-done.1 = bf16[8,64,128]{2,1,0:T(8,128)(2,1)S(1)} collective-permute-done((bf16[8,64,128]{2,1,0:T(8,128)(2,1)S(1)}, bf16[8,64,128]{2,1,0:T(8,128)(2,1)S(1)}, u32[]{:S(2)}, u32[]{:S(2)}) %collective-permute-start.1) | collective-permute-done | bytes 131104 | tf_op jit(solution)/shard_map/ppermute | solution.py:645
  8.1 0.0 copy-start
  8.2 0.0 copy-start.1
  8.3 0.0 copy-start.2
  8.3 1.8 %collective-permute-start.2 = (bf16[7,64,128]{2,1,0:T(8,128)(2,1)S(1)}, bf16[7,64,128]{2,1,0:T(8,128)(2,1)S(1)}, u32[]{:S(2)}, u32[]{:S(2)}) collective-permute-start(bf16[7,64,128]{2,1,0:T(8,128)(2,1)S(1)} %get-tuple-element.69), channel_id=1, source_target_pairs={{0,1},{1,0},{2,3},{3,2},{4,5},{5,4},{6,7},{7,6},{8,9},{9,8},{10,11... | collective-permute-start | bytes 344072 | tf_op jit(solution)/shard_map/ppermute | solution.py:644
  10.1 4.4 %collective-permute-start.3 = (bf16[7,64,128]{2,1,0:T(8,128)(2,1)S(1)}, bf16[7,64,128]{2,1,0:T(8,128)(2,1)S(1)}, u32[]{:S(2)}, u32[]{:S(2)}) collective-permute-start(bf16[7,64,128]{2,1,0:T(8,128)(2,1)S(1)} %get-tuple-element.68), channel_id=1, source_target_pairs={{1,2},{2,1},{3,4},{4,3},{5,6},{6,5},{7,8},{8,7},{9,10},{10,9},{11,... | collective-permute-start | bytes 344072 | tf_op jit(solution)/shard_map/ppermute | solution.py:645
  14.6 2.4 %inner_grads.1 = (f32[9,64,256]{2,1,0:T(8,128)S(1)}, f32[27,64,128]{2,1,0:T(8,128)S(1)}, bf16[256,256]{1,0:T(8,128)(2,1)S(1)}) custom-call(s32[1]{0:T(128)} %bitcast.1.odd.odd_x, bf16[4,8,64,64]{3,2,1,0:T(8,128)(2,1)S(1)} %copy-done, bf16[2,4,64,128]{3,2,1,0:T(8,128)(2,1)S(1)} %copy-done.2, bf16[8,64,128]{2,1,0:T(8,128)(2,1)S(1)} %collective-permute-done.core, ...), custom_call_target="tpu_custom_call" | custom-call | flops 2000000000 | bytes 4000000 | tf_op jit(solution)/shard_map/inner_grads/pallas_call | solution.py:260
  16.9 0.2 collective-permute-done.3
  17.1 0.0 collective-permute-done.2.near
  17.1 2.6 %outer_grads.1 = (bf16[1312,128]{1,0:T(8,128)(2,1)S(1)}, bf16[1312,128]{1,0:T(8,128)(2,1)S(1)}, bf16[256,256]{1,0:T(8,128)(2,1)S(1)}, bf16[4,64,128]{2,1,0:T(8,1...) custom-call(s32[1]{0:T(128)} %bitcast.1.odd.odd_x, ...), custom_call_target="tpu_custom_call" | custom-call | flops 2000000000 | bytes 4000000 | tf_op jit(solution)/shard_map/outer_grads/pallas_call | solution.py:362
  19.7 2.6 %collective-permute-start.4 = (bf16[1312,128]{1,0:T(8,128)(2,1)S(1)}, bf16[1312,128]{1,0:T(8,128)(2,1)S(1)}, u32[]{:S(2)}, u32[]{:S(2)}) collective-permute-start(bf16[1312,128]{1,0:T(8,128)(2,1)S(1)} %get-tuple-element.37), channel_id=1, source_target_pairs={{0,16},{16,0},{32,48},{48,32},{64,80},{80,64},{96,112},{112,96},{1... | collective-permute-start | bytes 1007624 | tf_op jit(solution)/shard_map/ppermute | solution.py:570
  22.3 0.1 collective-permute-start.5
  22.5 1.1 %collective-permute-done.4 = bf16[1312,128]{1,0:T(8,128)(2,1)S(1)} collective-permute-done((bf16[1312,128]{1,0:T(8,128)(2,1)S(1)}, bf16[1312,128]{1,0:T(8,128)(2,1)S(1)}, u32[]{:S(2)}, u32[]{:S(2)}) %collective-permute-start.4) | collective-permute-done | bytes 335904 | tf_op jit(solution)/shard_map/ppermute | solution.py:570
  23.6 0.1 add_convert_fusion
  23.7 0.1 collective-permute-start.8
  23.8 0.1 collective-permute-start.7
  23.9 2.5 %collective-permute-start.6 = (bf16[328,128]{1,0:T(8,128)(2,1)S(1)}, bf16[328,128]{1,0:T(8,128)(2,1)S(1)}, u32[]{:S(2)}, u32[]{:S(2)}) collective-permute-start(bf16[328,128]{1,0:T(8,128)(2,1)S(1)} %get-tuple-element.63), channel_id=1, source_target_pairs={{0,1},{1,0},{2,3},{3,2},{4,5},{5,4},{6,7},{7,6},{8,9},{9,8},{10,11... | collective-permute-start | bytes 251912 | tf_op jit(solution)/shard_map/ppermute | solution.py:570
  26.5 2.0 %collective-permute-done.8 = bf16[328,128]{1,0:T(8,128)(2,1)S(1)} collective-permute-done((bf16[328,128]{1,0:T(8,128)(2,1)S(1)}, bf16[328,128]{1,0:T(8,128)(2,1)S(1)}, u32[]{:S(2)}, u32[]{:S(2)}) %collective-permute-start.8) | collective-permute-done | bytes 84000 | tf_op jit(solution)/shard_map/ppermute | solution.py:570
  28.4 0.0 collective-permute-done.7
  28.4 2.4 %collective-permute-done.6 = bf16[328,128]{1,0:T(8,128)(2,1)S(1)} collective-permute-done((bf16[328,128]{1,0:T(8,128)(2,1)S(1)}, bf16[328,128]{1,0:T(8,128)(2,1)S(1)}, u32[]{:S(2)}, u32[]{:S(2)}) %collective-permute-start.6) | collective-permute-done | bytes 84000 | tf_op jit(solution)/shard_map/ppermute | solution.py:570
  30.9 2.9 %collective-permute-start.9 = (bf16[328,128]{1,0:T(8,128)(2,1)S(1)}, bf16[328,128]{1,0:T(8,128)(2,1)S(1)}, u32[]{:S(2)}, u32[]{:S(2)}) collective-permute-start(bf16[328,128]{1,0:T(8,128)(2,1)S(1)} %add_convert_fusion.5), channel_id=1, source_target_pairs={{0,112},{16,96},{32,80},{48,64},{64,48},{80,32},{96,16},{112,0},{1... | collective-permute-start | bytes 251912 | tf_op jit(solution)/shard_map/ppermute | solution.py:570
  33.8 0.1 collective-permute-start.12
  33.9 3.2 %collective-permute-done.9 = bf16[328,128]{1,0:T(8,128)(2,1)S(1)} collective-permute-done((bf16[328,128]{1,0:T(8,128)(2,1)S(1)}, bf16[328,128]{1,0:T(8,128)(2,1)S(1)}, u32[]{:S(2)}, u32[]{:S(2)}) %collective-permute-start.9) | collective-permute-done | bytes 84000 | tf_op jit(solution)/shard_map/ppermute | solution.py:570
  37.1 0.1 collective-permute-start.11
  37.2 1.7 %collective-permute-start.10 = (bf16[328,128]{1,0:T(8,128)(2,1)S(1)}, bf16[328,128]{1,0:T(8,128)(2,1)S(1)}, u32[]{:S(2)}, u32[]{:S(2)}) collective-permute-start(bf16[328,128]{1,0:T(8,128)(2,1)S(1)} %add_convert_fusion.4), channel_id=1, source_target_pairs={{0,48},{16,32},{32,16},{48,0},{64,112},{80,96},{96,80},{112,64},{1... | collective-permute-start | bytes 251912 | tf_op jit(solution)/shard_map/ppermute | solution.py:570
  38.9 0.0 collective-permute-done.12
  38.9 2.9 %collective-permute-done.11 = bf16[4,64,128]{2,1,0:T(8,128)(2,1)S(1)} collective-permute-done((bf16[4,64,128]{2,1,0:T(8,128)(2,1)S(1)}, bf16[4,64,128]{2,1,0:T(8,128)(2,1)S(1)}, u32[]{:S(2)}, u32[]{:S(2)}) %collective-permute-start.11) | collective-permute-done | bytes 65568 | tf_op jit(solution)/shard_map/ppermute | solution.py:570
  41.9 1.1 %collective-permute-done.10 = bf16[328,128]{1,0:T(8,128)(2,1)S(1)} collective-permute-done((bf16[328,128]{1,0:T(8,128)(2,1)S(1)}, bf16[328,128]{1,0:T(8,128)(2,1)S(1)}, u32[]{:S(2)}, u32[]{:S(2)}) %collective-permute-start.10) | collective-permute-done | bytes 84000 | tf_op jit(solution)/shard_map/ppermute | solution.py:570
  43.1 1.1 %collective-permute-start.13 = (bf16[520,128]{1,0:T(8,128)(2,1)S(1)}, bf16[520,128]{1,0:T(8,128)(2,1)S(1)}, u32[]{:S(2)}, u32[]{:S(2)}) collective-permute-start(bf16[520,128]{1,0:T(8,128)(2,1)S(1)} %pad_maximum_fusion.3), channel_id=1, source_target_pairs={{0,3},{1,2},{2,1},{3,0},{4,7},{5,6},{6,5},{7,4},{8,11},{9,10},{10,... | collective-permute-start | bytes 399368 | tf_op jit(solution)/shard_map/ppermute | solution.py:570
  44.2 0.0 collective-permute-start.14
  44.2 4.9 %collective-permute-done.13 = bf16[520,128]{1,0:T(8,128)(2,1)S(1)} collective-permute-done((bf16[520,128]{1,0:T(8,128)(2,1)S(1)}, bf16[520,128]{1,0:T(8,128)(2,1)S(1)}, u32[]{:S(2)}, u32[]{:S(2)}) %collective-permute-start.13) | collective-permute-done | bytes 133152 | tf_op jit(solution)/shard_map/ppermute | solution.py:570
  49.2 0.0 collective-permute-done.14.near
  49.2 2.5 %collective-permute-start.15 = (bf16[520,128]{1,0:T(8,128)(2,1)S(1)}, bf16[520,128]{1,0:T(8,128)(2,1)S(1)}, u32[]{:S(2)}, u32[]{:S(2)}) collective-permute-start(bf16[520,128]{1,0:T(8,128)(2,1)S(1)} %pad_maximum_fusion.2), channel_id=1, source_target_pairs={{0,12},{1,13},{2,14},{3,15},{4,8},{5,9},{6,10},{7,11},{8,4},{9,5},... | collective-permute-start | bytes 399368 | tf_op jit(solution)/shard_map/ppermute | solution.py:570
  51.7 1.3 %inner_input.1.part = f32[512,256]{1,0:T(8,128)S(1)} custom-call(s32[1]{0:T(128)} %bitcast.1.odd.odd_x, bf16[256,256]{1,0:T(8,128)(2,1)S(1)} %get-tuple-element.35.inner, bf16[256,256]{1,0:T(8,128)(2,1)S(1)} %get-tuple-element.50.outer, bf16[4,64,128]{2,1,0:T(8,128)(2,1)S(1)} %collective-permute-done.5.core, bf16[4,64,128]{2,1,0:T(8,128)(2,1)S(1)} %get-tuple-element.56.chip, ...), custom_call_target="tpu_custom_call" | custom-call | flops 500000000 | bytes 2000000 | tf_op jit(solution)/shard_map/inner_input/pallas_call | solution.py:442
  53.0 1.4 %collective-permute-done.15 = bf16[520,128]{1,0:T(8,128)(2,1)S(1)} collective-permute-done((bf16[520,128]{1,0:T(8,128)(2,1)S(1)}, bf16[520,128]{1,0:T(8,128)(2,1)S(1)}, u32[]{:S(2)}, u32[]{:S(2)}) %collective-permute-start.15) | collective-permute-done | bytes 133152 | tf_op jit(solution)/shard_map/ppermute | solution.py:570
  54.4 0.1 collective-permute-start.16
  54.5 0.1 collective-permute-start.17
  54.6 2.5 %collective-permute-start.18 = (bf16[328,128]{1,0:T(8,128)(2,1)S(1)}, bf16[328,128]{1,0:T(8,128)(2,1)S(1)}, u32[]{:S(2)}, u32[]{:S(2)}) collective-permute-start(bf16[328,128]{1,0:T(8,128)(2,1)S(1)} %add_convert_fusion.1), channel_id=1, source_target_pairs={{0,5},{1,4},{2,7},{3,6},{4,1},{5,0},{6,3},{7,2},{8,13},{9,12},{10,... | collective-permute-start | bytes 251912 | tf_op jit(solution)/shard_map/ppermute | solution.py:570
  57.1 0.8 %collective-permute-done.17 = bf16[328,128]{1,0:T(8,128)(2,1)S(1)} collective-permute-done((bf16[328,128]{1,0:T(8,128)(2,1)S(1)}, bf16[328,128]{1,0:T(8,128)(2,1)S(1)}, u32[]{:S(2)}, u32[]{:S(2)}) %collective-permute-start.17) | collective-permute-done | bytes 84000 | tf_op jit(solution)/shard_map/ppermute | solution.py:570
  57.9 1.5 %collective-permute-done.18 = bf16[328,128]{1,0:T(8,128)(2,1)S(1)} collective-permute-done((bf16[328,128]{1,0:T(8,128)(2,1)S(1)}, bf16[328,128]{1,0:T(8,128)(2,1)S(1)}, u32[]{:S(2)}, u32[]{:S(2)}) %collective-permute-start.18) | collective-permute-done | bytes 84000 | tf_op jit(solution)/shard_map/ppermute | solution.py:570
  59.4 0.1 broadcast_select_fusion.13
  59.6 3.4 %collective-permute-start.19 = (bf16[1312,128]{1,0:T(8,128)(2,1)S(1)}, bf16[1312,128]{1,0:T(8,128)(2,1)S(1)}, u32[]{:S(2)}, u32[]{:S(2)}) collective-permute-start(bf16[1312,128]{1,0:T(8,128)(2,1)S(1)} %pad_maximum_fusion.mine), channel_id=1, source_target_pairs={{0,16},{16,0},{32,48},{48,32},{64,80},{80,64},{96,112},{112,96},{1... | collective-permute-start | bytes 1007624 | tf_op jit(solution)/shard_map/ppermute | solution.py:570
  63.0 1.4 %outer_input.1 = bf16[4,8,64,64]{3,2,1,0:T(8,128)(2,1)} custom-call(s32[1]{0:T(128)} %bitcast.odd_y, bf16[3,64,128]{2,1,0:T(8,128)(2,1)S(1)} %collective-permute-done.14.near, bf16[3,64,128]{2,1,0:T(8,128)(2,1)S(1)} %bitcast.5, bf16[3,3,3,64,64]{4,3,2,1,0:T(8,128)(2,1)S(1)} %copy-done.1, f32[512,256]{1,0:T(8,128)S(1)} %inner_input.1.part), custom_call_target="tpu_custom_call" | custom-call | flops 300000000 | bytes 4000000 | tf_op jit(solution)/shard_map/outer_input/pallas_call | solution.py:486
  64.4 1.4 %unpack.1 = (f32[3,3,3,64,64]{4,3,2,1,0:T(8,128)}, f32[3,3,3,64,128]{4,3,2,1,0:T(8,128)}) custom-call(s32[1]{0:T(128)} %bitcast.2.part.odd, bf16[1312,128]{1,0:T(8,128)(2,1)S(1)} %pad_maximum_fusion.mine, bf16[1312,128]{1,0:T(8,128)(2,1)S(1)} %collective-permute-done.19.other), custom_call_target="tpu_custom_call" | custom-call | tf_op jit(solution)/shard_map/unpack/pallas_call | solution.py:538
  (35 shorter events, 0.5 us)
Async XLA Ops:
  1.9 2.9 %collective-permute-start = (bf16[8,64,128]{2,1,0:T(8,128)(2,1)S(1)}, bf16[8,64,128]{2,1,0:T(8,128)(2,1)S(1)}, u32[]{:S(2)}, u32[]{:S(2)}) collective-permute-start(bf16[8,64,128]{2,1,0:T(8,128)(2,1)S(1)} %get-tuple-element.29), channel_id=1, source_target_pairs={{0,16},{16,0},{32,48},{48,32},{64,80},{80,64},{96,112},{112,96},{1... | collective-permute-start | bytes 393224 | tf_op jit(solution)/shard_map/ppermute | solution.py:644
  3.4 4.7 %collective-permute-start.1 = (bf16[8,64,128]{2,1,0:T(8,128)(2,1)S(1)}, bf16[8,64,128]{2,1,0:T(8,128)(2,1)S(1)}, u32[]{:S(2)}, u32[]{:S(2)}) collective-permute-start(bf16[8,64,128]{2,1,0:T(8,128)(2,1)S(1)} %get-tuple-element.30), channel_id=1, source_target_pairs={{16,32},{32,16},{48,64},{64,48},{80,96},{96,80},{112,0},{0,112},{1... | collective-permute-start | bytes 393224 | tf_op jit(solution)/shard_map/ppermute | solution.py:645
  8.1 6.4 %copy-start.3 = (bf16[3,3,3,64,128]{4,3,2,1,0:T(8,128)(2,1)S(1)}, bf16[3,3,3,64,128]{4,3,2,1,0:T(8,128)(2,1)}, u32[]{:S(2)}) copy-start(bf16[3,3,3,64,128]{4,3,2,1,0:T(8,128)(2,1)} %w_deep.3) | copy-start | bytes 1327108
  8.1 6.4 %copy-start = (bf16[4,8,64,64]{3,2,1,0:T(8,128)(2,1)S(1)}, bf16[4,8,64,64]{3,2,1,0:T(8,128)(2,1)}, u32[]{:S(2)}) copy-start(bf16[4,8,64,64]{3,2,1,0:T(8,128)(2,1)} %own.5) | copy-start | bytes 786436
  8.2 6.4 %copy-start.1 = (bf16[3,3,3,64,64]{4,3,2,1,0:T(8,128)(2,1)S(1)}, bf16[3,3,3,64,64]{4,3,2,1,0:T(8,128)(2,1)}, u32[]{:S(2)}) copy-start(bf16[3,3,3,64,64]{4,3,2,1,0:T(8,128)(2,1)} %w_up.7) | copy-start | bytes 663556
  8.3 6.3 %copy-start.2 = (bf16[2,4,64,128]{3,2,1,0:T(8,128)(2,1)S(1)}, bf16[2,4,64,128]{3,2,1,0:T(8,128)(2,1)}, u32[]{:S(2)}) copy-start(bf16[2,4,64,128]{3,2,1,0:T(8,128)(2,1)} %cot.5) | copy-start | bytes 393220
  8.3 8.8 %collective-permute-start.2 = (bf16[7,64,128]{2,1,0:T(8,128)(2,1)S(1)}, bf16[7,64,128]{2,1,0:T(8,128)(2,1)S(1)}, u32[]{:S(2)}, u32[]{:S(2)}) collective-permute-start(bf16[7,64,128]{2,1,0:T(8,128)(2,1)S(1)} %get-tuple-element.69), channel_id=1, source_target_pairs={{0,1},{1,0},{2,3},{3,2},{4,5},{5,4},{6,7},{7,6},{8,9},{9,8},{10,11... | collective-permute-start | bytes 344072 | tf_op jit(solution)/shard_map/ppermute | solution.py:644
  10.1 7.0 %collective-permute-start.3 = (bf16[7,64,128]{2,1,0:T(8,128)(2,1)S(1)}, bf16[7,64,128]{2,1,0:T(8,128)(2,1)S(1)}, u32[]{:S(2)}, u32[]{:S(2)}) collective-permute-start(bf16[7,64,128]{2,1,0:T(8,128)(2,1)S(1)} %get-tuple-element.68), channel_id=1, source_target_pairs={{1,2},{2,1},{3,4},{4,3},{5,6},{6,5},{7,8},{8,7},{9,10},{10,9},{11,... | collective-permute-start | bytes 344072 | tf_op jit(solution)/shard_map/ppermute | solution.py:645
  19.7 3.9 %collective-permute-start.4 = (bf16[1312,128]{1,0:T(8,128)(2,1)S(1)}, bf16[1312,128]{1,0:T(8,128)(2,1)S(1)}, u32[]{:S(2)}, u32[]{:S(2)}) collective-permute-start(bf16[1312,128]{1,0:T(8,128)(2,1)S(1)} %get-tuple-element.37), channel_id=1, source_target_pairs={{0,16},{16,0},{32,48},{48,32},{64,80},{80,64},{96,112},{112,96},{1... | collective-permute-start | bytes 1007624 | tf_op jit(solution)/shard_map/ppermute | solution.py:570
  22.3 1.4 %collective-permute-start.5 = (bf16[4,64,128]{2,1,0:T(8,128)(2,1)S(1)}, bf16[4,64,128]{2,1,0:T(8,128)(2,1)S(1)}, u32[]{:S(2)}, u32[]{:S(2)}) collective-permute-start(bf16[4,64,128]{2,1,0:T(8,128)(2,1)S(1)} %get-tuple-element.38), channel_id=1, source_target_pairs={{0,16},{16,0},{32,48},{48,32},{64,80},{80,64},{96,112},{112,96},{1... | collective-permute-start | bytes 196616 | tf_op jit(solution)/shard_map/ppermute | solution.py:696
  23.7 4.7 %collective-permute-start.8 = (bf16[328,128]{1,0:T(8,128)(2,1)S(1)}, bf16[328,128]{1,0:T(8,128)(2,1)S(1)}, u32[]{:S(2)}, u32[]{:S(2)}) collective-permute-start(bf16[328,128]{1,0:T(8,128)(2,1)S(1)} %get-tuple-element.64), channel_id=1, source_target_pairs={{0,5},{1,4},{2,7},{3,6},{4,1},{5,0},{6,3},{7,2},{8,13},{9,12},{10,... | collective-permute-start | bytes 251912 | tf_op jit(solution)/shard_map/ppermute | solution.py:570
  23.8 4.6 %collective-permute-start.7 = (bf16[328,128]{1,0:T(8,128)(2,1)S(1)}, bf16[328,128]{1,0:T(8,128)(2,1)S(1)}, u32[]{:S(2)}, u32[]{:S(2)}) collective-permute-start(bf16[328,128]{1,0:T(8,128)(2,1)S(1)} %get-tuple-element.65), channel_id=1, source_target_pairs={{0,4},{1,5},{2,6},{3,7},{4,0},{5,1},{6,2},{7,3},{8,12},{9,13},{10,... | collective-permute-start | bytes 251912 | tf_op jit(solution)/shard_map/ppermute | solution.py:570
  23.9 6.9 %collective-permute-start.6 = (bf16[328,128]{1,0:T(8,128)(2,1)S(1)}, bf16[328,128]{1,0:T(8,128)(2,1)S(1)}, u32[]{:S(2)}, u32[]{:S(2)}) collective-permute-start(bf16[328,128]{1,0:T(8,128)(2,1)S(1)} %get-tuple-element.63), channel_id=1, source_target_pairs={{0,1},{1,0},{2,3},{3,2},{4,5},{5,4},{6,7},{7,6},{8,9},{9,8},{10,11... | collective-permute-start | bytes 251912 | tf_op jit(solution)/shard_map/ppermute | solution.py:570
  30.9 6.2 %collective-permute-start.9 = (bf16[328,128]{1,0:T(8,128)(2,1)S(1)}, bf16[328,128]{1,0:T(8,128)(2,1)S(1)}, u32[]{:S(2)}, u32[]{:S(2)}) collective-permute-start(bf16[328,128]{1,0:T(8,128)(2,1)S(1)} %add_convert_fusion.5), channel_id=1, source_target_pairs={{0,112},{16,96},{32,80},{48,64},{64,48},{80,32},{96,16},{112,0},{1... | collective-permute-start | bytes 251912 | tf_op jit(solution)/shard_map/ppermute | solution.py:570
  33.8 5.1 %collective-permute-start.12 = (bf16[4,64,128]{2,1,0:T(8,128)(2,1)S(1)}, bf16[4,64,128]{2,1,0:T(8,128)(2,1)S(1)}, u32[]{:S(2)}, u32[]{:S(2)}) collective-permute-start(bf16[4,64,128]{2,1,0:T(8,128)(2,1)S(1)} %get-tuple-element.45), channel_id=1, source_target_pairs={{0,112},{16,96},{32,80},{48,64},{64,48},{80,32},{96,16},{112,0},{1... | collective-permute-start | bytes 196616 | tf_op jit(solution)/shard_map/ppermute | solution.py:570
  37.1 4.8 %collective-permute-start.11 = (bf16[4,64,128]{2,1,0:T(8,128)(2,1)S(1)}, bf16[4,64,128]{2,1,0:T(8,128)(2,1)S(1)}, u32[]{:S(2)}, u32[]{:S(2)}) collective-permute-start(bf16[4,64,128]{2,1,0:T(8,128)(2,1)S(1)} %get-tuple-element.45), channel_id=1, source_target_pairs={{0,48},{16,32},{32,16},{48,0},{64,112},{80,96},{96,80},{112,64},{1... | collective-permute-start | bytes 196616 | tf_op jit(solution)/shard_map/ppermute | solution.py:570
  37.2 5.9 %collective-permute-start.10 = (bf16[328,128]{1,0:T(8,128)(2,1)S(1)}, bf16[328,128]{1,0:T(8,128)(2,1)S(1)}, u32[]{:S(2)}, u32[]{:S(2)}) collective-permute-start(bf16[328,128]{1,0:T(8,128)(2,1)S(1)} %add_convert_fusion.4), channel_id=1, source_target_pairs={{0,48},{16,32},{32,16},{48,0},{64,112},{80,96},{96,80},{112,64},{1... | collective-permute-start | bytes 251912 | tf_op jit(solution)/shard_map/ppermute | solution.py:570
  43.1 6.0 %collective-permute-start.13 = (bf16[520,128]{1,0:T(8,128)(2,1)S(1)}, bf16[520,128]{1,0:T(8,128)(2,1)S(1)}, u32[]{:S(2)}, u32[]{:S(2)}) collective-permute-start(bf16[520,128]{1,0:T(8,128)(2,1)S(1)} %pad_maximum_fusion.3), channel_id=1, source_target_pairs={{0,3},{1,2},{2,1},{3,0},{4,7},{5,6},{6,5},{7,4},{8,11},{9,10},{10,... | collective-permute-start | bytes 399368 | tf_op jit(solution)/shard_map/ppermute | solution.py:570
  44.2 5.0 %collective-permute-start.14 = (bf16[3,64,128]{2,1,0:T(8,128)(2,1)S(1)}, bf16[3,64,128]{2,1,0:T(8,128)(2,1)S(1)}, u32[]{:S(2)}, u32[]{:S(2)}) collective-permute-start(bf16[3,64,128]{2,1,0:T(8,128)(2,1)S(1)} %get-tuple-element.76), channel_id=1, source_target_pairs={{0,1},{1,0},{2,3},{3,2},{4,5},{5,4},{6,7},{7,6},{8,9},{9,8},{10,11... | collective-permute-start | bytes 147464 | tf_op jit(solution)/shard_map/ppermute | solution.py:570
  49.2 5.1 %collective-permute-start.15 = (bf16[520,128]{1,0:T(8,128)(2,1)S(1)}, bf16[520,128]{1,0:T(8,128)(2,1)S(1)}, u32[]{:S(2)}, u32[]{:S(2)}) collective-permute-start(bf16[520,128]{1,0:T(8,128)(2,1)S(1)} %pad_maximum_fusion.2), channel_id=1, source_target_pairs={{0,12},{1,13},{2,14},{3,15},{4,8},{5,9},{6,10},{7,11},{8,4},{9,5},... | collective-permute-start | bytes 399368 | tf_op jit(solution)/shard_map/ppermute | solution.py:570
  54.4 5.0 %collective-permute-start.16 = (bf16[520,128]{1,0:T(8,128)(2,1)S(1)}, bf16[520,128]{1,0:T(8,128)(2,1)S(1)}, u32[]{:S(2)}, u32[]{:S(2)}) collective-permute-start(bf16[520,128]{1,0:T(8,128)(2,1)S(1)} %pad_maximum_fusion.1), channel_id=1, source_target_pairs={{0,4},{1,5},{2,6},{3,7},{4,0},{5,1},{6,2},{7,3},{8,12},{9,13},{10,... | collective-permute-start | bytes 399368 | tf_op jit(solution)/shard_map/ppermute | solution.py:570
  54.5 3.4 %collective-permute-start.17 = (bf16[328,128]{1,0:T(8,128)(2,1)S(1)}, bf16[328,128]{1,0:T(8,128)(2,1)S(1)}, u32[]{:S(2)}, u32[]{:S(2)}) collective-permute-start(bf16[328,128]{1,0:T(8,128)(2,1)S(1)} %add_convert_fusion.1), channel_id=1, source_target_pairs={{0,1},{1,0},{2,3},{3,2},{4,5},{5,4},{6,7},{7,6},{8,9},{9,8},{10,11... | collective-permute-start | bytes 251912 | tf_op jit(solution)/shard_map/ppermute | solution.py:570
  54.6 4.8 %collective-permute-start.18 = (bf16[328,128]{1,0:T(8,128)(2,1)S(1)}, bf16[328,128]{1,0:T(8,128)(2,1)S(1)}, u32[]{:S(2)}, u32[]{:S(2)}) collective-permute-start(bf16[328,128]{1,0:T(8,128)(2,1)S(1)} %add_convert_fusion.1), channel_id=1, source_target_pairs={{0,5},{1,4},{2,7},{3,6},{4,1},{5,0},{6,3},{7,2},{8,13},{9,12},{10,... | collective-permute-start | bytes 251912 | tf_op jit(solution)/shard_map/ppermute | solution.py:570
  59.6 4.8 %collective-permute-start.19 = (bf16[1312,128]{1,0:T(8,128)(2,1)S(1)}, bf16[1312,128]{1,0:T(8,128)(2,1)S(1)}, u32[]{:S(2)}, u32[]{:S(2)}) collective-permute-start(bf16[1312,128]{1,0:T(8,128)(2,1)S(1)} %pad_maximum_fusion.mine), channel_id=1, source_target_pairs={{0,16},{16,0},{32,48},{48,32},{64,80},{80,64},{96,112},{112,96},{1... | collective-permute-start | bytes 1007624 | tf_op jit(solution)/shard_map/ppermute | solution.py:570
